TPU v7x, 32 devices: a whole 2x2x4 slice. The times are simulated.
32 devices in a mesh: ta: 4 (over y, x), ha: 2 (over core), wa: 4 (over z).
Axes of the slice: x: 2, y: 2, z: 4, core: 2. Of those that a mesh axis runs over, the one named last changes fastest.
Arguments:
- queries: bfloat16 [12, 8, 32, 1536], P('ta', 'ha', 'wa'), may hold values from -6 to 6
- keys: bfloat16 [12, 8, 32, 1536], P('ta', 'ha', 'wa'), may hold values from -6 to 6
- values: bfloat16 [12, 8, 32, 1536], P('ta', 'ha', 'wa'), may hold values from -6 to 6
- radius: int32 [12, 3], replicated, may hold values from 0 to 1
- out_weight: bfloat16 [1536, 3072], P(('ha', 'wa')), may hold values from -0.15625 to 0.15625
Outputs:
- mixed_out: bfloat16 [12, 8, 32, 3072], P('ta', 'ha', 'wa')
All inputs are finite; a program needn't handle non-finite values.
Results may differ from a plain program's by a relative error of at most 0.0057.
Values may be sent and summed in bfloat16 or wider, within the bound.
No kernel may reach another device: no remote copies, remote signals or barrier semaphores. Data moves between devices by JAX's collectives and lax.ppermute only.
A program may use at most 128 MiB of HBM per device.

v0:
```python
import math

import jax
import jax.numpy as jnp
from jax import lax
from jax.sharding import PartitionSpec as P

D = 3072
TILE = 4


def padded(block, sides, width):
    for axis, dim in sides:
        count = lax.axis_size(axis)
        forward = [(i, i + 1) for i in range(count - 1)]
        backward = [(target, source) for source, target in forward]
        low = lax.ppermute(
            lax.slice_in_dim(block, block.shape[dim] - width, None, axis=dim), axis, forward
        )
        high = lax.ppermute(lax.slice_in_dim(block, 0, width, axis=dim), axis, backward)
        block = jnp.concatenate([low, block, high], axis=dim)
    return block


def shifted(value, axis, steps):
    count = lax.axis_size(axis)
    initial, last = (max(0, -steps), min(count, count - steps))
    return lax.ppermute(value, axis, [(source, source + steps) for source in range(initial, last)])


def allow_axis(base_index, count, margin, tile_len, total, reach):
    query_pos = base_index + jnp.arange(count, dtype=jnp.int32)
    key_pos = base_index - margin + jnp.arange(count + 2 * margin, dtype=jnp.int32)
    inside = (key_pos >= 0) & (key_pos < total)
    apart = jnp.abs(query_pos[:, None] // tile_len - key_pos[None, :] // tile_len)
    return (apart[None, :, :] <= reach[:, None, None]) & inside[None, None, :]


def shards(queries, keys, values, radius, out_weight):
    frame_count, row_count, column_count, features = queries.shape
    head_count = radius.shape[0]
    head_dim = features // head_count
    stacked = jnp.stack([keys, values])
    spread = padded(stacked, (("ha", 2), ("wa", 3)), TILE)
    earlier = shifted(spread[:, frame_count - 1 :], "ta", 1)
    later_frame = shifted(spread[:, :1], "ta", -1)
    window = jnp.concatenate([earlier, spread, later_frame], axis=1)
    allow_t = allow_axis(
        lax.axis_index("ta") * frame_count,
        frame_count,
        1,
        1,
        frame_count * lax.axis_size("ta"),
        radius[:, 0],
    )
    allow_h = allow_axis(
        lax.axis_index("ha") * row_count,
        row_count,
        TILE,
        TILE,
        row_count * lax.axis_size("ha"),
        radius[:, 1],
    )
    allow_w = allow_axis(
        lax.axis_index("wa") * column_count,
        column_count,
        TILE,
        TILE,
        column_count * lax.axis_size("wa"),
        radius[:, 2],
    )
    allowed = (
        allow_t[:, :, None, None, :, None, None]
        & allow_h[:, None, :, None, None, :, None]
        & allow_w[:, None, None, :, None, None, :]
    )
    query_count = frame_count * row_count * column_count
    allowed = allowed.reshape(head_count, query_count, -1)
    query_rows = queries.reshape(query_count, head_count, head_dim)
    key_rows = window[0].reshape(-1, head_count, head_dim)
    value_rows = window[1].reshape(-1, head_count, head_dim)
    scores = jnp.einsum(
        "qhd,khd->hqk", query_rows, key_rows, preferred_element_type=jnp.float32
    ) * (1.0 / math.sqrt(head_dim))
    scores = jnp.where(allowed, scores, -jnp.inf)
    biggest = jnp.max(scores, axis=-1, keepdims=True)
    expo = jnp.exp(scores - biggest)
    probs = (expo / jnp.sum(expo, axis=-1, keepdims=True)).astype(jnp.bfloat16)
    attended = jnp.einsum(
        "hqk,khd->qhd", probs, value_rows, preferred_element_type=jnp.float32
    ).astype(jnp.bfloat16)
    attended = attended.reshape(query_count, features)
    summed = jnp.dot(
        attended,
        lax.all_gather(out_weight, ("ha", "wa"), axis=0, tiled=True),
        preferred_element_type=jnp.float32,
    )
    result = summed.astype(jnp.bfloat16)
    return result.reshape(frame_count, row_count, column_count, D)


def solution(mesh):
    return jax.shard_map(
        shards,
        mesh=mesh,
        in_specs=(
            P("ta", "ha", "wa", None),
            P("ta", "ha", "wa", None),
            P("ta", "ha", "wa", None),
            P(),
            P(("ha", "wa"), None),
        ),
        out_specs=P("ta", "ha", "wa", None),
        check_vma=False,
    )
```

profile of v0, /device:TPU:0, one launch (start us, length us, event | category | flops | bytes accessed | tf_op | source)
XLA Modules:
  0.0 187.3 jit_solution(15822220043068717567)
XLA Ops:
  7.3 1.1 pad_maximum_fusion.8
  8.4 2.4 %collective-permute-start = (bf16[2,3,4,8,1536]{4,3,2,1,0:T(8,128)(2,1)S(1)}, bf16[2,3,4,8,1536]{4,3,2,1,0:T(8,128)(2,1)S(1)}, u32[]{:S(2)}, u32[]{:S(2)}) collective-permute-start(bf16[2,3,4,8,1536]{4,3,2,1,0:T(8,128)(2,1)S(1)} %pad_maximum_fusion.8), channel_id=1, source_target_pairs={{0,4},{1,5},{2,6},{3,7},{8,12},{9,13},{10,14},{11,15},{16,20},{17,... | collective-permute-start | bytes 1769480 | tf_op jit(solution)/shard_map/ppermute | solution.py:17
  10.8 1.3 collective-permute-start.1
  12.8 0.8 slice_bitcast_fusion.2
  13.6 1.9 %reshape.315 = bf16[96,12,128]{2,1,0:T(8,128)(2,1)} reshape(bf16[3,4,8,1536]{3,2,1,0:T(8,128)(2,1)} %param.5) | data formatting | bytes 589824 | tf_op jit(solution)/shard_map/reshape | solution.py:79
  16.6 4.4 %collective-permute-start.2 = (bf16[2,3,12,4,1536]{4,3,2,1,0:T(4,128)(2,1)S(1)}, bf16[2,3,12,4,1536]{4,3,2,1,0:T(4,128)(2,1)S(1)}, u32[]{:S(2)}, u32[]{:S(2)}) collective-permute-start(bf16[2,3,12,4,1536]{4,3,2,1,0:T(4,128)(2,1)S(1)} %get-tuple-element.9), channel_id=1, source_target_pairs={{0,1},{1,2},{2,3},{4,5},{5,6},{6,7},{8,9},{9,10},{10,11},{12,13},{... | collective-permute-start | bytes 2654216 | tf_op jit(solution)/shard_map/ppermute | solution.py:17
  21.0 1.3 collective-permute-start.3
  22.7 37.0 %collective-permute-done.2 = bf16[2,3,12,4,1536]{4,3,2,1,0:T(4,128)(2,1)S(1)} collective-permute-done((bf16[2,3,12,4,1536]{4,3,2,1,0:T(4,128)(2,1)S(1)}, bf16[2,3,12,4,1536]{4,3,2,1,0:T(4,128)(2,1)S(1)}, u32[]{:S(2)}, u32[]{:S(2)}) %collective-permute-start.2) | collective-permute-done | bytes 884768 | tf_op jit(solution)/shard_map/ppermute | solution.py:17
  59.7 23.7 %collective-permute-done.3 = bf16[2,3,12,4,1536]{4,3,2,1,0:T(4,128)(2,1)S(1)} collective-permute-done((bf16[2,3,12,4,1536]{4,3,2,1,0:T(4,128)(2,1)S(1)}, bf16[2,3,12,4,1536]{4,3,2,1,0:T(4,128)(2,1)S(1)}, u32[]{:S(2)}, u32[]{:S(2)}) %collective-permute-start.3) | collective-permute-done | bytes 884768 | tf_op jit(solution)/shard_map/ppermute | solution.py:20
  83.4 2.8 %pad_maximum_fusion.7 = (bf16[2,1,12,16,1536]{4,3,2,1,0:T(8,128)(2,1)}, bf16[2,1,12,16,1536]{4,3,2,1,0:T(8,128)(2,1)}) fusion(bf16[2,3,12,4,1536]{4,3,2,1,0:T(4,128)(2,1)S(1)} %collective-permute-done.3, bf16[2,3,12,4,1536]{4,3,2,1,0:T(4,128)(2,1)S(1)} %collective-permute-done.2, bf16[2,3,4,8,1536]{4,3,2,1,0:T(8,128)(2,1)S(1)} %collective-permute-done.1, ...), kind=kLoop, calls=%fused_computation.21 | loop fusion | flops 14155776 | bytes 5898240 | tf_op jit(solution)/shard_map/slice | solution.py:45
  86.2 4.4 %collective-permute-start.4 = (bf16[2,1,12,16,1536]{4,3,2,1,0:T(8,128)(2,1)}, bf16[2,1,12,16,1536]{4,3,2,1,0:T(8,128)(2,1)}, u32[]{:S(2)}, u32[]{:S(2)}) collective-permute-start(bf16[2,1,12,16,1536]{4,3,2,1,0:T(8,128)(2,1)} %get-tuple-element.7), channel_id=1, source_target_pairs={{0,8},{8,16},{16,24},{1,9},{9,17},{17,25},{2,10},{10,18},{18,26},{... | collective-permute-start | bytes 3538952 | tf_op jit(solution)/shard_map/ppermute | solution.py:28
  90.6 1.5 collective-permute-start.5
  92.1 7.1 %broadcast_and_fusion = pred[12,3,4,8,5,12,16]{6,5,4,3,2,1,0:T(8,128)(4,1)} fusion(pred[12,8,16]{2,1,0:T(8,128)(4,1)S(1)} %compare_and_fusion, pred[12,3,4,5,12]{4,3,2,1,0:T(8,128)(4,1)S(1)} %broadcast_and_fusion.1), kind=kLoop, calls=%fused_computation.1 | loop fusion | flops 1105920 | bytes 1116096 | tf_op jit(solution)/shard_map/and | solution.py:73
  99.1 20.0 %and.188 = pred[12,96,960]{2,1,0:T(32,128)(4,1)} reshape(pred[12,3,4,8,5,12,16]{6,5,4,3,2,1,0:T(8,128)(4,1)} %broadcast_and_fusion) | data formatting | bytes 2211840 | tf_op jit(solution)/shard_map/and | solution.py:73
  119.1 23.6 %collective-permute-done.5 = bf16[2,1,12,16,1536]{4,3,2,1,0:T(8,128)(2,1)} collective-permute-done((bf16[2,1,12,16,1536]{4,3,2,1,0:T(8,128)(2,1)}, bf16[2,1,12,16,1536]{4,3,2,1,0:T(8,128)(2,1)}, u32[]{:S(2)}, u32[]{:S(2)}) %collective-permute-start.5) | collective-permute-done | bytes 1179680 | tf_op jit(solution)/shard_map/ppermute | solution.py:28
  142.6 4.4 %pad_maximum_fusion = bf16[2,5,12,16,1536]{4,3,2,1,0:T(8,128)(2,1)S(1)} fusion(bf16[2,1,12,16,1536]{4,3,2,1,0:T(8,128)(2,1)} %collective-permute-done.5, bf16[2,3,12,4,1536]{4,3,2,1,0:T(4,128)(2,1)S(1)} %collective-permute-done.3, bf16[2,3,4,8,1536]{4,3,2,1,0:T(8,128)(2,1)S(1)} %collective-permute-done.1, bf16[1,3,4,8,1536]{4,3,2,1,0:T(8,128)(2,1)S(1)} %bitcast.36, ...), kind=kLoop, calls=%fused_computation.2 | loop fusion | flops 47185920 | bytes 11796480 | tf_op jit(solution)/shard_map/concatenate | solution.py:47
  147.1 2.2 %fusion.23 = (bf16[1,5,12,16,1536]{4,3,2,1,0:T(8,128)(2,1)}, bf16[1,5,12,16,1536]{4,3,2,1,0:T(8,128)(2,1)S(1)}) fusion(bf16[2,5,12,16,1536]{4,3,2,1,0:T(8,128)(2,1)S(1)} %pad_maximum_fusion), kind=kLoop, calls=%fused_computation.64 | loop fusion | bytes 11796480 | tf_op jit(solution)/shard_map/slice | solution.py:80
  149.3 6.5 %reshape_squeeze.7 = bf16[960,12,128]{2,1,0:T(8,128)(2,1)} reshape(bf16[1,5,12,16,1536]{4,3,2,1,0:T(8,128)(2,1)} %get-tuple-element.5) | data formatting | bytes 5898240 | tf_op jit(solution)/shard_map/reshape;squeeze | solution.py:80
  155.8 4.0 %reshape_squeeze.6 = bf16[960,12,128]{2,1,0:T(8,128)(2,1)} reshape(bf16[1,5,12,16,1536]{4,3,2,1,0:T(8,128)(2,1)S(1)} %get-tuple-element.6) | data formatting | bytes 5898240 | tf_op jit(solution)/shard_map/reshape;squeeze | solution.py:81
  159.8 4.0 %fusion.3 = f32[12,960,96]{1,2,0:T(8,128)S(1)} fusion(bf16[960,12,128]{2,1,0:T(8,128)(2,1)} %reshape_squeeze.7, bf16[96,12,128]{2,1,0:T(8,128)(2,1)S(1)} %copy-done.3), kind=kOutput, calls=%fused_computation.9 | convolution fusion | flops 283115520 | bytes 7667712 | tf_op jit(solution)/shard_map/qhd,khd->hqk/dot_general | solution.py:82
  163.9 2.1 %copy-done.2 = f32[12,960,96]{1,2,0:T(8,128)} copy-done((f32[12,960,96]{1,2,0:T(8,128)}, f32[12,960,96]{1,2,0:T(8,128)S(1)}, u32[]{:S(2)}) %copy-start.2) | copy-done | bytes 4423704
  166.0 1.7 fusion.25
  167.7 6.6 %fusion.11 = bf16[12,12,8,128]{3,2,1,0:T(8,128)(2,1)S(1)} fusion(bf16[960,12,128]{2,1,0:T(8,128)(2,1)} %reshape_squeeze.6, f32[12,96]{1,0:T(8,128)S(1)} %fusion.25, pred[12,96,960]{2,1,0:T(32,128)(4,1)S(1)} %copy-done.4, f32[12,960,96]{1,2,0:T(8,128)} %copy-done.2), kind=kOutput, calls=%fused_computation.22 | convolution fusion | flops 288794688 | bytes 8778240 | tf_op jit(solution)/shard_map/hqk,khd->qhd/dot_general | solution.py:89
  174.3 6.1 %convolution_convert_fusion = bf16[96,3072]{1,0:T(8,128)(2,1)} fusion(bf16[1536,3072]{1,0:T(8,128)(2,1)} %all-gather.2.cloned.1.call-done, bf16[12,12,8,128]{3,2,1,0:T(8,128)(2,1)S(1)} %fusion.11), kind=kOutput, calls=%fused_computation.6 | convolution fusion | flops 906264576 | bytes 10321920 | tf_op jit(solution)/shard_map/dot_general | solution.py:93
  (35 shorter events, 2.9 us)
Async XLA Ops:
  6.5 9.2 %copy-start.1 = (bf16[3,4,8,1536]{3,2,1,0:T(8,128)(2,1)S(1)}, bf16[3,4,8,1536]{3,2,1,0:T(8,128)(2,1)}, u32[]{:S(2)}) copy-start(bf16[3,4,8,1536]{3,2,1,0:T(8,128)(2,1)} %param.6) | copy-start | bytes 884740
  6.5 9.2 %copy-start = (bf16[3,4,8,1536]{3,2,1,0:T(8,128)(2,1)S(1)}, bf16[3,4,8,1536]{3,2,1,0:T(8,128)(2,1)}, u32[]{:S(2)}) copy-start(bf16[3,4,8,1536]{3,2,1,0:T(8,128)(2,1)} %param.7) | copy-start | bytes 884740
  6.5 167.8 %all-gather.2.cloned.1.call-start = ((), (), s32[]{:S(2)}) async-start(), calls=%async_computation | async-start | bytes 10616832 | tf_op jit(solution)/shard_map/all_gather | solution.py:95
  8.4 7.3 %collective-permute-start = (bf16[2,3,4,8,1536]{4,3,2,1,0:T(8,128)(2,1)S(1)}, bf16[2,3,4,8,1536]{4,3,2,1,0:T(8,128)(2,1)S(1)}, u32[]{:S(2)}, u32[]{:S(2)}) collective-permute-start(bf16[2,3,4,8,1536]{4,3,2,1,0:T(8,128)(2,1)S(1)} %pad_maximum_fusion.8), channel_id=1, source_target_pairs={{0,4},{1,5},{2,6},{3,7},{8,12},{9,13},{10,14},{11,15},{16,20},{17,... | collective-permute-start | bytes 1769480 | tf_op jit(solution)/shard_map/ppermute | solution.py:17
  10.8 4.9 %collective-permute-start.1 = (bf16[2,3,4,8,1536]{4,3,2,1,0:T(8,128)(2,1)S(1)}, bf16[2,3,4,8,1536]{4,3,2,1,0:T(8,128)(2,1)S(1)}, u32[]{:S(2)}, u32[]{:S(2)}) collective-permute-start(bf16[2,3,4,8,1536]{4,3,2,1,0:T(8,128)(2,1)S(1)} %pad_maximum_fusion.8), channel_id=1, source_target_pairs={{4,0},{5,1},{6,2},{7,3},{12,8},{13,9},{14,10},{15,11},{20,16},{21,... | collective-permute-start | bytes 1769480 | tf_op jit(solution)/shard_map/ppermute | solution.py:20
  15.7 6.6 %copy-start.5 = (s32[5]{0:T(128)S(1)}, s32[5]{0:T(128)}, u32[]{:S(2)}) copy-start(s32[5]{0:T(128)} %iota_add_fusion.2) | copy-start | bytes 64
  16.6 43.1 %collective-permute-start.2 = (bf16[2,3,12,4,1536]{4,3,2,1,0:T(4,128)(2,1)S(1)}, bf16[2,3,12,4,1536]{4,3,2,1,0:T(4,128)(2,1)S(1)}, u32[]{:S(2)}, u32[]{:S(2)}) collective-permute-start(bf16[2,3,12,4,1536]{4,3,2,1,0:T(4,128)(2,1)S(1)} %get-tuple-element.9), channel_id=1, source_target_pairs={{0,1},{1,2},{2,3},{4,5},{5,6},{6,7},{8,9},{9,10},{10,11},{12,13},{... | collective-permute-start | bytes 2654216 | tf_op jit(solution)/shard_map/ppermute | solution.py:17
  21.0 62.4 %collective-permute-start.3 = (bf16[2,3,12,4,1536]{4,3,2,1,0:T(4,128)(2,1)S(1)}, bf16[2,3,12,4,1536]{4,3,2,1,0:T(4,128)(2,1)S(1)}, u32[]{:S(2)}, u32[]{:S(2)}) collective-permute-start(bf16[2,3,12,4,1536]{4,3,2,1,0:T(4,128)(2,1)S(1)} %get-tuple-element.10), channel_id=1, source_target_pairs={{1,0},{2,1},{3,2},{5,4},{6,5},{7,6},{9,8},{10,9},{11,10},{13,12},{... | collective-permute-start | bytes 2654216 | tf_op jit(solution)/shard_map/ppermute | solution.py:20
  86.2 32.9 %collective-permute-start.4 = (bf16[2,1,12,16,1536]{4,3,2,1,0:T(8,128)(2,1)}, bf16[2,1,12,16,1536]{4,3,2,1,0:T(8,128)(2,1)}, u32[]{:S(2)}, u32[]{:S(2)}) collective-permute-start(bf16[2,1,12,16,1536]{4,3,2,1,0:T(8,128)(2,1)} %get-tuple-element.7), channel_id=1, source_target_pairs={{0,8},{8,16},{16,24},{1,9},{9,17},{17,25},{2,10},{10,18},{18,26},{... | collective-permute-start | bytes 3538952 | tf_op jit(solution)/shard_map/ppermute | solution.py:28
  90.6 52.0 %collective-permute-start.5 = (bf16[2,1,12,16,1536]{4,3,2,1,0:T(8,128)(2,1)}, bf16[2,1,12,16,1536]{4,3,2,1,0:T(8,128)(2,1)}, u32[]{:S(2)}, u32[]{:S(2)}) collective-permute-start(bf16[2,1,12,16,1536]{4,3,2,1,0:T(8,128)(2,1)} %get-tuple-element.8), channel_id=1, source_target_pairs={{8,0},{16,8},{24,16},{9,1},{17,9},{25,17},{10,2},{18,10},{26,18},{... | collective-permute-start | bytes 3538952 | tf_op jit(solution)/shard_map/ppermute | solution.py:28
  155.8 4.0 %copy-start.3 = (bf16[96,12,128]{2,1,0:T(8,128)(2,1)S(1)}, bf16[96,12,128]{2,1,0:T(8,128)(2,1)}, u32[]{:S(2)}) copy-start(bf16[96,12,128]{2,1,0:T(8,128)(2,1)} %reshape.315) | copy-start | bytes 884740
  159.8 6.2 %copy-start.4 = (pred[12,96,960]{2,1,0:T(32,128)(4,1)S(1)}, pred[12,96,960]{2,1,0:T(32,128)(4,1)}, u32[]{:S(2)}) copy-start(pred[12,96,960]{2,1,0:T(32,128)(4,1)} %and.188) | copy-start | bytes 3317764
  163.9 2.1 %copy-start.2 = (f32[12,960,96]{1,2,0:T(8,128)}, f32[12,960,96]{1,2,0:T(8,128)S(1)}, u32[]{:S(2)}) copy-start(f32[12,960,96]{1,2,0:T(8,128)S(1)} %fusion.3) | copy-start | bytes 13271044
Sparse Core Ops, SparseCore 0:
  9.0 112.1 all-gather.1
where the time goes:
time: 188 us; the launch traced here: 187 us
  waiting for transfers between devices  85 us (45%)
  local copies, waits for them, and re-layouts  38.3 us (20%)
  other arithmetic  18.5 us (10%)
  matrix products  16.7 us (9%)
  starting transfers between devices  15.2 us (8%)
  between operations  13.6 us (7%)
    ppermute x2, waiting for transfers between devices, padded(): lax.ppermute(lax.slice_in_dim(block, block.shape[dim] - width, None, axis...  37 us
    ppermute x2, waiting for transfers between devices, padded(): lax.ppermute(lax.slice_in_dim(block, 0, width, axis=dim), axis, backward)  23.7 us
    ppermute x2, waiting for transfers between devices, shifted(): lax.ppermute(value, axis, [(source, source + steps) for source in range(i...  23.6 us
    and x1, local copies, waits for them, and re-layouts, shards(): allow_t[:, :, None, None, :, None, None]  20 us
    and x2, other arithmetic, shards(): allow_t[:, :, None, None, :, None, None]  7.21 us
    ppermute x2, starting transfers between devices, padded(): lax.ppermute(lax.slice_in_dim(block, block.shape[dim] - width, None, axis...  6.76 us
    dot_general x1, matrix products, shards(): jnp.einsum('hqk,khd->qhd', probs, value_rows, preferred_element_type=jnp....  6.58 us
    another operation x1, local copies, waits for them, and re-layouts, shards(): key_rows = window[0].reshape(-1, head_count, head_dim)  6.52 us
  transfers between devices with their start and end apart: 7, of which 3 were waited for; matrix products, arithmetic and copies ran while one was open for 35% of the time, Pallas kernels for 0%

commit v1 on v0

v1 whole, which is shorter than its diff:
```python
import functools
import math

import jax
import jax.numpy as jnp
import numpy as np
from jax import lax
from jax.experimental import pallas as pl
from jax.experimental.pallas import tpu as pltpu
from jax.sharding import PartitionSpec as P

TILE = 4
PAIR = 2
FAR = -1e30
LANES = 128
VMEM = pl.BlockSpec(memory_space=pltpu.VMEM)
SMEM = pl.BlockSpec(memory_space=pltpu.SMEM)
HBM = pl.BlockSpec(memory_space=pl.ANY)
PARAMS = pltpu.CompilerParams(vmem_limit_bytes=40 * 1024 * 1024)


def line(count, step):
    return [(i, i + step) for i in range(count) if 0 <= i + step < count]


def cycle(count, step):
    return [(i, (i + step) % count) for i in range(count)]


def code_table(rows, cols, rims):
    tile_cols = cols // TILE
    span = rows // TILE
    tables = []
    for core in range(PAIR):
        own = core * span
        other = (1 - core) * span
        query_row, query_col, key_row, key_col = [], [], [], []
        for base in (own, other):
            for row in range(rows):
                for col in range(cols):
                    query_row.append(base + row // TILE)
                    query_col.append(col // TILE)
        blocks = [(own, rows), (other, rows)] + ([(-1, TILE), (2 * span, TILE)] if rims else [])
        for tile_col in [None, -1, tile_cols]:
            for base, length in blocks:
                for c in range(tile_cols) if tile_col is None else [tile_col]:
                    for row in range(length):
                        for _ in range(TILE):
                            key_row.append(base + row // TILE)
                            key_col.append(c)
        key_row, key_col = np.array(key_row)[None], np.array(key_col)[None]
        apart_row = np.abs(np.array(query_row)[:, None] - key_row)
        apart_col = np.abs(np.array(query_col)[:, None] - key_col)
        base_code = (
            2 * (apart_row == 1)
            + 4 * (apart_col == 1)
            + 8 * ((apart_row > 1) | (apart_col > 1))
        )
        outside = [key_col < 0, key_col >= tile_cols, key_row < 0, key_row >= 2 * span]
        for bits in range(16):
            code = base_code
            for which, mask in enumerate(outside):
                if bits >> which & 1:
                    code = np.where(mask, 8, code)
            tables.append(code)
            if not rims and bits == 3:
                break
    return np.stack(tables).astype(np.int32)


def split3(x):
    high = x.astype(jnp.bfloat16)
    rest = x - high.astype(jnp.float32)
    mid = rest.astype(jnp.bfloat16)
    return high, mid, (rest - mid.astype(jnp.float32)).astype(jnp.bfloat16)


def head_bias(code, radius_ref, head):
    barred = (
        8
        + jnp.where(radius_ref[head, 1] == 0, 2, 0)
        + jnp.where(radius_ref[head, 2] == 0, 4, 0)
    )
    return jnp.where((code & barred) == 0, 0.0, FAR)


def window(parts, kind, frame, lanes):
    own, other, rims, low, high = parts
    pieces = [own[1 + kind, frame, :, lanes], other[1 + kind, frame, :, lanes]]
    if rims is not None:
        pieces.append(rims[kind, frame, :, lanes])
    pieces += [low[kind, frame, :, lanes], high[kind, frame, :, lanes]]
    return jnp.concatenate(pieces, axis=0)


def scores_of(query, key, scale):
    return (
        lax.dot_general(
            query, key, (((1,), (1,)), ((), ())), preferred_element_type=jnp.float32
        )
        * scale
    )


def unpack(refs, rims):
    refs = list(refs)
    own, other = refs[:2]
    rim = refs[2] if rims else None
    rest = refs[3 if rims else 2 :]
    return (own, other, rim, rest[0], rest[1]), rest[2:]


def guest_kernel(rims, heads, width, meta_ref, radius_ref, code_ref, *refs):
    parts, rest = unpack(refs, rims)
    before_ref, after_ref, to_before, to_after = rest
    frames = parts[0].shape[1]
    code = code_ref[...]
    scale = 1.0 / math.sqrt(width)
    first = meta_ref[0] * heads
    lane = lax.broadcasted_iota(jnp.int32, (code.shape[0], LANES), 1)
    for query_ref, out_ref, frame in ((before_ref, to_before, 0), (after_ref, to_after, frames - 1)):
        stats = jnp.zeros((code.shape[0], LANES), jnp.float32)
        for head in range(heads):
            lanes = pl.ds(head * width, width)
            bias = head_bias(code, radius_ref, first + head)
            key = window(parts, 0, frame, lanes)
            value = window(parts, 1, frame, lanes)
            score = scores_of(query_ref[:, lanes], key, scale) + bias
            top = jnp.max(score, axis=1, keepdims=True)
            expo = jnp.exp(score - top)
            total = jnp.sum(expo, axis=1, keepdims=True)
            mixed = jnp.dot(
                expo.astype(jnp.bfloat16), value, preferred_element_type=jnp.float32
            )
            out_ref[:, lanes] = (mixed / total).astype(jnp.bfloat16)
            for spot, piece in enumerate(split3(top + jnp.log(total))):
                stats = jnp.where(
                    lane == 3 * head + spot, piece.astype(jnp.float32), stats
                )
        out_ref[:, pl.ds(heads * width, LANES)] = stats.astype(jnp.bfloat16)


def host_kernel(rims, heads, width, meta_ref, radius_ref, code_ref, *refs):
    parts, rest = unpack(refs, rims)
    mixed_ref, stats_ref = rest
    own, other = parts[:2]
    frames = own.shape[1]
    code = code_ref[...]
    count = code.shape[0]
    scale = 1.0 / math.sqrt(width)
    first = meta_ref[0] * heads
    lane = lax.broadcasted_iota(jnp.int32, (count, LANES), 1)
    stats = [jnp.zeros((count, LANES), jnp.float32) for _ in range(frames)]
    for head in range(heads):
        lanes = pl.ds(head * width, width)
        bias = head_bias(code, radius_ref, first + head)
        bias_apart = jnp.where(radius_ref[first + head, 0] == 0, FAR, bias)
        query = [
            jnp.concatenate([own[0, f, :, lanes], other[0, f, :, lanes]], axis=0)
            for f in range(frames)
        ]
        score = {}
        for frame in range(frames):
            near = range(max(0, frame - 1), min(frames, frame + 2))
            block = scores_of(
                jnp.concatenate([query[f] for f in near], axis=0),
                window(parts, 0, frame, lanes),
                scale,
            )
            for spot, f in enumerate(near):
                score[f, frame] = block[spot * count : (spot + 1) * count] + (
                    bias if f == frame else bias_apart
                )
        value = [window(parts, 1, f, lanes) for f in range(frames)]
        for f in range(frames):
            near = range(max(0, f - 1), min(frames, f + 2))
            row = jnp.concatenate([score[f, g] for g in near], axis=1)
            top = jnp.max(row, axis=1, keepdims=True)
            expo = jnp.exp(row - top)
            total = jnp.sum(expo, axis=1, keepdims=True)
            mixed = jnp.dot(
                expo.astype(jnp.bfloat16),
                jnp.concatenate([value[g] for g in near], axis=0),
                preferred_element_type=jnp.float32,
            )
            mixed_ref[f, :, lanes] = mixed / total
            stats[f] = jnp.where(lane == head, top + jnp.log(total), stats[f])
    for f in range(frames):
        stats_ref[f] = stats[f]


def merge_kernel(heads, width, meta_ref, radius_ref, mixed_ref, stats_ref, before_ref, after_ref, own_out, other_out):
    frames, count, _ = mixed_ref.shape
    half = count // PAIR
    first = meta_ref[0] * heads
    tail = pl.ds(heads * width, LANES)
    for f in range(frames):
        guests = []
        if f == 0:
            guests.append((before_ref, meta_ref[1]))
        if f == frames - 1:
            guests.append((after_ref, meta_ref[2]))
        guests = [(ref, ref[:, tail].astype(jnp.float32), there) for ref, there in guests]
        for head in range(heads):
            lanes = pl.ds(head * width, width)
            mixed = mixed_ref[f, :, lanes]
            if guests:
                logs = [stats_ref[f, :, head : head + 1]]
                values = [mixed]
                for ref, stats, there in guests:
                    use = (there != 0) & (radius_ref[first + head, 0] != 0)
                    log = (
                        stats[:, 3 * head : 3 * head + 1]
                        + stats[:, 3 * head + 1 : 3 * head + 2]
                        + stats[:, 3 * head + 2 : 3 * head + 3]
                    )
                    logs.append(jnp.where(use, log, FAR))
                    values.append(ref[:, lanes].astype(jnp.float32))
                top = functools.reduce(jnp.maximum, logs)
                weights = [jnp.exp(log - top) for log in logs]
                total = functools.reduce(jnp.add, weights)
                mixed = functools.reduce(
                    jnp.add, [v * (w / total) for v, w in zip(values, weights)]
                )
            mixed = mixed.astype(jnp.bfloat16)
            own_out[f, :, lanes] = mixed[:half]
            other_out[f, :, lanes] = mixed[half:]


def project_kernel(senders, pieces, shards, meta_ref, *refs):
    own, other = refs[:2]
    received = refs[2 : 2 + senders]
    weights = refs[2 + senders : 2 + senders + pieces]
    outs = refs[2 + senders + pieces : 3 + 2 * senders + pieces]
    held, weight, sems = refs[3 + 2 * senders + pieces :]
    half = own.shape[1]
    here = pl.ds(pl.multiple_of(meta_ref[0] * half, LANES), half)
    there = pl.ds(pl.multiple_of((1 - meta_ref[0]) * half, LANES), half)
    copies = [
        (own, held.at[0, :, here]),
        (other, held.at[0, :, there]),
    ]
    for spot, ref in enumerate(received):
        copies.append((ref.at[:, pl.ds(0, half)], held.at[1 + spot, :, here]))
        copies.append((ref.at[:, pl.ds(half, half)], held.at[1 + spot, :, there]))
    n_rows, n_cols = shards
    depth = weights[0].shape[0]
    for spot, ref in enumerate(weights):
        row = lax.rem(meta_ref[1] + n_rows - spot // n_cols, n_rows)
        col = lax.rem(meta_ref[2] + n_cols - spot % n_cols, n_cols)
        begin = pl.multiple_of((row * n_cols + col) * depth, depth)
        copies.append((ref, weight.at[pl.ds(begin, depth)]))
    copies = [pltpu.make_async_copy(a, b, sems.at[i]) for i, (a, b) in enumerate(copies)]
    for copy in copies:
        copy.start()
    for copy in copies:
        copy.wait()
    for spot, out in enumerate(outs):
        out[...] = jnp.dot(
            held[spot], weight[...], preferred_element_type=jnp.float32
        ).astype(jnp.bfloat16)


def place_kernel(count, meta_ref, *refs):
    pieces, out, sems = refs[:count], refs[count], refs[count + 1]
    wide = pieces[0].shape[-1]
    copies = []
    for spot, ref in enumerate(pieces):
        origin = lax.rem(meta_ref[3] + count - spot, count)
        where = pl.ds(pl.multiple_of(origin * wide, LANES), wide)
        copies.append(pltpu.make_async_copy(ref, out.at[:, where], sems.at[spot]))
    for copy in copies:
        copy.start()
    for copy in copies:
        copy.wait()


def cost(flops, size):
    return pl.CostEstimate(flops=flops, bytes_accessed=size, transcendentals=0)


def shards(queries, keys, values, radius, out_weight):
    n_time, n_rows, n_cols = (lax.axis_size(a) for a in ("ta", "ha", "wa"))
    at_time, at_row, at_col = (lax.axis_index(a) for a in ("ta", "ha", "wa"))
    core = at_row % PAIR
    frames, rows, cols, features = queries.shape
    heads = radius.shape[0] // PAIR
    width = features // radius.shape[0]
    half = features // PAIR
    tile_cols = cols // TILE
    area = rows * cols
    rims = n_rows > PAIR

    def tiled(block):
        block = block.reshape(frames, rows, tile_cols, TILE, block.shape[-1])
        return block.transpose(0, 2, 1, 3, 4).reshape(frames, area, block.shape[-1])

    def heads_of(which):
        def cut(x):
            return lax.dynamic_slice_in_dim(x, which * half, half, axis=-1)

        return jnp.stack(
            [cut(queries).reshape(frames, area, half), tiled(cut(keys)), tiled(cut(values))]
        )

    pairs = [(i, i ^ 1) for i in range(n_rows)]
    other = lax.ppermute(heads_of(1 - core), "ha", pairs)
    own = heads_of(core)

    def frame_queries(f):
        return jnp.concatenate([own[0, f], other[0, f]], axis=0)

    guest_after = lax.ppermute(frame_queries(0), "ta", line(n_time, -1))
    guest_before = lax.ppermute(frame_queries(frames - 1), "ta", line(n_time, 1))

    blocks = [x[1:].reshape(2, frames, tile_cols, rows * TILE, half) for x in (own, other)]
    rim = None
    if rims:
        even, odd = (jnp.where(core == i, blocks[0], blocks[1]) for i in range(PAIR))
        up = lax.ppermute(odd[:, :, :, -TILE * TILE :], "ha", line(n_rows, PAIR))
        down = lax.ppermute(even[:, :, :, : TILE * TILE], "ha", line(n_rows, -PAIR))
        blocks += [up, down]
        rim = jnp.concatenate(
            [x.reshape(2, frames, -1, half) for x in (up, down)], axis=2
        )
    low = lax.ppermute(
        jnp.concatenate([x[:, :, -1] for x in blocks], axis=2), "wa", line(n_cols, 1)
    )
    high = lax.ppermute(
        jnp.concatenate([x[:, :, 0] for x in blocks], axis=2), "wa", line(n_cols, -1)
    )

    slab = features // (n_rows * n_cols)
    wide = out_weight.shape[1] // n_time
    mine = lax.dynamic_slice_in_dim(out_weight, at_time * wide, wide, axis=1)
    mine, _ = lax.optimization_barrier((mine, other))
    weights = [mine] + [lax.ppermute(mine, "wa", cycle(n_cols, s)) for s in range(1, n_cols)]
    shard_cols = n_cols
    if slab % 16:
        weights = [jnp.roll(jnp.stack(weights[::-1]), at_col + 1, axis=0).reshape(-1, wide)]
        shard_cols = 1
    for step in range(1, n_rows):
        weights += [lax.ppermute(w, "ha", cycle(n_rows, step)) for w in weights[:shard_cols]]

    table = jnp.asarray(code_table(rows, cols, rims))
    spot = jnp.where(at_col == 0, 1, 0) + jnp.where(at_col == n_cols - 1, 2, 0)
    if rims:
        spot += jnp.where(at_row < PAIR, 4, 0) + jnp.where(at_row >= n_rows - PAIR, 8, 0)
    spot += core * (table.shape[0] // PAIR)
    code = lax.dynamic_index_in_dim(table, spot, 0, keepdims=False)
    meta = jnp.stack(
        [core, jnp.where(at_time > 0, 1, 0), jnp.where(at_time < n_time - 1, 1, 0)]
    ).astype(jnp.int32)
    place = jnp.stack([core, at_row, at_col, at_time]).astype(jnp.int32)

    parts = [own, other] + ([rim] if rims else []) + [low, high]
    count = PAIR * area
    unit = 4 * heads * width * count * code.shape[1]
    payload = jax.ShapeDtypeStruct((count, half + LANES), jnp.bfloat16)
    to_before, to_after = pl.pallas_call(
        functools.partial(guest_kernel, rims, heads, width),
        out_shape=(payload, payload),
        in_specs=[SMEM, SMEM] + [VMEM] * (1 + len(parts) + 2),
        out_specs=(VMEM, VMEM),
        compiler_params=PARAMS,
        cost_estimate=cost(2 * unit, 4_000_000),
        name="guest",
    )(meta, radius, code, *parts, guest_before, guest_after)
    from_after = lax.ppermute(to_before, "ta", line(n_time, -1))
    from_before = lax.ppermute(to_after, "ta", line(n_time, 1))
    mixed, stats = pl.pallas_call(
        functools.partial(host_kernel, rims, heads, width),
        out_shape=(
            jax.ShapeDtypeStruct((frames, count, half), jnp.float32),
            jax.ShapeDtypeStruct((frames, count, LANES), jnp.float32),
        ),
        in_specs=[SMEM, SMEM] + [VMEM] * (1 + len(parts)),
        out_specs=(VMEM, VMEM),
        compiler_params=PARAMS,
        cost_estimate=cost(7 * unit, 6_000_000),
        name="host",
    )(meta, radius, code, *parts)
    att = jax.ShapeDtypeStruct((frames, area, half), jnp.bfloat16)
    kept, given = pl.pallas_call(
        functools.partial(merge_kernel, heads, width),
        out_shape=(att, att),
        in_specs=[SMEM, SMEM] + [VMEM] * 4,
        out_specs=(VMEM, VMEM),
        compiler_params=PARAMS,
        cost_estimate=cost(1000, 3_000_000),
        name="merge",
    )(meta, radius, mixed, stats, from_before, from_after)
    tokens = frames * area
    kept = kept.reshape(tokens, half)
    taken = lax.ppermute(given, "ha", pairs).reshape(tokens, half)
    whole = jnp.concatenate([kept, taken], axis=1)
    received = [lax.ppermute(whole, "ta", cycle(n_time, s)) for s in range(1, n_time)]

    copies = 2 * n_time + len(weights)
    piece = jax.ShapeDtypeStruct((tokens, wide), jnp.bfloat16)
    products = pl.pallas_call(
        functools.partial(project_kernel, n_time - 1, len(weights), (n_rows, shard_cols)),
        out_shape=(piece,) * n_time,
        in_specs=[SMEM] + [HBM] * (1 + n_time + len(weights)),
        out_specs=(VMEM,) * n_time,
        scratch_shapes=[
            pltpu.VMEM((n_time, tokens, features), jnp.bfloat16),
            pltpu.VMEM((features, wide), jnp.bfloat16),
            pltpu.SemaphoreType.DMA((copies,)),
        ],
        compiler_params=PARAMS,
        cost_estimate=cost(2 * n_time * tokens * features * wide, 6_000_000),
        name="project",
    )(place, kept, taken, *received, *weights)
    back = [products[0]] + [
        lax.ppermute(products[n_time - s], "ta", cycle(n_time, s)) for s in range(1, n_time)
    ]
    out = pl.pallas_call(
        functools.partial(place_kernel, n_time),
        out_shape=jax.ShapeDtypeStruct((tokens, wide * n_time), jnp.bfloat16),
        in_specs=[SMEM] + [HBM] * n_time,
        out_specs=HBM,
        scratch_shapes=[pltpu.SemaphoreType.DMA((n_time,))],
        compiler_params=PARAMS,
        cost_estimate=cost(1000, 1_200_000),
        name="place",
    )(place, *back)
    return out.reshape(frames, rows, cols, wide * n_time)


def solution(mesh):
    return jax.shard_map(
        shards,
        mesh=mesh,
        in_specs=(
            P("ta", "ha", "wa", None),
            P("ta", "ha", "wa", None),
            P("ta", "ha", "wa", None),
            P(),
            P(("ha", "wa"), None),
        ),
        out_specs=P("ta", "ha", "wa", None),
        check_vma=False,
    )
```

time: 188 us -> 82.4 us (0.44)
  waiting for transfers between devices: 85 us -> 29.8 us
  local copies, waits for them, and re-layouts: 38.3 us -> 4.11 us
  starting transfers between devices: 15.2 us -> 32.6 us
  other arithmetic: 18.5 us -> 1.77 us
  matrix products: 16.7 us -> 0 us
  Pallas kernels: 0 us -> 13.4 us
  between operations: 13.6 us -> 0.35 us
    ppermute x6 -> x21, waiting for transfers between devices: 84.3 us -> 29.8 us  [the longest x3 12.6 us: shards(): lax.ppermute(whole, 'ta', cycle(n_time, s))]
    and x1 -> x0, local copies, waits for them, and re-layouts: 20 us -> none  [shards(): allow_t[:, :, None, None, :, None, None]]
    ppermute x6 -> x21, starting transfers between devices: 15.2 us -> 32.6 us  [the longest x3 7.07 us: shards(): lax.ppermute(mine, 'wa', cycle(n_cols, s))]
    dot_general x3 -> x0, matrix products: 16.7 us -> none  [the longest x1 6.58 us: shards(): jnp.einsum('hqk,khd->qhd', probs, value_rows, preferred_element_type=jnp....]
    pallas_call x0 -> x5, Pallas kernels: none -> 13.4 us  [the longest x1 3.71 us: shards(): pl.pallas_call(functools.partial(guest_kernel, rims, heads, width), out_s...]
    another operation x2 -> x8, local copies, waits for them, and re-layouts: 10.6 us -> 1.35 us  [heads_of(): jnp.stack([cut(queries).reshape(frames, area, half), tiled(cut(keys)), ti...]
    and x8 -> x0, other arithmetic: 7.47 us -> none  [the longest x2 7.21 us: shards(): allow_t[:, :, None, None, :, None, None]]
    concatenate x2 -> x5, other arithmetic: 4.63 us -> 1.51 us  [the longest x1 0.74 us: shards(): jnp.concatenate([x[:, :, 0] for x in blocks], axis=2)]
  transfers between devices with their start and end apart: 7 -> 21, of which waited for: 3 -> 9; matrix products, arithmetic and copies ran while one was open for 35% -> 4% of each run, Pallas kernels for 0% -> 10%
where the time goes in v1:
time: 82.4 us; the launch traced here: 82 us
  starting transfers between devices  32.6 us (40%)
  waiting for transfers between devices  29.8 us (36%)
  Pallas kernels  13.4 us (16%)
  local copies, waits for them, and re-layouts  4.11 us (5%)
  other arithmetic  1.77 us (2%)
    ppermute x3, waiting for transfers between devices, shards(): lax.ppermute(whole, 'ta', cycle(n_time, s))  12.6 us
    ppermute x3, waiting for transfers between devices, shards(): lax.ppermute(mine, 'wa', cycle(n_cols, s))  8.27 us
    ppermute x3, starting transfers between devices, shards(): lax.ppermute(mine, 'wa', cycle(n_cols, s))  7.07 us
    ppermute x1, starting transfers between devices, shards(): lax.ppermute(frame_queries(frames - 1), 'ta', line(n_time, 1))  4.78 us
    ppermute x3, starting transfers between devices, shards(): lax.ppermute(products[n_time - s], 'ta', cycle(n_time, s))  4.7 us
    ppermute x3, waiting for transfers between devices, shards(): lax.ppermute(products[n_time - s], 'ta', cycle(n_time, s))  4.13 us
    pallas_call x1, Pallas kernels, shards(): pl.pallas_call(functools.partial(guest_kernel, rims, heads, width), out_s...  3.71 us
    ppermute x3, starting transfers between devices, shards(): lax.ppermute(whole, 'ta', cycle(n_time, s))  3.6 us
  transfers between devices with their start and end apart: 21, of which 9 were waited for; matrix products, arithmetic and copies ran while one was open for 4% of the time, Pallas kernels for 10%

profile of v1, /device:TPU:0, one launch (start us, length us, event | category | flops | bytes accessed | tf_op | source)
XLA Modules:
  0.0 82.0 jit_solution(1810560018499404375)
XLA Ops:
  1.1 1.2 %constant_dynamic-slice_fusion.1 = (bf16[3,4,8,768]{3,2,1,0:T(8,128)(2,1)S(1)}, bf16[3,4,8,768]{3,2,1,0:T(8,128)(2,1)S(1)}, bf16[3,4,8,768]{3,2,1,0:T(8,128)(2,1)S(1)}, bf16[3,4,8,768]{3,2,1,0:T(8,128)(2,1)S(1)}) fusion(bf16[3,4,8,1536]{3,2,1,0:T(8,128)(2,1)} %param.8, s32[]{:T(128)S(6)} %select_n.44, s32[]{:T(128)S(6)} %select_n.43, ...), kind=kLoop, calls=%fused_computation.21 | loop fusion | bytes 1179656 | tf_op jit(solution)/shard_map/dynamic_slice | solution.py:300
  4.7 4.8 %collective-permute-start.3 = (bf16[64,768]{1,0:T(8,128)(2,1)S(1)}, bf16[64,768]{1,0:T(8,128)(2,1)S(1)}, u32[]{:S(2)}, u32[]{:S(2)}) collective-permute-start(bf16[64,768]{1,0:T(8,128)(2,1)S(1)} %pad_maximum_fusion.5), channel_id=1, source_target_pairs={{0,8},{8,16},{16,24},{1,9},{9,17},{17,25},{2,10},{10,18},{18,26},{... | collective-permute-start | bytes 294920 | tf_op jit(solution)/shard_map/ppermute | solution.py:314
  10.2 3.5 %collective-permute-start.1 = (bf16[2,3,32,768]{3,2,1,0:T(8,128)(2,1)}, bf16[2,3,32,768]{3,2,1,0:T(8,128)(2,1)S(1)}, u32[]{:S(2)}, u32[]{:S(2)}) collective-permute-start(bf16[2,3,32,768]{3,2,1,0:T(8,128)(2,1)} %pad_maximum_fusion.2), channel_id=1, source_target_pairs={{0,1},{1,2},{2,3},{4,5},{5,6},{6,7},{8,9},{9,10},{10,11},{12,13},{... | collective-permute-start | bytes 884744 | tf_op jit(solution)/shard_map/ppermute | solution.py:326
  14.5 1.3 %collective-permute-start.2 = (bf16[2,3,32,768]{3,2,1,0:T(8,128)(2,1)}, bf16[2,3,32,768]{3,2,1,0:T(8,128)(2,1)S(1)}, u32[]{:S(2)}, u32[]{:S(2)}) collective-permute-start(bf16[2,3,32,768]{3,2,1,0:T(8,128)(2,1)} %pad_maximum_fusion.3), channel_id=1, source_target_pairs={{1,0},{2,1},{3,2},{5,4},{6,5},{7,6},{9,8},{10,9},{11,10},{13,12},{... | collective-permute-start | bytes 884744 | tf_op jit(solution)/shard_map/ppermute | solution.py:329
  15.8 1.3 %collective-permute-start.4 = (bf16[64,768]{1,0:T(8,128)(2,1)S(1)}, bf16[64,768]{1,0:T(8,128)(2,1)S(1)}, u32[]{:S(2)}, u32[]{:S(2)}) collective-permute-start(bf16[64,768]{1,0:T(8,128)(2,1)S(1)} %pad_maximum_fusion.6), channel_id=1, source_target_pairs={{8,0},{16,8},{24,16},{9,1},{17,9},{25,17},{10,2},{18,10},{26,18},{... | collective-permute-start | bytes 294920 | tf_op jit(solution)/shard_map/ppermute | solution.py:313
  17.8 4.7 %collective-permute-start.13 = (bf16[192,768]{1,0:T(8,128)(2,1)S(1)}, bf16[192,768]{1,0:T(8,128)(2,1)S(1)}, u32[]{:S(2)}, u32[]{:S(2)}) collective-permute-start(bf16[192,768]{1,0:T(8,128)(2,1)S(1)} %constant_dynamic-slice_fusion.refs_5_), channel_id=1, source_target_pairs={{0,3},{1,0},{2,1},{3,2},{4,7},{5,4},{6,5},{7,6},{8,11},{9,8},{10,9... | collective-permute-start | bytes 884744 | tf_op jit(solution)/shard_map/ppermute | solution.py:337
  22.5 2.4 %collective-permute-start.11 = (bf16[192,768]{1,0:T(8,128)(2,1)S(1)}, bf16[192,768]{1,0:T(8,128)(2,1)}, u32[]{:S(2)}, u32[]{:S(2)}) collective-permute-start(bf16[192,768]{1,0:T(8,128)(2,1)S(1)} %constant_dynamic-slice_fusion.refs_5_), channel_id=1, source_target_pairs={{0,1},{1,2},{2,3},{3,0},{4,5},{5,6},{6,7},{7,4},{8,9},{9,10},{10,1... | collective-permute-start | bytes 884744 | tf_op jit(solution)/shard_map/ppermute | solution.py:337
  25.1 1.4 %collective-permute-done.2.refs_3_ = bf16[2,3,32,768]{3,2,1,0:T(8,128)(2,1)S(1)} collective-permute-done((bf16[2,3,32,768]{3,2,1,0:T(8,128)(2,1)}, bf16[2,3,32,768]{3,2,1,0:T(8,128)(2,1)S(1)}, u32[]{:S(2)}, u32[]{:S(2)}) %collective-permute-start.2) | collective-permute-done | bytes 294944 | tf_op jit(solution)/shard_map/ppermute | solution.py:329
  26.5 3.7 %guest.1 = (bf16[64,896]{1,0:T(8,128)(2,1)S(1)}, bf16[64,896]{1,0:T(8,128)(2,1)S(1)}) custom-call(s32[3]{0:T(128)S(1)} %pad_add_fusion.1.meta_ref, s32[12,3]{1,0:T(8,128)S(1)} %copy.28.radius_ref, s32[64,128]{1,0:T(8,128)S(1)} %dynamic-slice_bitcast_fusion.2.code_ref, bf16[3,3,32,768]{3,2,1,0:T(8,128)(2,1)S(1)} %pad_maximum_fusion.refs_0_, ...), custom_call_target="tpu_custom_call" | custom-call | flops 50331648 | bytes 4000000 | tf_op jit(solution)/shard_map/guest/pallas_call | solution.py:360
  30.2 3.4 %collective-permute-start.5 = (bf16[64,896]{1,0:T(8,128)(2,1)S(1)}, bf16[64,896]{1,0:T(8,128)(2,1)S(1)}, u32[]{:S(2)}, u32[]{:S(2)}) collective-permute-start(bf16[64,896]{1,0:T(8,128)(2,1)S(1)} %get-tuple-element.18), channel_id=1, source_target_pairs={{0,8},{8,16},{16,24},{1,9},{9,17},{17,25},{2,10},{10,18},{18,26},{... | collective-permute-start | bytes 344072 | tf_op jit(solution)/shard_map/ppermute | solution.py:370
  33.6 1.3 %collective-permute-start.6 = (bf16[64,896]{1,0:T(8,128)(2,1)S(1)}, bf16[64,896]{1,0:T(8,128)(2,1)S(1)}, u32[]{:S(2)}, u32[]{:S(2)}) collective-permute-start(bf16[64,896]{1,0:T(8,128)(2,1)S(1)} %get-tuple-element.19), channel_id=1, source_target_pairs={{8,0},{16,8},{24,16},{9,1},{17,9},{25,17},{10,2},{18,10},{26,18},{... | collective-permute-start | bytes 344072 | tf_op jit(solution)/shard_map/ppermute | solution.py:369
  34.9 2.5 %host.1 = (f32[3,64,768]{2,1,0:T(8,128)S(1)}, f32[3,64,128]{2,1,0:T(8,128)S(1)}) custom-call(s32[3]{0:T(128)S(1)} %pad_add_fusion.1.meta_ref, s32[12,3]{1,0:T(8,128)S(1)} %copy.28.radius_ref, s32[64,128]{1,0:T(8,128)S(1)} %dynamic-slice_bitcast_fusion.2.code_ref, bf16[3,3,32,768]{3,2,1,0:T(8,128)(2,1)S(1)} %pad_maximum_fusion.refs_0_, ...), custom_call_target="tpu_custom_call" | custom-call | flops 176160768 | bytes 6000000 | tf_op jit(solution)/shard_map/host/pallas_call | solution.py:371
  37.5 2.8 %collective-permute-done.6.after_ref = bf16[64,896]{1,0:T(8,128)(2,1)S(1)} collective-permute-done((bf16[64,896]{1,0:T(8,128)(2,1)S(1)}, bf16[64,896]{1,0:T(8,128)(2,1)S(1)}, u32[]{:S(2)}, u32[]{:S(2)}) %collective-permute-start.6) | collective-permute-done | bytes 114720 | tf_op jit(solution)/shard_map/ppermute | solution.py:369
  40.3 2.2 %merge.1 = (bf16[3,32,768]{2,1,0:T(8,128)(2,1)S(1)}, bf16[3,32,768]{2,1,0:T(8,128)(2,1)S(1)}) custom-call(s32[3]{0:T(128)S(1)} %pad_add_fusion.1.meta_ref, s32[12,3]{1,0:T(8,128)S(1)} %copy.28.radius_ref, f32[3,64,768]{2,1,0:T(8,128)S(1)} %get-tuple-element.16.mixed_ref, f32[3,64,128]{2,1,0:T(8,128)S(1)} %get-tuple-element.17.stats_ref, ...), custom_call_target="tpu_custom_call" | custom-call | flops 1000 | bytes 3000000 | tf_op jit(solution)/shard_map/merge/pallas_call | solution.py:384
  43.2 8.3 %collective-permute-done.12.refs_7_ = bf16[192,768]{1,0:T(8,128)(2,1)} collective-permute-done((bf16[192,768]{1,0:T(8,128)(2,1)S(1)}, bf16[192,768]{1,0:T(8,128)(2,1)}, u32[]{:S(2)}, u32[]{:S(2)}) %collective-permute-start.12) | collective-permute-done | bytes 294944 | tf_op jit(solution)/shard_map/ppermute | solution.py:337
  52.6 2.3 %collective-permute-start.9 = (bf16[96,1536]{1,0:T(8,128)(2,1)S(1)}, bf16[96,1536]{1,0:T(8,128)(2,1)S(1)}, u32[]{:S(2)}, u32[]{:S(2)}) collective-permute-start(bf16[96,1536]{1,0:T(8,128)(2,1)S(1)} %pad_maximum_fusion.4), channel_id=1, source_target_pairs={{0,16},{8,24},{16,0},{24,8},{1,17},{9,25},{17,1},{25,9},{2,18},{10... | collective-permute-start | bytes 884744 | tf_op jit(solution)/shard_map/ppermute | solution.py:397
  55.7 6.2 %collective-permute-done.10.refs_4_ = bf16[96,1536]{1,0:T(8,128)(2,1)S(1)} collective-permute-done((bf16[96,1536]{1,0:T(8,128)(2,1)S(1)}, bf16[96,1536]{1,0:T(8,128)(2,1)S(1)}, u32[]{:S(2)}, u32[]{:S(2)}) %collective-permute-start.10) | collective-permute-done | bytes 294944 | tf_op jit(solution)/shard_map/ppermute | solution.py:397
  61.9 5.6 %collective-permute-done.9.refs_3_ = bf16[96,1536]{1,0:T(8,128)(2,1)S(1)} collective-permute-done((bf16[96,1536]{1,0:T(8,128)(2,1)S(1)}, bf16[96,1536]{1,0:T(8,128)(2,1)S(1)}, u32[]{:S(2)}, u32[]{:S(2)}) %collective-permute-start.9) | collective-permute-done | bytes 294944 | tf_op jit(solution)/shard_map/ppermute | solution.py:397
  68.2 3.6 %project.1 = (bf16[96,768]{1,0:T(8,128)(2,1)S(1)}, bf16[96,768]{1,0:T(8,128)(2,1)S(1)}, bf16[96,768]{1,0:T(8,128)(2,1)S(1)}, bf16[96,768]{1,0:T(8,128)(2,1)S(1)}) custom-call(s32[4]{0:T(128)S(1)} %pad_add_fusion.meta_ref, bf16[96,768]{1,0:T(8,128)(2,1)S(1)} %bitcast.53, bf16[96,768]{1,0:T(8,128)(2,1)S(1)} %bitcast.55, ...), custom_call_target="tpu_custom_call" | custom-call | flops 905969664 | bytes 6000000 | tf_op jit(solution)/shard_map/project/pallas_call | solution.py:401
  72.7 1.2 %collective-permute-start.19 = (bf16[96,768]{1,0:T(8,128)(2,1)S(1)}, bf16[96,768]{1,0:T(8,128)(2,1)S(1)}, u32[]{:S(2)}, u32[]{:S(2)}) collective-permute-start(bf16[96,768]{1,0:T(8,128)(2,1)S(1)} %get-tuple-element.25), channel_id=1, source_target_pairs={{0,16},{8,24},{16,0},{24,8},{1,17},{9,25},{17,1},{25,9},{2,18},{10... | collective-permute-start | bytes 442376 | tf_op jit(solution)/shard_map/ppermute | solution.py:416
  73.9 2.6 %collective-permute-start.20 = (bf16[96,768]{1,0:T(8,128)(2,1)S(1)}, bf16[96,768]{1,0:T(8,128)(2,1)S(1)}, u32[]{:S(2)}, u32[]{:S(2)}) collective-permute-start(bf16[96,768]{1,0:T(8,128)(2,1)S(1)} %get-tuple-element.26), channel_id=1, source_target_pairs={{0,24},{8,0},{16,8},{24,16},{1,25},{9,1},{17,9},{25,17},{2,26},{10... | collective-permute-start | bytes 442376 | tf_op jit(solution)/shard_map/ppermute | solution.py:416
  76.5 2.8 %collective-permute-done.18.refs_1_ = bf16[96,768]{1,0:T(8,128)(2,1)S(1)} collective-permute-done((bf16[96,768]{1,0:T(8,128)(2,1)S(1)}, bf16[96,768]{1,0:T(8,128)(2,1)S(1)}, u32[]{:S(2)}, u32[]{:S(2)}) %collective-permute-start.18) | collective-permute-done | bytes 147488 | tf_op jit(solution)/shard_map/ppermute | solution.py:416
  79.3 1.3 %collective-permute-done.19.refs_2_ = bf16[96,768]{1,0:T(8,128)(2,1)S(1)} collective-permute-done((bf16[96,768]{1,0:T(8,128)(2,1)S(1)}, bf16[96,768]{1,0:T(8,128)(2,1)S(1)}, u32[]{:S(2)}, u32[]{:S(2)}) %collective-permute-start.19) | collective-permute-done | bytes 147488 | tf_op jit(solution)/shard_map/ppermute | solution.py:416
  80.6 1.4 %place.1 = bf16[96,3072]{1,0:T(8,128)(2,1)} custom-call(s32[4]{0:T(128)S(1)} %pad_add_fusion.meta_ref, bf16[96,768]{1,0:T(8,128)(2,1)S(1)} %get-tuple-element.23.refs_0_, bf16[96,768]{1,0:T(8,128)(2,1)S(1)} %collective-permute-done.18.refs_1_, bf16[96,768]{1,0:T(8,128)(2,1)S(1)} %collective-permute-done.19.refs_2_, ...), custom_call_target="tpu_custom_call" | custom-call | flops 1000 | bytes 1200000 | tf_op jit(solution)/shard_map/place/pallas_call | solution.py:418
  (64 shorter events, 9.9 us)
Async XLA Ops:
  0.0 3.8 %copy-start = (bf16[192,3072]{1,0:T(8,128)(2,1)S(1)}, bf16[192,3072]{1,0:T(8,128)(2,1)}, u32[]{:S(2)}) copy-start(bf16[192,3072]{1,0:T(8,128)(2,1)} %param.10) | copy-start | bytes 3538948
  2.7 1.9 %collective-permute-start = (bf16[3,3,32,768]{3,2,1,0:T(8,128)(2,1)S(1)}, bf16[3,3,32,768]{3,2,1,0:T(8,128)(2,1)S(1)}, u32[]{:S(2)}, u32[]{:S(2)}) collective-permute-start(bf16[3,3,32,768]{3,2,1,0:T(8,128)(2,1)S(1)} %pad_maximum_fusion.1), channel_id=1, source_target_pairs={{0,4},{4,0},{1,5},{5,1},{2,6},{6,2},{3,7},{7,3},{8,12},{12,8},{9,1... | collective-permute-start | bytes 1327112 | tf_op jit(solution)/shard_map/ppermute | solution.py:307
  4.6 20.4 %copy-start.1 = (s32[12,3]{0,1:T(4,128)S(1)}, s32[12,3]{0,1:T(4,128)}, u32[]{:S(2)}) copy-start(s32[12,3]{0,1:T(4,128)} %param.9) | copy-start | bytes 436
  4.7 17.9 %collective-permute-start.3 = (bf16[64,768]{1,0:T(8,128)(2,1)S(1)}, bf16[64,768]{1,0:T(8,128)(2,1)S(1)}, u32[]{:S(2)}, u32[]{:S(2)}) collective-permute-start(bf16[64,768]{1,0:T(8,128)(2,1)S(1)} %pad_maximum_fusion.5), channel_id=1, source_target_pairs={{0,8},{8,16},{16,24},{1,9},{9,17},{17,25},{2,10},{10,18},{18,26},{... | collective-permute-start | bytes 294920 | tf_op jit(solution)/shard_map/ppermute | solution.py:314
  10.2 14.9 %collective-permute-start.1 = (bf16[2,3,32,768]{3,2,1,0:T(8,128)(2,1)}, bf16[2,3,32,768]{3,2,1,0:T(8,128)(2,1)S(1)}, u32[]{:S(2)}, u32[]{:S(2)}) collective-permute-start(bf16[2,3,32,768]{3,2,1,0:T(8,128)(2,1)} %pad_maximum_fusion.2), channel_id=1, source_target_pairs={{0,1},{1,2},{2,3},{4,5},{5,6},{6,7},{8,9},{9,10},{10,11},{12,13},{... | collective-permute-start | bytes 884744 | tf_op jit(solution)/shard_map/ppermute | solution.py:326
  14.5 12.0 %collective-permute-start.2 = (bf16[2,3,32,768]{3,2,1,0:T(8,128)(2,1)}, bf16[2,3,32,768]{3,2,1,0:T(8,128)(2,1)S(1)}, u32[]{:S(2)}, u32[]{:S(2)}) collective-permute-start(bf16[2,3,32,768]{3,2,1,0:T(8,128)(2,1)} %pad_maximum_fusion.3), channel_id=1, source_target_pairs={{1,0},{2,1},{3,2},{5,4},{6,5},{7,6},{9,8},{10,9},{11,10},{13,12},{... | collective-permute-start | bytes 884744 | tf_op jit(solution)/shard_map/ppermute | solution.py:329
  15.8 6.7 %collective-permute-start.4 = (bf16[64,768]{1,0:T(8,128)(2,1)S(1)}, bf16[64,768]{1,0:T(8,128)(2,1)S(1)}, u32[]{:S(2)}, u32[]{:S(2)}) collective-permute-start(bf16[64,768]{1,0:T(8,128)(2,1)S(1)} %pad_maximum_fusion.6), channel_id=1, source_target_pairs={{8,0},{16,8},{24,16},{9,1},{17,9},{25,17},{10,2},{18,10},{26,18},{... | collective-permute-start | bytes 294920 | tf_op jit(solution)/shard_map/ppermute | solution.py:313
  17.8 25.2 %collective-permute-start.13 = (bf16[192,768]{1,0:T(8,128)(2,1)S(1)}, bf16[192,768]{1,0:T(8,128)(2,1)S(1)}, u32[]{:S(2)}, u32[]{:S(2)}) collective-permute-start(bf16[192,768]{1,0:T(8,128)(2,1)S(1)} %constant_dynamic-slice_fusion.refs_5_), channel_id=1, source_target_pairs={{0,3},{1,0},{2,1},{3,2},{4,7},{5,4},{6,5},{7,6},{8,11},{9,8},{10,9... | collective-permute-start | bytes 884744 | tf_op jit(solution)/shard_map/ppermute | solution.py:337
  22.5 28.9 %collective-permute-start.12 = (bf16[192,768]{1,0:T(8,128)(2,1)S(1)}, bf16[192,768]{1,0:T(8,128)(2,1)}, u32[]{:S(2)}, u32[]{:S(2)}) collective-permute-start(bf16[192,768]{1,0:T(8,128)(2,1)S(1)} %constant_dynamic-slice_fusion.refs_5_), channel_id=1, source_target_pairs={{0,2},{1,3},{2,0},{3,1},{4,6},{5,7},{6,4},{7,5},{8,10},{9,11},{10,... | collective-permute-start | bytes 884744 | tf_op jit(solution)/shard_map/ppermute | solution.py:337
  22.5 28.9 %collective-permute-start.11 = (bf16[192,768]{1,0:T(8,128)(2,1)S(1)}, bf16[192,768]{1,0:T(8,128)(2,1)}, u32[]{:S(2)}, u32[]{:S(2)}) collective-permute-start(bf16[192,768]{1,0:T(8,128)(2,1)S(1)} %constant_dynamic-slice_fusion.refs_5_), channel_id=1, source_target_pairs={{0,1},{1,2},{2,3},{3,0},{4,5},{5,6},{6,7},{7,4},{8,9},{9,10},{10,1... | collective-permute-start | bytes 884744 | tf_op jit(solution)/shard_map/ppermute | solution.py:337
  30.2 7.3 %collective-permute-start.5 = (bf16[64,896]{1,0:T(8,128)(2,1)S(1)}, bf16[64,896]{1,0:T(8,128)(2,1)S(1)}, u32[]{:S(2)}, u32[]{:S(2)}) collective-permute-start(bf16[64,896]{1,0:T(8,128)(2,1)S(1)} %get-tuple-element.18), channel_id=1, source_target_pairs={{0,8},{8,16},{16,24},{1,9},{9,17},{17,25},{2,10},{10,18},{18,26},{... | collective-permute-start | bytes 344072 | tf_op jit(solution)/shard_map/ppermute | solution.py:370
  33.6 6.7 %collective-permute-start.6 = (bf16[64,896]{1,0:T(8,128)(2,1)S(1)}, bf16[64,896]{1,0:T(8,128)(2,1)S(1)}, u32[]{:S(2)}, u32[]{:S(2)}) collective-permute-start(bf16[64,896]{1,0:T(8,128)(2,1)S(1)} %get-tuple-element.19), channel_id=1, source_target_pairs={{8,0},{16,8},{24,16},{9,1},{17,9},{25,17},{10,2},{18,10},{26,18},{... | collective-permute-start | bytes 344072 | tf_op jit(solution)/shard_map/ppermute | solution.py:369
  42.5 9.4 %collective-permute-start.7 = (bf16[3,32,768]{2,1,0:T(8,128)(2,1)S(1)}, bf16[3,32,768]{2,1,0:T(8,128)(2,1)S(1)}, u32[]{:S(2)}, u32[]{:S(2)}) collective-permute-start(bf16[3,32,768]{2,1,0:T(8,128)(2,1)S(1)} %get-tuple-element.21), channel_id=1, source_target_pairs={{0,4},{4,0},{1,5},{5,1},{2,6},{6,2},{3,7},{7,3},{8,12},{12,8},{9,1... | collective-permute-start | bytes 442376 | tf_op jit(solution)/shard_map/ppermute | solution.py:395
  42.6 10.1 %collective-permute-start.14 = (bf16[192,768]{1,0:T(8,128)(2,1)S(1)}, bf16[192,768]{1,0:T(8,128)(2,1)S(1)}, u32[]{:S(2)}, u32[]{:S(2)}) collective-permute-start(bf16[192,768]{1,0:T(8,128)(2,1)S(1)} %constant_dynamic-slice_fusion.refs_5_), channel_id=1, source_target_pairs={{0,4},{4,0},{1,5},{5,1},{2,6},{6,2},{3,7},{7,3},{8,12},{12,8},{9,1... | collective-permute-start | bytes 884744 | tf_op jit(solution)/shard_map/ppermute | solution.py:343
  43.1 11.9 %collective-permute-start.17 = (bf16[192,768]{1,0:T(8,128)(2,1)S(1)}, bf16[192,768]{1,0:T(8,128)(2,1)S(1)}, u32[]{:S(2)}, u32[]{:S(2)}) collective-permute-start(bf16[192,768]{1,0:T(8,128)(2,1)S(1)} %collective-permute-done.13.refs_8_), channel_id=1, source_target_pairs={{0,4},{4,0},{1,5},{5,1},{2,6},{6,2},{3,7},{7,3},{8,12},{12,8},{9,1... | collective-permute-start | bytes 884744 | tf_op jit(solution)/shard_map/ppermute | solution.py:343
  51.4 4.2 %collective-permute-start.16 = (bf16[192,768]{1,0:T(8,128)(2,1)}, bf16[192,768]{1,0:T(8,128)(2,1)S(1)}, u32[]{:S(2)}, u32[]{:S(2)}) collective-permute-start(bf16[192,768]{1,0:T(8,128)(2,1)} %collective-permute-done.12.refs_7_), channel_id=1, source_target_pairs={{0,4},{4,0},{1,5},{5,1},{2,6},{6,2},{3,7},{7,3},{8,12},{12,8},{9,1... | collective-permute-start | bytes 884744 | tf_op jit(solution)/shard_map/ppermute | solution.py:343
  51.4 4.2 %collective-permute-start.15 = (bf16[192,768]{1,0:T(8,128)(2,1)}, bf16[192,768]{1,0:T(8,128)(2,1)S(1)}, u32[]{:S(2)}, u32[]{:S(2)}) collective-permute-start(bf16[192,768]{1,0:T(8,128)(2,1)} %collective-permute-done.11.refs_6_), channel_id=1, source_target_pairs={{0,4},{4,0},{1,5},{5,1},{2,6},{6,2},{3,7},{7,3},{8,12},{12,8},{9,1... | collective-permute-start | bytes 884744 | tf_op jit(solution)/shard_map/ppermute | solution.py:343
  52.0 9.9 %collective-permute-start.10 = (bf16[96,1536]{1,0:T(8,128)(2,1)S(1)}, bf16[96,1536]{1,0:T(8,128)(2,1)S(1)}, u32[]{:S(2)}, u32[]{:S(2)}) collective-permute-start(bf16[96,1536]{1,0:T(8,128)(2,1)S(1)} %pad_maximum_fusion.4), channel_id=1, source_target_pairs={{0,24},{8,0},{16,8},{24,16},{1,25},{9,1},{17,9},{25,17},{2,26},{10... | collective-permute-start | bytes 884744 | tf_op jit(solution)/shard_map/ppermute | solution.py:397
  52.6 14.8 %collective-permute-start.9 = (bf16[96,1536]{1,0:T(8,128)(2,1)S(1)}, bf16[96,1536]{1,0:T(8,128)(2,1)S(1)}, u32[]{:S(2)}, u32[]{:S(2)}) collective-permute-start(bf16[96,1536]{1,0:T(8,128)(2,1)S(1)} %pad_maximum_fusion.4), channel_id=1, source_target_pairs={{0,16},{8,24},{16,0},{24,8},{1,17},{9,25},{17,1},{25,9},{2,18},{10... | collective-permute-start | bytes 884744 | tf_op jit(solution)/shard_map/ppermute | solution.py:397
  55.0 13.2 %collective-permute-start.8 = (bf16[96,1536]{1,0:T(8,128)(2,1)S(1)}, bf16[96,1536]{1,0:T(8,128)(2,1)S(1)}, u32[]{:S(2)}, u32[]{:S(2)}) collective-permute-start(bf16[96,1536]{1,0:T(8,128)(2,1)S(1)} %pad_maximum_fusion.4), channel_id=1, source_target_pairs={{0,8},{8,16},{16,24},{24,0},{1,9},{9,17},{17,25},{25,1},{2,10},{10... | collective-permute-start | bytes 884744 | tf_op jit(solution)/shard_map/ppermute | solution.py:397
  71.8 7.5 %collective-permute-start.18 = (bf16[96,768]{1,0:T(8,128)(2,1)S(1)}, bf16[96,768]{1,0:T(8,128)(2,1)S(1)}, u32[]{:S(2)}, u32[]{:S(2)}) collective-permute-start(bf16[96,768]{1,0:T(8,128)(2,1)S(1)} %get-tuple-element.24), channel_id=1, source_target_pairs={{0,8},{8,16},{16,24},{24,0},{1,9},{9,17},{17,25},{25,1},{2,10},{10... | collective-permute-start | bytes 442376 | tf_op jit(solution)/shard_map/ppermute | solution.py:416
  72.7 8.0 %collective-permute-start.19 = (bf16[96,768]{1,0:T(8,128)(2,1)S(1)}, bf16[96,768]{1,0:T(8,128)(2,1)S(1)}, u32[]{:S(2)}, u32[]{:S(2)}) collective-permute-start(bf16[96,768]{1,0:T(8,128)(2,1)S(1)} %get-tuple-element.25), channel_id=1, source_target_pairs={{0,16},{8,24},{16,0},{24,8},{1,17},{9,25},{17,1},{25,9},{2,18},{10... | collective-permute-start | bytes 442376 | tf_op jit(solution)/shard_map/ppermute | solution.py:416
  73.9 6.7 %collective-permute-start.20 = (bf16[96,768]{1,0:T(8,128)(2,1)S(1)}, bf16[96,768]{1,0:T(8,128)(2,1)S(1)}, u32[]{:S(2)}, u32[]{:S(2)}) collective-permute-start(bf16[96,768]{1,0:T(8,128)(2,1)S(1)} %get-tuple-element.26), channel_id=1, source_target_pairs={{0,24},{8,0},{16,8},{24,16},{1,25},{9,1},{17,9},{25,17},{2,26},{10... | collective-permute-start | bytes 442376 | tf_op jit(solution)/shard_map/ppermute | solution.py:416

commit v2 on v0

v2 whole, which is shorter than its diff:
```python
import functools
import math

import jax
import jax.numpy as jnp
import numpy as np
from jax import lax
from jax.experimental import pallas as pl
from jax.experimental.pallas import tpu as pltpu
from jax.sharding import PartitionSpec as P

TILE = 4
PAIR = 2
FAR = -1e30
LANES = 128
STRIDE = 32
VMEM = pl.BlockSpec(memory_space=pltpu.VMEM)
SMEM = pl.BlockSpec(memory_space=pltpu.SMEM)
HBM = pl.BlockSpec(memory_space=pl.ANY)
PARAMS = pltpu.CompilerParams(vmem_limit_bytes=16 * 1024 * 1024)


def cycle(count, step):
    return [(i, (i + step) % count) for i in range(count)]


def swaps(count, phase):
    partners = [(i ^ 1) if phase == 0 else ((i + 1) ^ 1) - 1 for i in range(count)]
    return [(i, p if 0 <= p < count else i) for i, p in enumerate(partners)]


def line(count, step):
    return [(i, i + step) for i in range(count) if 0 <= i + step < count]


def sides(index, count):
    even = index % 2 == 0
    inside_after, inside_before = index < count - 1, index > 0
    return (even, ~even), (
        jnp.where(even, inside_after, inside_before),
        jnp.where(even, inside_before, inside_after),
    )


def code_table(rows, cols, rims):
    tile_cols = cols // TILE
    span = rows // TILE
    tables = []
    for core in range(PAIR):
        own = core * span
        other = (1 - core) * span
        blocks = [(own, rows), (other, rows)] + ([(-1, TILE), (2 * span, TILE)] if rims else [])
        for odd in range(2):
            query_row, query_col, key_row, key_col, key_side = [], [], [], [], []
            for base in (own, other):
                for row in range(rows):
                    for col in range(cols):
                        query_row.append(base + row // TILE)
                        query_col.append(col // TILE)
            for base, length in blocks:
                for row in range(length):
                    for col in range(cols):
                        key_row.append(base + row // TILE)
                        key_col.append(col // TILE)
                        key_side.append(-1)
            for phase in range(2):
                for base, length in blocks:
                    for row in range(length):
                        for _ in range(TILE):
                            key_row.append(base + row // TILE)
                            key_col.append(tile_cols if phase == odd else -1)
                            key_side.append(phase)
            key_row, key_col, key_side = (np.array(x)[None] for x in (key_row, key_col, key_side))
            apart_row = np.abs(np.array(query_row)[:, None] - key_row)
            apart_col = np.abs(np.array(query_col)[:, None] - key_col)
            base_code = (
                2 * (apart_row == 1)
                + 4 * (apart_col == 1)
                + 8 * ((apart_row > 1) | (apart_col > 1))
            )
            outside = [key_side == 0, key_side == 1]
            outside += [key_row < 0, key_row >= 2 * span] if rims else []
            for bits in range(2 ** len(outside)):
                code = base_code
                for which, mask in enumerate(outside):
                    if bits >> which & 1:
                        code = np.where(mask, 8, code)
                tables.append(code)
    return np.stack(tables).astype(np.int32)


def head_bias(code, radius_ref, head):
    barred = (
        8
        + jnp.where(radius_ref[head, 1] == 0, 2, 0)
        + jnp.where(radius_ref[head, 2] == 0, 4, 0)
    )
    return jnp.where((code & barred) == 0, 0.0, FAR)


class Window:
    def __init__(self, refs, rims, heads, width):
        refs = list(refs)
        self.blocks = refs[:2]
        self.extra = refs[2 : 5 if rims else 4]
        self.rest = refs[5 if rims else 4 :]
        self.frames = self.blocks[0].shape[1]
        self.width = width

    def near(self, kind, frame, head):
        lanes = pl.ds(head * self.width, self.width)
        return [ref[kind, frame, :, lanes] for ref in self.blocks]

    def query(self, frame, head):
        return jnp.concatenate(self.near(0, frame, head), axis=0)

    def pair(self, frame, head):
        lanes = pl.ds(head * self.width, self.width)
        return [
            jnp.concatenate(
                self.near(1 + kind, frame, head)
                + [ref[kind, frame, :, lanes] for ref in self.extra],
                axis=0,
            )
            for kind in range(2)
        ]


def scores_of(query, key, scale):
    return (
        lax.dot_general(
            query, key, (((1,), (1,)), ((), ())), preferred_element_type=jnp.float32
        )
        * scale
    )


def edge_kernel(rims, cols, meta_ref, *refs):
    own, other = refs[:2]
    rim = refs[2] if rims else None
    sides_out, query_out = refs[-4:-2], refs[-2:]
    frames, area, half = other.shape[1:]

    def pick(rows):
        deep = rows * TILE
        shape = (2 * deep, rows * cols)
        to, of = (lax.broadcasted_iota(jnp.int32, shape, d) for d in range(2))
        spot = jnp.where(to < deep, meta_ref[5], meta_ref[6])
        to = lax.rem(to, deep)
        wanted = (to // TILE) * cols + spot * TILE + lax.rem(to, TILE)
        return deep, (of == wanted).astype(jnp.bfloat16)

    block = pick(area // cols)
    strip = pick(TILE)
    for kind in range(2):
        for frame in range(frames):
            work = [
                (own[1 + kind, frame], block),
                (other[1 + kind, frame], block),
            ]
            if rims:
                band = TILE * cols
                work += [(rim[kind, frame, i * band : (i + 1) * band], strip) for i in range(2)]
            begin = 0
            for rows, (deep, chosen) in work:
                found = jnp.dot(chosen, rows, preferred_element_type=jnp.float32)
                found = found.astype(jnp.bfloat16)
                for phase in range(2):
                    sides_out[phase][kind, frame, begin : begin + deep] = found[
                        phase * deep : (phase + 1) * deep
                    ]
                begin += deep
    for phase in range(2):
        frame = meta_ref[1 + phase]
        query_out[phase][:area] = own[0, frame]
        query_out[phase][area:] = other[0, frame]


def guest_kernel(rims, heads, width, meta_ref, radius_ref, code_ref, *refs):
    window = Window(refs, rims, heads, width)
    guests, (shard, _, *outs, sent, sem) = window.rest[:2], window.rest[2:]
    passing = pltpu.make_async_copy(shard, sent, sem)
    passing.start()
    code = code_ref[...]
    count = code.shape[0]
    scale = 1.0 / math.sqrt(width)
    first = meta_ref[0] * heads
    lane = lax.broadcasted_iota(jnp.int32, (count, LANES), 1)
    tops = [jnp.zeros((count, LANES), jnp.float32) for _ in guests]
    totals = [jnp.ones((count, LANES), jnp.float32) for _ in guests]
    work = [(head, phase) for head in range(heads) for phase in range(2)]
    score, value = {}, {}
    for head in range(heads):
        bias = head_bias(code, radius_ref, first + head)
        for phase in range(2):
            key, value[head, phase] = window.pair(meta_ref[1 + phase], head)
            query = guests[phase][:, pl.ds(head * width, width)]
            score[head, phase] = scores_of(query, key, scale) + bias
    top = {at: jnp.max(score[at], axis=1, keepdims=True) for at in work}
    expo = {at: jnp.exp(score[at] - top[at]) for at in work}
    total = {at: jnp.sum(expo[at], axis=1, keepdims=True) for at in work}
    for at in work:
        head, phase = at
        probs = (expo[at] * (1.0 / total[at])).astype(jnp.bfloat16)
        mixed = jnp.dot(probs, value[at], preferred_element_type=jnp.float32)
        outs[phase][:, pl.ds(head * width, width)] = mixed.astype(jnp.bfloat16)
        tops[phase] = jnp.where(lane == head, top[at], tops[phase])
        totals[phase] = jnp.where(lane == head, total[at], totals[phase])
    for out_ref, top, total in zip(outs, tops, totals):
        rest = top + jnp.log(total)
        stats = jnp.zeros((count, LANES), jnp.float32)
        for part in range(3):
            piece = rest.astype(jnp.bfloat16).astype(jnp.float32)
            rest = rest - piece
            stats = stats + (pltpu.roll(piece, part * STRIDE, 1) if part else piece)
        out_ref[:, pl.ds(heads * width, LANES)] = stats.astype(jnp.bfloat16)
    passing.wait()


def host_kernel(rims, heads, width, meta_ref, radius_ref, code_ref, *refs):
    window = Window(refs, rims, heads, width)
    mixed_ref, stats_ref = window.rest
    frames = window.frames
    code = code_ref[...]
    count = code.shape[0]
    scale = 1.0 / math.sqrt(width)
    first = meta_ref[0] * heads
    lane = lax.broadcasted_iota(jnp.int32, (count, LANES), 1)
    tops = [jnp.zeros((count, LANES), jnp.float32) for _ in range(frames)]
    totals = [jnp.ones((count, LANES), jnp.float32) for _ in range(frames)]
    work = [(head, f) for head in range(heads) for f in range(frames)]
    score, value = {}, {}
    for head in range(heads):
        bias = head_bias(code, radius_ref, first + head)
        bias_apart = jnp.where(radius_ref[first + head, 0] == 0, FAR, bias)
        query = [window.query(f, head) for f in range(frames)]
        pairs = [window.pair(f, head) for f in range(frames)]
        blocks = {}
        for frame in range(frames):
            near = range(max(0, frame - 1), min(frames, frame + 2))
            block = scores_of(
                jnp.concatenate([query[f] for f in near], axis=0), pairs[frame][0], scale
            )
            for spot, f in enumerate(near):
                blocks[f, frame] = block[spot * count : (spot + 1) * count] + (
                    bias if f == frame else bias_apart
                )
        for f in range(frames):
            near = range(max(0, f - 1), min(frames, f + 2))
            score[head, f] = jnp.concatenate([blocks[f, g] for g in near], axis=1)
            value[head, f] = jnp.concatenate([pairs[g][1] for g in near], axis=0)
    top = {at: jnp.max(score[at], axis=1, keepdims=True) for at in work}
    expo = {at: jnp.exp(score[at] - top[at]) for at in work}
    total = {at: jnp.sum(expo[at], axis=1, keepdims=True) for at in work}
    for at in work:
        head, f = at
        probs = (expo[at] * (1.0 / total[at])).astype(jnp.bfloat16)
        mixed_ref[f, :, pl.ds(head * width, width)] = jnp.dot(
            probs, value[at], preferred_element_type=jnp.float32
        )
        tops[f] = jnp.where(lane == head, top[at], tops[f])
        totals[f] = jnp.where(lane == head, total[at], totals[f])
    for f in range(frames):
        stats_ref[f] = tops[f] + jnp.log(totals[f])


def merge_kernel(
    heads, width, meta_ref, radius_ref, mixed_ref, stats_ref, ref_0, ref_1, _, own_out, other_out, held, logs
):
    frames, count, _ = mixed_ref.shape
    half = count // PAIR
    first = meta_ref[0] * heads
    lane = lax.broadcasted_iota(jnp.int32, (count, LANES), 1)
    use = jnp.zeros((count, LANES), jnp.int32)
    for head in range(heads):
        use = jnp.where(lane == head, radius_ref[first + head, 0], use)
    held[...] = mixed_ref[...]
    logs[...] = stats_ref[...]
    for phase, ref in enumerate((ref_0, ref_1)):
        f = meta_ref[1 + phase]
        there = jnp.where(meta_ref[3 + phase] == 0, 0, use)
        stats = ref[:, pl.ds(heads * width, LANES)].astype(jnp.float32)
        guest = (
            stats
            + pltpu.roll(stats, LANES - STRIDE, 1)
            + pltpu.roll(stats, LANES - 2 * STRIDE, 1)
        )
        guest = jnp.where(there == 0, FAR, guest)
        own = logs[f]
        top = jnp.maximum(own, guest)
        own_weight, guest_weight = jnp.exp(own - top), jnp.exp(guest - top)
        total = own_weight + guest_weight
        if frames == 1:
            logs[f] = top + jnp.log(total)
        own_weight, guest_weight = own_weight / total, guest_weight / total
        for head in range(heads):
            lanes = pl.ds(head * width, width)
            held[f, :, lanes] = (
                held[f, :, lanes] * own_weight[:, head : head + 1]
                + ref[:, lanes].astype(jnp.float32) * guest_weight[:, head : head + 1]
            )
    mixed = held[...].astype(jnp.bfloat16)
    own_out[...] = mixed[:, :half]
    other_out[...] = mixed[:, half:]


def join_kernel(count, meta_ref, *refs):
    pieces, out = refs[:count], refs[-1]
    depth = pieces[0].shape[0]
    for spot, ref in enumerate(pieces):
        begin = pl.multiple_of(meta_ref[spot] * depth, depth)
        out[pl.ds(begin, depth)] = ref[...]


def project_kernel(*refs):
    rows, (near, far), out = refs[:-3], refs[-3:-1], refs[-1]
    half = near.shape[0]
    if len(rows) == 1:
        first, second = rows[0][:, :half], rows[0][:, half:]
    else:
        first, second = rows[0][...], rows[1][...]
    out[...] = (
        jnp.dot(first, near[...], preferred_element_type=jnp.float32)
        + jnp.dot(second, far[...], preferred_element_type=jnp.float32)
    ).astype(out.dtype)


def place_kernel(count, meta_ref, *refs):
    pieces, out, sems = refs[:count], refs[count], refs[count + 1]
    wide = pieces[0].shape[-1]
    copies = []
    for spot, ref in enumerate(pieces):
        origin = lax.rem(meta_ref[0] + count - spot, count)
        where = pl.ds(pl.multiple_of(origin * wide, LANES), wide)
        copies.append(pltpu.make_async_copy(ref, out.at[:, where], sems.at[spot]))
    for copy in copies:
        copy.start()
    for copy in copies:
        copy.wait()


def cost(flops, size):
    return pl.CostEstimate(flops=flops, bytes_accessed=size, transcendentals=0)


def shards(queries, keys, values, radius, out_weight):
    n_time, n_rows, n_cols = (lax.axis_size(a) for a in ("ta", "ha", "wa"))
    at_time, at_row, at_col = (lax.axis_index(a) for a in ("ta", "ha", "wa"))
    core = at_row % PAIR
    frames, rows, cols, features = queries.shape
    heads = radius.shape[0] // PAIR
    width = features // radius.shape[0]
    half = features // PAIR
    tile_cols = cols // TILE
    area = rows * cols
    rims = n_rows > PAIR

    after, there = sides(at_col, n_cols)
    later, present = sides(at_time, n_time)
    ends = [jnp.where(x, frames - 1, 0) for x in later]
    borders = [jnp.where(x, tile_cols - 1, 0) for x in after]
    meta = jnp.stack([core, *ends, *present, *borders]).astype(jnp.int32)

    raw = [x.reshape(frames, area, features) for x in (queries, keys, values)]
    pairs = [(i, i ^ 1) for i in range(n_rows)]
    own, other = (
        jnp.stack([lax.dynamic_slice_in_dim(x, which * half, half, axis=2) for x in raw])
        for which in (core, 1 - core)
    )
    other = lax.ppermute(other, "ha", pairs)
    rim = None
    if rims:
        even, odd = (jnp.where(core == i, own[1:], other[1:]) for i in range(PAIR))
        band = TILE * cols
        up = lax.ppermute(odd[:, :, -band:], "ha", line(n_rows, PAIR))
        down = lax.ppermute(even[:, :, :band], "ha", line(n_rows, -PAIR))
        rim = jnp.concatenate([up, down], axis=2)
    deep = PAIR * rows * TILE + (PAIR * TILE * TILE if rims else 0)
    side = jax.ShapeDtypeStruct((2, frames, deep, half), queries.dtype)
    end = jax.ShapeDtypeStruct((PAIR * area, half), queries.dtype)
    *edges, first_end, second_end = pl.pallas_call(
        functools.partial(edge_kernel, rims, cols),
        out_shape=(side, side, end, end),
        in_specs=[SMEM] + [VMEM] * (3 if rims else 2),
        out_specs=(VMEM,) * 4,
        compiler_params=PARAMS,
        cost_estimate=cost(1000, 2_000_000),
        name="edge",
    )(meta, own, other, *([rim] if rims else []))
    beside = [lax.ppermute(x, "wa", swaps(n_cols, phase)) for phase, x in enumerate(edges)]
    guests = [
        lax.ppermute(x, "ta", swaps(n_time, phase))
        for phase, x in enumerate((first_end, second_end))
    ]

    slab = features // (n_rows * n_cols)
    wide = out_weight.shape[1] // n_time
    mine = lax.dynamic_slice_in_dim(out_weight, at_time * wide, wide, axis=1)
    held = {0: mine}
    if n_cols > 1:
        held[n_cols - 1] = lax.ppermute(mine, "wa", cycle(n_cols, n_cols - 1))

    table = jnp.asarray(code_table(rows, cols, rims))
    absent = [~x for x in there]
    if rims:
        absent += [at_row < PAIR, at_row >= n_rows - PAIR]
    spot = core * 2 + at_col % 2
    spot = spot * 2 ** len(absent) + sum(jnp.where(x, 2**i, 0) for i, x in enumerate(absent))
    code = lax.dynamic_index_in_dim(table, spot, 0, keepdims=False)
    place = jnp.stack([at_time]).astype(jnp.int32)

    parts = [own, other] + ([rim] if rims else []) + beside
    count = PAIR * area
    unit = 4 * heads * width * count * code.shape[1]
    payload = jax.ShapeDtypeStruct((count, half + LANES), jnp.bfloat16)
    *answers, sent = pl.pallas_call(
        functools.partial(guest_kernel, rims, heads, width),
        out_shape=(payload, payload, jax.ShapeDtypeStruct(mine.shape, mine.dtype)),
        in_specs=[SMEM, SMEM] + [VMEM] * (1 + len(parts) + 2) + [VMEM, HBM],
        out_specs=(VMEM, VMEM, VMEM),
        scratch_shapes=[pltpu.SemaphoreType.DMA],
        compiler_params=PARAMS,
        cost_estimate=cost(2 * unit, 4_000_000),
        name="guest",
    )(meta, radius, code, *parts, *guests, mine, held[max(held)])
    if n_cols > 2:
        held[1] = lax.ppermute(sent, "wa", cycle(n_cols, 1))
    answers = [
        lax.ppermute(x, "ta", swaps(n_time, phase)) for phase, x in enumerate(answers)
    ]
    mixed_shape, stats_shape = (frames, count, half), (frames, count, LANES)
    mixed, stats = pl.pallas_call(
        functools.partial(host_kernel, rims, heads, width),
        out_shape=(
            jax.ShapeDtypeStruct(mixed_shape, jnp.float32),
            jax.ShapeDtypeStruct(stats_shape, jnp.float32),
        ),
        in_specs=[SMEM, SMEM] + [VMEM] * (1 + len(parts)),
        out_specs=(VMEM, VMEM),
        compiler_params=PARAMS,
        cost_estimate=cost(7 * unit, 6_000_000),
        name="host",
    )(meta, radius, code, *parts)
    att = jax.ShapeDtypeStruct((frames, area, half), jnp.bfloat16)
    kept, given = pl.pallas_call(
        functools.partial(merge_kernel, heads, width),
        out_shape=(att, att),
        in_specs=[SMEM, SMEM] + [VMEM] * 4 + [HBM],
        out_specs=(VMEM, VMEM),
        scratch_shapes=[
            pltpu.VMEM(mixed_shape, jnp.float32),
            pltpu.VMEM(stats_shape, jnp.float32),
        ],
        compiler_params=PARAMS,
        cost_estimate=cost(1000, 3_000_000),
        name="merge",
    )(meta, radius, mixed, stats, *answers, held[min(1, n_cols - 1)])
    tokens = frames * area
    kept = kept.reshape(tokens, half)
    taken = lax.ppermute(given, "ha", pairs).reshape(tokens, half)
    whole = jnp.concatenate([kept, taken], axis=1)
    for s in range(1, n_cols):
        if s not in held:
            held[s] = lax.ppermute(sent, "wa", cycle(n_cols, s))
    received = [lax.ppermute(whole, "ta", cycle(n_time, s)) for s in range(1, n_time)]

    def joined(shards, at):
        count = len(shards)
        spots = jnp.stack([(at - s) % count for s in range(count)]).astype(jnp.int32)
        if shards[0].shape[0] % 16:
            return jnp.roll(jnp.stack(shards[::-1]), at + 1, axis=0).reshape(-1, wide)
        return pl.pallas_call(
            functools.partial(join_kernel, count),
            out_shape=jax.ShapeDtypeStruct((count * shards[0].shape[0], wide), mine.dtype),
            in_specs=[SMEM] + [VMEM] * count + [HBM] * len(received),
            out_specs=VMEM,
            compiler_params=PARAMS,
            cost_estimate=cost(1000, 2_400_000),
            name="join",
        )(spots, *shards, *received)

    near = joined([held[s] for s in range(n_cols)], at_col)
    across = [lax.ppermute(near, "ha", cycle(n_rows, r)) for r in range(1, n_rows)]
    if n_rows == PAIR:
        far = across[0]
    else:
        full = joined([near, *across], at_row)
        near, far = (
            lax.dynamic_slice_in_dim(full, which * half, half, axis=0)
            for which in (core, 1 - core)
        )

    def project(*rows):
        return pl.pallas_call(
            project_kernel,
            out_shape=jax.ShapeDtypeStruct((tokens, wide), queries.dtype),
            in_specs=[VMEM] * (len(rows) + 2),
            out_specs=VMEM,
            compiler_params=PARAMS,
            cost_estimate=cost(2 * tokens * features * wide, 3_000_000),
            name="project",
        )(*rows, near, far)

    products = [project(kept, taken)] + [project(x) for x in received]
    back = [products[0]] + [
        lax.ppermute(products[n_time - s], "ta", cycle(n_time, s)) for s in range(1, n_time)
    ]
    out = pl.pallas_call(
        functools.partial(place_kernel, n_time),
        out_shape=jax.ShapeDtypeStruct((tokens, wide * n_time), jnp.bfloat16),
        in_specs=[SMEM] + [HBM] * n_time,
        out_specs=HBM,
        scratch_shapes=[pltpu.SemaphoreType.DMA((n_time,))],
        compiler_params=PARAMS,
        cost_estimate=cost(1000, 1_200_000),
        name="place",
    )(place, *back)
    return out.reshape(frames, rows, cols, wide * n_time)


def solution(mesh):
    return jax.shard_map(
        shards,
        mesh=mesh,
        in_specs=(
            P("ta", "ha", "wa", None),
            P("ta", "ha", "wa", None),
            P("ta", "ha", "wa", None),
            P(),
            P(("ha", "wa"), None),
        ),
        out_specs=P("ta", "ha", "wa", None),
        check_vma=False,
    )
```

time: 188 us -> 70.8 us (0.38)
  waiting for transfers between devices: 85 us -> 33.3 us
  local copies, waits for them, and re-layouts: 38.3 us -> 3.25 us
  other arithmetic: 18.5 us -> 0.9 us
  matrix products: 16.7 us -> 0 us
  between operations: 13.6 us -> 0.12 us
  Pallas kernels: 0 us -> 10.2 us
  starting transfers between devices: 15.2 us -> 22.8 us
    ppermute x6 -> x18, waiting for transfers between devices: 84.3 us -> 33.3 us  [the longest x1 9.3 us: shards(): held[s] = lax.ppermute(sent, 'wa', cycle(n_cols, s))]
    and x1 -> x0, local copies, waits for them, and re-layouts: 20 us -> none  [shards(): allow_t[:, :, None, None, :, None, None]]
    dot_general x3 -> x0, matrix products: 16.7 us -> none  [the longest x1 6.58 us: shards(): jnp.einsum('hqk,khd->qhd', probs, value_rows, preferred_element_type=jnp....]
    pallas_call x0 -> x10, Pallas kernels: none -> 10.2 us  [the longest x1 2.16 us: shards(): pl.pallas_call(functools.partial(guest_kernel, rims, heads, width), out_s...]
    another operation x2 -> x3, local copies, waits for them, and re-layouts: 10.6 us -> 2.35 us  [the longest x2 2.27 us: shards(): jnp.stack([lax.dynamic_slice_in_dim(x, which * half, half, axis=2) for x...]
    ppermute x6 -> x18, starting transfers between devices: 15.2 us -> 22.8 us  [the longest x1 4.7 us: shards(): held[n_cols - 1] = lax.ppermute(mine, 'wa', cycle(n_cols, n_cols - 1))]
    and x8 -> x0, other arithmetic: 7.47 us -> none  [the longest x2 7.21 us: shards(): allow_t[:, :, None, None, :, None, None]]
    concatenate x2 -> x1, other arithmetic: 4.63 us -> 0.73 us  [shards(): whole = jnp.concatenate([kept, taken], axis=1)]
  transfers between devices with their start and end apart: 7 -> 18, of which waited for: 3 -> 11; matrix products, arithmetic and copies ran while one was open for 35% -> 3% of each run, Pallas kernels for 0% -> 7%
where the time goes in v2:
time: 70.8 us; the launch traced here: 70.5 us
  waiting for transfers between devices  33.3 us (47%)
  starting transfers between devices  22.8 us (32%)
  Pallas kernels  10.2 us (14%)
  local copies, waits for them, and re-layouts  3.25 us (5%)
  other arithmetic  0.9 us (1%)
    ppermute x1, waiting for transfers between devices, shards(): held[s] = lax.ppermute(sent, 'wa', cycle(n_cols, s))  9.3 us
    ppermute x2, waiting for transfers between devices, shards(): lax.ppermute(x, 'wa', swaps(n_cols, phase))  4.76 us
    ppermute x1, starting transfers between devices, shards(): held[n_cols - 1] = lax.ppermute(mine, 'wa', cycle(n_cols, n_cols - 1))  4.7 us
    ppermute x3, waiting for transfers between devices, shards(): lax.ppermute(products[n_time - s], 'ta', cycle(n_time, s))  4.49 us
    ppermute x3, starting transfers between devices, shards(): lax.ppermute(whole, 'ta', cycle(n_time, s))  4.47 us
    ppermute x1, waiting for transfers between devices, shards(): held[1] = lax.ppermute(sent, 'wa', cycle(n_cols, 1))  4.37 us
    ppermute x4, starting transfers between devices, shards(): lax.ppermute(x, 'ta', swaps(n_time, phase))  4.29 us
    ppermute x3, waiting for transfers between devices, shards(): lax.ppermute(whole, 'ta', cycle(n_time, s))  3.9 us
  transfers between devices with their start and end apart: 18, of which 11 were waited for; matrix products, arithmetic and copies ran while one was open for 3% of the time, Pallas kernels for 7%

profile of v2, /device:TPU:0, one launch (start us, length us, event | category | flops | bytes accessed | tf_op | source)
XLA Modules:
  0.0 70.5 jit_solution(10370281991939845249)
XLA Ops:
  0.0 1.1 %dynamic-slice_bitcast_fusion.2 = (bf16[1,3,32,768]{3,2,1,0:T(8,128)(2,1)S(1)}, bf16[1,3,32,768]{3,2,1,0:T(8,128)(2,1)S(1)}) fusion(bf16[3,32,1536]{2,1,0:T(8,128)(2,1)} %bitcast.36, s32[]{:T(128)S(6)} %select_n.97, s32[]{:T(128)S(6)} %select_n.96), kind=kLoop, calls=%fused_computation.5 | loop fusion | bytes 589832 | tf_op jit(solution)/shard_map/stack | solution.py:367
  1.1 1.2 %dynamic-slice_bitcast_fusion = (bf16[1,3,32,768]{3,2,1,0:T(8,128)(2,1)S(1)}, bf16[1,3,32,768]{3,2,1,0:T(8,128)(2,1)S(1)}, bf16[1,3,32,768]{3,2,1,0:T(8,128)(2,1)S(1)}, bf16[1,3,32,768]{3,2,1,0:T(8,128)(2,1)S(1)}) fusion(bf16[3,32,1536]{2,1,0:T(8,128)(2,1)} %bitcast.37, s32[]{:T(128)S(6)} %select_n.97, s32[]{:T(128)S(6)} %select_n.96, ...), kind=kLoop, calls=%fused_computation.3 | loop fusion | bytes 1179656 | tf_op jit(solution)/shard_map/stack | solution.py:367
  2.9 4.7 %collective-permute-start.5 = (bf16[192,768]{1,0:T(8,128)(2,1)S(1)}, bf16[192,768]{1,0:T(8,128)(2,1)S(1)}, u32[]{:S(2)}, u32[]{:S(2)}) collective-permute-start(bf16[192,768]{1,0:T(8,128)(2,1)S(1)} %constant_dynamic-slice_fusion.refs_6_.refs_0_), channel_id=1, source_target_pairs={{0,3},{1,0},{2,1},{3,2},{4,7},{5,4},{6,5},{7,6},{8,11},{9,8},{10,9... | collective-permute-start | bytes 884744 | tf_op jit(solution)/shard_map/ppermute | solution.py:401
  7.7 1.7 %edge.1 = (bf16[2,3,32,768]{3,2,1,0:T(8,128)(2,1)}, bf16[2,3,32,768]{3,2,1,0:T(8,128)(2,1)}, bf16[64,768]{1,0:T(8,128)(2,1)}, bf16[64,768]{1,0:T(8,128)(2,1)S(1)}) custom-call(s32[7]{0:T(128)S(1)} %stack.82.meta_ref, bf16[3,3,32,768]{3,2,1,0:T(8,128)(2,1)S(1)} %pad_maximum_fusion.refs_0_, bf16[3,3,32,768]{3,2,1,0:T(8,128)(2,1)S(1)} %collective-permute-done.refs_1_), custom_call_target="tpu_custom_call" | custom-call | flops 1000 | bytes 2000000 | tf_op jit(solution)/shard_map/edge/pallas_call | solution.py:381
  9.4 1.6 %collective-permute-start.2 = (bf16[2,3,32,768]{3,2,1,0:T(8,128)(2,1)}, bf16[2,3,32,768]{3,2,1,0:T(8,128)(2,1)S(1)}, u32[]{:S(2)}, u32[]{:S(2)}) collective-permute-start(bf16[2,3,32,768]{3,2,1,0:T(8,128)(2,1)} %get-tuple-element.17), channel_id=1, source_target_pairs={{0,0},{1,2},{2,1},{3,3},{4,4},{5,6},{6,5},{7,7},{8,8},{9,10},{10,9... | collective-permute-start | bytes 884744 | tf_op jit(solution)/shard_map/ppermute | solution.py:390
  11.1 1.5 %collective-permute-start.3 = (bf16[64,768]{1,0:T(8,128)(2,1)}, bf16[64,768]{1,0:T(8,128)(2,1)S(1)}, u32[]{:S(2)}, u32[]{:S(2)}) collective-permute-start(bf16[64,768]{1,0:T(8,128)(2,1)} %get-tuple-element.20), channel_id=1, source_target_pairs={{0,8},{8,0},{16,24},{24,16},{1,9},{9,1},{17,25},{25,17},{2,10},{10... | collective-permute-start | bytes 294920 | tf_op jit(solution)/shard_map/ppermute | solution.py:392
  15.0 1.2 %collective-permute-done.3.refs_4_ = bf16[64,768]{1,0:T(8,128)(2,1)S(1)} collective-permute-done((bf16[64,768]{1,0:T(8,128)(2,1)}, bf16[64,768]{1,0:T(8,128)(2,1)S(1)}, u32[]{:S(2)}, u32[]{:S(2)}) %collective-permute-start.3) | collective-permute-done | bytes 98336 | tf_op jit(solution)/shard_map/ppermute | solution.py:392
  16.2 4.8 %collective-permute-done.1.refs_2_ = bf16[2,3,32,768]{3,2,1,0:T(8,128)(2,1)S(1)} collective-permute-done((bf16[2,3,32,768]{3,2,1,0:T(8,128)(2,1)}, bf16[2,3,32,768]{3,2,1,0:T(8,128)(2,1)S(1)}, u32[]{:S(2)}, u32[]{:S(2)}) %collective-permute-start.1) | collective-permute-done | bytes 294944 | tf_op jit(solution)/shard_map/ppermute | solution.py:390
  21.0 2.2 %guest.1 = (bf16[64,896]{1,0:T(8,128)(2,1)S(1)}, bf16[64,896]{1,0:T(8,128)(2,1)S(1)}, bf16[192,768]{1,0:T(8,128)(2,1)}) custom-call(s32[7]{0:T(128)S(1)} %stack.82.meta_ref, s32[12,3]{1,0:T(8,128)S(1)} %copy.9.radius_ref, s32[64,128]{1,0:T(8,128)S(1)} %dynamic-slice_bitcast_fusion.6.code_ref, bf16[3,3,32,768]{3,2,1,0:T(8,128)(2,1)S(1)} %pad_maximum_fusion.refs_0_, ...), custom_call_target="tpu_custom_call" | custom-call | flops 50331648 | bytes 4000000 | tf_op jit(solution)/shard_map/guest/pallas_call | solution.py:416
  23.1 2.4 %collective-permute-start.8 = (bf16[192,768]{1,0:T(8,128)(2,1)}, bf16[192,768]{1,0:T(8,128)(2,1)S(1)}, u32[]{:S(2)}, u32[]{:S(2)}) collective-permute-start(bf16[192,768]{1,0:T(8,128)(2,1)} %get-tuple-element.24), channel_id=1, source_target_pairs={{0,1},{1,2},{2,3},{3,0},{4,5},{5,6},{6,7},{7,4},{8,9},{9,10},{10,1... | collective-permute-start | bytes 884744 | tf_op jit(solution)/shard_map/ppermute | solution.py:427
  25.6 1.5 %collective-permute-start.6 = (bf16[64,896]{1,0:T(8,128)(2,1)S(1)}, bf16[64,896]{1,0:T(8,128)(2,1)S(1)}, u32[]{:S(2)}, u32[]{:S(2)}) collective-permute-start(bf16[64,896]{1,0:T(8,128)(2,1)S(1)} %get-tuple-element.22), channel_id=1, source_target_pairs={{0,8},{8,0},{16,24},{24,16},{1,9},{9,1},{17,25},{25,17},{2,10},{10... | collective-permute-start | bytes 344072 | tf_op jit(solution)/shard_map/ppermute | solution.py:429
  27.7 1.6 %host.1 = (f32[3,64,768]{2,1,0:T(8,128)S(1)}, f32[3,64,128]{2,1,0:T(8,128)S(1)}) custom-call(s32[7]{0:T(128)S(1)} %stack.82.meta_ref, s32[12,3]{1,0:T(8,128)S(1)} %copy.9.radius_ref, s32[64,128]{1,0:T(8,128)S(1)} %dynamic-slice_bitcast_fusion.6.code_ref, bf16[3,3,32,768]{3,2,1,0:T(8,128)(2,1)S(1)} %pad_maximum_fusion.refs_0_, ...), custom_call_target="tpu_custom_call" | custom-call | flops 176160768 | bytes 6000000 | tf_op jit(solution)/shard_map/host/pallas_call | solution.py:432
  29.3 1.0 %collective-permute-done.6.ref_0 = bf16[64,896]{1,0:T(8,128)(2,1)S(1)} collective-permute-done((bf16[64,896]{1,0:T(8,128)(2,1)S(1)}, bf16[64,896]{1,0:T(8,128)(2,1)S(1)}, u32[]{:S(2)}, u32[]{:S(2)}) %collective-permute-start.6) | collective-permute-done | bytes 114720 | tf_op jit(solution)/shard_map/ppermute | solution.py:429
  30.4 4.4 %collective-permute-done.8._.refs_1_ = bf16[192,768]{1,0:T(8,128)(2,1)S(1)} collective-permute-done((bf16[192,768]{1,0:T(8,128)(2,1)}, bf16[192,768]{1,0:T(8,128)(2,1)S(1)}, u32[]{:S(2)}, u32[]{:S(2)}) %collective-permute-start.8) | collective-permute-done | bytes 294944 | tf_op jit(solution)/shard_map/ppermute | solution.py:427
  34.7 1.2 %merge.1 = (bf16[3,32,768]{2,1,0:T(8,128)(2,1)S(1)}, bf16[3,32,768]{2,1,0:T(8,128)(2,1)S(1)}) custom-call(s32[7]{0:T(128)S(1)} %stack.82.meta_ref, s32[12,3]{1,0:T(8,128)S(1)} %copy.9.radius_ref, f32[3,64,768]{2,1,0:T(8,128)S(1)} %get-tuple-element.18.mixed_ref, f32[3,64,128]{2,1,0:T(8,128)S(1)} %get-tuple-element.19.stats_ref, ...), custom_call_target="tpu_custom_call" | custom-call | flops 1000 | bytes 3000000 | tf_op jit(solution)/shard_map/merge/pallas_call | solution.py:445
  38.1 2.4 %collective-permute-start.13 = (bf16[96,1536]{1,0:T(8,128)(2,1)}, bf16[96,1536]{1,0:T(8,128)(2,1)S(1)}, u32[]{:S(2)}, u32[]{:S(2)}) collective-permute-start(bf16[96,1536]{1,0:T(8,128)(2,1)} %pad_maximum_fusion.2), channel_id=1, source_target_pairs={{0,24},{8,0},{16,8},{24,16},{1,25},{9,1},{17,9},{25,17},{2,26},{10... | collective-permute-start | bytes 884744 | tf_op jit(solution)/shard_map/ppermute | solution.py:465
  41.2 1.4 %collective-permute-start.11 = (bf16[96,1536]{1,0:T(8,128)(2,1)}, bf16[96,1536]{1,0:T(8,128)(2,1)S(1)}, u32[]{:S(2)}, u32[]{:S(2)}) collective-permute-start(bf16[96,1536]{1,0:T(8,128)(2,1)} %pad_maximum_fusion.2), channel_id=1, source_target_pairs={{0,8},{8,16},{16,24},{24,0},{1,9},{9,17},{17,25},{25,1},{2,10},{10... | collective-permute-start | bytes 884744 | tf_op jit(solution)/shard_map/ppermute | solution.py:465
  42.7 9.3 %collective-permute-done.10.refs_2_ = bf16[192,768]{1,0:T(8,128)(2,1)S(1)} collective-permute-done((bf16[192,768]{1,0:T(8,128)(2,1)}, bf16[192,768]{1,0:T(8,128)(2,1)S(1)}, u32[]{:S(2)}, u32[]{:S(2)}) %collective-permute-start.10) | collective-permute-done | bytes 294944 | tf_op jit(solution)/shard_map/ppermute | solution.py:464
  52.0 3.9 %collective-permute-done.12.refs_5_.refs_0_ = bf16[96,1536]{1,0:T(8,128)(2,1)S(1)} collective-permute-done((bf16[96,1536]{1,0:T(8,128)(2,1)}, bf16[96,1536]{1,0:T(8,128)(2,1)S(1)}, u32[]{:S(2)}, u32[]{:S(2)}) %collective-permute-start.12) | collective-permute-done | bytes 294944 | tf_op jit(solution)/shard_map/ppermute | solution.py:465
  56.6 2.8 %collective-permute-done.14.refs_3_.refs_2_ = bf16[768,768]{1,0:T(8,128)(2,1)S(1)} collective-permute-done((bf16[768,768]{1,0:T(8,128)(2,1)S(1)}, bf16[768,768]{1,0:T(8,128)(2,1)S(1)}, u32[]{:S(2)}, u32[]{:S(2)}) %collective-permute-start.14) | collective-permute-done | bytes 1179680 | tf_op jit(solution)/shard_map/ppermute | solution.py:483
  60.8 1.5 %collective-permute-start.16 = (bf16[96,768]{1,0:T(8,128)(2,1)S(1)}, bf16[96,768]{1,0:T(8,128)(2,1)S(1)}, u32[]{:S(2)}, u32[]{:S(2)}) collective-permute-start(bf16[96,768]{1,0:T(8,128)(2,1)S(1)} %project.6), channel_id=1, source_target_pairs={{0,16},{8,24},{16,0},{24,8},{1,17},{9,25},{17,1},{25,9},{2,18},{10... | collective-permute-start | bytes 442376 | tf_op jit(solution)/shard_map/ppermute | solution.py:506
  62.8 1.8 %collective-permute-start.17 = (bf16[96,768]{1,0:T(8,128)(2,1)S(1)}, bf16[96,768]{1,0:T(8,128)(2,1)S(1)}, u32[]{:S(2)}, u32[]{:S(2)}) collective-permute-start(bf16[96,768]{1,0:T(8,128)(2,1)S(1)} %project.7), channel_id=1, source_target_pairs={{0,24},{8,0},{16,8},{24,16},{1,25},{9,1},{17,9},{25,17},{2,26},{10... | collective-permute-start | bytes 442376 | tf_op jit(solution)/shard_map/ppermute | solution.py:506
  65.2 2.5 %collective-permute-done.15.refs_1_ = bf16[96,768]{1,0:T(8,128)(2,1)S(1)} collective-permute-done((bf16[96,768]{1,0:T(8,128)(2,1)S(1)}, bf16[96,768]{1,0:T(8,128)(2,1)S(1)}, u32[]{:S(2)}, u32[]{:S(2)}) %collective-permute-start.15) | collective-permute-done | bytes 147488 | tf_op jit(solution)/shard_map/ppermute | solution.py:506
  67.6 2.0 %collective-permute-done.16.refs_2_ = bf16[96,768]{1,0:T(8,128)(2,1)S(1)} collective-permute-done((bf16[96,768]{1,0:T(8,128)(2,1)S(1)}, bf16[96,768]{1,0:T(8,128)(2,1)S(1)}, u32[]{:S(2)}, u32[]{:S(2)}) %collective-permute-start.16) | collective-permute-done | bytes 147488 | tf_op jit(solution)/shard_map/ppermute | solution.py:506
  (36 shorter events, 10.6 us)
Async XLA Ops:
  0.0 2.9 %copy-start = (bf16[192,3072]{1,0:T(8,128)(2,1)S(1)}, bf16[192,3072]{1,0:T(8,128)(2,1)}, u32[]{:S(2)}) copy-start(bf16[192,3072]{1,0:T(8,128)(2,1)} %param.10) | copy-start | bytes 3538948
  2.3 5.4 %collective-permute-start = (bf16[3,3,32,768]{3,2,1,0:T(8,128)(2,1)S(1)}, bf16[3,3,32,768]{3,2,1,0:T(8,128)(2,1)S(1)}, u32[]{:S(2)}, u32[]{:S(2)}) collective-permute-start(bf16[3,3,32,768]{3,2,1,0:T(8,128)(2,1)S(1)} %pad_maximum_fusion.1), channel_id=1, source_target_pairs={{0,4},{4,0},{1,5},{5,1},{2,6},{6,2},{3,7},{7,3},{8,12},{12,8},{9,1... | collective-permute-start | bytes 1327112 | tf_op jit(solution)/shard_map/ppermute | solution.py:370
  2.9 8.1 %copy-start.1 = (s32[12,3]{0,1:T(4,128)S(1)}, s32[12,3]{0,1:T(4,128)}, u32[]{:S(2)}) copy-start(s32[12,3]{0,1:T(4,128)} %param.9) | copy-start | bytes 436
  2.9 12.1 %collective-permute-start.5 = (bf16[192,768]{1,0:T(8,128)(2,1)S(1)}, bf16[192,768]{1,0:T(8,128)(2,1)S(1)}, u32[]{:S(2)}, u32[]{:S(2)}) collective-permute-start(bf16[192,768]{1,0:T(8,128)(2,1)S(1)} %constant_dynamic-slice_fusion.refs_6_.refs_0_), channel_id=1, source_target_pairs={{0,3},{1,0},{2,1},{3,2},{4,7},{5,4},{6,5},{7,6},{8,11},{9,8},{10,9... | collective-permute-start | bytes 884744 | tf_op jit(solution)/shard_map/ppermute | solution.py:401
  9.4 11.6 %collective-permute-start.1 = (bf16[2,3,32,768]{3,2,1,0:T(8,128)(2,1)}, bf16[2,3,32,768]{3,2,1,0:T(8,128)(2,1)S(1)}, u32[]{:S(2)}, u32[]{:S(2)}) collective-permute-start(bf16[2,3,32,768]{3,2,1,0:T(8,128)(2,1)} %get-tuple-element.16), channel_id=1, source_target_pairs={{0,1},{1,0},{2,3},{3,2},{4,5},{5,4},{6,7},{7,6},{8,9},{9,8},{10,11... | collective-permute-start | bytes 884744 | tf_op jit(solution)/shard_map/ppermute | solution.py:390
  9.4 11.6 %collective-permute-start.2 = (bf16[2,3,32,768]{3,2,1,0:T(8,128)(2,1)}, bf16[2,3,32,768]{3,2,1,0:T(8,128)(2,1)S(1)}, u32[]{:S(2)}, u32[]{:S(2)}) collective-permute-start(bf16[2,3,32,768]{3,2,1,0:T(8,128)(2,1)} %get-tuple-element.17), channel_id=1, source_target_pairs={{0,0},{1,2},{2,1},{3,3},{4,4},{5,6},{6,5},{7,7},{8,8},{9,10},{10,9... | collective-permute-start | bytes 884744 | tf_op jit(solution)/shard_map/ppermute | solution.py:390
  11.1 5.1 %collective-permute-start.3 = (bf16[64,768]{1,0:T(8,128)(2,1)}, bf16[64,768]{1,0:T(8,128)(2,1)S(1)}, u32[]{:S(2)}, u32[]{:S(2)}) collective-permute-start(bf16[64,768]{1,0:T(8,128)(2,1)} %get-tuple-element.20), channel_id=1, source_target_pairs={{0,8},{8,0},{16,24},{24,16},{1,9},{9,1},{17,25},{25,17},{2,10},{10... | collective-permute-start | bytes 294920 | tf_op jit(solution)/shard_map/ppermute | solution.py:392
  12.6 3.6 %collective-permute-start.4 = (bf16[64,768]{1,0:T(8,128)(2,1)S(1)}, bf16[64,768]{1,0:T(8,128)(2,1)S(1)}, u32[]{:S(2)}, u32[]{:S(2)}) collective-permute-start(bf16[64,768]{1,0:T(8,128)(2,1)S(1)} %get-tuple-element.21), channel_id=1, source_target_pairs={{0,0},{8,16},{16,8},{24,24},{1,1},{9,17},{17,9},{25,25},{2,2},{10,... | collective-permute-start | bytes 294920 | tf_op jit(solution)/shard_map/ppermute | solution.py:392
  23.1 11.6 %collective-permute-start.8 = (bf16[192,768]{1,0:T(8,128)(2,1)}, bf16[192,768]{1,0:T(8,128)(2,1)S(1)}, u32[]{:S(2)}, u32[]{:S(2)}) collective-permute-start(bf16[192,768]{1,0:T(8,128)(2,1)} %get-tuple-element.24), channel_id=1, source_target_pairs={{0,1},{1,2},{2,3},{3,0},{4,5},{5,6},{6,7},{7,4},{8,9},{9,10},{10,1... | collective-permute-start | bytes 884744 | tf_op jit(solution)/shard_map/ppermute | solution.py:427
  25.6 4.8 %collective-permute-start.6 = (bf16[64,896]{1,0:T(8,128)(2,1)S(1)}, bf16[64,896]{1,0:T(8,128)(2,1)S(1)}, u32[]{:S(2)}, u32[]{:S(2)}) collective-permute-start(bf16[64,896]{1,0:T(8,128)(2,1)S(1)} %get-tuple-element.22), channel_id=1, source_target_pairs={{0,8},{8,0},{16,24},{24,16},{1,9},{9,1},{17,25},{25,17},{2,10},{10... | collective-permute-start | bytes 344072 | tf_op jit(solution)/shard_map/ppermute | solution.py:429
  27.0 3.3 %collective-permute-start.7 = (bf16[64,896]{1,0:T(8,128)(2,1)S(1)}, bf16[64,896]{1,0:T(8,128)(2,1)S(1)}, u32[]{:S(2)}, u32[]{:S(2)}) collective-permute-start(bf16[64,896]{1,0:T(8,128)(2,1)S(1)} %get-tuple-element.23), channel_id=1, source_target_pairs={{0,0},{8,16},{16,8},{24,24},{1,1},{9,17},{17,9},{25,25},{2,2},{10,... | collective-permute-start | bytes 344072 | tf_op jit(solution)/shard_map/ppermute | solution.py:429
  36.0 1.4 %collective-permute-start.9 = (bf16[3,32,768]{2,1,0:T(8,128)(2,1)S(1)}, bf16[3,32,768]{2,1,0:T(8,128)(2,1)S(1)}, u32[]{:S(2)}, u32[]{:S(2)}) collective-permute-start(bf16[3,32,768]{2,1,0:T(8,128)(2,1)S(1)} %get-tuple-element.26), channel_id=1, source_target_pairs={{0,4},{4,0},{1,5},{5,1},{2,6},{6,2},{3,7},{7,3},{8,12},{12,8},{9,1... | collective-permute-start | bytes 442376 | tf_op jit(solution)/shard_map/ppermute | solution.py:460
  36.0 15.9 %collective-permute-start.10 = (bf16[192,768]{1,0:T(8,128)(2,1)}, bf16[192,768]{1,0:T(8,128)(2,1)S(1)}, u32[]{:S(2)}, u32[]{:S(2)}) collective-permute-start(bf16[192,768]{1,0:T(8,128)(2,1)} %get-tuple-element.24), channel_id=1, source_target_pairs={{0,2},{1,3},{2,0},{3,1},{4,6},{5,7},{6,4},{7,5},{8,10},{9,11},{10,... | collective-permute-start | bytes 884744 | tf_op jit(solution)/shard_map/ppermute | solution.py:464
  38.1 13.9 %collective-permute-start.13 = (bf16[96,1536]{1,0:T(8,128)(2,1)}, bf16[96,1536]{1,0:T(8,128)(2,1)S(1)}, u32[]{:S(2)}, u32[]{:S(2)}) collective-permute-start(bf16[96,1536]{1,0:T(8,128)(2,1)} %pad_maximum_fusion.2), channel_id=1, source_target_pairs={{0,24},{8,0},{16,8},{24,16},{1,25},{9,1},{17,9},{25,17},{2,26},{10... | collective-permute-start | bytes 884744 | tf_op jit(solution)/shard_map/ppermute | solution.py:465
  40.6 15.3 %collective-permute-start.12 = (bf16[96,1536]{1,0:T(8,128)(2,1)}, bf16[96,1536]{1,0:T(8,128)(2,1)S(1)}, u32[]{:S(2)}, u32[]{:S(2)}) collective-permute-start(bf16[96,1536]{1,0:T(8,128)(2,1)} %pad_maximum_fusion.2), channel_id=1, source_target_pairs={{0,16},{8,24},{16,0},{24,8},{1,17},{9,25},{17,1},{25,9},{2,18},{10... | collective-permute-start | bytes 884744 | tf_op jit(solution)/shard_map/ppermute | solution.py:465
  41.2 14.7 %collective-permute-start.11 = (bf16[96,1536]{1,0:T(8,128)(2,1)}, bf16[96,1536]{1,0:T(8,128)(2,1)S(1)}, u32[]{:S(2)}, u32[]{:S(2)}) collective-permute-start(bf16[96,1536]{1,0:T(8,128)(2,1)} %pad_maximum_fusion.2), channel_id=1, source_target_pairs={{0,8},{8,16},{16,24},{24,0},{1,9},{9,17},{17,25},{25,1},{2,10},{10... | collective-permute-start | bytes 884744 | tf_op jit(solution)/shard_map/ppermute | solution.py:465
  56.5 2.9 %collective-permute-start.14 = (bf16[768,768]{1,0:T(8,128)(2,1)S(1)}, bf16[768,768]{1,0:T(8,128)(2,1)S(1)}, u32[]{:S(2)}, u32[]{:S(2)}) collective-permute-start(bf16[768,768]{1,0:T(8,128)(2,1)S(1)} %join.1.refs_2_.refs_1_), channel_id=1, source_target_pairs={{0,4},{4,0},{1,5},{5,1},{2,6},{6,2},{3,7},{7,3},{8,12},{12,8},{9,1... | collective-permute-start | bytes 3538952 | tf_op jit(solution)/shard_map/ppermute | solution.py:483
  59.9 7.7 %collective-permute-start.15 = (bf16[96,768]{1,0:T(8,128)(2,1)S(1)}, bf16[96,768]{1,0:T(8,128)(2,1)S(1)}, u32[]{:S(2)}, u32[]{:S(2)}) collective-permute-start(bf16[96,768]{1,0:T(8,128)(2,1)S(1)} %project.5), channel_id=1, source_target_pairs={{0,8},{8,16},{16,24},{24,0},{1,9},{9,17},{17,25},{25,1},{2,10},{10... | collective-permute-start | bytes 442376 | tf_op jit(solution)/shard_map/ppermute | solution.py:506
  60.8 8.8 %collective-permute-start.16 = (bf16[96,768]{1,0:T(8,128)(2,1)S(1)}, bf16[96,768]{1,0:T(8,128)(2,1)S(1)}, u32[]{:S(2)}, u32[]{:S(2)}) collective-permute-start(bf16[96,768]{1,0:T(8,128)(2,1)S(1)} %project.6), channel_id=1, source_target_pairs={{0,16},{8,24},{16,0},{24,8},{1,17},{9,25},{17,1},{25,9},{2,18},{10... | collective-permute-start | bytes 442376 | tf_op jit(solution)/shard_map/ppermute | solution.py:506
  62.8 6.8 %collective-permute-start.17 = (bf16[96,768]{1,0:T(8,128)(2,1)S(1)}, bf16[96,768]{1,0:T(8,128)(2,1)S(1)}, u32[]{:S(2)}, u32[]{:S(2)}) collective-permute-start(bf16[96,768]{1,0:T(8,128)(2,1)S(1)} %project.7), channel_id=1, source_target_pairs={{0,24},{8,0},{16,8},{24,16},{1,25},{9,1},{17,9},{25,17},{2,26},{10... | collective-permute-start | bytes 442376 | tf_op jit(solution)/shard_map/ppermute | solution.py:506

commit v3 on v2

--- a/solution.py
+++ b/solution.py
@@ -178,7 +178,7 @@
 
 def guest_kernel(rims, heads, width, meta_ref, radius_ref, code_ref, *refs):
     window = Window(refs, rims, heads, width)
-    guests, (shard, _, *outs, sent, sem) = window.rest[:2], window.rest[2:]
+    guests, (shard, *outs, sent, sem) = window.rest[:2], window.rest[2:]
     passing = pltpu.make_async_copy(shard, sent, sem)
     passing.start()
     code = code_ref[...]
@@ -265,7 +265,7 @@
 
 
 def merge_kernel(
-    heads, width, meta_ref, radius_ref, mixed_ref, stats_ref, ref_0, ref_1, _, own_out, other_out, held, logs
+    heads, width, meta_ref, radius_ref, mixed_ref, stats_ref, ref_0, ref_1, out_ref, held, logs
 ):
     frames, count, _ = mixed_ref.shape
     half = count // PAIR
@@ -300,8 +300,8 @@
                 + ref[:, lanes].astype(jnp.float32) * guest_weight[:, head : head + 1]
             )
     mixed = held[...].astype(jnp.bfloat16)
-    own_out[...] = mixed[:, :half]
-    other_out[...] = mixed[:, half:]
+    for part in range(PAIR):
+        out_ref[part] = mixed[:, part * half : (part + 1) * half]
 
 
 def join_kernel(count, meta_ref, *refs):
@@ -312,17 +312,15 @@
         out[pl.ds(begin, depth)] = ref[...]
 
 
-def project_kernel(*refs):
-    rows, (near, far), out = refs[:-3], refs[-3:-1], refs[-1]
-    half = near.shape[0]
-    if len(rows) == 1:
-        first, second = rows[0][:, :half], rows[0][:, half:]
-    else:
-        first, second = rows[0][...], rows[1][...]
-    out[...] = (
-        jnp.dot(first, near[...], preferred_element_type=jnp.float32)
-        + jnp.dot(second, far[...], preferred_element_type=jnp.float32)
-    ).astype(out.dtype)
+def project_kernel(rows, near, own_out, other_out):
+    both = jnp.dot(rows[...], near[...], preferred_element_type=jnp.float32)
+    half = own_out.shape[0]
+    own_out[...] = both[:half]
+    other_out[...] = both[half:]
+
+
+def total_kernel(part, partner, out):
+    out[...] = (part[...] + partner[...]).astype(out.dtype)
 
 
 def place_kernel(count, meta_ref, *refs):
@@ -398,7 +396,7 @@
     mine = lax.dynamic_slice_in_dim(out_weight, at_time * wide, wide, axis=1)
     held = {0: mine}
     if n_cols > 1:
-        held[n_cols - 1] = lax.ppermute(mine, "wa", cycle(n_cols, n_cols - 1))
+        held[1] = lax.ppermute(mine, "wa", cycle(n_cols, 1))
 
     table = jnp.asarray(code_table(rows, cols, rims))
     absent = [~x for x in there]
@@ -416,15 +414,15 @@
     *answers, sent = pl.pallas_call(
         functools.partial(guest_kernel, rims, heads, width),
         out_shape=(payload, payload, jax.ShapeDtypeStruct(mine.shape, mine.dtype)),
-        in_specs=[SMEM, SMEM] + [VMEM] * (1 + len(parts) + 2) + [VMEM, HBM],
+        in_specs=[SMEM, SMEM] + [VMEM] * (1 + len(parts) + 2) + [VMEM],
         out_specs=(VMEM, VMEM, VMEM),
         scratch_shapes=[pltpu.SemaphoreType.DMA],
         compiler_params=PARAMS,
         cost_estimate=cost(2 * unit, 4_000_000),
         name="guest",
-    )(meta, radius, code, *parts, *guests, mine, held[max(held)])
+    )(meta, radius, code, *parts, *guests, held[min(1, n_cols - 1)])
     if n_cols > 2:
-        held[1] = lax.ppermute(sent, "wa", cycle(n_cols, 1))
+        held[2] = lax.ppermute(sent, "wa", cycle(n_cols, 1))
     answers = [
         lax.ppermute(x, "ta", swaps(n_time, phase)) for phase, x in enumerate(answers)
     ]
@@ -441,12 +439,11 @@
         cost_estimate=cost(7 * unit, 6_000_000),
         name="host",
     )(meta, radius, code, *parts)
-    att = jax.ShapeDtypeStruct((frames, area, half), jnp.bfloat16)
-    kept, given = pl.pallas_call(
+    attended = pl.pallas_call(
         functools.partial(merge_kernel, heads, width),
-        out_shape=(att, att),
-        in_specs=[SMEM, SMEM] + [VMEM] * 4 + [HBM],
-        out_specs=(VMEM, VMEM),
+        out_shape=jax.ShapeDtypeStruct((PAIR, frames, area, half), jnp.bfloat16),
+        in_specs=[SMEM, SMEM] + [VMEM] * 4,
+        out_specs=VMEM,
         scratch_shapes=[
             pltpu.VMEM(mixed_shape, jnp.float32),
             pltpu.VMEM(stats_shape, jnp.float32),
@@ -454,15 +451,12 @@
         compiler_params=PARAMS,
         cost_estimate=cost(1000, 3_000_000),
         name="merge",
-    )(meta, radius, mixed, stats, *answers, held[min(1, n_cols - 1)])
+    )(meta, radius, mixed, stats, *answers)
     tokens = frames * area
-    kept = kept.reshape(tokens, half)
-    taken = lax.ppermute(given, "ha", pairs).reshape(tokens, half)
-    whole = jnp.concatenate([kept, taken], axis=1)
-    for s in range(1, n_cols):
-        if s not in held:
-            held[s] = lax.ppermute(sent, "wa", cycle(n_cols, s))
-    received = [lax.ppermute(whole, "ta", cycle(n_time, s)) for s in range(1, n_time)]
+    attended = attended.reshape(PAIR * tokens, half)
+    for s in range(3, n_cols):
+        held[s] = lax.ppermute(held[s - 1], "wa", cycle(n_cols, 1))
+    received = [lax.ppermute(attended, "ta", cycle(n_time, s)) for s in range(1, n_time)]
 
     def joined(shards, at):
         count = len(shards)
@@ -472,36 +466,45 @@
         return pl.pallas_call(
             functools.partial(join_kernel, count),
             out_shape=jax.ShapeDtypeStruct((count * shards[0].shape[0], wide), mine.dtype),
-            in_specs=[SMEM] + [VMEM] * count + [HBM] * len(received),
+            in_specs=[SMEM] + [VMEM] * count + [HBM],
             out_specs=VMEM,
             compiler_params=PARAMS,
             cost_estimate=cost(1000, 2_400_000),
             name="join",
-        )(spots, *shards, *received)
+        )(spots, *shards, received[0])
 
     near = joined([held[s] for s in range(n_cols)], at_col)
-    across = [lax.ppermute(near, "ha", cycle(n_rows, r)) for r in range(1, n_rows)]
-    if n_rows == PAIR:
-        far = across[0]
-    else:
-        full = joined([near, *across], at_row)
-        near, far = (
-            lax.dynamic_slice_in_dim(full, which * half, half, axis=0)
-            for which in (core, 1 - core)
-        )
-
-    def project(*rows):
+    if n_rows > PAIR:
+        across = [lax.ppermute(near, "ha", cycle(n_rows, r)) for r in range(1, n_rows)]
+        near = lax.dynamic_slice_in_dim(joined([near, *across], at_row), core * half, half, axis=0)
+
+    def project(block):
+        part = jax.ShapeDtypeStruct((tokens, wide), jnp.float32)
         return pl.pallas_call(
             project_kernel,
-            out_shape=jax.ShapeDtypeStruct((tokens, wide), queries.dtype),
-            in_specs=[VMEM] * (len(rows) + 2),
-            out_specs=VMEM,
+            out_shape=(part, part),
+            in_specs=[VMEM, VMEM],
+            out_specs=(VMEM, VMEM),
             compiler_params=PARAMS,
             cost_estimate=cost(2 * tokens * features * wide, 3_000_000),
             name="project",
-        )(*rows, near, far)
-
-    products = [project(kept, taken)] + [project(x) for x in received]
+        )(block, near)
+
+    def total(part, partner):
+        return pl.pallas_call(
+            total_kernel,
+            out_shape=jax.ShapeDtypeStruct((tokens, wide), queries.dtype),
+            in_specs=[VMEM, VMEM],
+            out_specs=VMEM,
+            compiler_params=PARAMS,
+            cost_estimate=cost(tokens * wide, 3_000_000),
+            name="total",
+        )(part, partner)
+
+    products = []
+    for block in [attended, *received]:
+        part, given = project(block)
+        products.append(total(part, lax.ppermute(given, "ha", pairs)))
     back = [products[0]] + [
         lax.ppermute(products[n_time - s], "ta", cycle(n_time, s)) for s in range(1, n_time)
     ]

time: 70.8 us -> 63.1 us (0.89)
  waiting for transfers between devices: 33.3 us -> 23.2 us
  starting transfers between devices: 22.8 us -> 26.3 us
  Pallas kernels: 10.2 us -> 9.07 us
  other arithmetic: 0.9 us -> 0.18 us
    ppermute x8 -> x10, waiting for transfers between devices: 21.8 us -> 8.87 us  [the longest x3 5.62 us: shards(): lax.ppermute(attended, 'ta', cycle(n_time, s))]
    ppermute x3, waiting for transfers between devices: 4.49 us -> 7.76 us  [shards(): lax.ppermute(products[n_time - s], 'ta', cycle(n_time, s))]
    ppermute x4, waiting for transfers between devices: 2.25 us -> 0.49 us  [shards(): lax.ppermute(x, 'ta', swaps(n_time, phase))]
    ppermute x4, starting transfers between devices: 4.29 us -> 5.79 us  [shards(): lax.ppermute(x, 'ta', swaps(n_time, phase))]
    ppermute x2, waiting for transfers between devices: 4.76 us -> 6.09 us  [shards(): lax.ppermute(x, 'wa', swaps(n_cols, phase))]
    ppermute x8 -> x10, starting transfers between devices: 12.7 us -> 13.9 us  [the longest x3 8.76 us: shards(): lax.ppermute(attended, 'ta', cycle(n_time, s))]
    concatenate x1 -> x0, other arithmetic: 0.73 us -> none  [shards(): whole = jnp.concatenate([kept, taken], axis=1)]
    pallas_call x1, Pallas kernels: 2.16 us -> 1.45 us  [shards(): pl.pallas_call(functools.partial(guest_kernel, rims, heads, width), out_s...]
  transfers between devices with their start and end apart: 18 -> 20, of which waited for: 11 -> 9; matrix products, arithmetic and copies ran while one was open for 3% -> 2% of each run, Pallas kernels for 7% -> 11%
where the time goes in v3:
time: 63.1 us; the launch traced here: 62.8 us
  starting transfers between devices  26.3 us (42%)
  waiting for transfers between devices  23.2 us (37%)
  Pallas kernels  9.07 us (14%)
  local copies, waits for them, and re-layouts  3.88 us (6%)
    ppermute x3, starting transfers between devices, shards(): lax.ppermute(attended, 'ta', cycle(n_time, s))  8.76 us
    ppermute x3, waiting for transfers between devices, shards(): lax.ppermute(products[n_time - s], 'ta', cycle(n_time, s))  7.76 us
    ppermute x2, waiting for transfers between devices, shards(): lax.ppermute(x, 'wa', swaps(n_cols, phase))  6.09 us
    ppermute x4, starting transfers between devices, shards(): lax.ppermute(x, 'ta', swaps(n_time, phase))  5.79 us
    ppermute x3, waiting for transfers between devices, shards(): lax.ppermute(attended, 'ta', cycle(n_time, s))  5.62 us
    ppermute x3, starting transfers between devices, shards(): lax.ppermute(products[n_time - s], 'ta', cycle(n_time, s))  3.85 us
    ppermute x1, starting transfers between devices, shards(): held[1] = lax.ppermute(mine, 'wa', cycle(n_cols, 1))  2.67 us
    another operation x2, local copies, waits for them, and re-layouts, shards(): jnp.stack([lax.dynamic_slice_in_dim(x, which * half, half, axis=2) for x...  2.27 us
  transfers between devices with their start and end apart: 20, of which 9 were waited for; matrix products, arithmetic and copies ran while one was open for 2% of the time, Pallas kernels for 11%

profile of v3, /device:TPU:0, one launch (start us, length us, event | category | flops | bytes accessed | tf_op | source)
XLA Modules:
  0.0 62.8 jit_solution(6608049378943778226)
XLA Ops:
  0.0 1.1 %dynamic-slice_bitcast_fusion.2 = (bf16[1,3,32,768]{3,2,1,0:T(8,128)(2,1)S(1)}, bf16[1,3,32,768]{3,2,1,0:T(8,128)(2,1)S(1)}) fusion(bf16[3,32,1536]{2,1,0:T(8,128)(2,1)} %bitcast.35, s32[]{:T(128)S(6)} %select_n.97, s32[]{:T(128)S(6)} %select_n.96), kind=kLoop, calls=%fused_computation.4 | loop fusion | bytes 589832 | tf_op jit(solution)/shard_map/stack | solution.py:365
  1.1 1.2 %dynamic-slice_bitcast_fusion = (bf16[1,3,32,768]{3,2,1,0:T(8,128)(2,1)S(1)}, bf16[1,3,32,768]{3,2,1,0:T(8,128)(2,1)S(1)}, bf16[1,3,32,768]{3,2,1,0:T(8,128)(2,1)S(1)}, bf16[1,3,32,768]{3,2,1,0:T(8,128)(2,1)S(1)}) fusion(bf16[3,32,1536]{2,1,0:T(8,128)(2,1)} %bitcast.36, s32[]{:T(128)S(6)} %select_n.97, s32[]{:T(128)S(6)} %select_n.96, ...), kind=kLoop, calls=%fused_computation.2 | loop fusion | bytes 1179656 | tf_op jit(solution)/shard_map/stack | solution.py:365
  2.9 2.7 %collective-permute-start.5 = (bf16[192,768]{1,0:T(8,128)(2,1)S(1)}, bf16[192,768]{1,0:T(8,128)(2,1)S(1)}, u32[]{:S(2)}, u32[]{:S(2)}) collective-permute-start(bf16[192,768]{1,0:T(8,128)(2,1)S(1)} %constant_dynamic-slice_fusion.refs_0_), channel_id=1, source_target_pairs={{0,1},{1,2},{2,3},{3,0},{4,5},{5,6},{6,7},{7,4},{8,9},{9,10},{10,1... | collective-permute-start | bytes 884744 | tf_op jit(solution)/shard_map/ppermute | solution.py:399
  5.7 1.5 %edge.1 = (bf16[2,3,32,768]{3,2,1,0:T(8,128)(2,1)}, bf16[2,3,32,768]{3,2,1,0:T(8,128)(2,1)S(1)}, bf16[64,768]{1,0:T(8,128)(2,1)S(1)}, bf16[64,768]{1,0:T(8,128)(2,1)S(1)}) custom-call(s32[7]{0:T(128)S(1)} %stack.82.meta_ref, bf16[3,3,32,768]{3,2,1,0:T(8,128)(2,1)S(1)} %pad_maximum_fusion.refs_0_, bf16[3,3,32,768]{3,2,1,0:T(8,128)(2,1)S(1)} %collective-permute-done.refs_1_), custom_call_target="tpu_custom_call" | custom-call | flops 1000 | bytes 2000000 | tf_op jit(solution)/shard_map/edge/pallas_call | solution.py:379
  7.9 1.6 %collective-permute-start.1 = (bf16[2,3,32,768]{3,2,1,0:T(8,128)(2,1)}, bf16[2,3,32,768]{3,2,1,0:T(8,128)(2,1)S(1)}, u32[]{:S(2)}, u32[]{:S(2)}) collective-permute-start(bf16[2,3,32,768]{3,2,1,0:T(8,128)(2,1)} %get-tuple-element.22), channel_id=1, source_target_pairs={{0,1},{1,0},{2,3},{3,2},{4,5},{5,4},{6,7},{7,6},{8,9},{9,8},{10,11... | collective-permute-start | bytes 884744 | tf_op jit(solution)/shard_map/ppermute | solution.py:388
  10.3 1.5 %collective-permute-start.3 = (bf16[64,768]{1,0:T(8,128)(2,1)}, bf16[64,768]{1,0:T(8,128)(2,1)S(1)}, u32[]{:S(2)}, u32[]{:S(2)}) collective-permute-start(bf16[64,768]{1,0:T(8,128)(2,1)} %copy-done.2), channel_id=1, source_target_pairs={{0,8},{8,0},{16,24},{24,16},{1,9},{9,1},{17,25},{25,17},{2,10},{10... | collective-permute-start | bytes 294920 | tf_op jit(solution)/shard_map/ppermute | solution.py:390
  11.8 1.5 %collective-permute-start.4 = (bf16[64,768]{1,0:T(8,128)(2,1)}, bf16[64,768]{1,0:T(8,128)(2,1)S(1)}, u32[]{:S(2)}, u32[]{:S(2)}) collective-permute-start(bf16[64,768]{1,0:T(8,128)(2,1)} %copy-done.1), channel_id=1, source_target_pairs={{0,0},{8,16},{16,8},{24,24},{1,1},{9,17},{17,9},{25,25},{2,2},{10,... | collective-permute-start | bytes 294920 | tf_op jit(solution)/shard_map/ppermute | solution.py:390
  14.1 1.4 %collective-permute-done.5.refs_6_.refs_1_ = bf16[192,768]{1,0:T(8,128)(2,1)S(1)} collective-permute-done((bf16[192,768]{1,0:T(8,128)(2,1)S(1)}, bf16[192,768]{1,0:T(8,128)(2,1)S(1)}, u32[]{:S(2)}, u32[]{:S(2)}) %collective-permute-start.5) | collective-permute-done | bytes 294944 | tf_op jit(solution)/shard_map/ppermute | solution.py:399
  15.5 6.1 %collective-permute-done.1.refs_2_ = bf16[2,3,32,768]{3,2,1,0:T(8,128)(2,1)S(1)} collective-permute-done((bf16[2,3,32,768]{3,2,1,0:T(8,128)(2,1)}, bf16[2,3,32,768]{3,2,1,0:T(8,128)(2,1)S(1)}, u32[]{:S(2)}, u32[]{:S(2)}) %collective-permute-start.1) | collective-permute-done | bytes 294944 | tf_op jit(solution)/shard_map/ppermute | solution.py:388
  21.6 1.4 %guest.1 = (bf16[64,896]{1,0:T(8,128)(2,1)S(1)}, bf16[64,896]{1,0:T(8,128)(2,1)S(1)}, bf16[192,768]{1,0:T(8,128)(2,1)S(1)}) custom-call(s32[7]{0:T(128)S(1)} %stack.82.meta_ref, s32[12,3]{1,0:T(8,128)S(1)} %copy.9.radius_ref, s32[64,128]{1,0:T(8,128)S(1)} %dynamic-slice_bitcast_fusion.6.code_ref, bf16[3,3,32,768]{3,2,1,0:T(8,128)(2,1)S(1)} %pad_maximum_fusion.refs_0_, ...), custom_call_target="tpu_custom_call" | custom-call | flops 50331648 | bytes 4000000 | tf_op jit(solution)/shard_map/guest/pallas_call | solution.py:414
  23.7 2.1 %collective-permute-start.6 = (bf16[64,896]{1,0:T(8,128)(2,1)S(1)}, bf16[64,896]{1,0:T(8,128)(2,1)S(1)}, u32[]{:S(2)}, u32[]{:S(2)}) collective-permute-start(bf16[64,896]{1,0:T(8,128)(2,1)S(1)} %get-tuple-element.28), channel_id=1, source_target_pairs={{0,8},{8,0},{16,24},{24,16},{1,9},{9,1},{17,25},{25,17},{2,10},{10... | collective-permute-start | bytes 344072 | tf_op jit(solution)/shard_map/ppermute | solution.py:427
  26.4 1.6 %host.1 = (f32[3,64,768]{2,1,0:T(8,128)S(1)}, f32[3,64,128]{2,1,0:T(8,128)S(1)}) custom-call(s32[7]{0:T(128)S(1)} %stack.82.meta_ref, s32[12,3]{1,0:T(8,128)S(1)} %copy.9.radius_ref, s32[64,128]{1,0:T(8,128)S(1)} %dynamic-slice_bitcast_fusion.6.code_ref, bf16[3,3,32,768]{3,2,1,0:T(8,128)(2,1)S(1)} %pad_maximum_fusion.refs_0_, ...), custom_call_target="tpu_custom_call" | custom-call | flops 176160768 | bytes 6000000 | tf_op jit(solution)/shard_map/host/pallas_call | solution.py:430
  28.5 1.2 %merge.1 = bf16[2,3,32,768]{3,2,1,0:T(8,128)(2,1)S(1)} custom-call(s32[7]{0:T(128)S(1)} %stack.82.meta_ref, s32[12,3]{1,0:T(8,128)S(1)} %copy.9.radius_ref, f32[3,64,768]{2,1,0:T(8,128)S(1)} %get-tuple-element.24.mixed_ref, f32[3,64,128]{2,1,0:T(8,128)S(1)} %get-tuple-element.25.stats_ref, bf16[64,896]{1,0:T(8,128)(2,1)S(1)} %collective-permute-done.6.ref_0, ...), custom_call_target="tpu_custom_call" | custom-call | flops 1000 | bytes 3000000 | tf_op jit(solution)/shard_map/merge/pallas_call | solution.py:442
  29.8 4.9 %collective-permute-start.10 = (bf16[192,768]{1,0:T(8,128)(2,1)S(1)}, bf16[192,768]{1,0:T(8,128)(2,1)S(1)}, u32[]{:S(2)}, u32[]{:S(2)}) collective-permute-start(bf16[192,768]{1,0:T(8,128)(2,1)S(1)} %bitcast.31), channel_id=1, source_target_pairs={{0,8},{8,16},{16,24},{24,0},{1,9},{9,17},{17,25},{25,1},{2,10},{10... | collective-permute-start | bytes 884744 | tf_op jit(solution)/shard_map/ppermute | solution.py:459
  34.7 1.0 %collective-permute-start.9 = (bf16[192,768]{1,0:T(8,128)(2,1)S(1)}, bf16[192,768]{1,0:T(8,128)(2,1)S(1)}, u32[]{:S(2)}, u32[]{:S(2)}) collective-permute-start(bf16[192,768]{1,0:T(8,128)(2,1)S(1)} %collective-permute-done.8.refs_2_), channel_id=1, source_target_pairs={{0,1},{1,2},{2,3},{3,0},{4,5},{5,6},{6,7},{7,4},{8,9},{9,10},{10,1... | collective-permute-start | bytes 884744 | tf_op jit(solution)/shard_map/ppermute | solution.py:458
  35.7 1.0 %collective-permute-start.15 = (bf16[192,768]{1,0:T(8,128)(2,1)S(1)}, bf16[192,768]{1,0:T(8,128)(2,1)S(1)}, u32[]{:S(2)}, u32[]{:S(2)}) collective-permute-start(bf16[192,768]{1,0:T(8,128)(2,1)S(1)} %bitcast.32), channel_id=1, source_target_pairs={{0,16},{8,24},{16,0},{24,8},{1,17},{9,25},{17,1},{25,9},{2,18},{10... | collective-permute-start | bytes 884744 | tf_op jit(solution)/shard_map/ppermute | solution.py:459
  36.7 2.9 %collective-permute-start.12 = (bf16[192,768]{1,0:T(8,128)(2,1)S(1)}, bf16[192,768]{1,0:T(8,128)(2,1)S(1)}, u32[]{:S(2)}, u32[]{:S(2)}) collective-permute-start(bf16[192,768]{1,0:T(8,128)(2,1)S(1)} %bitcast.33), channel_id=1, source_target_pairs={{0,24},{8,0},{16,8},{24,16},{1,25},{9,1},{17,9},{25,17},{2,26},{10... | collective-permute-start | bytes 884744 | tf_op jit(solution)/shard_map/ppermute | solution.py:459
  39.6 2.6 %collective-permute-done.10.refs_4_.rows = bf16[192,768]{1,0:T(8,128)(2,1)S(1)} collective-permute-done((bf16[192,768]{1,0:T(8,128)(2,1)S(1)}, bf16[192,768]{1,0:T(8,128)(2,1)S(1)}, u32[]{:S(2)}, u32[]{:S(2)}) %collective-permute-start.10) | collective-permute-done | bytes 294944 | tf_op jit(solution)/shard_map/ppermute | solution.py:459
  42.2 1.9 %collective-permute-done.9.refs_3_ = bf16[192,768]{1,0:T(8,128)(2,1)S(1)} collective-permute-done((bf16[192,768]{1,0:T(8,128)(2,1)S(1)}, bf16[192,768]{1,0:T(8,128)(2,1)S(1)}, u32[]{:S(2)}, u32[]{:S(2)}) %collective-permute-start.9) | collective-permute-done | bytes 294944 | tf_op jit(solution)/shard_map/ppermute | solution.py:458
  45.2 2.1 %collective-permute-done.15.rows = bf16[192,768]{1,0:T(8,128)(2,1)S(1)} collective-permute-done((bf16[192,768]{1,0:T(8,128)(2,1)S(1)}, bf16[192,768]{1,0:T(8,128)(2,1)S(1)}, u32[]{:S(2)}, u32[]{:S(2)}) %collective-permute-start.15) | collective-permute-done | bytes 294944 | tf_op jit(solution)/shard_map/ppermute | solution.py:459
  50.2 2.5 %collective-permute-start.19 = (bf16[96,768]{1,0:T(8,128)(2,1)S(1)}, bf16[96,768]{1,0:T(8,128)(2,1)S(1)}, u32[]{:S(2)}, u32[]{:S(2)}) collective-permute-start(bf16[96,768]{1,0:T(8,128)(2,1)S(1)} %total.7), channel_id=1, source_target_pairs={{0,24},{8,0},{16,8},{24,16},{1,25},{9,1},{17,9},{25,17},{2,26},{10... | collective-permute-start | bytes 442376 | tf_op jit(solution)/shard_map/ppermute | solution.py:509
  52.8 1.3 %collective-permute-start.17 = (bf16[96,768]{1,0:T(8,128)(2,1)S(1)}, bf16[96,768]{1,0:T(8,128)(2,1)S(1)}, u32[]{:S(2)}, u32[]{:S(2)}) collective-permute-start(bf16[96,768]{1,0:T(8,128)(2,1)S(1)} %total.6), channel_id=1, source_target_pairs={{0,16},{8,24},{16,0},{24,8},{1,17},{9,25},{17,1},{25,9},{2,18},{10... | collective-permute-start | bytes 442376 | tf_op jit(solution)/shard_map/ppermute | solution.py:509
  54.2 2.8 %collective-permute-done.19.refs_3_ = bf16[96,768]{1,0:T(8,128)(2,1)S(1)} collective-permute-done((bf16[96,768]{1,0:T(8,128)(2,1)S(1)}, bf16[96,768]{1,0:T(8,128)(2,1)S(1)}, u32[]{:S(2)}, u32[]{:S(2)}) %collective-permute-start.19) | collective-permute-done | bytes 147488 | tf_op jit(solution)/shard_map/ppermute | solution.py:509
  57.0 5.0 %collective-permute-done.17.refs_2_ = bf16[96,768]{1,0:T(8,128)(2,1)S(1)} collective-permute-done((bf16[96,768]{1,0:T(8,128)(2,1)S(1)}, bf16[96,768]{1,0:T(8,128)(2,1)S(1)}, u32[]{:S(2)}, u32[]{:S(2)}) %collective-permute-start.17) | collective-permute-done | bytes 147488 | tf_op jit(solution)/shard_map/ppermute | solution.py:509
  (47 shorter events, 9.8 us)
Async XLA Ops:
  0.0 2.9 %copy-start = (bf16[192,3072]{1,0:T(8,128)(2,1)S(1)}, bf16[192,3072]{1,0:T(8,128)(2,1)}, u32[]{:S(2)}) copy-start(bf16[192,3072]{1,0:T(8,128)(2,1)} %param.10) | copy-start | bytes 3538948
  2.3 3.4 %collective-permute-start = (bf16[3,3,32,768]{3,2,1,0:T(8,128)(2,1)S(1)}, bf16[3,3,32,768]{3,2,1,0:T(8,128)(2,1)S(1)}, u32[]{:S(2)}, u32[]{:S(2)}) collective-permute-start(bf16[3,3,32,768]{3,2,1,0:T(8,128)(2,1)S(1)} %pad_maximum_fusion.1), channel_id=1, source_target_pairs={{0,4},{4,0},{1,5},{5,1},{2,6},{6,2},{3,7},{7,3},{8,12},{12,8},{9,1... | collective-permute-start | bytes 1327112 | tf_op jit(solution)/shard_map/ppermute | solution.py:368
  2.9 7.3 %copy-start.3 = (s32[12,3]{0,1:T(4,128)S(1)}, s32[12,3]{0,1:T(4,128)}, u32[]{:S(2)}) copy-start(s32[12,3]{0,1:T(4,128)} %param.9) | copy-start | bytes 436
  2.9 12.6 %collective-permute-start.5 = (bf16[192,768]{1,0:T(8,128)(2,1)S(1)}, bf16[192,768]{1,0:T(8,128)(2,1)S(1)}, u32[]{:S(2)}, u32[]{:S(2)}) collective-permute-start(bf16[192,768]{1,0:T(8,128)(2,1)S(1)} %constant_dynamic-slice_fusion.refs_0_), channel_id=1, source_target_pairs={{0,1},{1,2},{2,3},{3,0},{4,5},{5,6},{6,7},{7,4},{8,9},{9,10},{10,1... | collective-permute-start | bytes 884744 | tf_op jit(solution)/shard_map/ppermute | solution.py:399
  7.3 0.6 %copy-start.2 = (bf16[64,768]{1,0:T(8,128)(2,1)}, bf16[64,768]{1,0:T(8,128)(2,1)S(1)}, u32[]{:S(2)}) copy-start(bf16[64,768]{1,0:T(8,128)(2,1)S(1)} %get-tuple-element.26) | copy-start | bytes 294916
  7.9 1.6 %copy-start.1 = (bf16[64,768]{1,0:T(8,128)(2,1)}, bf16[64,768]{1,0:T(8,128)(2,1)S(1)}, u32[]{:S(2)}) copy-start(bf16[64,768]{1,0:T(8,128)(2,1)S(1)} %get-tuple-element.27) | copy-start | bytes 294916
  7.9 13.6 %collective-permute-start.1 = (bf16[2,3,32,768]{3,2,1,0:T(8,128)(2,1)}, bf16[2,3,32,768]{3,2,1,0:T(8,128)(2,1)S(1)}, u32[]{:S(2)}, u32[]{:S(2)}) collective-permute-start(bf16[2,3,32,768]{3,2,1,0:T(8,128)(2,1)} %get-tuple-element.22), channel_id=1, source_target_pairs={{0,1},{1,0},{2,3},{3,2},{4,5},{5,4},{6,7},{7,6},{8,9},{9,8},{10,11... | collective-permute-start | bytes 884744 | tf_op jit(solution)/shard_map/ppermute | solution.py:388
  9.5 12.1 %collective-permute-start.2 = (bf16[2,3,32,768]{3,2,1,0:T(8,128)(2,1)S(1)}, bf16[2,3,32,768]{3,2,1,0:T(8,128)(2,1)S(1)}, u32[]{:S(2)}, u32[]{:S(2)}) collective-permute-start(bf16[2,3,32,768]{3,2,1,0:T(8,128)(2,1)S(1)} %get-tuple-element.23), channel_id=1, source_target_pairs={{0,0},{1,2},{2,1},{3,3},{4,4},{5,6},{6,5},{7,7},{8,8},{9,10},{10,9... | collective-permute-start | bytes 884744 | tf_op jit(solution)/shard_map/ppermute | solution.py:388
  10.3 5.2 %collective-permute-start.3 = (bf16[64,768]{1,0:T(8,128)(2,1)}, bf16[64,768]{1,0:T(8,128)(2,1)S(1)}, u32[]{:S(2)}, u32[]{:S(2)}) collective-permute-start(bf16[64,768]{1,0:T(8,128)(2,1)} %copy-done.2), channel_id=1, source_target_pairs={{0,8},{8,0},{16,24},{24,16},{1,9},{9,1},{17,25},{25,17},{2,10},{10... | collective-permute-start | bytes 294920 | tf_op jit(solution)/shard_map/ppermute | solution.py:390
  11.8 3.7 %collective-permute-start.4 = (bf16[64,768]{1,0:T(8,128)(2,1)}, bf16[64,768]{1,0:T(8,128)(2,1)S(1)}, u32[]{:S(2)}, u32[]{:S(2)}) collective-permute-start(bf16[64,768]{1,0:T(8,128)(2,1)} %copy-done.1), channel_id=1, source_target_pairs={{0,0},{8,16},{16,8},{24,24},{1,1},{9,17},{17,9},{25,25},{2,2},{10,... | collective-permute-start | bytes 294920 | tf_op jit(solution)/shard_map/ppermute | solution.py:390
  23.0 11.7 %collective-permute-start.8 = (bf16[192,768]{1,0:T(8,128)(2,1)S(1)}, bf16[192,768]{1,0:T(8,128)(2,1)S(1)}, u32[]{:S(2)}, u32[]{:S(2)}) collective-permute-start(bf16[192,768]{1,0:T(8,128)(2,1)S(1)} %get-tuple-element.30), channel_id=1, source_target_pairs={{0,1},{1,2},{2,3},{3,0},{4,5},{5,6},{6,7},{7,4},{8,9},{9,10},{10,1... | collective-permute-start | bytes 884744 | tf_op jit(solution)/shard_map/ppermute | solution.py:425
  23.7 4.9 %collective-permute-start.6 = (bf16[64,896]{1,0:T(8,128)(2,1)S(1)}, bf16[64,896]{1,0:T(8,128)(2,1)S(1)}, u32[]{:S(2)}, u32[]{:S(2)}) collective-permute-start(bf16[64,896]{1,0:T(8,128)(2,1)S(1)} %get-tuple-element.28), channel_id=1, source_target_pairs={{0,8},{8,0},{16,24},{24,16},{1,9},{9,1},{17,25},{25,17},{2,10},{10... | collective-permute-start | bytes 344072 | tf_op jit(solution)/shard_map/ppermute | solution.py:427
  25.8 2.8 %collective-permute-start.7 = (bf16[64,896]{1,0:T(8,128)(2,1)S(1)}, bf16[64,896]{1,0:T(8,128)(2,1)S(1)}, u32[]{:S(2)}, u32[]{:S(2)}) collective-permute-start(bf16[64,896]{1,0:T(8,128)(2,1)S(1)} %get-tuple-element.29), channel_id=1, source_target_pairs={{0,0},{8,16},{16,8},{24,24},{1,1},{9,17},{17,9},{25,25},{2,2},{10,... | collective-permute-start | bytes 344072 | tf_op jit(solution)/shard_map/ppermute | solution.py:427
  29.8 12.4 %collective-permute-start.10 = (bf16[192,768]{1,0:T(8,128)(2,1)S(1)}, bf16[192,768]{1,0:T(8,128)(2,1)S(1)}, u32[]{:S(2)}, u32[]{:S(2)}) collective-permute-start(bf16[192,768]{1,0:T(8,128)(2,1)S(1)} %bitcast.31), channel_id=1, source_target_pairs={{0,8},{8,16},{16,24},{24,0},{1,9},{9,17},{17,25},{25,1},{2,10},{10... | collective-permute-start | bytes 884744 | tf_op jit(solution)/shard_map/ppermute | solution.py:459
  34.7 9.3 %collective-permute-start.9 = (bf16[192,768]{1,0:T(8,128)(2,1)S(1)}, bf16[192,768]{1,0:T(8,128)(2,1)S(1)}, u32[]{:S(2)}, u32[]{:S(2)}) collective-permute-start(bf16[192,768]{1,0:T(8,128)(2,1)S(1)} %collective-permute-done.8.refs_2_), channel_id=1, source_target_pairs={{0,1},{1,2},{2,3},{3,0},{4,5},{5,6},{6,7},{7,4},{8,9},{9,10},{10,1... | collective-permute-start | bytes 884744 | tf_op jit(solution)/shard_map/ppermute | solution.py:458
  35.7 11.6 %collective-permute-start.15 = (bf16[192,768]{1,0:T(8,128)(2,1)S(1)}, bf16[192,768]{1,0:T(8,128)(2,1)S(1)}, u32[]{:S(2)}, u32[]{:S(2)}) collective-permute-start(bf16[192,768]{1,0:T(8,128)(2,1)S(1)} %bitcast.32), channel_id=1, source_target_pairs={{0,16},{8,24},{16,0},{24,8},{1,17},{9,25},{17,1},{25,9},{2,18},{10... | collective-permute-start | bytes 884744 | tf_op jit(solution)/shard_map/ppermute | solution.py:459
  36.7 12.0 %collective-permute-start.12 = (bf16[192,768]{1,0:T(8,128)(2,1)S(1)}, bf16[192,768]{1,0:T(8,128)(2,1)S(1)}, u32[]{:S(2)}, u32[]{:S(2)}) collective-permute-start(bf16[192,768]{1,0:T(8,128)(2,1)S(1)} %bitcast.33), channel_id=1, source_target_pairs={{0,24},{8,0},{16,8},{24,16},{1,25},{9,1},{17,9},{25,17},{2,26},{10... | collective-permute-start | bytes 884744 | tf_op jit(solution)/shard_map/ppermute | solution.py:459
  45.1 5.1 %collective-permute-start.18 = (f32[96,768]{1,0:T(8,128)S(1)}, f32[96,768]{1,0:T(8,128)S(1)}, u32[]{:S(2)}, u32[]{:S(2)}) collective-permute-start(f32[96,768]{1,0:T(8,128)S(1)} %get-tuple-element.38), channel_id=1, source_target_pairs={{0,4},{4,0},{1,5},{5,1},{2,6},{6,2},{3,7},{7,3},{8,12},{12,8},{9,1... | collective-permute-start | bytes 884744 | tf_op jit(solution)/shard_map/ppermute | solution.py:507
  47.7 5.1 %collective-permute-start.16 = (f32[96,768]{1,0:T(8,128)S(1)}, f32[96,768]{1,0:T(8,128)S(1)}, u32[]{:S(2)}, u32[]{:S(2)}) collective-permute-start(f32[96,768]{1,0:T(8,128)S(1)} %get-tuple-element.36), channel_id=1, source_target_pairs={{0,4},{4,0},{1,5},{5,1},{2,6},{6,2},{3,7},{7,3},{8,12},{12,8},{9,1... | collective-permute-start | bytes 884744 | tf_op jit(solution)/shard_map/ppermute | solution.py:507
  49.1 4.9 %collective-permute-start.13 = (f32[96,768]{1,0:T(8,128)S(1)}, f32[96,768]{1,0:T(8,128)S(1)}, u32[]{:S(2)}, u32[]{:S(2)}) collective-permute-start(f32[96,768]{1,0:T(8,128)S(1)} %get-tuple-element.34), channel_id=1, source_target_pairs={{0,4},{4,0},{1,5},{5,1},{2,6},{6,2},{3,7},{7,3},{8,12},{12,8},{9,1... | collective-permute-start | bytes 884744 | tf_op jit(solution)/shard_map/ppermute | solution.py:507
  49.6 4.6 %collective-permute-start.11 = (f32[96,768]{1,0:T(8,128)S(1)}, f32[96,768]{1,0:T(8,128)S(1)}, u32[]{:S(2)}, u32[]{:S(2)}) collective-permute-start(f32[96,768]{1,0:T(8,128)S(1)} %get-tuple-element.32), channel_id=1, source_target_pairs={{0,4},{4,0},{1,5},{5,1},{2,6},{6,2},{3,7},{7,3},{8,12},{12,8},{9,1... | collective-permute-start | bytes 884744 | tf_op jit(solution)/shard_map/ppermute | solution.py:507
  50.2 6.8 %collective-permute-start.19 = (bf16[96,768]{1,0:T(8,128)(2,1)S(1)}, bf16[96,768]{1,0:T(8,128)(2,1)S(1)}, u32[]{:S(2)}, u32[]{:S(2)}) collective-permute-start(bf16[96,768]{1,0:T(8,128)(2,1)S(1)} %total.7), channel_id=1, source_target_pairs={{0,24},{8,0},{16,8},{24,16},{1,25},{9,1},{17,9},{25,17},{2,26},{10... | collective-permute-start | bytes 442376 | tf_op jit(solution)/shard_map/ppermute | solution.py:509
  52.8 9.2 %collective-permute-start.17 = (bf16[96,768]{1,0:T(8,128)(2,1)S(1)}, bf16[96,768]{1,0:T(8,128)(2,1)S(1)}, u32[]{:S(2)}, u32[]{:S(2)}) collective-permute-start(bf16[96,768]{1,0:T(8,128)(2,1)S(1)} %total.6), channel_id=1, source_target_pairs={{0,16},{8,24},{16,0},{24,8},{1,17},{9,25},{17,1},{25,9},{2,18},{10... | collective-permute-start | bytes 442376 | tf_op jit(solution)/shard_map/ppermute | solution.py:509
  54.1 7.9 %collective-permute-start.14 = (bf16[96,768]{1,0:T(8,128)(2,1)S(1)}, bf16[96,768]{1,0:T(8,128)(2,1)S(1)}, u32[]{:S(2)}, u32[]{:S(2)}) collective-permute-start(bf16[96,768]{1,0:T(8,128)(2,1)S(1)} %total.5), channel_id=1, source_target_pairs={{0,8},{8,16},{16,24},{24,0},{1,9},{9,17},{17,25},{25,1},{2,10},{10... | collective-permute-start | bytes 442376 | tf_op jit(solution)/shard_map/ppermute | solution.py:509

commit v4 on v3

--- a/solution.py
+++ b/solution.py
@@ -24,9 +24,14 @@
     return [(i, (i + step) % count) for i in range(count)]
 
 
-def swaps(count, phase):
-    partners = [(i ^ 1) if phase == 0 else ((i + 1) ^ 1) - 1 for i in range(count)]
-    return [(i, p if 0 <= p < count else i) for i, p in enumerate(partners)]
+def swaps(count, phase, n_rows, rows_first):
+    pairs = []
+    for row in range(n_rows):
+        for i in range(count):
+            p = (i ^ 1) if phase == 0 else ((i + 1) ^ 1) - 1
+            ends = ((row, i), (row, p) if 0 <= p < count else (row ^ 1, i))
+            pairs.append(tuple(r * count + j if rows_first else j * n_rows + r for r, j in ends))
+    return pairs
 
 
 def line(count, step):
@@ -361,9 +366,9 @@
 
     raw = [x.reshape(frames, area, features) for x in (queries, keys, values)]
     pairs = [(i, i ^ 1) for i in range(n_rows)]
+    stacked = jnp.stack(raw)
     own, other = (
-        jnp.stack([lax.dynamic_slice_in_dim(x, which * half, half, axis=2) for x in raw])
-        for which in (core, 1 - core)
+        lax.dynamic_slice_in_dim(stacked, which * half, half, axis=3) for which in (core, 1 - core)
     )
     other = lax.ppermute(other, "ha", pairs)
     rim = None
@@ -385,9 +390,9 @@
         cost_estimate=cost(1000, 2_000_000),
         name="edge",
     )(meta, own, other, *([rim] if rims else []))
-    beside = [lax.ppermute(x, "wa", swaps(n_cols, phase)) for phase, x in enumerate(edges)]
+    beside = [lax.ppermute(x, ("ha", "wa"), swaps(n_cols, phase, n_rows, True)) for phase, x in enumerate(edges)]
     guests = [
-        lax.ppermute(x, "ta", swaps(n_time, phase))
+        lax.ppermute(x, ("ta", "ha"), swaps(n_time, phase, n_rows, False))
         for phase, x in enumerate((first_end, second_end))
     ]
 
@@ -424,7 +429,7 @@
     if n_cols > 2:
         held[2] = lax.ppermute(sent, "wa", cycle(n_cols, 1))
     answers = [
-        lax.ppermute(x, "ta", swaps(n_time, phase)) for phase, x in enumerate(answers)
+        lax.ppermute(x, ("ta", "ha"), swaps(n_time, phase, n_rows, False)) for phase, x in enumerate(answers)
     ]
     mixed_shape, stats_shape = (frames, count, half), (frames, count, LANES)
     mixed, stats = pl.pallas_call(

time: 63.1 us -> 62.1 us (0.984)
  starting transfers between devices: 26.3 us -> 21.3 us
  waiting for transfers between devices: 23.2 us -> 27.7 us
  local copies, waits for them, and re-layouts: 3.88 us -> 2.31 us
  other arithmetic: 0.18 us -> 1.41 us
    ppermute x6, starting transfers between devices: 8.04 us -> 4.79 us  [the longest x4 3.21 us: shards(): lax.ppermute(x, ('ta', 'ha'), swaps(n_time, phase, n_rows, False))]
    another operation x2 -> x0, local copies, waits for them, and re-layouts: 2.27 us -> none  [shards(): jnp.stack([lax.dynamic_slice_in_dim(x, which * half, half, axis=2) for x...]
    ppermute x3, starting transfers between devices: 8.76 us -> 6.89 us  [shards(): lax.ppermute(attended, 'ta', cycle(n_time, s))]
    ppermute x1, waiting for transfers between devices: 1.36 us -> 2.89 us  [shards(): held[1] = lax.ppermute(mine, 'wa', cycle(n_cols, 1))]
    ppermute x6, waiting for transfers between devices: 6.57 us -> 8.03 us  [the longest x2 5.99 us: shards(): lax.ppermute(x, ('ha', 'wa'), swaps(n_cols, phase, n_rows, True))]
    another operation x2 -> x1, other arithmetic: 0.1 us -> 1.33 us  [shards(): stacked = jnp.stack(raw)]
    ppermute x3, waiting for transfers between devices: 5.62 us -> 6.48 us  [shards(): lax.ppermute(attended, 'ta', cycle(n_time, s))]
    ppermute x3, starting transfers between devices: 3.85 us -> 4.66 us  [shards(): lax.ppermute(products[n_time - s], 'ta', cycle(n_time, s))]
where the time goes in v4:
time: 62.1 us; the launch traced here: 61.9 us
  waiting for transfers between devices  27.7 us (45%)
  starting transfers between devices  21.3 us (34%)
  Pallas kernels  9.05 us (15%)
  local copies, waits for them, and re-layouts  2.31 us (4%)
  other arithmetic  1.41 us (2%)
    ppermute x3, waiting for transfers between devices, shards(): lax.ppermute(products[n_time - s], 'ta', cycle(n_time, s))  8.41 us
    ppermute x3, starting transfers between devices, shards(): lax.ppermute(attended, 'ta', cycle(n_time, s))  6.89 us
    ppermute x3, waiting for transfers between devices, shards(): lax.ppermute(attended, 'ta', cycle(n_time, s))  6.48 us
    ppermute x2, waiting for transfers between devices, shards(): lax.ppermute(x, ('ha', 'wa'), swaps(n_cols, phase, n_rows, True))  5.99 us
    ppermute x3, starting transfers between devices, shards(): lax.ppermute(products[n_time - s], 'ta', cycle(n_time, s))  4.66 us
    ppermute x4, starting transfers between devices, shards(): lax.ppermute(x, ('ta', 'ha'), swaps(n_time, phase, n_rows, False))  3.21 us
    ppermute x1, waiting for transfers between devices, shards(): held[1] = lax.ppermute(mine, 'wa', cycle(n_cols, 1))  2.89 us
    ppermute x1, starting transfers between devices, shards(): held[1] = lax.ppermute(mine, 'wa', cycle(n_cols, 1))  2.67 us
  transfers between devices with their start and end apart: 20, of which 9 were waited for; matrix products, arithmetic and copies ran while one was open for 2% of the time, Pallas kernels for 11%

profile of v4, /device:TPU:0, one launch (start us, length us, event | category | flops | bytes accessed | tf_op | source)
XLA Modules:
  0.0 61.9 jit_solution(1494366686084546625)
XLA Ops:
  0.0 1.3 %pad_maximum_fusion = bf16[3,3,32,1536]{3,2,1,0:T(8,128)(2,1)S(1)} fusion(bf16[1,3,32,1536]{3,2,1,0:T(8,128)(2,1)} %bitcast.23, bf16[1,3,32,1536]{3,2,1,0:T(8,128)(2,1)} %bitcast.24, bf16[1,3,32,1536]{3,2,1,0:T(8,128)(2,1)} %bitcast.25), kind=kLoop, calls=%fused_computation | loop fusion | flops 884736 | bytes 1769472 | tf_op jit(solution)/shard_map/stack | solution.py:369
  2.0 2.7 %collective-permute-start.5 = (bf16[192,768]{1,0:T(8,128)(2,1)S(1)}, bf16[192,768]{1,0:T(8,128)(2,1)S(1)}, u32[]{:S(2)}, u32[]{:S(2)}) collective-permute-start(bf16[192,768]{1,0:T(8,128)(2,1)S(1)} %constant_dynamic-slice_fusion.refs_0_), channel_id=1, source_target_pairs={{0,1},{1,2},{2,3},{3,0},{4,5},{5,6},{6,7},{7,4},{8,9},{9,10},{10,1... | collective-permute-start | bytes 884744 | tf_op jit(solution)/shard_map/ppermute | solution.py:404
  4.7 1.5 %edge.1 = (bf16[2,3,32,768]{3,2,1,0:T(8,128)(2,1)}, bf16[2,3,32,768]{3,2,1,0:T(8,128)(2,1)S(1)}, bf16[64,768]{1,0:T(8,128)(2,1)S(1)}, bf16[64,768]{1,0:T(8,128)(2,1)S(1)}) custom-call(s32[7]{0:T(128)S(1)} %stack.61.meta_ref, bf16[3,3,32,768]{3,2,1,0:T(8,128)(2,1)S(1)} %get-tuple-element.40.refs_0_, bf16[3,3,32,768]{3,2,1,0:T(8,128)(2,1)S(1)} %collective-permute-done.refs_1_), custom_call_target="tpu_custom_call" | custom-call | flops 1000 | bytes 2000000 | tf_op jit(solution)/shard_map/edge/pallas_call | solution.py:384
  6.3 0.6 %copy-done.1 = bf16[64,768]{1,0:T(8,128)(2,1)} copy-done((bf16[64,768]{1,0:T(8,128)(2,1)}, bf16[64,768]{1,0:T(8,128)(2,1)S(1)}, u32[]{:S(2)}) %copy-start.1) | copy-done | bytes 98328
  7.5 1.6 %collective-permute-start.1 = (bf16[2,3,32,768]{3,2,1,0:T(8,128)(2,1)}, bf16[2,3,32,768]{3,2,1,0:T(8,128)(2,1)S(1)}, u32[]{:S(2)}, u32[]{:S(2)}) collective-permute-start(bf16[2,3,32,768]{3,2,1,0:T(8,128)(2,1)} %get-tuple-element.22), channel_id=1, source_target_pairs={{0,1},{1,0},{2,3},{3,2},{4,5},{5,4},{6,7},{7,6},{8,9},{9,8},{10,11... | collective-permute-start | bytes 884744 | tf_op jit(solution)/shard_map/ppermute | solution.py:393
  9.2 1.5 %collective-permute-start.3 = (bf16[64,768]{1,0:T(8,128)(2,1)}, bf16[64,768]{1,0:T(8,128)(2,1)S(1)}, u32[]{:S(2)}, u32[]{:S(2)}) collective-permute-start(bf16[64,768]{1,0:T(8,128)(2,1)} %copy-done.2), channel_id=1, source_target_pairs={{0,8},{8,0},{16,24},{24,16},{4,12},{12,4},{20,28},{28,20},{1,9},{9... | collective-permute-start | bytes 294920 | tf_op jit(solution)/shard_map/ppermute | solution.py:395
  10.9 0.8 %dynamic-slice_bitcast_fusion.code_ref = s32[64,128]{1,0:T(8,128)S(1)} fusion(s32[16,64,128]{2,1,0:T(8,128)} %constant.79.clone, s32[]{:T(128)S(6)} %select_n.91), kind=kLoop, calls=%fused_computation.1 | loop fusion | bytes 65540 | tf_op jit(solution)/shard_map/jit(dynamic_index_in_dim)/squeeze | solution.py:412
  11.7 2.9 %collective-permute-done.5.refs_6_.refs_1_ = bf16[192,768]{1,0:T(8,128)(2,1)S(1)} collective-permute-done((bf16[192,768]{1,0:T(8,128)(2,1)S(1)}, bf16[192,768]{1,0:T(8,128)(2,1)S(1)}, u32[]{:S(2)}, u32[]{:S(2)}) %collective-permute-start.5) | collective-permute-done | bytes 294944 | tf_op jit(solution)/shard_map/ppermute | solution.py:404
  14.6 6.0 %collective-permute-done.1.refs_2_ = bf16[2,3,32,768]{3,2,1,0:T(8,128)(2,1)S(1)} collective-permute-done((bf16[2,3,32,768]{3,2,1,0:T(8,128)(2,1)}, bf16[2,3,32,768]{3,2,1,0:T(8,128)(2,1)S(1)}, u32[]{:S(2)}, u32[]{:S(2)}) %collective-permute-start.1) | collective-permute-done | bytes 294944 | tf_op jit(solution)/shard_map/ppermute | solution.py:393
  20.6 1.4 %guest.1 = (bf16[64,896]{1,0:T(8,128)(2,1)S(1)}, bf16[64,896]{1,0:T(8,128)(2,1)S(1)}, bf16[192,768]{1,0:T(8,128)(2,1)S(1)}) custom-call(s32[7]{0:T(128)S(1)} %stack.61.meta_ref, s32[12,3]{1,0:T(8,128)S(1)} %copy.9.radius_ref, s32[64,128]{1,0:T(8,128)S(1)} %dynamic-slice_bitcast_fusion.code_ref, bf16[3,3,32,768]{3,2,1,0:T(8,128)(2,1)S(1)} %get-tuple-element.40.refs_0_, ...), custom_call_target="tpu_custom_call" | custom-call | flops 50331648 | bytes 4000000 | tf_op jit(solution)/shard_map/guest/pallas_call | solution.py:419
  22.1 0.7 %collective-permute-start.8 = (bf16[192,768]{1,0:T(8,128)(2,1)S(1)}, bf16[192,768]{1,0:T(8,128)(2,1)S(1)}, u32[]{:S(2)}, u32[]{:S(2)}) collective-permute-start(bf16[192,768]{1,0:T(8,128)(2,1)S(1)} %get-tuple-element.30), channel_id=1, source_target_pairs={{0,1},{1,2},{2,3},{3,0},{4,5},{5,6},{6,7},{7,4},{8,9},{9,10},{10,1... | collective-permute-start | bytes 884744 | tf_op jit(solution)/shard_map/ppermute | solution.py:430
  22.7 1.5 %collective-permute-start.6 = (bf16[64,896]{1,0:T(8,128)(2,1)S(1)}, bf16[64,896]{1,0:T(8,128)(2,1)S(1)}, u32[]{:S(2)}, u32[]{:S(2)}) collective-permute-start(bf16[64,896]{1,0:T(8,128)(2,1)S(1)} %get-tuple-element.28), channel_id=1, source_target_pairs={{0,8},{8,0},{16,24},{24,16},{4,12},{12,4},{20,28},{28,20},{1,9},{9... | collective-permute-start | bytes 344072 | tf_op jit(solution)/shard_map/ppermute | solution.py:432
  24.2 1.6 %host.1 = (f32[3,64,768]{2,1,0:T(8,128)S(1)}, f32[3,64,128]{2,1,0:T(8,128)S(1)}) custom-call(s32[7]{0:T(128)S(1)} %stack.61.meta_ref, s32[12,3]{1,0:T(8,128)S(1)} %copy.9.radius_ref, s32[64,128]{1,0:T(8,128)S(1)} %dynamic-slice_bitcast_fusion.code_ref, bf16[3,3,32,768]{3,2,1,0:T(8,128)(2,1)S(1)} %get-tuple-element.40.refs_0_, ...), custom_call_target="tpu_custom_call" | custom-call | flops 176160768 | bytes 6000000 | tf_op jit(solution)/shard_map/host/pallas_call | solution.py:435
  25.9 2.0 %collective-permute-done.6.ref_0 = bf16[64,896]{1,0:T(8,128)(2,1)S(1)} collective-permute-done((bf16[64,896]{1,0:T(8,128)(2,1)S(1)}, bf16[64,896]{1,0:T(8,128)(2,1)S(1)}, u32[]{:S(2)}, u32[]{:S(2)}) %collective-permute-start.6) | collective-permute-done | bytes 114720 | tf_op jit(solution)/shard_map/ppermute | solution.py:432
  27.9 1.2 %merge.1 = bf16[2,3,32,768]{3,2,1,0:T(8,128)(2,1)S(1)} custom-call(s32[7]{0:T(128)S(1)} %stack.61.meta_ref, s32[12,3]{1,0:T(8,128)S(1)} %copy.9.radius_ref, f32[3,64,768]{2,1,0:T(8,128)S(1)} %get-tuple-element.24.mixed_ref, f32[3,64,128]{2,1,0:T(8,128)S(1)} %get-tuple-element.25.stats_ref, bf16[64,896]{1,0:T(8,128)(2,1)S(1)} %collective-permute-done.6.ref_0, ...), custom_call_target="tpu_custom_call" | custom-call | flops 1000 | bytes 3000000 | tf_op jit(solution)/shard_map/merge/pallas_call | solution.py:447
  29.1 4.6 %collective-permute-start.10 = (bf16[192,768]{1,0:T(8,128)(2,1)S(1)}, bf16[192,768]{1,0:T(8,128)(2,1)S(1)}, u32[]{:S(2)}, u32[]{:S(2)}) collective-permute-start(bf16[192,768]{1,0:T(8,128)(2,1)S(1)} %bitcast.19), channel_id=1, source_target_pairs={{0,8},{8,16},{16,24},{24,0},{1,9},{9,17},{17,25},{25,1},{2,10},{10... | collective-permute-start | bytes 884744 | tf_op jit(solution)/shard_map/ppermute | solution.py:464
  34.4 1.9 %collective-permute-start.12 = (bf16[192,768]{1,0:T(8,128)(2,1)S(1)}, bf16[192,768]{1,0:T(8,128)(2,1)S(1)}, u32[]{:S(2)}, u32[]{:S(2)}) collective-permute-start(bf16[192,768]{1,0:T(8,128)(2,1)S(1)} %bitcast.21), channel_id=1, source_target_pairs={{0,24},{8,0},{16,8},{24,16},{1,25},{9,1},{17,9},{25,17},{2,26},{10... | collective-permute-start | bytes 884744 | tf_op jit(solution)/shard_map/ppermute | solution.py:464
  36.4 4.8 %collective-permute-done.10.refs_4_.rows = bf16[192,768]{1,0:T(8,128)(2,1)S(1)} collective-permute-done((bf16[192,768]{1,0:T(8,128)(2,1)S(1)}, bf16[192,768]{1,0:T(8,128)(2,1)S(1)}, u32[]{:S(2)}, u32[]{:S(2)}) %collective-permute-start.10) | collective-permute-done | bytes 294944 | tf_op jit(solution)/shard_map/ppermute | solution.py:464
  41.2 1.8 %collective-permute-done.9.refs_3_ = bf16[192,768]{1,0:T(8,128)(2,1)S(1)} collective-permute-done((bf16[192,768]{1,0:T(8,128)(2,1)S(1)}, bf16[192,768]{1,0:T(8,128)(2,1)S(1)}, u32[]{:S(2)}, u32[]{:S(2)}) %collective-permute-start.9) | collective-permute-done | bytes 294944 | tf_op jit(solution)/shard_map/ppermute | solution.py:463
  44.2 1.2 %collective-permute-done.15.rows = bf16[192,768]{1,0:T(8,128)(2,1)S(1)} collective-permute-done((bf16[192,768]{1,0:T(8,128)(2,1)S(1)}, bf16[192,768]{1,0:T(8,128)(2,1)S(1)}, u32[]{:S(2)}, u32[]{:S(2)}) %collective-permute-start.15) | collective-permute-done | bytes 294944 | tf_op jit(solution)/shard_map/ppermute | solution.py:464
  47.9 4.0 %collective-permute-start.19 = (bf16[96,768]{1,0:T(8,128)(2,1)S(1)}, bf16[96,768]{1,0:T(8,128)(2,1)S(1)}, u32[]{:S(2)}, u32[]{:S(2)}) collective-permute-start(bf16[96,768]{1,0:T(8,128)(2,1)S(1)} %total.7), channel_id=1, source_target_pairs={{0,24},{8,0},{16,8},{24,16},{1,25},{9,1},{17,9},{25,17},{2,26},{10... | collective-permute-start | bytes 442376 | tf_op jit(solution)/shard_map/ppermute | solution.py:514
  52.6 3.4 %collective-permute-done.19.refs_3_ = bf16[96,768]{1,0:T(8,128)(2,1)S(1)} collective-permute-done((bf16[96,768]{1,0:T(8,128)(2,1)S(1)}, bf16[96,768]{1,0:T(8,128)(2,1)S(1)}, u32[]{:S(2)}, u32[]{:S(2)}) %collective-permute-start.19) | collective-permute-done | bytes 147488 | tf_op jit(solution)/shard_map/ppermute | solution.py:514
  56.0 5.0 %collective-permute-done.17.refs_2_ = bf16[96,768]{1,0:T(8,128)(2,1)S(1)} collective-permute-done((bf16[96,768]{1,0:T(8,128)(2,1)S(1)}, bf16[96,768]{1,0:T(8,128)(2,1)S(1)}, u32[]{:S(2)}, u32[]{:S(2)}) %collective-permute-start.17) | collective-permute-done | bytes 147488 | tf_op jit(solution)/shard_map/ppermute | solution.py:514
  61.0 0.8 %place.1 = bf16[96,3072]{1,0:T(8,128)(2,1)} custom-call(s32[1]{0:T(128)} %bitcast.meta_ref, bf16[96,768]{1,0:T(8,128)(2,1)S(1)} %total.4.refs_0_, bf16[96,768]{1,0:T(8,128)(2,1)S(1)} %collective-permute-done.14.refs_1_, bf16[96,768]{1,0:T(8,128)(2,1)S(1)} %collective-permute-done.17.refs_2_, bf16[96,768]{1,0:T(8,128)(2,1)S(1)} %collective-permute-done.19.refs_3_), custom_call_target="tpu_custom_call" | custom-call | flops 1000 | bytes 1200000 | tf_op jit(solution)/shard_map/place/pallas_call | solution.py:516
  (45 shorter events, 6.9 us)
Async XLA Ops:
  0.0 1.9 %copy-start = (bf16[192,3072]{1,0:T(8,128)(2,1)S(1)}, bf16[192,3072]{1,0:T(8,128)(2,1)}, u32[]{:S(2)}) copy-start(bf16[192,3072]{1,0:T(8,128)(2,1)} %param.10) | copy-start | bytes 3538948
  1.4 7.7 %copy-start.3 = (s32[12,3]{0,1:T(4,128)S(1)}, s32[12,3]{0,1:T(4,128)}, u32[]{:S(2)}) copy-start(s32[12,3]{0,1:T(4,128)} %param.9) | copy-start | bytes 436
  1.4 3.3 %collective-permute-start = (bf16[3,3,32,768]{3,2,1,0:T(8,128)(2,1)S(1)}, bf16[3,3,32,768]{3,2,1,0:T(8,128)(2,1)S(1)}, u32[]{:S(2)}, u32[]{:S(2)}) collective-permute-start(bf16[3,3,32,768]{3,2,1,0:T(8,128)(2,1)S(1)} %get-tuple-element.39), channel_id=1, source_target_pairs={{0,4},{4,0},{1,5},{5,1},{2,6},{6,2},{3,7},{7,3},{8,12},{12,8},{9,1... | collective-permute-start | bytes 1327112 | tf_op jit(solution)/shard_map/ppermute | solution.py:373
  2.0 12.6 %collective-permute-start.5 = (bf16[192,768]{1,0:T(8,128)(2,1)S(1)}, bf16[192,768]{1,0:T(8,128)(2,1)S(1)}, u32[]{:S(2)}, u32[]{:S(2)}) collective-permute-start(bf16[192,768]{1,0:T(8,128)(2,1)S(1)} %constant_dynamic-slice_fusion.refs_0_), channel_id=1, source_target_pairs={{0,1},{1,2},{2,3},{3,0},{4,5},{5,6},{6,7},{7,4},{8,9},{9,10},{10,1... | collective-permute-start | bytes 884744 | tf_op jit(solution)/shard_map/ppermute | solution.py:404
  6.3 0.6 %copy-start.1 = (bf16[64,768]{1,0:T(8,128)(2,1)}, bf16[64,768]{1,0:T(8,128)(2,1)S(1)}, u32[]{:S(2)}) copy-start(bf16[64,768]{1,0:T(8,128)(2,1)S(1)} %get-tuple-element.27) | copy-start | bytes 294916
  6.9 0.6 %copy-start.2 = (bf16[64,768]{1,0:T(8,128)(2,1)}, bf16[64,768]{1,0:T(8,128)(2,1)S(1)}, u32[]{:S(2)}) copy-start(bf16[64,768]{1,0:T(8,128)(2,1)S(1)} %get-tuple-element.26) | copy-start | bytes 294916
  7.5 13.1 %collective-permute-start.1 = (bf16[2,3,32,768]{3,2,1,0:T(8,128)(2,1)}, bf16[2,3,32,768]{3,2,1,0:T(8,128)(2,1)S(1)}, u32[]{:S(2)}, u32[]{:S(2)}) collective-permute-start(bf16[2,3,32,768]{3,2,1,0:T(8,128)(2,1)} %get-tuple-element.22), channel_id=1, source_target_pairs={{0,1},{1,0},{2,3},{3,2},{4,5},{5,4},{6,7},{7,6},{8,9},{9,8},{10,11... | collective-permute-start | bytes 884744 | tf_op jit(solution)/shard_map/ppermute | solution.py:393
  9.1 11.5 %collective-permute-start.2 = (bf16[2,3,32,768]{3,2,1,0:T(8,128)(2,1)S(1)}, bf16[2,3,32,768]{3,2,1,0:T(8,128)(2,1)S(1)}, u32[]{:S(2)}, u32[]{:S(2)}) collective-permute-start(bf16[2,3,32,768]{3,2,1,0:T(8,128)(2,1)S(1)} %get-tuple-element.23), channel_id=1, source_target_pairs={{0,4},{1,2},{2,1},{3,7},{4,0},{5,6},{6,5},{7,3},{8,12},{9,10},{10,... | collective-permute-start | bytes 884744 | tf_op jit(solution)/shard_map/ppermute | solution.py:393
  9.2 5.4 %collective-permute-start.3 = (bf16[64,768]{1,0:T(8,128)(2,1)}, bf16[64,768]{1,0:T(8,128)(2,1)S(1)}, u32[]{:S(2)}, u32[]{:S(2)}) collective-permute-start(bf16[64,768]{1,0:T(8,128)(2,1)} %copy-done.2), channel_id=1, source_target_pairs={{0,8},{8,0},{16,24},{24,16},{4,12},{12,4},{20,28},{28,20},{1,9},{9... | collective-permute-start | bytes 294920 | tf_op jit(solution)/shard_map/ppermute | solution.py:395
  10.7 3.9 %collective-permute-start.4 = (bf16[64,768]{1,0:T(8,128)(2,1)}, bf16[64,768]{1,0:T(8,128)(2,1)S(1)}, u32[]{:S(2)}, u32[]{:S(2)}) collective-permute-start(bf16[64,768]{1,0:T(8,128)(2,1)} %copy-done.1), channel_id=1, source_target_pairs={{0,4},{8,16},{16,8},{24,28},{4,0},{12,20},{20,12},{28,24},{1,5},{9... | collective-permute-start | bytes 294920 | tf_op jit(solution)/shard_map/ppermute | solution.py:395
  22.1 11.7 %collective-permute-start.8 = (bf16[192,768]{1,0:T(8,128)(2,1)S(1)}, bf16[192,768]{1,0:T(8,128)(2,1)S(1)}, u32[]{:S(2)}, u32[]{:S(2)}) collective-permute-start(bf16[192,768]{1,0:T(8,128)(2,1)S(1)} %get-tuple-element.30), channel_id=1, source_target_pairs={{0,1},{1,2},{2,3},{3,0},{4,5},{5,6},{6,7},{7,4},{8,9},{9,10},{10,1... | collective-permute-start | bytes 884744 | tf_op jit(solution)/shard_map/ppermute | solution.py:430
  22.7 5.1 %collective-permute-start.6 = (bf16[64,896]{1,0:T(8,128)(2,1)S(1)}, bf16[64,896]{1,0:T(8,128)(2,1)S(1)}, u32[]{:S(2)}, u32[]{:S(2)}) collective-permute-start(bf16[64,896]{1,0:T(8,128)(2,1)S(1)} %get-tuple-element.28), channel_id=1, source_target_pairs={{0,8},{8,0},{16,24},{24,16},{4,12},{12,4},{20,28},{28,20},{1,9},{9... | collective-permute-start | bytes 344072 | tf_op jit(solution)/shard_map/ppermute | solution.py:432
  24.2 3.6 %collective-permute-start.7 = (bf16[64,896]{1,0:T(8,128)(2,1)S(1)}, bf16[64,896]{1,0:T(8,128)(2,1)S(1)}, u32[]{:S(2)}, u32[]{:S(2)}) collective-permute-start(bf16[64,896]{1,0:T(8,128)(2,1)S(1)} %get-tuple-element.29), channel_id=1, source_target_pairs={{0,4},{8,16},{16,8},{24,28},{4,0},{12,20},{20,12},{28,24},{1,5},{9... | collective-permute-start | bytes 344072 | tf_op jit(solution)/shard_map/ppermute | solution.py:432
  29.1 12.1 %collective-permute-start.10 = (bf16[192,768]{1,0:T(8,128)(2,1)S(1)}, bf16[192,768]{1,0:T(8,128)(2,1)S(1)}, u32[]{:S(2)}, u32[]{:S(2)}) collective-permute-start(bf16[192,768]{1,0:T(8,128)(2,1)S(1)} %bitcast.19), channel_id=1, source_target_pairs={{0,8},{8,16},{16,24},{24,0},{1,9},{9,17},{17,25},{25,1},{2,10},{10... | collective-permute-start | bytes 884744 | tf_op jit(solution)/shard_map/ppermute | solution.py:464
  33.7 9.3 %collective-permute-start.9 = (bf16[192,768]{1,0:T(8,128)(2,1)S(1)}, bf16[192,768]{1,0:T(8,128)(2,1)S(1)}, u32[]{:S(2)}, u32[]{:S(2)}) collective-permute-start(bf16[192,768]{1,0:T(8,128)(2,1)S(1)} %collective-permute-done.8.refs_2_), channel_id=1, source_target_pairs={{0,1},{1,2},{2,3},{3,0},{4,5},{5,6},{6,7},{7,4},{8,9},{9,10},{10,1... | collective-permute-start | bytes 884744 | tf_op jit(solution)/shard_map/ppermute | solution.py:463
  34.1 11.2 %collective-permute-start.15 = (bf16[192,768]{1,0:T(8,128)(2,1)S(1)}, bf16[192,768]{1,0:T(8,128)(2,1)S(1)}, u32[]{:S(2)}, u32[]{:S(2)}) collective-permute-start(bf16[192,768]{1,0:T(8,128)(2,1)S(1)} %bitcast.20), channel_id=1, source_target_pairs={{0,16},{8,24},{16,0},{24,8},{1,17},{9,25},{17,1},{25,9},{2,18},{10... | collective-permute-start | bytes 884744 | tf_op jit(solution)/shard_map/ppermute | solution.py:464
  34.4 12.0 %collective-permute-start.12 = (bf16[192,768]{1,0:T(8,128)(2,1)S(1)}, bf16[192,768]{1,0:T(8,128)(2,1)S(1)}, u32[]{:S(2)}, u32[]{:S(2)}) collective-permute-start(bf16[192,768]{1,0:T(8,128)(2,1)S(1)} %bitcast.21), channel_id=1, source_target_pairs={{0,24},{8,0},{16,8},{24,16},{1,25},{9,1},{17,9},{25,17},{2,26},{10... | collective-permute-start | bytes 884744 | tf_op jit(solution)/shard_map/ppermute | solution.py:464
  44.1 3.8 %collective-permute-start.18 = (f32[96,768]{1,0:T(8,128)S(1)}, f32[96,768]{1,0:T(8,128)S(1)}, u32[]{:S(2)}, u32[]{:S(2)}) collective-permute-start(f32[96,768]{1,0:T(8,128)S(1)} %get-tuple-element.38), channel_id=1, source_target_pairs={{0,4},{4,0},{1,5},{5,1},{2,6},{6,2},{3,7},{7,3},{8,12},{12,8},{9,1... | collective-permute-start | bytes 884744 | tf_op jit(solution)/shard_map/ppermute | solution.py:512
  45.7 6.1 %collective-permute-start.16 = (f32[96,768]{1,0:T(8,128)S(1)}, f32[96,768]{1,0:T(8,128)S(1)}, u32[]{:S(2)}, u32[]{:S(2)}) collective-permute-start(f32[96,768]{1,0:T(8,128)S(1)} %get-tuple-element.36), channel_id=1, source_target_pairs={{0,4},{4,0},{1,5},{5,1},{2,6},{6,2},{3,7},{7,3},{8,12},{12,8},{9,1... | collective-permute-start | bytes 884744 | tf_op jit(solution)/shard_map/ppermute | solution.py:512
  46.8 5.6 %collective-permute-start.13 = (f32[96,768]{1,0:T(8,128)S(1)}, f32[96,768]{1,0:T(8,128)S(1)}, u32[]{:S(2)}, u32[]{:S(2)}) collective-permute-start(f32[96,768]{1,0:T(8,128)S(1)} %get-tuple-element.34), channel_id=1, source_target_pairs={{0,4},{4,0},{1,5},{5,1},{2,6},{6,2},{3,7},{7,3},{8,12},{12,8},{9,1... | collective-permute-start | bytes 884744 | tf_op jit(solution)/shard_map/ppermute | solution.py:512
  47.3 5.3 %collective-permute-start.11 = (f32[96,768]{1,0:T(8,128)S(1)}, f32[96,768]{1,0:T(8,128)S(1)}, u32[]{:S(2)}, u32[]{:S(2)}) collective-permute-start(f32[96,768]{1,0:T(8,128)S(1)} %get-tuple-element.32), channel_id=1, source_target_pairs={{0,4},{4,0},{1,5},{5,1},{2,6},{6,2},{3,7},{7,3},{8,12},{12,8},{9,1... | collective-permute-start | bytes 884744 | tf_op jit(solution)/shard_map/ppermute | solution.py:512
  47.9 8.2 %collective-permute-start.19 = (bf16[96,768]{1,0:T(8,128)(2,1)S(1)}, bf16[96,768]{1,0:T(8,128)(2,1)S(1)}, u32[]{:S(2)}, u32[]{:S(2)}) collective-permute-start(bf16[96,768]{1,0:T(8,128)(2,1)S(1)} %total.7), channel_id=1, source_target_pairs={{0,24},{8,0},{16,8},{24,16},{1,25},{9,1},{17,9},{25,17},{2,26},{10... | collective-permute-start | bytes 442376 | tf_op jit(solution)/shard_map/ppermute | solution.py:514
  51.9 9.2 %collective-permute-start.17 = (bf16[96,768]{1,0:T(8,128)(2,1)S(1)}, bf16[96,768]{1,0:T(8,128)(2,1)S(1)}, u32[]{:S(2)}, u32[]{:S(2)}) collective-permute-start(bf16[96,768]{1,0:T(8,128)(2,1)S(1)} %total.6), channel_id=1, source_target_pairs={{0,16},{8,24},{16,0},{24,8},{1,17},{9,25},{17,1},{25,9},{2,18},{10... | collective-permute-start | bytes 442376 | tf_op jit(solution)/shard_map/ppermute | solution.py:514
  52.5 8.6 %collective-permute-start.14 = (bf16[96,768]{1,0:T(8,128)(2,1)S(1)}, bf16[96,768]{1,0:T(8,128)(2,1)S(1)}, u32[]{:S(2)}, u32[]{:S(2)}) collective-permute-start(bf16[96,768]{1,0:T(8,128)(2,1)S(1)} %total.5), channel_id=1, source_target_pairs={{0,8},{8,16},{16,24},{24,0},{1,9},{9,17},{17,25},{25,1},{2,10},{10... | collective-permute-start | bytes 442376 | tf_op jit(solution)/shard_map/ppermute | solution.py:514

commit v5 on v4

--- a/solution.py
+++ b/solution.py
@@ -17,7 +17,7 @@
 VMEM = pl.BlockSpec(memory_space=pltpu.VMEM)
 SMEM = pl.BlockSpec(memory_space=pltpu.SMEM)
 HBM = pl.BlockSpec(memory_space=pl.ANY)
-PARAMS = pltpu.CompilerParams(vmem_limit_bytes=16 * 1024 * 1024)
+PARAMS = pltpu.CompilerParams(vmem_limit_bytes=6 * 1024 * 1024)
 
 
 def cycle(count, step):
@@ -400,8 +400,6 @@
     wide = out_weight.shape[1] // n_time
     mine = lax.dynamic_slice_in_dim(out_weight, at_time * wide, wide, axis=1)
     held = {0: mine}
-    if n_cols > 1:
-        held[1] = lax.ppermute(mine, "wa", cycle(n_cols, 1))
 
     table = jnp.asarray(code_table(rows, cols, rims))
     absent = [~x for x in there]
@@ -419,15 +417,15 @@
     *answers, sent = pl.pallas_call(
         functools.partial(guest_kernel, rims, heads, width),
         out_shape=(payload, payload, jax.ShapeDtypeStruct(mine.shape, mine.dtype)),
-        in_specs=[SMEM, SMEM] + [VMEM] * (1 + len(parts) + 2) + [VMEM],
-        out_specs=(VMEM, VMEM, VMEM),
+        in_specs=[SMEM, SMEM] + [VMEM] * (1 + len(parts) + 2) + [HBM],
+        out_specs=(VMEM, VMEM, HBM),
         scratch_shapes=[pltpu.SemaphoreType.DMA],
         compiler_params=PARAMS,
         cost_estimate=cost(2 * unit, 4_000_000),
         name="guest",
-    )(meta, radius, code, *parts, *guests, held[min(1, n_cols - 1)])
-    if n_cols > 2:
-        held[2] = lax.ppermute(sent, "wa", cycle(n_cols, 1))
+    )(meta, radius, code, *parts, *guests, mine)
+    if n_cols > 1:
+        held[1] = lax.ppermute(sent, "wa", cycle(n_cols, 1))
     answers = [
         lax.ppermute(x, ("ta", "ha"), swaps(n_time, phase, n_rows, False)) for phase, x in enumerate(answers)
     ]
@@ -459,7 +457,9 @@
     )(meta, radius, mixed, stats, *answers)
     tokens = frames * area
     attended = attended.reshape(PAIR * tokens, half)
-    for s in range(3, n_cols):
+    if n_cols > 2:
+        held[n_cols - 1] = lax.ppermute(sent, "wa", cycle(n_cols, -1))
+    for s in range(2, n_cols - 1):
         held[s] = lax.ppermute(held[s - 1], "wa", cycle(n_cols, 1))
     received = [lax.ppermute(attended, "ta", cycle(n_time, s)) for s in range(1, n_time)]
 
@@ -476,7 +476,7 @@
             compiler_params=PARAMS,
             cost_estimate=cost(1000, 2_400_000),
             name="join",
-        )(spots, *shards, received[0])
+        )(spots, *shards, received[1])
 
     near = joined([held[s] for s in range(n_cols)], at_col)
     if n_rows > PAIR:

time: 62.1 us -> 57.2 us (0.921)
  waiting for transfers between devices: 27.7 us -> 20.9 us
  starting transfers between devices: 21.3 us -> 24.3 us
  local copies, waits for them, and re-layouts: 2.31 us -> 1.04 us
    ppermute x2, waiting for transfers between devices: 5.99 us -> 1.82 us  [shards(): lax.ppermute(x, ('ha', 'wa'), swaps(n_cols, phase, n_rows, True))]
    ppermute x2, waiting for transfers between devices: 2.89 us -> 0.35 us  [the longest x1 0.34 us: shards(): held[n_cols - 1] = lax.ppermute(sent, 'wa', cycle(n_cols, -1))]
    ppermute x3, waiting for transfers between devices: 8.41 us -> 6.12 us  [shards(): lax.ppermute(products[n_time - s], 'ta', cycle(n_time, s))]
    ppermute x1, waiting for transfers between devices: 1.84 us -> 0.01 us  [shards(): held[s] = lax.ppermute(held[s - 1], 'wa', cycle(n_cols, 1))]
    ppermute x4, waiting for transfers between devices: 2.04 us -> 3.71 us  [shards(): lax.ppermute(x, ('ta', 'ha'), swaps(n_time, phase, n_rows, False))]
    ppermute x2, starting transfers between devices: 1.58 us -> 2.95 us  [shards(): lax.ppermute(x, ('ha', 'wa'), swaps(n_cols, phase, n_rows, True))]
    ppermute x1, waiting for transfers between devices: 0.01 us -> 1.34 us  [shards(): other = lax.ppermute(other, 'ha', pairs)]
    unnamed x9 -> x5, local copies, waits for them, and re-layouts: 1.37 us -> 0.1 us
  transfers between devices with their start and end apart: 20 -> 20, of which waited for: 9 -> 9; matrix products, arithmetic and copies ran while one was open for 2% -> 2% of each run, Pallas kernels for 11% -> 9%
where the time goes in v5:
time: 57.2 us; the launch traced here: 57 us
  starting transfers between devices  24.3 us (42%)
  waiting for transfers between devices  20.9 us (37%)
  Pallas kernels  9.31 us (16%)
  other arithmetic  1.41 us (2%)
  local copies, waits for them, and re-layouts  1.04 us (2%)
    ppermute x3, waiting for transfers between devices, shards(): lax.ppermute(attended, 'ta', cycle(n_time, s))  7.52 us
    ppermute x3, waiting for transfers between devices, shards(): lax.ppermute(products[n_time - s], 'ta', cycle(n_time, s))  6.12 us
    ppermute x3, starting transfers between devices, shards(): lax.ppermute(attended, 'ta', cycle(n_time, s))  5.7 us
    ppermute x4, starting transfers between devices, shards(): lax.ppermute(x, ('ta', 'ha'), swaps(n_time, phase, n_rows, False))  4 us
    ppermute x3, starting transfers between devices, shards(): lax.ppermute(products[n_time - s], 'ta', cycle(n_time, s))  3.93 us
    ppermute x4, waiting for transfers between devices, shards(): lax.ppermute(x, ('ta', 'ha'), swaps(n_time, phase, n_rows, False))  3.71 us
    ppermute x2, starting transfers between devices, shards(): lax.ppermute(x, ('ha', 'wa'), swaps(n_cols, phase, n_rows, True))  2.95 us
    ppermute x1, starting transfers between devices, shards(): held[1] = lax.ppermute(sent, 'wa', cycle(n_cols, 1))  2.72 us
  transfers between devices with their start and end apart: 20, of which 9 were waited for; matrix products, arithmetic and copies ran while one was open for 2% of the time, Pallas kernels for 9%

profile of v5, /device:TPU:0, one launch (start us, length us, event | category | flops | bytes accessed | tf_op | source)
XLA Modules:
  0.0 57.0 jit_solution(6861821241104394692)
XLA Ops:
  0.0 1.3 %pad_maximum_fusion = bf16[3,3,32,1536]{3,2,1,0:T(8,128)(2,1)S(1)} fusion(bf16[1,3,32,1536]{3,2,1,0:T(8,128)(2,1)} %bitcast.23, bf16[1,3,32,1536]{3,2,1,0:T(8,128)(2,1)} %bitcast.24, bf16[1,3,32,1536]{3,2,1,0:T(8,128)(2,1)} %bitcast.25), kind=kLoop, calls=%fused_computation | loop fusion | flops 884736 | bytes 1769472 | tf_op jit(solution)/shard_map/stack | solution.py:369
  2.0 1.3 %collective-permute-done.refs_1_ = bf16[3,3,32,768]{3,2,1,0:T(8,128)(2,1)S(1)} collective-permute-done((bf16[3,3,32,768]{3,2,1,0:T(8,128)(2,1)S(1)}, bf16[3,3,32,768]{3,2,1,0:T(8,128)(2,1)S(1)}, u32[]{:S(2)}, u32[]{:S(2)}) %collective-permute-start) | collective-permute-done | bytes 442400 | tf_op jit(solution)/shard_map/ppermute | solution.py:373
  3.4 1.5 %edge.1 = (bf16[2,3,32,768]{3,2,1,0:T(8,128)(2,1)}, bf16[2,3,32,768]{3,2,1,0:T(8,128)(2,1)S(1)}, bf16[64,768]{1,0:T(8,128)(2,1)}, bf16[64,768]{1,0:T(8,128)(2,1)S(1)}) custom-call(s32[7]{0:T(128)S(1)} %stack.61.meta_ref, bf16[3,3,32,768]{3,2,1,0:T(8,128)(2,1)S(1)} %get-tuple-element.40.refs_0_, bf16[3,3,32,768]{3,2,1,0:T(8,128)(2,1)S(1)} %collective-permute-done.refs_1_), custom_call_target="tpu_custom_call" | custom-call | flops 1000 | bytes 2000000 | tf_op jit(solution)/shard_map/edge/pallas_call | solution.py:384
  4.9 2.9 %collective-permute-start.1 = (bf16[2,3,32,768]{3,2,1,0:T(8,128)(2,1)}, bf16[2,3,32,768]{3,2,1,0:T(8,128)(2,1)S(1)}, u32[]{:S(2)}, u32[]{:S(2)}) collective-permute-start(bf16[2,3,32,768]{3,2,1,0:T(8,128)(2,1)} %get-tuple-element.22), channel_id=1, source_target_pairs={{0,1},{1,0},{2,3},{3,2},{4,5},{5,4},{6,7},{7,6},{8,9},{9,8},{10,11... | collective-permute-start | bytes 884744 | tf_op jit(solution)/shard_map/ppermute | solution.py:393
  8.0 1.6 %collective-permute-start.3 = (bf16[64,768]{1,0:T(8,128)(2,1)}, bf16[64,768]{1,0:T(8,128)(2,1)S(1)}, u32[]{:S(2)}, u32[]{:S(2)}) collective-permute-start(bf16[64,768]{1,0:T(8,128)(2,1)} %get-tuple-element.26), channel_id=1, source_target_pairs={{0,8},{8,0},{16,24},{24,16},{4,12},{12,4},{20,28},{28,20},{1,9},{9... | collective-permute-start | bytes 294920 | tf_op jit(solution)/shard_map/ppermute | solution.py:395
  10.5 3.0 %collective-permute-done.3.refs_4_ = bf16[64,768]{1,0:T(8,128)(2,1)S(1)} collective-permute-done((bf16[64,768]{1,0:T(8,128)(2,1)}, bf16[64,768]{1,0:T(8,128)(2,1)S(1)}, u32[]{:S(2)}, u32[]{:S(2)}) %collective-permute-start.3) | collective-permute-done | bytes 98336 | tf_op jit(solution)/shard_map/ppermute | solution.py:395
  13.6 1.8 %collective-permute-done.1.refs_2_ = bf16[2,3,32,768]{3,2,1,0:T(8,128)(2,1)S(1)} collective-permute-done((bf16[2,3,32,768]{3,2,1,0:T(8,128)(2,1)}, bf16[2,3,32,768]{3,2,1,0:T(8,128)(2,1)S(1)}, u32[]{:S(2)}, u32[]{:S(2)}) %collective-permute-start.1) | collective-permute-done | bytes 294944 | tf_op jit(solution)/shard_map/ppermute | solution.py:393
  15.4 1.7 %guest.1 = (bf16[64,896]{1,0:T(8,128)(2,1)S(1)}, bf16[64,896]{1,0:T(8,128)(2,1)S(1)}, bf16[192,768]{1,0:T(8,128)(2,1)}) custom-call(s32[7]{0:T(128)S(1)} %stack.61.meta_ref, s32[12,3]{1,0:T(8,128)S(1)} %copy.9.radius_ref, s32[64,128]{1,0:T(8,128)S(1)} %dynamic-slice_bitcast_fusion.code_ref, bf16[3,3,32,768]{3,2,1,0:T(8,128)(2,1)S(1)} %get-tuple-element.40.refs_0_, ...), custom_call_target="tpu_custom_call" | custom-call | flops 50331648 | bytes 4000000 | tf_op jit(solution)/shard_map/guest/pallas_call | solution.py:417
  17.1 2.7 %collective-permute-start.7 = (bf16[192,768]{1,0:T(8,128)(2,1)}, bf16[192,768]{1,0:T(8,128)(2,1)S(1)}, u32[]{:S(2)}, u32[]{:S(2)}) collective-permute-start(bf16[192,768]{1,0:T(8,128)(2,1)} %get-tuple-element.30), channel_id=1, source_target_pairs={{0,1},{1,2},{2,3},{3,0},{4,5},{5,6},{6,7},{7,4},{8,9},{9,10},{10,1... | collective-permute-start | bytes 884744 | tf_op jit(solution)/shard_map/ppermute | solution.py:428
  19.8 2.2 %collective-permute-start.5 = (bf16[64,896]{1,0:T(8,128)(2,1)S(1)}, bf16[64,896]{1,0:T(8,128)(2,1)S(1)}, u32[]{:S(2)}, u32[]{:S(2)}) collective-permute-start(bf16[64,896]{1,0:T(8,128)(2,1)S(1)} %get-tuple-element.28), channel_id=1, source_target_pairs={{0,8},{8,0},{16,24},{24,16},{4,12},{12,4},{20,28},{28,20},{1,9},{9... | collective-permute-start | bytes 344072 | tf_op jit(solution)/shard_map/ppermute | solution.py:430
  22.0 1.6 %collective-permute-start.9 = (bf16[192,768]{1,0:T(8,128)(2,1)}, bf16[192,768]{1,0:T(8,128)(2,1)S(1)}, u32[]{:S(2)}, u32[]{:S(2)}) collective-permute-start(bf16[192,768]{1,0:T(8,128)(2,1)} %get-tuple-element.30), channel_id=1, source_target_pairs={{0,3},{1,0},{2,1},{3,2},{4,7},{5,4},{6,5},{7,6},{8,11},{9,8},{10,9... | collective-permute-start | bytes 884744 | tf_op jit(solution)/shard_map/ppermute | solution.py:461
  23.6 1.6 %host.1 = (f32[3,64,768]{2,1,0:T(8,128)S(1)}, f32[3,64,128]{2,1,0:T(8,128)S(1)}) custom-call(s32[7]{0:T(128)S(1)} %stack.61.meta_ref, s32[12,3]{1,0:T(8,128)S(1)} %copy.9.radius_ref, s32[64,128]{1,0:T(8,128)S(1)} %dynamic-slice_bitcast_fusion.code_ref, bf16[3,3,32,768]{3,2,1,0:T(8,128)(2,1)S(1)} %get-tuple-element.40.refs_0_, ...), custom_call_target="tpu_custom_call" | custom-call | flops 176160768 | bytes 6000000 | tf_op jit(solution)/shard_map/host/pallas_call | solution.py:433
  26.0 1.2 %merge.1 = bf16[2,3,32,768]{3,2,1,0:T(8,128)(2,1)S(1)} custom-call(s32[7]{0:T(128)S(1)} %stack.61.meta_ref, s32[12,3]{1,0:T(8,128)S(1)} %copy.9.radius_ref, f32[3,64,768]{2,1,0:T(8,128)S(1)} %get-tuple-element.24.mixed_ref, f32[3,64,128]{2,1,0:T(8,128)S(1)} %get-tuple-element.25.stats_ref, bf16[64,896]{1,0:T(8,128)(2,1)S(1)} %collective-permute-done.5.ref_0, ...), custom_call_target="tpu_custom_call" | custom-call | flops 1000 | bytes 3000000 | tf_op jit(solution)/shard_map/merge/pallas_call | solution.py:445
  27.2 2.8 %collective-permute-start.10 = (bf16[192,768]{1,0:T(8,128)(2,1)S(1)}, bf16[192,768]{1,0:T(8,128)(2,1)S(1)}, u32[]{:S(2)}, u32[]{:S(2)}) collective-permute-start(bf16[192,768]{1,0:T(8,128)(2,1)S(1)} %bitcast.19), channel_id=1, source_target_pairs={{0,16},{8,24},{16,0},{24,8},{1,17},{9,25},{17,1},{25,9},{2,18},{10... | collective-permute-start | bytes 884744 | tf_op jit(solution)/shard_map/ppermute | solution.py:464
  30.0 1.5 %collective-permute-start.8 = (bf16[192,768]{1,0:T(8,128)(2,1)S(1)}, bf16[192,768]{1,0:T(8,128)(2,1)S(1)}, u32[]{:S(2)}, u32[]{:S(2)}) collective-permute-start(bf16[192,768]{1,0:T(8,128)(2,1)S(1)} %collective-permute-done.7.refs_1_), channel_id=1, source_target_pairs={{0,1},{1,2},{2,3},{3,0},{4,5},{5,6},{6,7},{7,4},{8,9},{9,10},{10,1... | collective-permute-start | bytes 884744 | tf_op jit(solution)/shard_map/ppermute | solution.py:463
  32.2 2.3 %collective-permute-start.12 = (bf16[192,768]{1,0:T(8,128)(2,1)S(1)}, bf16[192,768]{1,0:T(8,128)(2,1)S(1)}, u32[]{:S(2)}, u32[]{:S(2)}) collective-permute-start(bf16[192,768]{1,0:T(8,128)(2,1)S(1)} %bitcast.21), channel_id=1, source_target_pairs={{0,24},{8,0},{16,8},{24,16},{1,25},{9,1},{17,9},{25,17},{2,26},{10... | collective-permute-start | bytes 884744 | tf_op jit(solution)/shard_map/ppermute | solution.py:464
  34.9 7.5 %collective-permute-done.10.refs_4_.rows = bf16[192,768]{1,0:T(8,128)(2,1)S(1)} collective-permute-done((bf16[192,768]{1,0:T(8,128)(2,1)S(1)}, bf16[192,768]{1,0:T(8,128)(2,1)S(1)}, u32[]{:S(2)}, u32[]{:S(2)}) %collective-permute-start.10) | collective-permute-done | bytes 294944 | tf_op jit(solution)/shard_map/ppermute | solution.py:464
  46.0 1.3 %collective-permute-start.19 = (bf16[96,768]{1,0:T(8,128)(2,1)S(1)}, bf16[96,768]{1,0:T(8,128)(2,1)S(1)}, u32[]{:S(2)}, u32[]{:S(2)}) collective-permute-start(bf16[96,768]{1,0:T(8,128)(2,1)S(1)} %total.7), channel_id=1, source_target_pairs={{0,24},{8,0},{16,8},{24,16},{1,25},{9,1},{17,9},{25,17},{2,26},{10... | collective-permute-start | bytes 442376 | tf_op jit(solution)/shard_map/ppermute | solution.py:514
  47.4 1.0 %collective-permute-start.16 = (bf16[96,768]{1,0:T(8,128)(2,1)S(1)}, bf16[96,768]{1,0:T(8,128)(2,1)S(1)}, u32[]{:S(2)}, u32[]{:S(2)}) collective-permute-start(bf16[96,768]{1,0:T(8,128)(2,1)S(1)} %total.6), channel_id=1, source_target_pairs={{0,16},{8,24},{16,0},{24,8},{1,17},{9,25},{17,1},{25,9},{2,18},{10... | collective-permute-start | bytes 442376 | tf_op jit(solution)/shard_map/ppermute | solution.py:514
  48.4 1.6 %collective-permute-start.14 = (bf16[96,768]{1,0:T(8,128)(2,1)S(1)}, bf16[96,768]{1,0:T(8,128)(2,1)S(1)}, u32[]{:S(2)}, u32[]{:S(2)}) collective-permute-start(bf16[96,768]{1,0:T(8,128)(2,1)S(1)} %total.5), channel_id=1, source_target_pairs={{0,8},{8,16},{16,24},{24,0},{1,9},{9,17},{17,25},{25,1},{2,10},{10... | collective-permute-start | bytes 442376 | tf_op jit(solution)/shard_map/ppermute | solution.py:514
  50.1 2.5 %collective-permute-done.19.refs_3_ = bf16[96,768]{1,0:T(8,128)(2,1)S(1)} collective-permute-done((bf16[96,768]{1,0:T(8,128)(2,1)S(1)}, bf16[96,768]{1,0:T(8,128)(2,1)S(1)}, u32[]{:S(2)}, u32[]{:S(2)}) %collective-permute-start.19) | collective-permute-done | bytes 147488 | tf_op jit(solution)/shard_map/ppermute | solution.py:514
  52.6 2.0 %collective-permute-done.16.refs_2_ = bf16[96,768]{1,0:T(8,128)(2,1)S(1)} collective-permute-done((bf16[96,768]{1,0:T(8,128)(2,1)S(1)}, bf16[96,768]{1,0:T(8,128)(2,1)S(1)}, u32[]{:S(2)}, u32[]{:S(2)}) %collective-permute-start.16) | collective-permute-done | bytes 147488 | tf_op jit(solution)/shard_map/ppermute | solution.py:514
  54.6 1.6 %collective-permute-done.14.refs_1_ = bf16[96,768]{1,0:T(8,128)(2,1)S(1)} collective-permute-done((bf16[96,768]{1,0:T(8,128)(2,1)S(1)}, bf16[96,768]{1,0:T(8,128)(2,1)S(1)}, u32[]{:S(2)}, u32[]{:S(2)}) %collective-permute-start.14) | collective-permute-done | bytes 147488 | tf_op jit(solution)/shard_map/ppermute | solution.py:514
  56.2 0.8 %place.1 = bf16[96,3072]{1,0:T(8,128)(2,1)} custom-call(s32[1]{0:T(128)} %bitcast.meta_ref, bf16[96,768]{1,0:T(8,128)(2,1)S(1)} %total.4.refs_0_, bf16[96,768]{1,0:T(8,128)(2,1)S(1)} %collective-permute-done.14.refs_1_, bf16[96,768]{1,0:T(8,128)(2,1)S(1)} %collective-permute-done.16.refs_2_, bf16[96,768]{1,0:T(8,128)(2,1)S(1)} %collective-permute-done.19.refs_3_), custom_call_target="tpu_custom_call" | custom-call | flops 1000 | bytes 1200000 | tf_op jit(solution)/shard_map/place/pallas_call | solution.py:516
  (41 shorter events, 7.2 us)
Async XLA Ops:
  0.0 8.0 %copy-start = (bf16[192,3072]{1,0:T(8,128)(2,1)S(1)}, bf16[192,3072]{1,0:T(8,128)(2,1)}, u32[]{:S(2)}) copy-start(bf16[192,3072]{1,0:T(8,128)(2,1)} %param.10) | copy-start | bytes 3538948
  1.3 6.5 %copy-start.1 = (s32[12,3]{0,1:T(4,128)S(1)}, s32[12,3]{0,1:T(4,128)}, u32[]{:S(2)}) copy-start(s32[12,3]{0,1:T(4,128)} %param.9) | copy-start | bytes 436
  1.4 1.9 %collective-permute-start = (bf16[3,3,32,768]{3,2,1,0:T(8,128)(2,1)S(1)}, bf16[3,3,32,768]{3,2,1,0:T(8,128)(2,1)S(1)}, u32[]{:S(2)}, u32[]{:S(2)}) collective-permute-start(bf16[3,3,32,768]{3,2,1,0:T(8,128)(2,1)S(1)} %get-tuple-element.39), channel_id=1, source_target_pairs={{0,4},{4,0},{1,5},{5,1},{2,6},{6,2},{3,7},{7,3},{8,12},{12,8},{9,1... | collective-permute-start | bytes 1327112 | tf_op jit(solution)/shard_map/ppermute | solution.py:373
  4.9 10.5 %collective-permute-start.1 = (bf16[2,3,32,768]{3,2,1,0:T(8,128)(2,1)}, bf16[2,3,32,768]{3,2,1,0:T(8,128)(2,1)S(1)}, u32[]{:S(2)}, u32[]{:S(2)}) collective-permute-start(bf16[2,3,32,768]{3,2,1,0:T(8,128)(2,1)} %get-tuple-element.22), channel_id=1, source_target_pairs={{0,1},{1,0},{2,3},{3,2},{4,5},{5,4},{6,7},{7,6},{8,9},{9,8},{10,11... | collective-permute-start | bytes 884744 | tf_op jit(solution)/shard_map/ppermute | solution.py:393
  7.9 7.5 %collective-permute-start.2 = (bf16[2,3,32,768]{3,2,1,0:T(8,128)(2,1)S(1)}, bf16[2,3,32,768]{3,2,1,0:T(8,128)(2,1)S(1)}, u32[]{:S(2)}, u32[]{:S(2)}) collective-permute-start(bf16[2,3,32,768]{3,2,1,0:T(8,128)(2,1)S(1)} %get-tuple-element.23), channel_id=1, source_target_pairs={{0,4},{1,2},{2,1},{3,7},{4,0},{5,6},{6,5},{7,3},{8,12},{9,10},{10,... | collective-permute-start | bytes 884744 | tf_op jit(solution)/shard_map/ppermute | solution.py:393
  8.0 5.6 %collective-permute-start.3 = (bf16[64,768]{1,0:T(8,128)(2,1)}, bf16[64,768]{1,0:T(8,128)(2,1)S(1)}, u32[]{:S(2)}, u32[]{:S(2)}) collective-permute-start(bf16[64,768]{1,0:T(8,128)(2,1)} %get-tuple-element.26), channel_id=1, source_target_pairs={{0,8},{8,0},{16,24},{24,16},{4,12},{12,4},{20,28},{28,20},{1,9},{9... | collective-permute-start | bytes 294920 | tf_op jit(solution)/shard_map/ppermute | solution.py:395
  9.6 4.0 %collective-permute-start.4 = (bf16[64,768]{1,0:T(8,128)(2,1)S(1)}, bf16[64,768]{1,0:T(8,128)(2,1)S(1)}, u32[]{:S(2)}, u32[]{:S(2)}) collective-permute-start(bf16[64,768]{1,0:T(8,128)(2,1)S(1)} %get-tuple-element.27), channel_id=1, source_target_pairs={{0,4},{8,16},{16,8},{24,28},{4,0},{12,20},{20,12},{28,24},{1,5},{9... | collective-permute-start | bytes 294920 | tf_op jit(solution)/shard_map/ppermute | solution.py:395
  17.1 12.9 %collective-permute-start.7 = (bf16[192,768]{1,0:T(8,128)(2,1)}, bf16[192,768]{1,0:T(8,128)(2,1)S(1)}, u32[]{:S(2)}, u32[]{:S(2)}) collective-permute-start(bf16[192,768]{1,0:T(8,128)(2,1)} %get-tuple-element.30), channel_id=1, source_target_pairs={{0,1},{1,2},{2,3},{3,0},{4,5},{5,6},{6,7},{7,4},{8,9},{9,10},{10,1... | collective-permute-start | bytes 884744 | tf_op jit(solution)/shard_map/ppermute | solution.py:428
  19.8 6.2 %collective-permute-start.5 = (bf16[64,896]{1,0:T(8,128)(2,1)S(1)}, bf16[64,896]{1,0:T(8,128)(2,1)S(1)}, u32[]{:S(2)}, u32[]{:S(2)}) collective-permute-start(bf16[64,896]{1,0:T(8,128)(2,1)S(1)} %get-tuple-element.28), channel_id=1, source_target_pairs={{0,8},{8,0},{16,24},{24,16},{4,12},{12,4},{20,28},{28,20},{1,9},{9... | collective-permute-start | bytes 344072 | tf_op jit(solution)/shard_map/ppermute | solution.py:430
  22.0 4.0 %collective-permute-start.6 = (bf16[64,896]{1,0:T(8,128)(2,1)S(1)}, bf16[64,896]{1,0:T(8,128)(2,1)S(1)}, u32[]{:S(2)}, u32[]{:S(2)}) collective-permute-start(bf16[64,896]{1,0:T(8,128)(2,1)S(1)} %get-tuple-element.29), channel_id=1, source_target_pairs={{0,4},{8,16},{16,8},{24,28},{4,0},{12,20},{20,12},{28,24},{1,5},{9... | collective-permute-start | bytes 344072 | tf_op jit(solution)/shard_map/ppermute | solution.py:430
  22.0 12.9 %collective-permute-start.9 = (bf16[192,768]{1,0:T(8,128)(2,1)}, bf16[192,768]{1,0:T(8,128)(2,1)S(1)}, u32[]{:S(2)}, u32[]{:S(2)}) collective-permute-start(bf16[192,768]{1,0:T(8,128)(2,1)} %get-tuple-element.30), channel_id=1, source_target_pairs={{0,3},{1,0},{2,1},{3,2},{4,7},{5,4},{6,5},{7,6},{8,11},{9,8},{10,9... | collective-permute-start | bytes 884744 | tf_op jit(solution)/shard_map/ppermute | solution.py:461
  27.2 15.2 %collective-permute-start.10 = (bf16[192,768]{1,0:T(8,128)(2,1)S(1)}, bf16[192,768]{1,0:T(8,128)(2,1)S(1)}, u32[]{:S(2)}, u32[]{:S(2)}) collective-permute-start(bf16[192,768]{1,0:T(8,128)(2,1)S(1)} %bitcast.19), channel_id=1, source_target_pairs={{0,16},{8,24},{16,0},{24,8},{1,17},{9,25},{17,1},{25,9},{2,18},{10... | collective-permute-start | bytes 884744 | tf_op jit(solution)/shard_map/ppermute | solution.py:464
  30.0 12.4 %collective-permute-start.8 = (bf16[192,768]{1,0:T(8,128)(2,1)S(1)}, bf16[192,768]{1,0:T(8,128)(2,1)S(1)}, u32[]{:S(2)}, u32[]{:S(2)}) collective-permute-start(bf16[192,768]{1,0:T(8,128)(2,1)S(1)} %collective-permute-done.7.refs_1_), channel_id=1, source_target_pairs={{0,1},{1,2},{2,3},{3,0},{4,5},{5,6},{6,7},{7,4},{8,9},{9,10},{10,1... | collective-permute-start | bytes 884744 | tf_op jit(solution)/shard_map/ppermute | solution.py:463
  31.6 11.5 %collective-permute-start.17 = (bf16[192,768]{1,0:T(8,128)(2,1)S(1)}, bf16[192,768]{1,0:T(8,128)(2,1)S(1)}, u32[]{:S(2)}, u32[]{:S(2)}) collective-permute-start(bf16[192,768]{1,0:T(8,128)(2,1)S(1)} %bitcast.20), channel_id=1, source_target_pairs={{0,8},{8,16},{16,24},{24,0},{1,9},{9,17},{17,25},{25,1},{2,10},{10... | collective-permute-start | bytes 884744 | tf_op jit(solution)/shard_map/ppermute | solution.py:464
  32.2 12.3 %collective-permute-start.12 = (bf16[192,768]{1,0:T(8,128)(2,1)S(1)}, bf16[192,768]{1,0:T(8,128)(2,1)S(1)}, u32[]{:S(2)}, u32[]{:S(2)}) collective-permute-start(bf16[192,768]{1,0:T(8,128)(2,1)S(1)} %bitcast.21), channel_id=1, source_target_pairs={{0,24},{8,0},{16,8},{24,16},{1,25},{9,1},{17,9},{25,17},{2,26},{10... | collective-permute-start | bytes 884744 | tf_op jit(solution)/shard_map/ppermute | solution.py:464
  43.5 2.5 %collective-permute-start.18 = (f32[96,768]{1,0:T(8,128)S(1)}, f32[96,768]{1,0:T(8,128)S(1)}, u32[]{:S(2)}, u32[]{:S(2)}) collective-permute-start(f32[96,768]{1,0:T(8,128)S(1)} %get-tuple-element.38), channel_id=1, source_target_pairs={{0,4},{4,0},{1,5},{5,1},{2,6},{6,2},{3,7},{7,3},{8,12},{12,8},{9,1... | collective-permute-start | bytes 884744 | tf_op jit(solution)/shard_map/ppermute | solution.py:512
  44.0 3.4 %collective-permute-start.15 = (f32[96,768]{1,0:T(8,128)S(1)}, f32[96,768]{1,0:T(8,128)S(1)}, u32[]{:S(2)}, u32[]{:S(2)}) collective-permute-start(f32[96,768]{1,0:T(8,128)S(1)} %get-tuple-element.36), channel_id=1, source_target_pairs={{0,4},{4,0},{1,5},{5,1},{2,6},{6,2},{3,7},{7,3},{8,12},{12,8},{9,1... | collective-permute-start | bytes 884744 | tf_op jit(solution)/shard_map/ppermute | solution.py:512
  44.9 3.4 %collective-permute-start.13 = (f32[96,768]{1,0:T(8,128)S(1)}, f32[96,768]{1,0:T(8,128)S(1)}, u32[]{:S(2)}, u32[]{:S(2)}) collective-permute-start(f32[96,768]{1,0:T(8,128)S(1)} %get-tuple-element.34), channel_id=1, source_target_pairs={{0,4},{4,0},{1,5},{5,1},{2,6},{6,2},{3,7},{7,3},{8,12},{12,8},{9,1... | collective-permute-start | bytes 884744 | tf_op jit(solution)/shard_map/ppermute | solution.py:512
  45.4 4.6 %collective-permute-start.11 = (f32[96,768]{1,0:T(8,128)S(1)}, f32[96,768]{1,0:T(8,128)S(1)}, u32[]{:S(2)}, u32[]{:S(2)}) collective-permute-start(f32[96,768]{1,0:T(8,128)S(1)} %get-tuple-element.32), channel_id=1, source_target_pairs={{0,4},{4,0},{1,5},{5,1},{2,6},{6,2},{3,7},{7,3},{8,12},{12,8},{9,1... | collective-permute-start | bytes 884744 | tf_op jit(solution)/shard_map/ppermute | solution.py:512
  46.0 6.6 %collective-permute-start.19 = (bf16[96,768]{1,0:T(8,128)(2,1)S(1)}, bf16[96,768]{1,0:T(8,128)(2,1)S(1)}, u32[]{:S(2)}, u32[]{:S(2)}) collective-permute-start(bf16[96,768]{1,0:T(8,128)(2,1)S(1)} %total.7), channel_id=1, source_target_pairs={{0,24},{8,0},{16,8},{24,16},{1,25},{9,1},{17,9},{25,17},{2,26},{10... | collective-permute-start | bytes 442376 | tf_op jit(solution)/shard_map/ppermute | solution.py:514
  47.4 7.2 %collective-permute-start.16 = (bf16[96,768]{1,0:T(8,128)(2,1)S(1)}, bf16[96,768]{1,0:T(8,128)(2,1)S(1)}, u32[]{:S(2)}, u32[]{:S(2)}) collective-permute-start(bf16[96,768]{1,0:T(8,128)(2,1)S(1)} %total.6), channel_id=1, source_target_pairs={{0,16},{8,24},{16,0},{24,8},{1,17},{9,25},{17,1},{25,9},{2,18},{10... | collective-permute-start | bytes 442376 | tf_op jit(solution)/shard_map/ppermute | solution.py:514
  48.4 7.8 %collective-permute-start.14 = (bf16[96,768]{1,0:T(8,128)(2,1)S(1)}, bf16[96,768]{1,0:T(8,128)(2,1)S(1)}, u32[]{:S(2)}, u32[]{:S(2)}) collective-permute-start(bf16[96,768]{1,0:T(8,128)(2,1)S(1)} %total.5), channel_id=1, source_target_pairs={{0,8},{8,16},{16,24},{24,0},{1,9},{9,17},{17,25},{25,1},{2,10},{10... | collective-permute-start | bytes 442376 | tf_op jit(solution)/shard_map/ppermute | solution.py:514

commit v6 on v5

--- a/solution.py
+++ b/solution.py
@@ -143,7 +143,7 @@
 def edge_kernel(rims, cols, meta_ref, *refs):
     own, other = refs[:2]
     rim = refs[2] if rims else None
-    sides_out, query_out = refs[-4:-2], refs[-2:]
+    sides_out = refs[-2:]
     frames, area, half = other.shape[1:]
 
     def pick(rows):
@@ -175,10 +175,6 @@
                         phase * deep : (phase + 1) * deep
                     ]
                 begin += deep
-    for phase in range(2):
-        frame = meta_ref[1 + phase]
-        query_out[phase][:area] = own[0, frame]
-        query_out[phase][area:] = other[0, frame]
 
 
 def guest_kernel(rims, heads, width, meta_ref, radius_ref, code_ref, *refs):
@@ -270,7 +266,7 @@
 
 
 def merge_kernel(
-    heads, width, meta_ref, radius_ref, mixed_ref, stats_ref, ref_0, ref_1, out_ref, held, logs
+    heads, width, meta_ref, radius_ref, mixed_ref, stats_ref, ref_0, ref_1, out_ref
 ):
     frames, count, _ = mixed_ref.shape
     half = count // PAIR
@@ -279,10 +275,8 @@
     use = jnp.zeros((count, LANES), jnp.int32)
     for head in range(heads):
         use = jnp.where(lane == head, radius_ref[first + head, 0], use)
-    held[...] = mixed_ref[...]
-    logs[...] = stats_ref[...]
+    logs, shares = [], []
     for phase, ref in enumerate((ref_0, ref_1)):
-        f = meta_ref[1 + phase]
         there = jnp.where(meta_ref[3 + phase] == 0, 0, use)
         stats = ref[:, pl.ds(heads * width, LANES)].astype(jnp.float32)
         guest = (
@@ -291,22 +285,36 @@
             + pltpu.roll(stats, LANES - 2 * STRIDE, 1)
         )
         guest = jnp.where(there == 0, FAR, guest)
-        own = logs[f]
+        own = stats_ref[meta_ref[1 + phase]]
+        if frames == 1 and phase == 1:
+            own = logs[0]
         top = jnp.maximum(own, guest)
-        own_weight, guest_weight = jnp.exp(own - top), jnp.exp(guest - top)
-        total = own_weight + guest_weight
-        if frames == 1:
-            logs[f] = top + jnp.log(total)
-        own_weight, guest_weight = own_weight / total, guest_weight / total
+        guest_weight = jnp.exp(guest - top)
+        total = jnp.exp(own - top) + guest_weight
+        logs.append(top + jnp.log(total) if frames == 1 else None)
+        shares.append(guest_weight / total)
+
+    def store(f, lanes, mixed):
+        mixed = mixed.astype(out_ref.dtype)
+        for part in range(PAIR):
+            out_ref[part, f, :, lanes] = mixed[part * half : (part + 1) * half]
+
+    def boundary(spots):
         for head in range(heads):
             lanes = pl.ds(head * width, width)
-            held[f, :, lanes] = (
-                held[f, :, lanes] * own_weight[:, head : head + 1]
-                + ref[:, lanes].astype(jnp.float32) * guest_weight[:, head : head + 1]
-            )
-    mixed = held[...].astype(jnp.bfloat16)
-    for part in range(PAIR):
-        out_ref[part] = mixed[:, part * half : (part + 1) * half]
+            for f in sorted(set(spots)):
+                mixed = mixed_ref[f, :, lanes]
+                for phase, ref in enumerate((ref_0, ref_1)):
+                    if spots[phase] == f:
+                        guest = ref[:, lanes].astype(jnp.float32)
+                        mixed = mixed + (guest - mixed) * shares[phase][:, head : head + 1]
+                store(f, lanes, mixed)
+
+    pl.when(meta_ref[1] == 0)(lambda: boundary((0, frames - 1)))
+    if frames > 1:
+        pl.when(meta_ref[1] != 0)(lambda: boundary((frames - 1, 0)))
+    for f in range(1, frames - 1):
+        store(f, slice(None), mixed_ref[f])
 
 
 def join_kernel(count, meta_ref, *refs):
@@ -329,12 +337,11 @@
 
 
 def place_kernel(count, meta_ref, *refs):
-    pieces, out, sems = refs[:count], refs[count], refs[count + 1]
+    pieces, out, sems = refs[:count], refs[-2], refs[-1]
     wide = pieces[0].shape[-1]
     copies = []
     for spot, ref in enumerate(pieces):
-        origin = lax.rem(meta_ref[0] + count - spot, count)
-        where = pl.ds(pl.multiple_of(origin * wide, LANES), wide)
+        where = pl.ds(pl.multiple_of(meta_ref[spot] * wide, LANES), wide)
         copies.append(pltpu.make_async_copy(ref, out.at[:, where], sems.at[spot]))
     for copy in copies:
         copy.start()
@@ -380,21 +387,21 @@
         rim = jnp.concatenate([up, down], axis=2)
     deep = PAIR * rows * TILE + (PAIR * TILE * TILE if rims else 0)
     side = jax.ShapeDtypeStruct((2, frames, deep, half), queries.dtype)
-    end = jax.ShapeDtypeStruct((PAIR * area, half), queries.dtype)
-    *edges, first_end, second_end = pl.pallas_call(
+    edges = pl.pallas_call(
         functools.partial(edge_kernel, rims, cols),
-        out_shape=(side, side, end, end),
+        out_shape=(side, side),
         in_specs=[SMEM] + [VMEM] * (3 if rims else 2),
-        out_specs=(VMEM,) * 4,
+        out_specs=(VMEM,) * 2,
         compiler_params=PARAMS,
         cost_estimate=cost(1000, 2_000_000),
         name="edge",
     )(meta, own, other, *([rim] if rims else []))
     beside = [lax.ppermute(x, ("ha", "wa"), swaps(n_cols, phase, n_rows, True)) for phase, x in enumerate(edges)]
-    guests = [
-        lax.ppermute(x, ("ta", "ha"), swaps(n_time, phase, n_rows, False))
-        for phase, x in enumerate((first_end, second_end))
-    ]
+    guests = []
+    for phase, frame in enumerate(ends):
+        end = [lax.dynamic_index_in_dim(x[0], frame, 0, keepdims=False) for x in (own, other)]
+        end = jnp.concatenate(end, axis=0)
+        guests.append(lax.ppermute(end, ("ta", "ha"), swaps(n_time, phase, n_rows, False)))
 
     slab = features // (n_rows * n_cols)
     wide = out_weight.shape[1] // n_time
@@ -408,7 +415,6 @@
     spot = core * 2 + at_col % 2
     spot = spot * 2 ** len(absent) + sum(jnp.where(x, 2**i, 0) for i, x in enumerate(absent))
     code = lax.dynamic_index_in_dim(table, spot, 0, keepdims=False)
-    place = jnp.stack([at_time]).astype(jnp.int32)
 
     parts = [own, other] + ([rim] if rims else []) + beside
     count = PAIR * area
@@ -447,10 +453,6 @@
         out_shape=jax.ShapeDtypeStruct((PAIR, frames, area, half), jnp.bfloat16),
         in_specs=[SMEM, SMEM] + [VMEM] * 4,
         out_specs=VMEM,
-        scratch_shapes=[
-            pltpu.VMEM(mixed_shape, jnp.float32),
-            pltpu.VMEM(stats_shape, jnp.float32),
-        ],
         compiler_params=PARAMS,
         cost_estimate=cost(1000, 3_000_000),
         name="merge",
@@ -513,16 +515,22 @@
     back = [products[0]] + [
         lax.ppermute(products[n_time - s], "ta", cycle(n_time, s)) for s in range(1, n_time)
     ]
-    out = pl.pallas_call(
-        functools.partial(place_kernel, n_time),
-        out_shape=jax.ShapeDtypeStruct((tokens, wide * n_time), jnp.bfloat16),
-        in_specs=[SMEM] + [HBM] * n_time,
-        out_specs=HBM,
-        scratch_shapes=[pltpu.SemaphoreType.DMA((n_time,))],
-        compiler_params=PARAMS,
-        cost_estimate=cost(1000, 1_200_000),
-        name="place",
-    )(place, *back)
+    late = 1 % n_time
+    out = None
+    for group in ([s for s in range(n_time) if s != late], [late] if n_time > 1 else []):
+        if group:
+            origins = jnp.stack([(at_time - s) % n_time for s in group]).astype(jnp.int32)
+            out = pl.pallas_call(
+                functools.partial(place_kernel, len(group)),
+                out_shape=jax.ShapeDtypeStruct((tokens, wide * n_time), jnp.bfloat16),
+                in_specs=[SMEM] + [HBM] * (len(group) + (out is not None)),
+                out_specs=HBM,
+                input_output_aliases={} if out is None else {1 + len(group): 0},
+                scratch_shapes=[pltpu.SemaphoreType.DMA((len(group),))],
+                compiler_params=PARAMS,
+                cost_estimate=cost(1000, 1_200_000),
+                name="place",
+            )(origins, *[back[s] for s in group], *([] if out is None else [out]))
     return out.reshape(frames, rows, cols, wide * n_time)
 
 

time: 57.2 us -> 56.2 us (0.983)
  waiting for transfers between devices: 20.9 us -> 19.1 us
    ppermute x4 -> x2, waiting for transfers between devices: 3.71 us -> 0.66 us  [shards(): lax.ppermute(x, ('ta', 'ha'), swaps(n_time, phase, n_rows, False))]
    ppermute x0 -> x2, waiting for transfers between devices: none -> 2.66 us  [shards(): lax.ppermute(end, ('ta', 'ha'), swaps(n_time, phase, n_rows, False))]
    ppermute x4 -> x2, starting transfers between devices: 4 us -> 1.88 us  [shards(): lax.ppermute(x, ('ta', 'ha'), swaps(n_time, phase, n_rows, False))]
    ppermute x0 -> x2, starting transfers between devices: none -> 1.84 us  [shards(): lax.ppermute(end, ('ta', 'ha'), swaps(n_time, phase, n_rows, False))]
    ppermute x3, waiting for transfers between devices: 6.12 us -> 4.77 us  [shards(): lax.ppermute(products[n_time - s], 'ta', cycle(n_time, s))]
    pallas_call x1 -> x2, Pallas kernels: 0.84 us -> 2 us  [shards(): pl.pallas_call(functools.partial(place_kernel, len(group)), out_shape=jax...]
    pallas_call x1, Pallas kernels: 1.54 us -> 0.84 us  [shards(): pl.pallas_call(functools.partial(edge_kernel, rims, cols), out_shape=(sid...]
  transfers between devices with their start and end apart: 20 -> 20, of which waited for: 9 -> 10; matrix products, arithmetic and copies ran while one was open for 2% -> 2% of each run, Pallas kernels for 9% -> 11%
where the time goes in v6:
time: 56.2 us; the launch traced here: 55.9 us
  starting transfers between devices  24.5 us (44%)
  waiting for transfers between devices  19.1 us (34%)
  Pallas kernels  9.5 us (17%)
  other arithmetic  1.5 us (3%)
  local copies, waits for them, and re-layouts  1.16 us (2%)
    ppermute x3, waiting for transfers between devices, shards(): lax.ppermute(attended, 'ta', cycle(n_time, s))  7.1 us
    ppermute x3, starting transfers between devices, shards(): lax.ppermute(attended, 'ta', cycle(n_time, s))  5.9 us
    ppermute x3, waiting for transfers between devices, shards(): lax.ppermute(products[n_time - s], 'ta', cycle(n_time, s))  4.77 us
    ppermute x3, starting transfers between devices, shards(): lax.ppermute(products[n_time - s], 'ta', cycle(n_time, s))  3.87 us
    ppermute x2, starting transfers between devices, shards(): lax.ppermute(x, ('ha', 'wa'), swaps(n_cols, phase, n_rows, True))  3 us
    ppermute x1, starting transfers between devices, shards(): held[1] = lax.ppermute(sent, 'wa', cycle(n_cols, 1))  2.91 us
    ppermute x2, waiting for transfers between devices, shards(): lax.ppermute(end, ('ta', 'ha'), swaps(n_time, phase, n_rows, False))  2.66 us
    ppermute x2, waiting for transfers between devices, shards(): lax.ppermute(x, ('ha', 'wa'), swaps(n_cols, phase, n_rows, True))  2.04 us
  transfers between devices with their start and end apart: 20, of which 10 were waited for; matrix products, arithmetic and copies ran while one was open for 2% of the time, Pallas kernels for 11%

profile of v6, /device:TPU:0, one launch (start us, length us, event | category | flops | bytes accessed | tf_op | source)
XLA Modules:
  0.0 55.9 jit_solution(9584278782795830600)
XLA Ops:
  0.0 1.3 %pad_maximum_fusion = bf16[3,3,32,1536]{3,2,1,0:T(8,128)(2,1)S(1)} fusion(bf16[1,3,32,1536]{3,2,1,0:T(8,128)(2,1)} %bitcast.34, bf16[1,3,32,1536]{3,2,1,0:T(8,128)(2,1)} %bitcast.35, bf16[1,3,32,1536]{3,2,1,0:T(8,128)(2,1)} %bitcast.36), kind=kLoop, calls=%fused_computation | loop fusion | flops 884736 | bytes 1769472 | tf_op jit(solution)/shard_map/stack | solution.py:376
  2.3 1.1 %collective-permute-done.refs_1_ = bf16[3,3,32,768]{3,2,1,0:T(8,128)(2,1)S(1)} collective-permute-done((bf16[3,3,32,768]{3,2,1,0:T(8,128)(2,1)S(1)}, bf16[3,3,32,768]{3,2,1,0:T(8,128)(2,1)S(1)}, u32[]{:S(2)}, u32[]{:S(2)}) %collective-permute-start) | collective-permute-done | bytes 442400 | tf_op jit(solution)/shard_map/ppermute | solution.py:380
  3.4 0.8 %edge.1 = (bf16[2,3,32,768]{3,2,1,0:T(8,128)(2,1)S(1)}, bf16[2,3,32,768]{3,2,1,0:T(8,128)(2,1)S(1)}) custom-call(s32[7]{0:T(128)S(1)} %stack.73.meta_ref, bf16[3,3,32,768]{3,2,1,0:T(8,128)(2,1)S(1)} %get-tuple-element.38.refs_0_, bf16[3,3,32,768]{3,2,1,0:T(8,128)(2,1)S(1)} %collective-permute-done.refs_1_), custom_call_target="tpu_custom_call" | custom-call | flops 1000 | bytes 2000000 | tf_op jit(solution)/shard_map/edge/pallas_call | solution.py:390
  4.3 3.0 %collective-permute-start.1 = (bf16[2,3,32,768]{3,2,1,0:T(8,128)(2,1)S(1)}, bf16[2,3,32,768]{3,2,1,0:T(8,128)(2,1)S(1)}, u32[]{:S(2)}, u32[]{:S(2)}) collective-permute-start(bf16[2,3,32,768]{3,2,1,0:T(8,128)(2,1)S(1)} %get-tuple-element.20), channel_id=1, source_target_pairs={{0,1},{1,0},{2,3},{3,2},{4,5},{5,4},{6,7},{7,6},{8,9},{9,8},{10,11... | collective-permute-start | bytes 884744 | tf_op jit(solution)/shard_map/ppermute | solution.py:399
  7.3 1.6 %collective-permute-start.3 = (bf16[64,768]{1,0:T(8,128)(2,1)S(1)}, bf16[64,768]{1,0:T(8,128)(2,1)S(1)}, u32[]{:S(2)}, u32[]{:S(2)}) collective-permute-start(bf16[64,768]{1,0:T(8,128)(2,1)S(1)} %pad_maximum_fusion.1), channel_id=1, source_target_pairs={{0,8},{8,0},{16,24},{24,16},{4,12},{12,4},{20,28},{28,20},{1,9},{9... | collective-permute-start | bytes 294920 | tf_op jit(solution)/shard_map/ppermute | solution.py:404
  9.1 0.8 %dynamic-slice_bitcast_fusion.4.code_ref = s32[64,128]{1,0:T(8,128)S(1)} fusion(s32[16,64,128]{2,1,0:T(8,128)} %constant.114.clone, s32[]{:T(128)S(6)} %select_n.113), kind=kLoop, calls=%fused_computation.7 | loop fusion | bytes 65540 | tf_op jit(solution)/shard_map/jit(dynamic_index_in_dim)/squeeze | solution.py:417
  9.9 2.7 %collective-permute-done.3.refs_4_ = bf16[64,768]{1,0:T(8,128)(2,1)S(1)} collective-permute-done((bf16[64,768]{1,0:T(8,128)(2,1)S(1)}, bf16[64,768]{1,0:T(8,128)(2,1)S(1)}, u32[]{:S(2)}, u32[]{:S(2)}) %collective-permute-start.3) | collective-permute-done | bytes 98336 | tf_op jit(solution)/shard_map/ppermute | solution.py:404
  12.5 2.0 %collective-permute-done.1.refs_2_ = bf16[2,3,32,768]{3,2,1,0:T(8,128)(2,1)S(1)} collective-permute-done((bf16[2,3,32,768]{3,2,1,0:T(8,128)(2,1)S(1)}, bf16[2,3,32,768]{3,2,1,0:T(8,128)(2,1)S(1)}, u32[]{:S(2)}, u32[]{:S(2)}) %collective-permute-start.1) | collective-permute-done | bytes 294944 | tf_op jit(solution)/shard_map/ppermute | solution.py:399
  14.6 1.7 %guest.1 = (bf16[64,896]{1,0:T(8,128)(2,1)S(1)}, bf16[64,896]{1,0:T(8,128)(2,1)S(1)}, bf16[192,768]{1,0:T(8,128)(2,1)}) custom-call(s32[7]{0:T(128)S(1)} %stack.73.meta_ref, s32[12,3]{1,0:T(8,128)S(1)} %copy.10.radius_ref, s32[64,128]{1,0:T(8,128)S(1)} %dynamic-slice_bitcast_fusion.4.code_ref, bf16[3,3,32,768]{3,2,1,0:T(8,128)(2,1)S(1)} %get-tuple-element.38.refs_0_, ...), custom_call_target="tpu_custom_call" | custom-call | flops 50331648 | bytes 4000000 | tf_op jit(solution)/shard_map/guest/pallas_call | solution.py:423
  16.3 2.9 %collective-permute-start.8 = (bf16[192,768]{1,0:T(8,128)(2,1)}, bf16[192,768]{1,0:T(8,128)(2,1)S(1)}, u32[]{:S(2)}, u32[]{:S(2)}) collective-permute-start(bf16[192,768]{1,0:T(8,128)(2,1)} %get-tuple-element.26), channel_id=1, source_target_pairs={{0,1},{1,2},{2,3},{3,0},{4,5},{5,6},{6,7},{7,4},{8,9},{9,10},{10,1... | collective-permute-start | bytes 884744 | tf_op jit(solution)/shard_map/ppermute | solution.py:434
  19.2 1.9 %collective-permute-start.5 = (bf16[64,896]{1,0:T(8,128)(2,1)S(1)}, bf16[64,896]{1,0:T(8,128)(2,1)S(1)}, u32[]{:S(2)}, u32[]{:S(2)}) collective-permute-start(bf16[64,896]{1,0:T(8,128)(2,1)S(1)} %get-tuple-element.24), channel_id=1, source_target_pairs={{0,8},{8,0},{16,24},{24,16},{4,12},{12,4},{20,28},{28,20},{1,9},{9... | collective-permute-start | bytes 344072 | tf_op jit(solution)/shard_map/ppermute | solution.py:436
  21.1 1.6 %collective-permute-start.10 = (bf16[192,768]{1,0:T(8,128)(2,1)}, bf16[192,768]{1,0:T(8,128)(2,1)S(1)}, u32[]{:S(2)}, u32[]{:S(2)}) collective-permute-start(bf16[192,768]{1,0:T(8,128)(2,1)} %get-tuple-element.26), channel_id=1, source_target_pairs={{0,3},{1,0},{2,1},{3,2},{4,7},{5,4},{6,5},{7,6},{8,11},{9,8},{10,9... | collective-permute-start | bytes 884744 | tf_op jit(solution)/shard_map/ppermute | solution.py:463
  22.7 1.6 %host.1 = (f32[3,64,768]{2,1,0:T(8,128)S(1)}, f32[3,64,128]{2,1,0:T(8,128)S(1)}) custom-call(s32[7]{0:T(128)S(1)} %stack.73.meta_ref, s32[12,3]{1,0:T(8,128)S(1)} %copy.10.radius_ref, s32[64,128]{1,0:T(8,128)S(1)} %dynamic-slice_bitcast_fusion.4.code_ref, bf16[3,3,32,768]{3,2,1,0:T(8,128)(2,1)S(1)} %get-tuple-element.38.refs_0_, ...), custom_call_target="tpu_custom_call" | custom-call | flops 176160768 | bytes 6000000 | tf_op jit(solution)/shard_map/host/pallas_call | solution.py:439
  25.0 1.0 %merge.1 = bf16[2,3,32,768]{3,2,1,0:T(8,128)(2,1)S(1)} custom-call(s32[7]{0:T(128)S(1)} %stack.73.meta_ref, s32[12,3]{1,0:T(8,128)S(1)} %copy.10.radius_ref, f32[3,64,768]{2,1,0:T(8,128)S(1)} %get-tuple-element.22.mixed_ref, f32[3,64,128]{2,1,0:T(8,128)S(1)} %get-tuple-element.23.stats_ref, bf16[64,896]{1,0:T(8,128)(2,1)S(1)} %collective-permute-done.5.ref_0, ...), custom_call_target="tpu_custom_call" | custom-call | flops 1000 | bytes 3000000 | tf_op jit(solution)/shard_map/merge/pallas_call | solution.py:451
  26.0 3.0 %collective-permute-start.11 = (bf16[192,768]{1,0:T(8,128)(2,1)S(1)}, bf16[192,768]{1,0:T(8,128)(2,1)S(1)}, u32[]{:S(2)}, u32[]{:S(2)}) collective-permute-start(bf16[192,768]{1,0:T(8,128)(2,1)S(1)} %bitcast.30), channel_id=1, source_target_pairs={{0,16},{8,24},{16,0},{24,8},{1,17},{9,25},{17,1},{25,9},{2,18},{10... | collective-permute-start | bytes 884744 | tf_op jit(solution)/shard_map/ppermute | solution.py:466
  29.0 1.7 %collective-permute-start.9 = (bf16[192,768]{1,0:T(8,128)(2,1)S(1)}, bf16[192,768]{1,0:T(8,128)(2,1)S(1)}, u32[]{:S(2)}, u32[]{:S(2)}) collective-permute-start(bf16[192,768]{1,0:T(8,128)(2,1)S(1)} %collective-permute-done.8.refs_1_), channel_id=1, source_target_pairs={{0,1},{1,2},{2,3},{3,0},{4,5},{5,6},{6,7},{7,4},{8,9},{9,10},{10,1... | collective-permute-start | bytes 884744 | tf_op jit(solution)/shard_map/ppermute | solution.py:465
  31.2 2.4 %collective-permute-start.7 = (bf16[192,768]{1,0:T(8,128)(2,1)S(1)}, bf16[192,768]{1,0:T(8,128)(2,1)S(1)}, u32[]{:S(2)}, u32[]{:S(2)}) collective-permute-start(bf16[192,768]{1,0:T(8,128)(2,1)S(1)} %bitcast.32), channel_id=1, source_target_pairs={{0,24},{8,0},{16,8},{24,16},{1,25},{9,1},{17,9},{25,17},{2,26},{10... | collective-permute-start | bytes 884744 | tf_op jit(solution)/shard_map/ppermute | solution.py:466
  34.4 6.7 %collective-permute-done.11.refs_4_.rows = bf16[192,768]{1,0:T(8,128)(2,1)S(1)} collective-permute-done((bf16[192,768]{1,0:T(8,128)(2,1)S(1)}, bf16[192,768]{1,0:T(8,128)(2,1)S(1)}, u32[]{:S(2)}, u32[]{:S(2)}) %collective-permute-start.11) | collective-permute-done | bytes 294944 | tf_op jit(solution)/shard_map/ppermute | solution.py:466
  45.1 1.4 %collective-permute-start.19 = (bf16[96,768]{1,0:T(8,128)(2,1)S(1)}, bf16[96,768]{1,0:T(8,128)(2,1)S(1)}, u32[]{:S(2)}, u32[]{:S(2)}) collective-permute-start(bf16[96,768]{1,0:T(8,128)(2,1)S(1)} %total.7), channel_id=1, source_target_pairs={{0,24},{8,0},{16,8},{24,16},{1,25},{9,1},{17,9},{25,17},{2,26},{10... | collective-permute-start | bytes 442376 | tf_op jit(solution)/shard_map/ppermute | solution.py:516
  46.6 0.9 %collective-permute-start.16 = (bf16[96,768]{1,0:T(8,128)(2,1)S(1)}, bf16[96,768]{1,0:T(8,128)(2,1)S(1)}, u32[]{:S(2)}, u32[]{:S(2)}) collective-permute-start(bf16[96,768]{1,0:T(8,128)(2,1)S(1)} %total.6), channel_id=1, source_target_pairs={{0,16},{8,24},{16,0},{24,8},{1,17},{9,25},{17,1},{25,9},{2,18},{10... | collective-permute-start | bytes 442376 | tf_op jit(solution)/shard_map/ppermute | solution.py:516
  47.4 1.6 %collective-permute-start.13 = (bf16[96,768]{1,0:T(8,128)(2,1)S(1)}, bf16[96,768]{1,0:T(8,128)(2,1)S(1)}, u32[]{:S(2)}, u32[]{:S(2)}) collective-permute-start(bf16[96,768]{1,0:T(8,128)(2,1)S(1)} %total.4), channel_id=1, source_target_pairs={{0,8},{8,16},{16,24},{24,0},{1,9},{9,17},{17,25},{25,1},{2,10},{10... | collective-permute-start | bytes 442376 | tf_op jit(solution)/shard_map/ppermute | solution.py:516
  49.2 2.4 %collective-permute-done.19.refs_2_ = bf16[96,768]{1,0:T(8,128)(2,1)S(1)} collective-permute-done((bf16[96,768]{1,0:T(8,128)(2,1)S(1)}, bf16[96,768]{1,0:T(8,128)(2,1)S(1)}, u32[]{:S(2)}, u32[]{:S(2)}) %collective-permute-start.19) | collective-permute-done | bytes 147488 | tf_op jit(solution)/shard_map/ppermute | solution.py:516
  51.6 2.0 %collective-permute-done.16.refs_1_ = bf16[96,768]{1,0:T(8,128)(2,1)S(1)} collective-permute-done((bf16[96,768]{1,0:T(8,128)(2,1)S(1)}, bf16[96,768]{1,0:T(8,128)(2,1)S(1)}, u32[]{:S(2)}, u32[]{:S(2)}) %collective-permute-start.16) | collective-permute-done | bytes 147488 | tf_op jit(solution)/shard_map/ppermute | solution.py:516
  53.6 1.3 %place.2.refs_1_ = bf16[96,3072]{1,0:T(8,128)(2,1)} custom-call(s32[3]{0:T(128)S(1)} %pad_add_fusion.1.meta_ref, bf16[96,768]{1,0:T(8,128)(2,1)S(1)} %total.5.refs_0_, bf16[96,768]{1,0:T(8,128)(2,1)S(1)} %collective-permute-done.16.refs_1_, bf16[96,768]{1,0:T(8,128)(2,1)S(1)} %collective-permute-done.19.refs_2_), custom_call_target="tpu_custom_call" | custom-call | flops 1000 | bytes 1200000 | tf_op jit(solution)/shard_map/place/pallas_call | solution.py:523
  (48 shorter events, 8.3 us)
Async XLA Ops:
  0.0 2.2 %copy-start = (bf16[192,3072]{1,0:T(8,128)(2,1)S(1)}, bf16[192,3072]{1,0:T(8,128)(2,1)}, u32[]{:S(2)}) copy-start(bf16[192,3072]{1,0:T(8,128)(2,1)} %param.10) | copy-start | bytes 3538948
  1.3 0.7 %copy-start.1 = (s32[12,3]{0,1:T(4,128)S(1)}, s32[12,3]{0,1:T(4,128)}, u32[]{:S(2)}) copy-start(s32[12,3]{0,1:T(4,128)} %param.9) | copy-start | bytes 436
  1.4 1.9 %collective-permute-start = (bf16[3,3,32,768]{3,2,1,0:T(8,128)(2,1)S(1)}, bf16[3,3,32,768]{3,2,1,0:T(8,128)(2,1)S(1)}, u32[]{:S(2)}, u32[]{:S(2)}) collective-permute-start(bf16[3,3,32,768]{3,2,1,0:T(8,128)(2,1)S(1)} %get-tuple-element.37), channel_id=1, source_target_pairs={{0,4},{4,0},{1,5},{5,1},{2,6},{6,2},{3,7},{7,3},{8,12},{12,8},{9,1... | collective-permute-start | bytes 1327112 | tf_op jit(solution)/shard_map/ppermute | solution.py:380
  4.3 10.3 %collective-permute-start.1 = (bf16[2,3,32,768]{3,2,1,0:T(8,128)(2,1)S(1)}, bf16[2,3,32,768]{3,2,1,0:T(8,128)(2,1)S(1)}, u32[]{:S(2)}, u32[]{:S(2)}) collective-permute-start(bf16[2,3,32,768]{3,2,1,0:T(8,128)(2,1)S(1)} %get-tuple-element.20), channel_id=1, source_target_pairs={{0,1},{1,0},{2,3},{3,2},{4,5},{5,4},{6,7},{7,6},{8,9},{9,8},{10,11... | collective-permute-start | bytes 884744 | tf_op jit(solution)/shard_map/ppermute | solution.py:399
  7.3 7.3 %collective-permute-start.2 = (bf16[2,3,32,768]{3,2,1,0:T(8,128)(2,1)S(1)}, bf16[2,3,32,768]{3,2,1,0:T(8,128)(2,1)S(1)}, u32[]{:S(2)}, u32[]{:S(2)}) collective-permute-start(bf16[2,3,32,768]{3,2,1,0:T(8,128)(2,1)S(1)} %get-tuple-element.21), channel_id=1, source_target_pairs={{0,4},{1,2},{2,1},{3,7},{4,0},{5,6},{6,5},{7,3},{8,12},{9,10},{10,... | collective-permute-start | bytes 884744 | tf_op jit(solution)/shard_map/ppermute | solution.py:399
  7.3 5.3 %collective-permute-start.3 = (bf16[64,768]{1,0:T(8,128)(2,1)S(1)}, bf16[64,768]{1,0:T(8,128)(2,1)S(1)}, u32[]{:S(2)}, u32[]{:S(2)}) collective-permute-start(bf16[64,768]{1,0:T(8,128)(2,1)S(1)} %pad_maximum_fusion.1), channel_id=1, source_target_pairs={{0,8},{8,0},{16,24},{24,16},{4,12},{12,4},{20,28},{28,20},{1,9},{9... | collective-permute-start | bytes 294920 | tf_op jit(solution)/shard_map/ppermute | solution.py:404
  8.8 3.7 %collective-permute-start.4 = (bf16[64,768]{1,0:T(8,128)(2,1)S(1)}, bf16[64,768]{1,0:T(8,128)(2,1)S(1)}, u32[]{:S(2)}, u32[]{:S(2)}) collective-permute-start(bf16[64,768]{1,0:T(8,128)(2,1)S(1)} %pad_maximum_fusion.2), channel_id=1, source_target_pairs={{0,4},{8,16},{16,8},{24,28},{4,0},{12,20},{20,12},{28,24},{1,5},{9... | collective-permute-start | bytes 294920 | tf_op jit(solution)/shard_map/ppermute | solution.py:404
  16.3 12.7 %collective-permute-start.8 = (bf16[192,768]{1,0:T(8,128)(2,1)}, bf16[192,768]{1,0:T(8,128)(2,1)S(1)}, u32[]{:S(2)}, u32[]{:S(2)}) collective-permute-start(bf16[192,768]{1,0:T(8,128)(2,1)} %get-tuple-element.26), channel_id=1, source_target_pairs={{0,1},{1,2},{2,3},{3,0},{4,5},{5,6},{6,7},{7,4},{8,9},{9,10},{10,1... | collective-permute-start | bytes 884744 | tf_op jit(solution)/shard_map/ppermute | solution.py:434
  19.2 5.8 %collective-permute-start.5 = (bf16[64,896]{1,0:T(8,128)(2,1)S(1)}, bf16[64,896]{1,0:T(8,128)(2,1)S(1)}, u32[]{:S(2)}, u32[]{:S(2)}) collective-permute-start(bf16[64,896]{1,0:T(8,128)(2,1)S(1)} %get-tuple-element.24), channel_id=1, source_target_pairs={{0,8},{8,0},{16,24},{24,16},{4,12},{12,4},{20,28},{28,20},{1,9},{9... | collective-permute-start | bytes 344072 | tf_op jit(solution)/shard_map/ppermute | solution.py:436
  21.1 3.9 %collective-permute-start.6 = (bf16[64,896]{1,0:T(8,128)(2,1)S(1)}, bf16[64,896]{1,0:T(8,128)(2,1)S(1)}, u32[]{:S(2)}, u32[]{:S(2)}) collective-permute-start(bf16[64,896]{1,0:T(8,128)(2,1)S(1)} %get-tuple-element.25), channel_id=1, source_target_pairs={{0,4},{8,16},{16,8},{24,28},{4,0},{12,20},{20,12},{28,24},{1,5},{9... | collective-permute-start | bytes 344072 | tf_op jit(solution)/shard_map/ppermute | solution.py:436
  21.1 13.3 %collective-permute-start.10 = (bf16[192,768]{1,0:T(8,128)(2,1)}, bf16[192,768]{1,0:T(8,128)(2,1)S(1)}, u32[]{:S(2)}, u32[]{:S(2)}) collective-permute-start(bf16[192,768]{1,0:T(8,128)(2,1)} %get-tuple-element.26), channel_id=1, source_target_pairs={{0,3},{1,0},{2,1},{3,2},{4,7},{5,4},{6,5},{7,6},{8,11},{9,8},{10,9... | collective-permute-start | bytes 884744 | tf_op jit(solution)/shard_map/ppermute | solution.py:463
  26.0 15.1 %collective-permute-start.11 = (bf16[192,768]{1,0:T(8,128)(2,1)S(1)}, bf16[192,768]{1,0:T(8,128)(2,1)S(1)}, u32[]{:S(2)}, u32[]{:S(2)}) collective-permute-start(bf16[192,768]{1,0:T(8,128)(2,1)S(1)} %bitcast.30), channel_id=1, source_target_pairs={{0,16},{8,24},{16,0},{24,8},{1,17},{9,25},{17,1},{25,9},{2,18},{10... | collective-permute-start | bytes 884744 | tf_op jit(solution)/shard_map/ppermute | solution.py:466
  29.0 12.2 %collective-permute-start.9 = (bf16[192,768]{1,0:T(8,128)(2,1)S(1)}, bf16[192,768]{1,0:T(8,128)(2,1)S(1)}, u32[]{:S(2)}, u32[]{:S(2)}) collective-permute-start(bf16[192,768]{1,0:T(8,128)(2,1)S(1)} %collective-permute-done.8.refs_1_), channel_id=1, source_target_pairs={{0,1},{1,2},{2,3},{3,0},{4,5},{5,6},{6,7},{7,4},{8,9},{9,10},{10,1... | collective-permute-start | bytes 884744 | tf_op jit(solution)/shard_map/ppermute | solution.py:465
  30.7 11.1 %collective-permute-start.17 = (bf16[192,768]{1,0:T(8,128)(2,1)S(1)}, bf16[192,768]{1,0:T(8,128)(2,1)S(1)}, u32[]{:S(2)}, u32[]{:S(2)}) collective-permute-start(bf16[192,768]{1,0:T(8,128)(2,1)S(1)} %bitcast.31), channel_id=1, source_target_pairs={{0,8},{8,16},{16,24},{24,0},{1,9},{9,17},{17,25},{25,1},{2,10},{10... | collective-permute-start | bytes 884744 | tf_op jit(solution)/shard_map/ppermute | solution.py:466
  31.2 12.4 %collective-permute-start.7 = (bf16[192,768]{1,0:T(8,128)(2,1)S(1)}, bf16[192,768]{1,0:T(8,128)(2,1)S(1)}, u32[]{:S(2)}, u32[]{:S(2)}) collective-permute-start(bf16[192,768]{1,0:T(8,128)(2,1)S(1)} %bitcast.32), channel_id=1, source_target_pairs={{0,24},{8,0},{16,8},{24,16},{1,25},{9,1},{17,9},{25,17},{2,26},{10... | collective-permute-start | bytes 884744 | tf_op jit(solution)/shard_map/ppermute | solution.py:466
  42.2 2.9 %collective-permute-start.18 = (f32[96,768]{1,0:T(8,128)S(1)}, f32[96,768]{1,0:T(8,128)S(1)}, u32[]{:S(2)}, u32[]{:S(2)}) collective-permute-start(f32[96,768]{1,0:T(8,128)S(1)} %get-tuple-element.34), channel_id=1, source_target_pairs={{0,4},{4,0},{1,5},{5,1},{2,6},{6,2},{3,7},{7,3},{8,12},{12,8},{9,1... | collective-permute-start | bytes 884744 | tf_op jit(solution)/shard_map/ppermute | solution.py:514
  42.7 3.8 %collective-permute-start.15 = (f32[96,768]{1,0:T(8,128)S(1)}, f32[96,768]{1,0:T(8,128)S(1)}, u32[]{:S(2)}, u32[]{:S(2)}) collective-permute-start(f32[96,768]{1,0:T(8,128)S(1)} %get-tuple-element.32), channel_id=1, source_target_pairs={{0,4},{4,0},{1,5},{5,1},{2,6},{6,2},{3,7},{7,3},{8,12},{12,8},{9,1... | collective-permute-start | bytes 884744 | tf_op jit(solution)/shard_map/ppermute | solution.py:514
  44.0 3.4 %collective-permute-start.12 = (f32[96,768]{1,0:T(8,128)S(1)}, f32[96,768]{1,0:T(8,128)S(1)}, u32[]{:S(2)}, u32[]{:S(2)}) collective-permute-start(f32[96,768]{1,0:T(8,128)S(1)} %get-tuple-element.28), channel_id=1, source_target_pairs={{0,4},{4,0},{1,5},{5,1},{2,6},{6,2},{3,7},{7,3},{8,12},{12,8},{9,1... | collective-permute-start | bytes 884744 | tf_op jit(solution)/shard_map/ppermute | solution.py:514
  44.5 4.6 %collective-permute-start.14 = (f32[96,768]{1,0:T(8,128)S(1)}, f32[96,768]{1,0:T(8,128)S(1)}, u32[]{:S(2)}, u32[]{:S(2)}) collective-permute-start(f32[96,768]{1,0:T(8,128)S(1)} %get-tuple-element.30), channel_id=1, source_target_pairs={{0,4},{4,0},{1,5},{5,1},{2,6},{6,2},{3,7},{7,3},{8,12},{12,8},{9,1... | collective-permute-start | bytes 884744 | tf_op jit(solution)/shard_map/ppermute | solution.py:514
  45.1 6.5 %collective-permute-start.19 = (bf16[96,768]{1,0:T(8,128)(2,1)S(1)}, bf16[96,768]{1,0:T(8,128)(2,1)S(1)}, u32[]{:S(2)}, u32[]{:S(2)}) collective-permute-start(bf16[96,768]{1,0:T(8,128)(2,1)S(1)} %total.7), channel_id=1, source_target_pairs={{0,24},{8,0},{16,8},{24,16},{1,25},{9,1},{17,9},{25,17},{2,26},{10... | collective-permute-start | bytes 442376 | tf_op jit(solution)/shard_map/ppermute | solution.py:516
  46.6 7.1 %collective-permute-start.16 = (bf16[96,768]{1,0:T(8,128)(2,1)S(1)}, bf16[96,768]{1,0:T(8,128)(2,1)S(1)}, u32[]{:S(2)}, u32[]{:S(2)}) collective-permute-start(bf16[96,768]{1,0:T(8,128)(2,1)S(1)} %total.6), channel_id=1, source_target_pairs={{0,16},{8,24},{16,0},{24,8},{1,17},{9,25},{17,1},{25,9},{2,18},{10... | collective-permute-start | bytes 442376 | tf_op jit(solution)/shard_map/ppermute | solution.py:516
  47.4 7.8 %collective-permute-start.13 = (bf16[96,768]{1,0:T(8,128)(2,1)S(1)}, bf16[96,768]{1,0:T(8,128)(2,1)S(1)}, u32[]{:S(2)}, u32[]{:S(2)}) collective-permute-start(bf16[96,768]{1,0:T(8,128)(2,1)S(1)} %total.4), channel_id=1, source_target_pairs={{0,8},{8,16},{16,24},{24,0},{1,9},{9,17},{17,25},{25,1},{2,10},{10... | collective-permute-start | bytes 442376 | tf_op jit(solution)/shard_map/ppermute | solution.py:516

commit v7 on v6

--- a/solution.py
+++ b/solution.py
@@ -179,9 +179,7 @@
 
 def guest_kernel(rims, heads, width, meta_ref, radius_ref, code_ref, *refs):
     window = Window(refs, rims, heads, width)
-    guests, (shard, *outs, sent, sem) = window.rest[:2], window.rest[2:]
-    passing = pltpu.make_async_copy(shard, sent, sem)
-    passing.start()
+    guests, outs = window.rest[:2], window.rest[3:5]
     code = code_ref[...]
     count = code.shape[0]
     scale = 1.0 / math.sqrt(width)
@@ -215,7 +213,6 @@
             rest = rest - piece
             stats = stats + (pltpu.roll(piece, part * STRIDE, 1) if part else piece)
         out_ref[:, pl.ds(heads * width, LANES)] = stats.astype(jnp.bfloat16)
-    passing.wait()
 
 
 def host_kernel(rims, heads, width, meta_ref, radius_ref, code_ref, *refs):
@@ -425,11 +422,12 @@
         out_shape=(payload, payload, jax.ShapeDtypeStruct(mine.shape, mine.dtype)),
         in_specs=[SMEM, SMEM] + [VMEM] * (1 + len(parts) + 2) + [HBM],
         out_specs=(VMEM, VMEM, HBM),
-        scratch_shapes=[pltpu.SemaphoreType.DMA],
+        input_output_aliases={5 + len(parts): 2},
         compiler_params=PARAMS,
         cost_estimate=cost(2 * unit, 4_000_000),
         name="guest",
     )(meta, radius, code, *parts, *guests, mine)
+    held[0] = sent
     if n_cols > 1:
         held[1] = lax.ppermute(sent, "wa", cycle(n_cols, 1))
     answers = [
@@ -485,6 +483,8 @@
         across = [lax.ppermute(near, "ha", cycle(n_rows, r)) for r in range(1, n_rows)]
         near = lax.dynamic_slice_in_dim(joined([near, *across], at_row), core * half, half, axis=0)
 
+    weight = 36 * 2 * tokens * features * wide
+
     def project(block):
         part = jax.ShapeDtypeStruct((tokens, wide), jnp.float32)
         return pl.pallas_call(
@@ -493,7 +493,7 @@
             in_specs=[VMEM, VMEM],
             out_specs=(VMEM, VMEM),
             compiler_params=PARAMS,
-            cost_estimate=cost(2 * tokens * features * wide, 3_000_000),
+            cost_estimate=cost(weight, 3_000_000),
             name="project",
         )(block, near)
 
@@ -504,7 +504,7 @@
             in_specs=[VMEM, VMEM],
             out_specs=VMEM,
             compiler_params=PARAMS,
-            cost_estimate=cost(tokens * wide, 3_000_000),
+            cost_estimate=cost(weight, 3_000_000),
             name="total",
         )(part, partner)
 

time: 56.2 us -> 55.6 us (0.989)
  no operation moved by 1% of the time
where the time goes in v7:
time: 55.6 us; the launch traced here: 55.4 us
  starting transfers between devices  24.7 us (44%)
  waiting for transfers between devices  18.7 us (34%)
  Pallas kernels  9.19 us (17%)
  other arithmetic  1.5 us (3%)
  local copies, waits for them, and re-layouts  1.16 us (2%)
    ppermute x3, waiting for transfers between devices, shards(): lax.ppermute(attended, 'ta', cycle(n_time, s))  7.19 us
    ppermute x3, starting transfers between devices, shards(): lax.ppermute(attended, 'ta', cycle(n_time, s))  5.9 us
    ppermute x3, waiting for transfers between devices, shards(): lax.ppermute(products[n_time - s], 'ta', cycle(n_time, s))  4.82 us
    ppermute x3, starting transfers between devices, shards(): lax.ppermute(products[n_time - s], 'ta', cycle(n_time, s))  4.29 us
    ppermute x2, starting transfers between devices, shards(): lax.ppermute(x, ('ha', 'wa'), swaps(n_cols, phase, n_rows, True))  3 us
    ppermute x1, starting transfers between devices, shards(): held[1] = lax.ppermute(sent, 'wa', cycle(n_cols, 1))  2.91 us
    ppermute x2, waiting for transfers between devices, shards(): lax.ppermute(end, ('ta', 'ha'), swaps(n_time, phase, n_rows, False))  2.66 us
    ppermute x2, waiting for transfers between devices, shards(): lax.ppermute(x, ('ha', 'wa'), swaps(n_cols, phase, n_rows, True))  2.04 us
  transfers between devices with their start and end apart: 20, of which 10 were waited for; matrix products, arithmetic and copies ran while one was open for 2% of the time, Pallas kernels for 11%

profile of v7, /device:TPU:0, one launch (start us, length us, event | category | flops | bytes accessed | tf_op | source)
XLA Modules:
  0.0 55.4 jit_solution(8193080858879073805)
XLA Ops:
  0.0 1.3 %pad_maximum_fusion = bf16[3,3,32,1536]{3,2,1,0:T(8,128)(2,1)S(1)} fusion(bf16[1,3,32,1536]{3,2,1,0:T(8,128)(2,1)} %bitcast.34, bf16[1,3,32,1536]{3,2,1,0:T(8,128)(2,1)} %bitcast.35, bf16[1,3,32,1536]{3,2,1,0:T(8,128)(2,1)} %bitcast.36), kind=kLoop, calls=%fused_computation | loop fusion | flops 884736 | bytes 1769472 | tf_op jit(solution)/shard_map/stack | solution.py:373
  2.3 1.1 %collective-permute-done.refs_1_ = bf16[3,3,32,768]{3,2,1,0:T(8,128)(2,1)S(1)} collective-permute-done((bf16[3,3,32,768]{3,2,1,0:T(8,128)(2,1)S(1)}, bf16[3,3,32,768]{3,2,1,0:T(8,128)(2,1)S(1)}, u32[]{:S(2)}, u32[]{:S(2)}) %collective-permute-start) | collective-permute-done | bytes 442400 | tf_op jit(solution)/shard_map/ppermute | solution.py:377
  3.4 0.8 %edge.1 = (bf16[2,3,32,768]{3,2,1,0:T(8,128)(2,1)S(1)}, bf16[2,3,32,768]{3,2,1,0:T(8,128)(2,1)S(1)}) custom-call(s32[7]{0:T(128)S(1)} %stack.73.meta_ref, bf16[3,3,32,768]{3,2,1,0:T(8,128)(2,1)S(1)} %get-tuple-element.38.refs_0_, bf16[3,3,32,768]{3,2,1,0:T(8,128)(2,1)S(1)} %collective-permute-done.refs_1_), custom_call_target="tpu_custom_call" | custom-call | flops 1000 | bytes 2000000 | tf_op jit(solution)/shard_map/edge/pallas_call | solution.py:387
  4.3 3.0 %collective-permute-start.1 = (bf16[2,3,32,768]{3,2,1,0:T(8,128)(2,1)S(1)}, bf16[2,3,32,768]{3,2,1,0:T(8,128)(2,1)S(1)}, u32[]{:S(2)}, u32[]{:S(2)}) collective-permute-start(bf16[2,3,32,768]{3,2,1,0:T(8,128)(2,1)S(1)} %get-tuple-element.20), channel_id=1, source_target_pairs={{0,1},{1,0},{2,3},{3,2},{4,5},{5,4},{6,7},{7,6},{8,9},{9,8},{10,11... | collective-permute-start | bytes 884744 | tf_op jit(solution)/shard_map/ppermute | solution.py:396
  7.3 1.6 %collective-permute-start.3 = (bf16[64,768]{1,0:T(8,128)(2,1)S(1)}, bf16[64,768]{1,0:T(8,128)(2,1)S(1)}, u32[]{:S(2)}, u32[]{:S(2)}) collective-permute-start(bf16[64,768]{1,0:T(8,128)(2,1)S(1)} %pad_maximum_fusion.1), channel_id=1, source_target_pairs={{0,8},{8,0},{16,24},{24,16},{4,12},{12,4},{20,28},{28,20},{1,9},{9... | collective-permute-start | bytes 294920 | tf_op jit(solution)/shard_map/ppermute | solution.py:401
  9.1 0.8 %dynamic-slice_bitcast_fusion.4.code_ref = s32[64,128]{1,0:T(8,128)S(1)} fusion(s32[16,64,128]{2,1,0:T(8,128)} %constant.114.clone, s32[]{:T(128)S(6)} %select_n.113), kind=kLoop, calls=%fused_computation.7 | loop fusion | bytes 65540 | tf_op jit(solution)/shard_map/jit(dynamic_index_in_dim)/squeeze | solution.py:414
  9.9 2.7 %collective-permute-done.3.refs_4_ = bf16[64,768]{1,0:T(8,128)(2,1)S(1)} collective-permute-done((bf16[64,768]{1,0:T(8,128)(2,1)S(1)}, bf16[64,768]{1,0:T(8,128)(2,1)S(1)}, u32[]{:S(2)}, u32[]{:S(2)}) %collective-permute-start.3) | collective-permute-done | bytes 98336 | tf_op jit(solution)/shard_map/ppermute | solution.py:401
  12.5 2.0 %collective-permute-done.1.refs_2_ = bf16[2,3,32,768]{3,2,1,0:T(8,128)(2,1)S(1)} collective-permute-done((bf16[2,3,32,768]{3,2,1,0:T(8,128)(2,1)S(1)}, bf16[2,3,32,768]{3,2,1,0:T(8,128)(2,1)S(1)}, u32[]{:S(2)}, u32[]{:S(2)}) %collective-permute-start.1) | collective-permute-done | bytes 294944 | tf_op jit(solution)/shard_map/ppermute | solution.py:396
  14.6 1.4 %guest.1 = (bf16[64,896]{1,0:T(8,128)(2,1)S(1)}, bf16[64,896]{1,0:T(8,128)(2,1)S(1)}, bf16[192,768]{1,0:T(8,128)(2,1)S(1)}) custom-call(s32[7]{0:T(128)S(1)} %stack.73.meta_ref, s32[12,3]{1,0:T(8,128)S(1)} %copy.11.radius_ref, s32[64,128]{1,0:T(8,128)S(1)} %dynamic-slice_bitcast_fusion.4.code_ref, ...), custom_call_target="tpu_custom_call", output_to_operand_aliasing={{2}: (9, {})} | custom-call | flops 50331648 | bytes 4000000 | tf_op jit(solution)/shard_map/guest/pallas_call | solution.py:420
  16.0 2.9 %collective-permute-start.8 = (bf16[192,768]{1,0:T(8,128)(2,1)S(1)}, bf16[192,768]{1,0:T(8,128)(2,1)S(1)}, u32[]{:S(2)}, u32[]{:S(2)}) collective-permute-start(bf16[192,768]{1,0:T(8,128)(2,1)S(1)} %get-tuple-element.26.refs_0_), channel_id=1, source_target_pairs={{0,1},{1,2},{2,3},{3,0},{4,5},{5,6},{6,7},{7,4},{8,9},{9,10},{10,1... | collective-permute-start | bytes 884744 | tf_op jit(solution)/shard_map/ppermute | solution.py:432
  18.9 1.9 %collective-permute-start.5 = (bf16[64,896]{1,0:T(8,128)(2,1)S(1)}, bf16[64,896]{1,0:T(8,128)(2,1)S(1)}, u32[]{:S(2)}, u32[]{:S(2)}) collective-permute-start(bf16[64,896]{1,0:T(8,128)(2,1)S(1)} %get-tuple-element.24), channel_id=1, source_target_pairs={{0,8},{8,0},{16,24},{24,16},{4,12},{12,4},{20,28},{28,20},{1,9},{9... | collective-permute-start | bytes 344072 | tf_op jit(solution)/shard_map/ppermute | solution.py:434
  20.7 1.6 %collective-permute-start.10 = (bf16[192,768]{1,0:T(8,128)(2,1)S(1)}, bf16[192,768]{1,0:T(8,128)(2,1)S(1)}, u32[]{:S(2)}, u32[]{:S(2)}) collective-permute-start(bf16[192,768]{1,0:T(8,128)(2,1)S(1)} %get-tuple-element.26.refs_0_), channel_id=1, source_target_pairs={{0,3},{1,0},{2,1},{3,2},{4,7},{5,4},{6,5},{7,6},{8,11},{9,8},{10,9... | collective-permute-start | bytes 884744 | tf_op jit(solution)/shard_map/ppermute | solution.py:461
  22.4 1.6 %host.1 = (f32[3,64,768]{2,1,0:T(8,128)S(1)}, f32[3,64,128]{2,1,0:T(8,128)S(1)}) custom-call(s32[7]{0:T(128)S(1)} %stack.73.meta_ref, s32[12,3]{1,0:T(8,128)S(1)} %copy.11.radius_ref, s32[64,128]{1,0:T(8,128)S(1)} %dynamic-slice_bitcast_fusion.4.code_ref, bf16[3,3,32,768]{3,2,1,0:T(8,128)(2,1)S(1)} %get-tuple-element.38.refs_0_, ...), custom_call_target="tpu_custom_call" | custom-call | flops 176160768 | bytes 6000000 | tf_op jit(solution)/shard_map/host/pallas_call | solution.py:437
  24.7 1.0 %merge.1 = bf16[2,3,32,768]{3,2,1,0:T(8,128)(2,1)S(1)} custom-call(s32[7]{0:T(128)S(1)} %stack.73.meta_ref, s32[12,3]{1,0:T(8,128)S(1)} %copy.11.radius_ref, f32[3,64,768]{2,1,0:T(8,128)S(1)} %get-tuple-element.22.mixed_ref, f32[3,64,128]{2,1,0:T(8,128)S(1)} %get-tuple-element.23.stats_ref, bf16[64,896]{1,0:T(8,128)(2,1)S(1)} %collective-permute-done.5.ref_0, ...), custom_call_target="tpu_custom_call" | custom-call | flops 1000 | bytes 3000000 | tf_op jit(solution)/shard_map/merge/pallas_call | solution.py:449
  25.6 3.0 %collective-permute-start.11 = (bf16[192,768]{1,0:T(8,128)(2,1)S(1)}, bf16[192,768]{1,0:T(8,128)(2,1)S(1)}, u32[]{:S(2)}, u32[]{:S(2)}) collective-permute-start(bf16[192,768]{1,0:T(8,128)(2,1)S(1)} %bitcast.30), channel_id=1, source_target_pairs={{0,16},{8,24},{16,0},{24,8},{1,17},{9,25},{17,1},{25,9},{2,18},{10... | collective-permute-start | bytes 884744 | tf_op jit(solution)/shard_map/ppermute | solution.py:464
  28.6 1.7 %collective-permute-start.9 = (bf16[192,768]{1,0:T(8,128)(2,1)S(1)}, bf16[192,768]{1,0:T(8,128)(2,1)S(1)}, u32[]{:S(2)}, u32[]{:S(2)}) collective-permute-start(bf16[192,768]{1,0:T(8,128)(2,1)S(1)} %collective-permute-done.8.refs_1_), channel_id=1, source_target_pairs={{0,1},{1,2},{2,3},{3,0},{4,5},{5,6},{6,7},{7,4},{8,9},{9,10},{10,1... | collective-permute-start | bytes 884744 | tf_op jit(solution)/shard_map/ppermute | solution.py:463
  30.8 2.6 %collective-permute-start.7 = (bf16[192,768]{1,0:T(8,128)(2,1)S(1)}, bf16[192,768]{1,0:T(8,128)(2,1)S(1)}, u32[]{:S(2)}, u32[]{:S(2)}) collective-permute-start(bf16[192,768]{1,0:T(8,128)(2,1)S(1)} %bitcast.32), channel_id=1, source_target_pairs={{0,24},{8,0},{16,8},{24,16},{1,25},{9,1},{17,9},{25,17},{2,26},{10... | collective-permute-start | bytes 884744 | tf_op jit(solution)/shard_map/ppermute | solution.py:464
  33.7 7.0 %collective-permute-done.11.refs_4_.rows = bf16[192,768]{1,0:T(8,128)(2,1)S(1)} collective-permute-done((bf16[192,768]{1,0:T(8,128)(2,1)S(1)}, bf16[192,768]{1,0:T(8,128)(2,1)S(1)}, u32[]{:S(2)}, u32[]{:S(2)}) %collective-permute-start.11) | collective-permute-done | bytes 294944 | tf_op jit(solution)/shard_map/ppermute | solution.py:464
  44.2 1.2 %collective-permute-start.19 = (bf16[96,768]{1,0:T(8,128)(2,1)S(1)}, bf16[96,768]{1,0:T(8,128)(2,1)S(1)}, u32[]{:S(2)}, u32[]{:S(2)}) collective-permute-start(bf16[96,768]{1,0:T(8,128)(2,1)S(1)} %total.7), channel_id=1, source_target_pairs={{0,24},{8,0},{16,8},{24,16},{1,25},{9,1},{17,9},{25,17},{2,26},{10... | collective-permute-start | bytes 442376 | tf_op jit(solution)/shard_map/ppermute | solution.py:516
  45.4 1.4 %collective-permute-start.16 = (bf16[96,768]{1,0:T(8,128)(2,1)S(1)}, bf16[96,768]{1,0:T(8,128)(2,1)S(1)}, u32[]{:S(2)}, u32[]{:S(2)}) collective-permute-start(bf16[96,768]{1,0:T(8,128)(2,1)S(1)} %total.6), channel_id=1, source_target_pairs={{0,16},{8,24},{16,0},{24,8},{1,17},{9,25},{17,1},{25,9},{2,18},{10... | collective-permute-start | bytes 442376 | tf_op jit(solution)/shard_map/ppermute | solution.py:516
  46.8 1.7 %collective-permute-start.13 = (bf16[96,768]{1,0:T(8,128)(2,1)S(1)}, bf16[96,768]{1,0:T(8,128)(2,1)S(1)}, u32[]{:S(2)}, u32[]{:S(2)}) collective-permute-start(bf16[96,768]{1,0:T(8,128)(2,1)S(1)} %total.4), channel_id=1, source_target_pairs={{0,8},{8,16},{16,24},{24,0},{1,9},{9,17},{17,25},{25,1},{2,10},{10... | collective-permute-start | bytes 442376 | tf_op jit(solution)/shard_map/ppermute | solution.py:516
  48.6 1.9 %collective-permute-done.19.refs_2_ = bf16[96,768]{1,0:T(8,128)(2,1)S(1)} collective-permute-done((bf16[96,768]{1,0:T(8,128)(2,1)S(1)}, bf16[96,768]{1,0:T(8,128)(2,1)S(1)}, u32[]{:S(2)}, u32[]{:S(2)}) %collective-permute-start.19) | collective-permute-done | bytes 147488 | tf_op jit(solution)/shard_map/ppermute | solution.py:516
  50.5 2.8 %collective-permute-done.16.refs_1_ = bf16[96,768]{1,0:T(8,128)(2,1)S(1)} collective-permute-done((bf16[96,768]{1,0:T(8,128)(2,1)S(1)}, bf16[96,768]{1,0:T(8,128)(2,1)S(1)}, u32[]{:S(2)}, u32[]{:S(2)}) %collective-permute-start.16) | collective-permute-done | bytes 147488 | tf_op jit(solution)/shard_map/ppermute | solution.py:516
  53.4 1.3 %place.2.refs_1_ = bf16[96,3072]{1,0:T(8,128)(2,1)} custom-call(s32[3]{0:T(128)S(1)} %pad_add_fusion.1.meta_ref, bf16[96,768]{1,0:T(8,128)(2,1)S(1)} %total.5.refs_0_, bf16[96,768]{1,0:T(8,128)(2,1)S(1)} %collective-permute-done.16.refs_1_, bf16[96,768]{1,0:T(8,128)(2,1)S(1)} %collective-permute-done.19.refs_2_), custom_call_target="tpu_custom_call" | custom-call | flops 1000 | bytes 1200000 | tf_op jit(solution)/shard_map/place/pallas_call | solution.py:523
  (48 shorter events, 6.9 us)
Async XLA Ops:
  0.0 2.2 %copy-start = (bf16[192,3072]{1,0:T(8,128)(2,1)S(1)}, bf16[192,3072]{1,0:T(8,128)(2,1)}, u32[]{:S(2)}) copy-start(bf16[192,3072]{1,0:T(8,128)(2,1)} %param.10) | copy-start | bytes 3538948
  1.3 0.7 %copy-start.1 = (s32[12,3]{0,1:T(4,128)S(1)}, s32[12,3]{0,1:T(4,128)}, u32[]{:S(2)}) copy-start(s32[12,3]{0,1:T(4,128)} %param.9) | copy-start | bytes 436
  1.4 1.9 %collective-permute-start = (bf16[3,3,32,768]{3,2,1,0:T(8,128)(2,1)S(1)}, bf16[3,3,32,768]{3,2,1,0:T(8,128)(2,1)S(1)}, u32[]{:S(2)}, u32[]{:S(2)}) collective-permute-start(bf16[3,3,32,768]{3,2,1,0:T(8,128)(2,1)S(1)} %get-tuple-element.37), channel_id=1, source_target_pairs={{0,4},{4,0},{1,5},{5,1},{2,6},{6,2},{3,7},{7,3},{8,12},{12,8},{9,1... | collective-permute-start | bytes 1327112 | tf_op jit(solution)/shard_map/ppermute | solution.py:377
  4.3 10.3 %collective-permute-start.1 = (bf16[2,3,32,768]{3,2,1,0:T(8,128)(2,1)S(1)}, bf16[2,3,32,768]{3,2,1,0:T(8,128)(2,1)S(1)}, u32[]{:S(2)}, u32[]{:S(2)}) collective-permute-start(bf16[2,3,32,768]{3,2,1,0:T(8,128)(2,1)S(1)} %get-tuple-element.20), channel_id=1, source_target_pairs={{0,1},{1,0},{2,3},{3,2},{4,5},{5,4},{6,7},{7,6},{8,9},{9,8},{10,11... | collective-permute-start | bytes 884744 | tf_op jit(solution)/shard_map/ppermute | solution.py:396
  7.3 7.3 %collective-permute-start.2 = (bf16[2,3,32,768]{3,2,1,0:T(8,128)(2,1)S(1)}, bf16[2,3,32,768]{3,2,1,0:T(8,128)(2,1)S(1)}, u32[]{:S(2)}, u32[]{:S(2)}) collective-permute-start(bf16[2,3,32,768]{3,2,1,0:T(8,128)(2,1)S(1)} %get-tuple-element.21), channel_id=1, source_target_pairs={{0,4},{1,2},{2,1},{3,7},{4,0},{5,6},{6,5},{7,3},{8,12},{9,10},{10,... | collective-permute-start | bytes 884744 | tf_op jit(solution)/shard_map/ppermute | solution.py:396
  7.3 5.3 %collective-permute-start.3 = (bf16[64,768]{1,0:T(8,128)(2,1)S(1)}, bf16[64,768]{1,0:T(8,128)(2,1)S(1)}, u32[]{:S(2)}, u32[]{:S(2)}) collective-permute-start(bf16[64,768]{1,0:T(8,128)(2,1)S(1)} %pad_maximum_fusion.1), channel_id=1, source_target_pairs={{0,8},{8,0},{16,24},{24,16},{4,12},{12,4},{20,28},{28,20},{1,9},{9... | collective-permute-start | bytes 294920 | tf_op jit(solution)/shard_map/ppermute | solution.py:401
  8.8 3.7 %collective-permute-start.4 = (bf16[64,768]{1,0:T(8,128)(2,1)S(1)}, bf16[64,768]{1,0:T(8,128)(2,1)S(1)}, u32[]{:S(2)}, u32[]{:S(2)}) collective-permute-start(bf16[64,768]{1,0:T(8,128)(2,1)S(1)} %pad_maximum_fusion.2), channel_id=1, source_target_pairs={{0,4},{8,16},{16,8},{24,28},{4,0},{12,20},{20,12},{28,24},{1,5},{9... | collective-permute-start | bytes 294920 | tf_op jit(solution)/shard_map/ppermute | solution.py:401
  16.0 12.7 %collective-permute-start.8 = (bf16[192,768]{1,0:T(8,128)(2,1)S(1)}, bf16[192,768]{1,0:T(8,128)(2,1)S(1)}, u32[]{:S(2)}, u32[]{:S(2)}) collective-permute-start(bf16[192,768]{1,0:T(8,128)(2,1)S(1)} %get-tuple-element.26.refs_0_), channel_id=1, source_target_pairs={{0,1},{1,2},{2,3},{3,0},{4,5},{5,6},{6,7},{7,4},{8,9},{9,10},{10,1... | collective-permute-start | bytes 884744 | tf_op jit(solution)/shard_map/ppermute | solution.py:432
  18.9 5.8 %collective-permute-start.5 = (bf16[64,896]{1,0:T(8,128)(2,1)S(1)}, bf16[64,896]{1,0:T(8,128)(2,1)S(1)}, u32[]{:S(2)}, u32[]{:S(2)}) collective-permute-start(bf16[64,896]{1,0:T(8,128)(2,1)S(1)} %get-tuple-element.24), channel_id=1, source_target_pairs={{0,8},{8,0},{16,24},{24,16},{4,12},{12,4},{20,28},{28,20},{1,9},{9... | collective-permute-start | bytes 344072 | tf_op jit(solution)/shard_map/ppermute | solution.py:434
  20.7 3.9 %collective-permute-start.6 = (bf16[64,896]{1,0:T(8,128)(2,1)S(1)}, bf16[64,896]{1,0:T(8,128)(2,1)S(1)}, u32[]{:S(2)}, u32[]{:S(2)}) collective-permute-start(bf16[64,896]{1,0:T(8,128)(2,1)S(1)} %get-tuple-element.25), channel_id=1, source_target_pairs={{0,4},{8,16},{16,8},{24,28},{4,0},{12,20},{20,12},{28,24},{1,5},{9... | collective-permute-start | bytes 344072 | tf_op jit(solution)/shard_map/ppermute | solution.py:434
  20.7 12.9 %collective-permute-start.10 = (bf16[192,768]{1,0:T(8,128)(2,1)S(1)}, bf16[192,768]{1,0:T(8,128)(2,1)S(1)}, u32[]{:S(2)}, u32[]{:S(2)}) collective-permute-start(bf16[192,768]{1,0:T(8,128)(2,1)S(1)} %get-tuple-element.26.refs_0_), channel_id=1, source_target_pairs={{0,3},{1,0},{2,1},{3,2},{4,7},{5,4},{6,5},{7,6},{8,11},{9,8},{10,9... | collective-permute-start | bytes 884744 | tf_op jit(solution)/shard_map/ppermute | solution.py:461
  25.6 15.0 %collective-permute-start.11 = (bf16[192,768]{1,0:T(8,128)(2,1)S(1)}, bf16[192,768]{1,0:T(8,128)(2,1)S(1)}, u32[]{:S(2)}, u32[]{:S(2)}) collective-permute-start(bf16[192,768]{1,0:T(8,128)(2,1)S(1)} %bitcast.30), channel_id=1, source_target_pairs={{0,16},{8,24},{16,0},{24,8},{1,17},{9,25},{17,1},{25,9},{2,18},{10... | collective-permute-start | bytes 884744 | tf_op jit(solution)/shard_map/ppermute | solution.py:464
  28.6 12.0 %collective-permute-start.9 = (bf16[192,768]{1,0:T(8,128)(2,1)S(1)}, bf16[192,768]{1,0:T(8,128)(2,1)S(1)}, u32[]{:S(2)}, u32[]{:S(2)}) collective-permute-start(bf16[192,768]{1,0:T(8,128)(2,1)S(1)} %collective-permute-done.8.refs_1_), channel_id=1, source_target_pairs={{0,1},{1,2},{2,3},{3,0},{4,5},{5,6},{6,7},{7,4},{8,9},{9,10},{10,1... | collective-permute-start | bytes 884744 | tf_op jit(solution)/shard_map/ppermute | solution.py:463
  30.5 11.2 %collective-permute-start.17 = (bf16[192,768]{1,0:T(8,128)(2,1)S(1)}, bf16[192,768]{1,0:T(8,128)(2,1)S(1)}, u32[]{:S(2)}, u32[]{:S(2)}) collective-permute-start(bf16[192,768]{1,0:T(8,128)(2,1)S(1)} %bitcast.31), channel_id=1, source_target_pairs={{0,8},{8,16},{16,24},{24,0},{1,9},{9,17},{17,25},{25,1},{2,10},{10... | collective-permute-start | bytes 884744 | tf_op jit(solution)/shard_map/ppermute | solution.py:464
  30.8 12.6 %collective-permute-start.7 = (bf16[192,768]{1,0:T(8,128)(2,1)S(1)}, bf16[192,768]{1,0:T(8,128)(2,1)S(1)}, u32[]{:S(2)}, u32[]{:S(2)}) collective-permute-start(bf16[192,768]{1,0:T(8,128)(2,1)S(1)} %bitcast.32), channel_id=1, source_target_pairs={{0,24},{8,0},{16,8},{24,16},{1,25},{9,1},{17,9},{25,17},{2,26},{10... | collective-permute-start | bytes 884744 | tf_op jit(solution)/shard_map/ppermute | solution.py:464
  42.1 2.0 %collective-permute-start.18 = (f32[96,768]{1,0:T(8,128)S(1)}, f32[96,768]{1,0:T(8,128)S(1)}, u32[]{:S(2)}, u32[]{:S(2)}) collective-permute-start(f32[96,768]{1,0:T(8,128)S(1)} %get-tuple-element.34), channel_id=1, source_target_pairs={{0,4},{4,0},{1,5},{5,1},{2,6},{6,2},{3,7},{7,3},{8,12},{12,8},{9,1... | collective-permute-start | bytes 884744 | tf_op jit(solution)/shard_map/ppermute | solution.py:514
  42.6 2.8 %collective-permute-start.15 = (f32[96,768]{1,0:T(8,128)S(1)}, f32[96,768]{1,0:T(8,128)S(1)}, u32[]{:S(2)}, u32[]{:S(2)}) collective-permute-start(f32[96,768]{1,0:T(8,128)S(1)} %get-tuple-element.32), channel_id=1, source_target_pairs={{0,4},{4,0},{1,5},{5,1},{2,6},{6,2},{3,7},{7,3},{8,12},{12,8},{9,1... | collective-permute-start | bytes 884744 | tf_op jit(solution)/shard_map/ppermute | solution.py:514
  43.2 5.4 %collective-permute-start.14 = (f32[96,768]{1,0:T(8,128)S(1)}, f32[96,768]{1,0:T(8,128)S(1)}, u32[]{:S(2)}, u32[]{:S(2)}) collective-permute-start(f32[96,768]{1,0:T(8,128)S(1)} %get-tuple-element.30), channel_id=1, source_target_pairs={{0,4},{4,0},{1,5},{5,1},{2,6},{6,2},{3,7},{7,3},{8,12},{12,8},{9,1... | collective-permute-start | bytes 884744 | tf_op jit(solution)/shard_map/ppermute | solution.py:514
  43.8 2.9 %collective-permute-start.12 = (f32[96,768]{1,0:T(8,128)S(1)}, f32[96,768]{1,0:T(8,128)S(1)}, u32[]{:S(2)}, u32[]{:S(2)}) collective-permute-start(f32[96,768]{1,0:T(8,128)S(1)} %get-tuple-element.28), channel_id=1, source_target_pairs={{0,4},{4,0},{1,5},{5,1},{2,6},{6,2},{3,7},{7,3},{8,12},{12,8},{9,1... | collective-permute-start | bytes 884744 | tf_op jit(solution)/shard_map/ppermute | solution.py:514
  44.2 6.4 %collective-permute-start.19 = (bf16[96,768]{1,0:T(8,128)(2,1)S(1)}, bf16[96,768]{1,0:T(8,128)(2,1)S(1)}, u32[]{:S(2)}, u32[]{:S(2)}) collective-permute-start(bf16[96,768]{1,0:T(8,128)(2,1)S(1)} %total.7), channel_id=1, source_target_pairs={{0,24},{8,0},{16,8},{24,16},{1,25},{9,1},{17,9},{25,17},{2,26},{10... | collective-permute-start | bytes 442376 | tf_op jit(solution)/shard_map/ppermute | solution.py:516
  45.4 8.0 %collective-permute-start.16 = (bf16[96,768]{1,0:T(8,128)(2,1)S(1)}, bf16[96,768]{1,0:T(8,128)(2,1)S(1)}, u32[]{:S(2)}, u32[]{:S(2)}) collective-permute-start(bf16[96,768]{1,0:T(8,128)(2,1)S(1)} %total.6), channel_id=1, source_target_pairs={{0,16},{8,24},{16,0},{24,8},{1,17},{9,25},{17,1},{25,9},{2,18},{10... | collective-permute-start | bytes 442376 | tf_op jit(solution)/shard_map/ppermute | solution.py:516
  46.8 7.9 %collective-permute-start.13 = (bf16[96,768]{1,0:T(8,128)(2,1)S(1)}, bf16[96,768]{1,0:T(8,128)(2,1)S(1)}, u32[]{:S(2)}, u32[]{:S(2)}) collective-permute-start(bf16[96,768]{1,0:T(8,128)(2,1)S(1)} %total.4), channel_id=1, source_target_pairs={{0,8},{8,16},{16,24},{24,0},{1,9},{9,17},{17,25},{25,1},{2,10},{10... | collective-permute-start | bytes 442376 | tf_op jit(solution)/shard_map/ppermute | solution.py:516

commit v8 on v7

--- a/solution.py
+++ b/solution.py
@@ -476,7 +476,7 @@
             compiler_params=PARAMS,
             cost_estimate=cost(1000, 2_400_000),
             name="join",
-        )(spots, *shards, received[1])
+        )(spots, *shards, (received + [attended] * 2)[1])
 
     near = joined([held[s] for s in range(n_cols)], at_col)
     if n_rows > PAIR:

time: 55.6 us -> 55.6 us (level)
  no operation moved by 1% of the time
where the time goes in v8:
time: 55.6 us; the launch traced here: 55.4 us
  starting transfers between devices  24.7 us (44%)
  waiting for transfers between devices  18.7 us (34%)
  Pallas kernels  9.19 us (17%)
  other arithmetic  1.5 us (3%)
  local copies, waits for them, and re-layouts  1.16 us (2%)
    ppermute x3, waiting for transfers between devices, shards(): lax.ppermute(attended, 'ta', cycle(n_time, s))  7.19 us
    ppermute x3, starting transfers between devices, shards(): lax.ppermute(attended, 'ta', cycle(n_time, s))  5.9 us
    ppermute x3, waiting for transfers between devices, shards(): lax.ppermute(products[n_time - s], 'ta', cycle(n_time, s))  4.82 us
    ppermute x3, starting transfers between devices, shards(): lax.ppermute(products[n_time - s], 'ta', cycle(n_time, s))  4.29 us
    ppermute x2, starting transfers between devices, shards(): lax.ppermute(x, ('ha', 'wa'), swaps(n_cols, phase, n_rows, True))  3 us
    ppermute x1, starting transfers between devices, shards(): held[1] = lax.ppermute(sent, 'wa', cycle(n_cols, 1))  2.91 us
    ppermute x2, waiting for transfers between devices, shards(): lax.ppermute(end, ('ta', 'ha'), swaps(n_time, phase, n_rows, False))  2.66 us
    ppermute x2, waiting for transfers between devices, shards(): lax.ppermute(x, ('ha', 'wa'), swaps(n_cols, phase, n_rows, True))  2.04 us
  transfers between devices with their start and end apart: 20, of which 10 were waited for; matrix products, arithmetic and copies ran while one was open for 2% of the time, Pallas kernels for 11%

profile of v8, /device:TPU:0, one launch (start us, length us, event | category | flops | bytes accessed | tf_op | source)
XLA Modules:
  0.0 55.4 jit_solution(8193080858879073805)
XLA Ops:
  0.0 1.3 %pad_maximum_fusion = bf16[3,3,32,1536]{3,2,1,0:T(8,128)(2,1)S(1)} fusion(bf16[1,3,32,1536]{3,2,1,0:T(8,128)(2,1)} %bitcast.34, bf16[1,3,32,1536]{3,2,1,0:T(8,128)(2,1)} %bitcast.35, bf16[1,3,32,1536]{3,2,1,0:T(8,128)(2,1)} %bitcast.36), kind=kLoop, calls=%fused_computation | loop fusion | flops 884736 | bytes 1769472 | tf_op jit(solution)/shard_map/stack | solution.py:373
  2.3 1.1 %collective-permute-done.refs_1_ = bf16[3,3,32,768]{3,2,1,0:T(8,128)(2,1)S(1)} collective-permute-done((bf16[3,3,32,768]{3,2,1,0:T(8,128)(2,1)S(1)}, bf16[3,3,32,768]{3,2,1,0:T(8,128)(2,1)S(1)}, u32[]{:S(2)}, u32[]{:S(2)}) %collective-permute-start) | collective-permute-done | bytes 442400 | tf_op jit(solution)/shard_map/ppermute | solution.py:377
  3.4 0.8 %edge.1 = (bf16[2,3,32,768]{3,2,1,0:T(8,128)(2,1)S(1)}, bf16[2,3,32,768]{3,2,1,0:T(8,128)(2,1)S(1)}) custom-call(s32[7]{0:T(128)S(1)} %stack.73.meta_ref, bf16[3,3,32,768]{3,2,1,0:T(8,128)(2,1)S(1)} %get-tuple-element.38.refs_0_, bf16[3,3,32,768]{3,2,1,0:T(8,128)(2,1)S(1)} %collective-permute-done.refs_1_), custom_call_target="tpu_custom_call" | custom-call | flops 1000 | bytes 2000000 | tf_op jit(solution)/shard_map/edge/pallas_call | solution.py:387
  4.3 3.0 %collective-permute-start.1 = (bf16[2,3,32,768]{3,2,1,0:T(8,128)(2,1)S(1)}, bf16[2,3,32,768]{3,2,1,0:T(8,128)(2,1)S(1)}, u32[]{:S(2)}, u32[]{:S(2)}) collective-permute-start(bf16[2,3,32,768]{3,2,1,0:T(8,128)(2,1)S(1)} %get-tuple-element.20), channel_id=1, source_target_pairs={{0,1},{1,0},{2,3},{3,2},{4,5},{5,4},{6,7},{7,6},{8,9},{9,8},{10,11... | collective-permute-start | bytes 884744 | tf_op jit(solution)/shard_map/ppermute | solution.py:396
  7.3 1.6 %collective-permute-start.3 = (bf16[64,768]{1,0:T(8,128)(2,1)S(1)}, bf16[64,768]{1,0:T(8,128)(2,1)S(1)}, u32[]{:S(2)}, u32[]{:S(2)}) collective-permute-start(bf16[64,768]{1,0:T(8,128)(2,1)S(1)} %pad_maximum_fusion.1), channel_id=1, source_target_pairs={{0,8},{8,0},{16,24},{24,16},{4,12},{12,4},{20,28},{28,20},{1,9},{9... | collective-permute-start | bytes 294920 | tf_op jit(solution)/shard_map/ppermute | solution.py:401
  9.1 0.8 %dynamic-slice_bitcast_fusion.4.code_ref = s32[64,128]{1,0:T(8,128)S(1)} fusion(s32[16,64,128]{2,1,0:T(8,128)} %constant.114.clone, s32[]{:T(128)S(6)} %select_n.113), kind=kLoop, calls=%fused_computation.7 | loop fusion | bytes 65540 | tf_op jit(solution)/shard_map/jit(dynamic_index_in_dim)/squeeze | solution.py:414
  9.9 2.7 %collective-permute-done.3.refs_4_ = bf16[64,768]{1,0:T(8,128)(2,1)S(1)} collective-permute-done((bf16[64,768]{1,0:T(8,128)(2,1)S(1)}, bf16[64,768]{1,0:T(8,128)(2,1)S(1)}, u32[]{:S(2)}, u32[]{:S(2)}) %collective-permute-start.3) | collective-permute-done | bytes 98336 | tf_op jit(solution)/shard_map/ppermute | solution.py:401
  12.5 2.0 %collective-permute-done.1.refs_2_ = bf16[2,3,32,768]{3,2,1,0:T(8,128)(2,1)S(1)} collective-permute-done((bf16[2,3,32,768]{3,2,1,0:T(8,128)(2,1)S(1)}, bf16[2,3,32,768]{3,2,1,0:T(8,128)(2,1)S(1)}, u32[]{:S(2)}, u32[]{:S(2)}) %collective-permute-start.1) | collective-permute-done | bytes 294944 | tf_op jit(solution)/shard_map/ppermute | solution.py:396
  14.6 1.4 %guest.1 = (bf16[64,896]{1,0:T(8,128)(2,1)S(1)}, bf16[64,896]{1,0:T(8,128)(2,1)S(1)}, bf16[192,768]{1,0:T(8,128)(2,1)S(1)}) custom-call(s32[7]{0:T(128)S(1)} %stack.73.meta_ref, s32[12,3]{1,0:T(8,128)S(1)} %copy.11.radius_ref, s32[64,128]{1,0:T(8,128)S(1)} %dynamic-slice_bitcast_fusion.4.code_ref, ...), custom_call_target="tpu_custom_call", output_to_operand_aliasing={{2}: (9, {})} | custom-call | flops 50331648 | bytes 4000000 | tf_op jit(solution)/shard_map/guest/pallas_call | solution.py:420
  16.0 2.9 %collective-permute-start.8 = (bf16[192,768]{1,0:T(8,128)(2,1)S(1)}, bf16[192,768]{1,0:T(8,128)(2,1)S(1)}, u32[]{:S(2)}, u32[]{:S(2)}) collective-permute-start(bf16[192,768]{1,0:T(8,128)(2,1)S(1)} %get-tuple-element.26.refs_0_), channel_id=1, source_target_pairs={{0,1},{1,2},{2,3},{3,0},{4,5},{5,6},{6,7},{7,4},{8,9},{9,10},{10,1... | collective-permute-start | bytes 884744 | tf_op jit(solution)/shard_map/ppermute | solution.py:432
  18.9 1.9 %collective-permute-start.5 = (bf16[64,896]{1,0:T(8,128)(2,1)S(1)}, bf16[64,896]{1,0:T(8,128)(2,1)S(1)}, u32[]{:S(2)}, u32[]{:S(2)}) collective-permute-start(bf16[64,896]{1,0:T(8,128)(2,1)S(1)} %get-tuple-element.24), channel_id=1, source_target_pairs={{0,8},{8,0},{16,24},{24,16},{4,12},{12,4},{20,28},{28,20},{1,9},{9... | collective-permute-start | bytes 344072 | tf_op jit(solution)/shard_map/ppermute | solution.py:434
  20.7 1.6 %collective-permute-start.10 = (bf16[192,768]{1,0:T(8,128)(2,1)S(1)}, bf16[192,768]{1,0:T(8,128)(2,1)S(1)}, u32[]{:S(2)}, u32[]{:S(2)}) collective-permute-start(bf16[192,768]{1,0:T(8,128)(2,1)S(1)} %get-tuple-element.26.refs_0_), channel_id=1, source_target_pairs={{0,3},{1,0},{2,1},{3,2},{4,7},{5,4},{6,5},{7,6},{8,11},{9,8},{10,9... | collective-permute-start | bytes 884744 | tf_op jit(solution)/shard_map/ppermute | solution.py:461
  22.4 1.6 %host.1 = (f32[3,64,768]{2,1,0:T(8,128)S(1)}, f32[3,64,128]{2,1,0:T(8,128)S(1)}) custom-call(s32[7]{0:T(128)S(1)} %stack.73.meta_ref, s32[12,3]{1,0:T(8,128)S(1)} %copy.11.radius_ref, s32[64,128]{1,0:T(8,128)S(1)} %dynamic-slice_bitcast_fusion.4.code_ref, bf16[3,3,32,768]{3,2,1,0:T(8,128)(2,1)S(1)} %get-tuple-element.38.refs_0_, ...), custom_call_target="tpu_custom_call" | custom-call | flops 176160768 | bytes 6000000 | tf_op jit(solution)/shard_map/host/pallas_call | solution.py:437
  24.7 1.0 %merge.1 = bf16[2,3,32,768]{3,2,1,0:T(8,128)(2,1)S(1)} custom-call(s32[7]{0:T(128)S(1)} %stack.73.meta_ref, s32[12,3]{1,0:T(8,128)S(1)} %copy.11.radius_ref, f32[3,64,768]{2,1,0:T(8,128)S(1)} %get-tuple-element.22.mixed_ref, f32[3,64,128]{2,1,0:T(8,128)S(1)} %get-tuple-element.23.stats_ref, bf16[64,896]{1,0:T(8,128)(2,1)S(1)} %collective-permute-done.5.ref_0, ...), custom_call_target="tpu_custom_call" | custom-call | flops 1000 | bytes 3000000 | tf_op jit(solution)/shard_map/merge/pallas_call | solution.py:449
  25.6 3.0 %collective-permute-start.11 = (bf16[192,768]{1,0:T(8,128)(2,1)S(1)}, bf16[192,768]{1,0:T(8,128)(2,1)S(1)}, u32[]{:S(2)}, u32[]{:S(2)}) collective-permute-start(bf16[192,768]{1,0:T(8,128)(2,1)S(1)} %bitcast.30), channel_id=1, source_target_pairs={{0,16},{8,24},{16,0},{24,8},{1,17},{9,25},{17,1},{25,9},{2,18},{10... | collective-permute-start | bytes 884744 | tf_op jit(solution)/shard_map/ppermute | solution.py:464
  28.6 1.7 %collective-permute-start.9 = (bf16[192,768]{1,0:T(8,128)(2,1)S(1)}, bf16[192,768]{1,0:T(8,128)(2,1)S(1)}, u32[]{:S(2)}, u32[]{:S(2)}) collective-permute-start(bf16[192,768]{1,0:T(8,128)(2,1)S(1)} %collective-permute-done.8.refs_1_), channel_id=1, source_target_pairs={{0,1},{1,2},{2,3},{3,0},{4,5},{5,6},{6,7},{7,4},{8,9},{9,10},{10,1... | collective-permute-start | bytes 884744 | tf_op jit(solution)/shard_map/ppermute | solution.py:463
  30.8 2.6 %collective-permute-start.7 = (bf16[192,768]{1,0:T(8,128)(2,1)S(1)}, bf16[192,768]{1,0:T(8,128)(2,1)S(1)}, u32[]{:S(2)}, u32[]{:S(2)}) collective-permute-start(bf16[192,768]{1,0:T(8,128)(2,1)S(1)} %bitcast.32), channel_id=1, source_target_pairs={{0,24},{8,0},{16,8},{24,16},{1,25},{9,1},{17,9},{25,17},{2,26},{10... | collective-permute-start | bytes 884744 | tf_op jit(solution)/shard_map/ppermute | solution.py:464
  33.7 7.0 %collective-permute-done.11.refs_4_.rows = bf16[192,768]{1,0:T(8,128)(2,1)S(1)} collective-permute-done((bf16[192,768]{1,0:T(8,128)(2,1)S(1)}, bf16[192,768]{1,0:T(8,128)(2,1)S(1)}, u32[]{:S(2)}, u32[]{:S(2)}) %collective-permute-start.11) | collective-permute-done | bytes 294944 | tf_op jit(solution)/shard_map/ppermute | solution.py:464
  44.2 1.2 %collective-permute-start.19 = (bf16[96,768]{1,0:T(8,128)(2,1)S(1)}, bf16[96,768]{1,0:T(8,128)(2,1)S(1)}, u32[]{:S(2)}, u32[]{:S(2)}) collective-permute-start(bf16[96,768]{1,0:T(8,128)(2,1)S(1)} %total.7), channel_id=1, source_target_pairs={{0,24},{8,0},{16,8},{24,16},{1,25},{9,1},{17,9},{25,17},{2,26},{10... | collective-permute-start | bytes 442376 | tf_op jit(solution)/shard_map/ppermute | solution.py:516
  45.4 1.4 %collective-permute-start.16 = (bf16[96,768]{1,0:T(8,128)(2,1)S(1)}, bf16[96,768]{1,0:T(8,128)(2,1)S(1)}, u32[]{:S(2)}, u32[]{:S(2)}) collective-permute-start(bf16[96,768]{1,0:T(8,128)(2,1)S(1)} %total.6), channel_id=1, source_target_pairs={{0,16},{8,24},{16,0},{24,8},{1,17},{9,25},{17,1},{25,9},{2,18},{10... | collective-permute-start | bytes 442376 | tf_op jit(solution)/shard_map/ppermute | solution.py:516
  46.8 1.7 %collective-permute-start.13 = (bf16[96,768]{1,0:T(8,128)(2,1)S(1)}, bf16[96,768]{1,0:T(8,128)(2,1)S(1)}, u32[]{:S(2)}, u32[]{:S(2)}) collective-permute-start(bf16[96,768]{1,0:T(8,128)(2,1)S(1)} %total.4), channel_id=1, source_target_pairs={{0,8},{8,16},{16,24},{24,0},{1,9},{9,17},{17,25},{25,1},{2,10},{10... | collective-permute-start | bytes 442376 | tf_op jit(solution)/shard_map/ppermute | solution.py:516
  48.6 1.9 %collective-permute-done.19.refs_2_ = bf16[96,768]{1,0:T(8,128)(2,1)S(1)} collective-permute-done((bf16[96,768]{1,0:T(8,128)(2,1)S(1)}, bf16[96,768]{1,0:T(8,128)(2,1)S(1)}, u32[]{:S(2)}, u32[]{:S(2)}) %collective-permute-start.19) | collective-permute-done | bytes 147488 | tf_op jit(solution)/shard_map/ppermute | solution.py:516
  50.5 2.8 %collective-permute-done.16.refs_1_ = bf16[96,768]{1,0:T(8,128)(2,1)S(1)} collective-permute-done((bf16[96,768]{1,0:T(8,128)(2,1)S(1)}, bf16[96,768]{1,0:T(8,128)(2,1)S(1)}, u32[]{:S(2)}, u32[]{:S(2)}) %collective-permute-start.16) | collective-permute-done | bytes 147488 | tf_op jit(solution)/shard_map/ppermute | solution.py:516
  53.4 1.3 %place.2.refs_1_ = bf16[96,3072]{1,0:T(8,128)(2,1)} custom-call(s32[3]{0:T(128)S(1)} %pad_add_fusion.1.meta_ref, bf16[96,768]{1,0:T(8,128)(2,1)S(1)} %total.5.refs_0_, bf16[96,768]{1,0:T(8,128)(2,1)S(1)} %collective-permute-done.16.refs_1_, bf16[96,768]{1,0:T(8,128)(2,1)S(1)} %collective-permute-done.19.refs_2_), custom_call_target="tpu_custom_call" | custom-call | flops 1000 | bytes 1200000 | tf_op jit(solution)/shard_map/place/pallas_call | solution.py:523
  (48 shorter events, 6.9 us)
Async XLA Ops:
  0.0 2.2 %copy-start = (bf16[192,3072]{1,0:T(8,128)(2,1)S(1)}, bf16[192,3072]{1,0:T(8,128)(2,1)}, u32[]{:S(2)}) copy-start(bf16[192,3072]{1,0:T(8,128)(2,1)} %param.10) | copy-start | bytes 3538948
  1.3 0.7 %copy-start.1 = (s32[12,3]{0,1:T(4,128)S(1)}, s32[12,3]{0,1:T(4,128)}, u32[]{:S(2)}) copy-start(s32[12,3]{0,1:T(4,128)} %param.9) | copy-start | bytes 436
  1.4 1.9 %collective-permute-start = (bf16[3,3,32,768]{3,2,1,0:T(8,128)(2,1)S(1)}, bf16[3,3,32,768]{3,2,1,0:T(8,128)(2,1)S(1)}, u32[]{:S(2)}, u32[]{:S(2)}) collective-permute-start(bf16[3,3,32,768]{3,2,1,0:T(8,128)(2,1)S(1)} %get-tuple-element.37), channel_id=1, source_target_pairs={{0,4},{4,0},{1,5},{5,1},{2,6},{6,2},{3,7},{7,3},{8,12},{12,8},{9,1... | collective-permute-start | bytes 1327112 | tf_op jit(solution)/shard_map/ppermute | solution.py:377
  4.3 10.3 %collective-permute-start.1 = (bf16[2,3,32,768]{3,2,1,0:T(8,128)(2,1)S(1)}, bf16[2,3,32,768]{3,2,1,0:T(8,128)(2,1)S(1)}, u32[]{:S(2)}, u32[]{:S(2)}) collective-permute-start(bf16[2,3,32,768]{3,2,1,0:T(8,128)(2,1)S(1)} %get-tuple-element.20), channel_id=1, source_target_pairs={{0,1},{1,0},{2,3},{3,2},{4,5},{5,4},{6,7},{7,6},{8,9},{9,8},{10,11... | collective-permute-start | bytes 884744 | tf_op jit(solution)/shard_map/ppermute | solution.py:396
  7.3 7.3 %collective-permute-start.2 = (bf16[2,3,32,768]{3,2,1,0:T(8,128)(2,1)S(1)}, bf16[2,3,32,768]{3,2,1,0:T(8,128)(2,1)S(1)}, u32[]{:S(2)}, u32[]{:S(2)}) collective-permute-start(bf16[2,3,32,768]{3,2,1,0:T(8,128)(2,1)S(1)} %get-tuple-element.21), channel_id=1, source_target_pairs={{0,4},{1,2},{2,1},{3,7},{4,0},{5,6},{6,5},{7,3},{8,12},{9,10},{10,... | collective-permute-start | bytes 884744 | tf_op jit(solution)/shard_map/ppermute | solution.py:396
  7.3 5.3 %collective-permute-start.3 = (bf16[64,768]{1,0:T(8,128)(2,1)S(1)}, bf16[64,768]{1,0:T(8,128)(2,1)S(1)}, u32[]{:S(2)}, u32[]{:S(2)}) collective-permute-start(bf16[64,768]{1,0:T(8,128)(2,1)S(1)} %pad_maximum_fusion.1), channel_id=1, source_target_pairs={{0,8},{8,0},{16,24},{24,16},{4,12},{12,4},{20,28},{28,20},{1,9},{9... | collective-permute-start | bytes 294920 | tf_op jit(solution)/shard_map/ppermute | solution.py:401
  8.8 3.7 %collective-permute-start.4 = (bf16[64,768]{1,0:T(8,128)(2,1)S(1)}, bf16[64,768]{1,0:T(8,128)(2,1)S(1)}, u32[]{:S(2)}, u32[]{:S(2)}) collective-permute-start(bf16[64,768]{1,0:T(8,128)(2,1)S(1)} %pad_maximum_fusion.2), channel_id=1, source_target_pairs={{0,4},{8,16},{16,8},{24,28},{4,0},{12,20},{20,12},{28,24},{1,5},{9... | collective-permute-start | bytes 294920 | tf_op jit(solution)/shard_map/ppermute | solution.py:401
  16.0 12.7 %collective-permute-start.8 = (bf16[192,768]{1,0:T(8,128)(2,1)S(1)}, bf16[192,768]{1,0:T(8,128)(2,1)S(1)}, u32[]{:S(2)}, u32[]{:S(2)}) collective-permute-start(bf16[192,768]{1,0:T(8,128)(2,1)S(1)} %get-tuple-element.26.refs_0_), channel_id=1, source_target_pairs={{0,1},{1,2},{2,3},{3,0},{4,5},{5,6},{6,7},{7,4},{8,9},{9,10},{10,1... | collective-permute-start | bytes 884744 | tf_op jit(solution)/shard_map/ppermute | solution.py:432
  18.9 5.8 %collective-permute-start.5 = (bf16[64,896]{1,0:T(8,128)(2,1)S(1)}, bf16[64,896]{1,0:T(8,128)(2,1)S(1)}, u32[]{:S(2)}, u32[]{:S(2)}) collective-permute-start(bf16[64,896]{1,0:T(8,128)(2,1)S(1)} %get-tuple-element.24), channel_id=1, source_target_pairs={{0,8},{8,0},{16,24},{24,16},{4,12},{12,4},{20,28},{28,20},{1,9},{9... | collective-permute-start | bytes 344072 | tf_op jit(solution)/shard_map/ppermute | solution.py:434
  20.7 3.9 %collective-permute-start.6 = (bf16[64,896]{1,0:T(8,128)(2,1)S(1)}, bf16[64,896]{1,0:T(8,128)(2,1)S(1)}, u32[]{:S(2)}, u32[]{:S(2)}) collective-permute-start(bf16[64,896]{1,0:T(8,128)(2,1)S(1)} %get-tuple-element.25), channel_id=1, source_target_pairs={{0,4},{8,16},{16,8},{24,28},{4,0},{12,20},{20,12},{28,24},{1,5},{9... | collective-permute-start | bytes 344072 | tf_op jit(solution)/shard_map/ppermute | solution.py:434
  20.7 12.9 %collective-permute-start.10 = (bf16[192,768]{1,0:T(8,128)(2,1)S(1)}, bf16[192,768]{1,0:T(8,128)(2,1)S(1)}, u32[]{:S(2)}, u32[]{:S(2)}) collective-permute-start(bf16[192,768]{1,0:T(8,128)(2,1)S(1)} %get-tuple-element.26.refs_0_), channel_id=1, source_target_pairs={{0,3},{1,0},{2,1},{3,2},{4,7},{5,4},{6,5},{7,6},{8,11},{9,8},{10,9... | collective-permute-start | bytes 884744 | tf_op jit(solution)/shard_map/ppermute | solution.py:461
  25.6 15.0 %collective-permute-start.11 = (bf16[192,768]{1,0:T(8,128)(2,1)S(1)}, bf16[192,768]{1,0:T(8,128)(2,1)S(1)}, u32[]{:S(2)}, u32[]{:S(2)}) collective-permute-start(bf16[192,768]{1,0:T(8,128)(2,1)S(1)} %bitcast.30), channel_id=1, source_target_pairs={{0,16},{8,24},{16,0},{24,8},{1,17},{9,25},{17,1},{25,9},{2,18},{10... | collective-permute-start | bytes 884744 | tf_op jit(solution)/shard_map/ppermute | solution.py:464
  28.6 12.0 %collective-permute-start.9 = (bf16[192,768]{1,0:T(8,128)(2,1)S(1)}, bf16[192,768]{1,0:T(8,128)(2,1)S(1)}, u32[]{:S(2)}, u32[]{:S(2)}) collective-permute-start(bf16[192,768]{1,0:T(8,128)(2,1)S(1)} %collective-permute-done.8.refs_1_), channel_id=1, source_target_pairs={{0,1},{1,2},{2,3},{3,0},{4,5},{5,6},{6,7},{7,4},{8,9},{9,10},{10,1... | collective-permute-start | bytes 884744 | tf_op jit(solution)/shard_map/ppermute | solution.py:463
  30.5 11.2 %collective-permute-start.17 = (bf16[192,768]{1,0:T(8,128)(2,1)S(1)}, bf16[192,768]{1,0:T(8,128)(2,1)S(1)}, u32[]{:S(2)}, u32[]{:S(2)}) collective-permute-start(bf16[192,768]{1,0:T(8,128)(2,1)S(1)} %bitcast.31), channel_id=1, source_target_pairs={{0,8},{8,16},{16,24},{24,0},{1,9},{9,17},{17,25},{25,1},{2,10},{10... | collective-permute-start | bytes 884744 | tf_op jit(solution)/shard_map/ppermute | solution.py:464
  30.8 12.6 %collective-permute-start.7 = (bf16[192,768]{1,0:T(8,128)(2,1)S(1)}, bf16[192,768]{1,0:T(8,128)(2,1)S(1)}, u32[]{:S(2)}, u32[]{:S(2)}) collective-permute-start(bf16[192,768]{1,0:T(8,128)(2,1)S(1)} %bitcast.32), channel_id=1, source_target_pairs={{0,24},{8,0},{16,8},{24,16},{1,25},{9,1},{17,9},{25,17},{2,26},{10... | collective-permute-start | bytes 884744 | tf_op jit(solution)/shard_map/ppermute | solution.py:464
  42.1 2.0 %collective-permute-start.18 = (f32[96,768]{1,0:T(8,128)S(1)}, f32[96,768]{1,0:T(8,128)S(1)}, u32[]{:S(2)}, u32[]{:S(2)}) collective-permute-start(f32[96,768]{1,0:T(8,128)S(1)} %get-tuple-element.34), channel_id=1, source_target_pairs={{0,4},{4,0},{1,5},{5,1},{2,6},{6,2},{3,7},{7,3},{8,12},{12,8},{9,1... | collective-permute-start | bytes 884744 | tf_op jit(solution)/shard_map/ppermute | solution.py:514
  42.6 2.8 %collective-permute-start.15 = (f32[96,768]{1,0:T(8,128)S(1)}, f32[96,768]{1,0:T(8,128)S(1)}, u32[]{:S(2)}, u32[]{:S(2)}) collective-permute-start(f32[96,768]{1,0:T(8,128)S(1)} %get-tuple-element.32), channel_id=1, source_target_pairs={{0,4},{4,0},{1,5},{5,1},{2,6},{6,2},{3,7},{7,3},{8,12},{12,8},{9,1... | collective-permute-start | bytes 884744 | tf_op jit(solution)/shard_map/ppermute | solution.py:514
  43.2 5.4 %collective-permute-start.14 = (f32[96,768]{1,0:T(8,128)S(1)}, f32[96,768]{1,0:T(8,128)S(1)}, u32[]{:S(2)}, u32[]{:S(2)}) collective-permute-start(f32[96,768]{1,0:T(8,128)S(1)} %get-tuple-element.30), channel_id=1, source_target_pairs={{0,4},{4,0},{1,5},{5,1},{2,6},{6,2},{3,7},{7,3},{8,12},{12,8},{9,1... | collective-permute-start | bytes 884744 | tf_op jit(solution)/shard_map/ppermute | solution.py:514
  43.8 2.9 %collective-permute-start.12 = (f32[96,768]{1,0:T(8,128)S(1)}, f32[96,768]{1,0:T(8,128)S(1)}, u32[]{:S(2)}, u32[]{:S(2)}) collective-permute-start(f32[96,768]{1,0:T(8,128)S(1)} %get-tuple-element.28), channel_id=1, source_target_pairs={{0,4},{4,0},{1,5},{5,1},{2,6},{6,2},{3,7},{7,3},{8,12},{12,8},{9,1... | collective-permute-start | bytes 884744 | tf_op jit(solution)/shard_map/ppermute | solution.py:514
  44.2 6.4 %collective-permute-start.19 = (bf16[96,768]{1,0:T(8,128)(2,1)S(1)}, bf16[96,768]{1,0:T(8,128)(2,1)S(1)}, u32[]{:S(2)}, u32[]{:S(2)}) collective-permute-start(bf16[96,768]{1,0:T(8,128)(2,1)S(1)} %total.7), channel_id=1, source_target_pairs={{0,24},{8,0},{16,8},{24,16},{1,25},{9,1},{17,9},{25,17},{2,26},{10... | collective-permute-start | bytes 442376 | tf_op jit(solution)/shard_map/ppermute | solution.py:516
  45.4 8.0 %collective-permute-start.16 = (bf16[96,768]{1,0:T(8,128)(2,1)S(1)}, bf16[96,768]{1,0:T(8,128)(2,1)S(1)}, u32[]{:S(2)}, u32[]{:S(2)}) collective-permute-start(bf16[96,768]{1,0:T(8,128)(2,1)S(1)} %total.6), channel_id=1, source_target_pairs={{0,16},{8,24},{16,0},{24,8},{1,17},{9,25},{17,1},{25,9},{2,18},{10... | collective-permute-start | bytes 442376 | tf_op jit(solution)/shard_map/ppermute | solution.py:516
  46.8 7.9 %collective-permute-start.13 = (bf16[96,768]{1,0:T(8,128)(2,1)S(1)}, bf16[96,768]{1,0:T(8,128)(2,1)S(1)}, u32[]{:S(2)}, u32[]{:S(2)}) collective-permute-start(bf16[96,768]{1,0:T(8,128)(2,1)S(1)} %total.4), channel_id=1, source_target_pairs={{0,8},{8,16},{16,24},{24,0},{1,9},{9,17},{17,25},{25,1},{2,10},{10... | collective-permute-start | bytes 442376 | tf_op jit(solution)/shard_map/ppermute | solution.py:516

commit v9 on v8

--- a/solution.py
+++ b/solution.py
@@ -326,11 +326,11 @@
     both = jnp.dot(rows[...], near[...], preferred_element_type=jnp.float32)
     half = own_out.shape[0]
     own_out[...] = both[:half]
-    other_out[...] = both[half:]
+    other_out[...] = both[half:].astype(other_out.dtype)
 
 
 def total_kernel(part, partner, out):
-    out[...] = (part[...] + partner[...]).astype(out.dtype)
+    out[...] = (part[...] + partner[...].astype(jnp.float32)).astype(out.dtype)
 
 
 def place_kernel(count, meta_ref, *refs):
@@ -489,7 +489,7 @@
         part = jax.ShapeDtypeStruct((tokens, wide), jnp.float32)
         return pl.pallas_call(
             project_kernel,
-            out_shape=(part, part),
+            out_shape=(part, jax.ShapeDtypeStruct(part.shape, queries.dtype)),
             in_specs=[VMEM, VMEM],
             out_specs=(VMEM, VMEM),
             compiler_params=PARAMS,

time: 55.6 us -> 55.6 us (level)
  no operation moved by 1% of the time
where the time goes in v9:
time: 55.6 us; the launch traced here: 55.4 us
  starting transfers between devices  24.7 us (44%)
  waiting for transfers between devices  18.7 us (34%)
  Pallas kernels  9.16 us (16%)
  other arithmetic  1.5 us (3%)
  local copies, waits for them, and re-layouts  1.16 us (2%)
    ppermute x3, waiting for transfers between devices, shards(): lax.ppermute(attended, 'ta', cycle(n_time, s))  7.19 us
    ppermute x3, starting transfers between devices, shards(): lax.ppermute(attended, 'ta', cycle(n_time, s))  5.9 us
    ppermute x3, waiting for transfers between devices, shards(): lax.ppermute(products[n_time - s], 'ta', cycle(n_time, s))  4.84 us
    ppermute x3, starting transfers between devices, shards(): lax.ppermute(products[n_time - s], 'ta', cycle(n_time, s))  4.3 us
    ppermute x2, starting transfers between devices, shards(): lax.ppermute(x, ('ha', 'wa'), swaps(n_cols, phase, n_rows, True))  3 us
    ppermute x1, starting transfers between devices, shards(): held[1] = lax.ppermute(sent, 'wa', cycle(n_cols, 1))  2.91 us
    ppermute x2, waiting for transfers between devices, shards(): lax.ppermute(end, ('ta', 'ha'), swaps(n_time, phase, n_rows, False))  2.66 us
    ppermute x2, waiting for transfers between devices, shards(): lax.ppermute(x, ('ha', 'wa'), swaps(n_cols, phase, n_rows, True))  2.04 us
  transfers between devices with their start and end apart: 20, of which 10 were waited for; matrix products, arithmetic and copies ran while one was open for 2% of the time, Pallas kernels for 11%

profile of v9, /device:TPU:0, one launch (start us, length us, event | category | flops | bytes accessed | tf_op | source)
XLA Modules:
  0.0 55.4 jit_solution(10810822916654951711)
XLA Ops:
  0.0 1.3 %pad_maximum_fusion = bf16[3,3,32,1536]{3,2,1,0:T(8,128)(2,1)S(1)} fusion(bf16[1,3,32,1536]{3,2,1,0:T(8,128)(2,1)} %bitcast.34, bf16[1,3,32,1536]{3,2,1,0:T(8,128)(2,1)} %bitcast.35, bf16[1,3,32,1536]{3,2,1,0:T(8,128)(2,1)} %bitcast.36), kind=kLoop, calls=%fused_computation | loop fusion | flops 884736 | bytes 1769472 | tf_op jit(solution)/shard_map/stack | solution.py:373
  2.3 1.1 %collective-permute-done.refs_1_ = bf16[3,3,32,768]{3,2,1,0:T(8,128)(2,1)S(1)} collective-permute-done((bf16[3,3,32,768]{3,2,1,0:T(8,128)(2,1)S(1)}, bf16[3,3,32,768]{3,2,1,0:T(8,128)(2,1)S(1)}, u32[]{:S(2)}, u32[]{:S(2)}) %collective-permute-start) | collective-permute-done | bytes 442400 | tf_op jit(solution)/shard_map/ppermute | solution.py:377
  3.4 0.8 %edge.1 = (bf16[2,3,32,768]{3,2,1,0:T(8,128)(2,1)S(1)}, bf16[2,3,32,768]{3,2,1,0:T(8,128)(2,1)S(1)}) custom-call(s32[7]{0:T(128)S(1)} %stack.73.meta_ref, bf16[3,3,32,768]{3,2,1,0:T(8,128)(2,1)S(1)} %get-tuple-element.38.refs_0_, bf16[3,3,32,768]{3,2,1,0:T(8,128)(2,1)S(1)} %collective-permute-done.refs_1_), custom_call_target="tpu_custom_call" | custom-call | flops 1000 | bytes 2000000 | tf_op jit(solution)/shard_map/edge/pallas_call | solution.py:387
  4.3 3.0 %collective-permute-start.1 = (bf16[2,3,32,768]{3,2,1,0:T(8,128)(2,1)S(1)}, bf16[2,3,32,768]{3,2,1,0:T(8,128)(2,1)S(1)}, u32[]{:S(2)}, u32[]{:S(2)}) collective-permute-start(bf16[2,3,32,768]{3,2,1,0:T(8,128)(2,1)S(1)} %get-tuple-element.20), channel_id=1, source_target_pairs={{0,1},{1,0},{2,3},{3,2},{4,5},{5,4},{6,7},{7,6},{8,9},{9,8},{10,11... | collective-permute-start | bytes 884744 | tf_op jit(solution)/shard_map/ppermute | solution.py:396
  7.3 1.6 %collective-permute-start.3 = (bf16[64,768]{1,0:T(8,128)(2,1)S(1)}, bf16[64,768]{1,0:T(8,128)(2,1)S(1)}, u32[]{:S(2)}, u32[]{:S(2)}) collective-permute-start(bf16[64,768]{1,0:T(8,128)(2,1)S(1)} %pad_maximum_fusion.1), channel_id=1, source_target_pairs={{0,8},{8,0},{16,24},{24,16},{4,12},{12,4},{20,28},{28,20},{1,9},{9... | collective-permute-start | bytes 294920 | tf_op jit(solution)/shard_map/ppermute | solution.py:401
  9.1 0.8 %dynamic-slice_bitcast_fusion.4.code_ref = s32[64,128]{1,0:T(8,128)S(1)} fusion(s32[16,64,128]{2,1,0:T(8,128)} %constant.114.clone, s32[]{:T(128)S(6)} %select_n.113), kind=kLoop, calls=%fused_computation.7 | loop fusion | bytes 65540 | tf_op jit(solution)/shard_map/jit(dynamic_index_in_dim)/squeeze | solution.py:414
  9.9 2.7 %collective-permute-done.3.refs_4_ = bf16[64,768]{1,0:T(8,128)(2,1)S(1)} collective-permute-done((bf16[64,768]{1,0:T(8,128)(2,1)S(1)}, bf16[64,768]{1,0:T(8,128)(2,1)S(1)}, u32[]{:S(2)}, u32[]{:S(2)}) %collective-permute-start.3) | collective-permute-done | bytes 98336 | tf_op jit(solution)/shard_map/ppermute | solution.py:401
  12.5 2.0 %collective-permute-done.1.refs_2_ = bf16[2,3,32,768]{3,2,1,0:T(8,128)(2,1)S(1)} collective-permute-done((bf16[2,3,32,768]{3,2,1,0:T(8,128)(2,1)S(1)}, bf16[2,3,32,768]{3,2,1,0:T(8,128)(2,1)S(1)}, u32[]{:S(2)}, u32[]{:S(2)}) %collective-permute-start.1) | collective-permute-done | bytes 294944 | tf_op jit(solution)/shard_map/ppermute | solution.py:396
  14.6 1.4 %guest.1 = (bf16[64,896]{1,0:T(8,128)(2,1)S(1)}, bf16[64,896]{1,0:T(8,128)(2,1)S(1)}, bf16[192,768]{1,0:T(8,128)(2,1)S(1)}) custom-call(s32[7]{0:T(128)S(1)} %stack.73.meta_ref, s32[12,3]{1,0:T(8,128)S(1)} %copy.11.radius_ref, s32[64,128]{1,0:T(8,128)S(1)} %dynamic-slice_bitcast_fusion.4.code_ref, ...), custom_call_target="tpu_custom_call", output_to_operand_aliasing={{2}: (9, {})} | custom-call | flops 50331648 | bytes 4000000 | tf_op jit(solution)/shard_map/guest/pallas_call | solution.py:420
  16.0 2.9 %collective-permute-start.8 = (bf16[192,768]{1,0:T(8,128)(2,1)S(1)}, bf16[192,768]{1,0:T(8,128)(2,1)S(1)}, u32[]{:S(2)}, u32[]{:S(2)}) collective-permute-start(bf16[192,768]{1,0:T(8,128)(2,1)S(1)} %get-tuple-element.26.refs_0_), channel_id=1, source_target_pairs={{0,1},{1,2},{2,3},{3,0},{4,5},{5,6},{6,7},{7,4},{8,9},{9,10},{10,1... | collective-permute-start | bytes 884744 | tf_op jit(solution)/shard_map/ppermute | solution.py:432
  18.9 1.9 %collective-permute-start.5 = (bf16[64,896]{1,0:T(8,128)(2,1)S(1)}, bf16[64,896]{1,0:T(8,128)(2,1)S(1)}, u32[]{:S(2)}, u32[]{:S(2)}) collective-permute-start(bf16[64,896]{1,0:T(8,128)(2,1)S(1)} %get-tuple-element.24), channel_id=1, source_target_pairs={{0,8},{8,0},{16,24},{24,16},{4,12},{12,4},{20,28},{28,20},{1,9},{9... | collective-permute-start | bytes 344072 | tf_op jit(solution)/shard_map/ppermute | solution.py:434
  20.7 1.6 %collective-permute-start.10 = (bf16[192,768]{1,0:T(8,128)(2,1)S(1)}, bf16[192,768]{1,0:T(8,128)(2,1)S(1)}, u32[]{:S(2)}, u32[]{:S(2)}) collective-permute-start(bf16[192,768]{1,0:T(8,128)(2,1)S(1)} %get-tuple-element.26.refs_0_), channel_id=1, source_target_pairs={{0,3},{1,0},{2,1},{3,2},{4,7},{5,4},{6,5},{7,6},{8,11},{9,8},{10,9... | collective-permute-start | bytes 884744 | tf_op jit(solution)/shard_map/ppermute | solution.py:461
  22.4 1.6 %host.1 = (f32[3,64,768]{2,1,0:T(8,128)S(1)}, f32[3,64,128]{2,1,0:T(8,128)S(1)}) custom-call(s32[7]{0:T(128)S(1)} %stack.73.meta_ref, s32[12,3]{1,0:T(8,128)S(1)} %copy.11.radius_ref, s32[64,128]{1,0:T(8,128)S(1)} %dynamic-slice_bitcast_fusion.4.code_ref, bf16[3,3,32,768]{3,2,1,0:T(8,128)(2,1)S(1)} %get-tuple-element.38.refs_0_, ...), custom_call_target="tpu_custom_call" | custom-call | flops 176160768 | bytes 6000000 | tf_op jit(solution)/shard_map/host/pallas_call | solution.py:437
  24.7 1.0 %merge.1 = bf16[2,3,32,768]{3,2,1,0:T(8,128)(2,1)S(1)} custom-call(s32[7]{0:T(128)S(1)} %stack.73.meta_ref, s32[12,3]{1,0:T(8,128)S(1)} %copy.11.radius_ref, f32[3,64,768]{2,1,0:T(8,128)S(1)} %get-tuple-element.22.mixed_ref, f32[3,64,128]{2,1,0:T(8,128)S(1)} %get-tuple-element.23.stats_ref, bf16[64,896]{1,0:T(8,128)(2,1)S(1)} %collective-permute-done.5.ref_0, ...), custom_call_target="tpu_custom_call" | custom-call | flops 1000 | bytes 3000000 | tf_op jit(solution)/shard_map/merge/pallas_call | solution.py:449
  25.6 3.0 %collective-permute-start.11 = (bf16[192,768]{1,0:T(8,128)(2,1)S(1)}, bf16[192,768]{1,0:T(8,128)(2,1)S(1)}, u32[]{:S(2)}, u32[]{:S(2)}) collective-permute-start(bf16[192,768]{1,0:T(8,128)(2,1)S(1)} %bitcast.30), channel_id=1, source_target_pairs={{0,16},{8,24},{16,0},{24,8},{1,17},{9,25},{17,1},{25,9},{2,18},{10... | collective-permute-start | bytes 884744 | tf_op jit(solution)/shard_map/ppermute | solution.py:464
  28.6 1.7 %collective-permute-start.9 = (bf16[192,768]{1,0:T(8,128)(2,1)S(1)}, bf16[192,768]{1,0:T(8,128)(2,1)S(1)}, u32[]{:S(2)}, u32[]{:S(2)}) collective-permute-start(bf16[192,768]{1,0:T(8,128)(2,1)S(1)} %collective-permute-done.8.refs_1_), channel_id=1, source_target_pairs={{0,1},{1,2},{2,3},{3,0},{4,5},{5,6},{6,7},{7,4},{8,9},{9,10},{10,1... | collective-permute-start | bytes 884744 | tf_op jit(solution)/shard_map/ppermute | solution.py:463
  30.8 2.6 %collective-permute-start.7 = (bf16[192,768]{1,0:T(8,128)(2,1)S(1)}, bf16[192,768]{1,0:T(8,128)(2,1)S(1)}, u32[]{:S(2)}, u32[]{:S(2)}) collective-permute-start(bf16[192,768]{1,0:T(8,128)(2,1)S(1)} %bitcast.32), channel_id=1, source_target_pairs={{0,24},{8,0},{16,8},{24,16},{1,25},{9,1},{17,9},{25,17},{2,26},{10... | collective-permute-start | bytes 884744 | tf_op jit(solution)/shard_map/ppermute | solution.py:464
  33.7 7.0 %collective-permute-done.11.refs_4_.rows = bf16[192,768]{1,0:T(8,128)(2,1)S(1)} collective-permute-done((bf16[192,768]{1,0:T(8,128)(2,1)S(1)}, bf16[192,768]{1,0:T(8,128)(2,1)S(1)}, u32[]{:S(2)}, u32[]{:S(2)}) %collective-permute-start.11) | collective-permute-done | bytes 294944 | tf_op jit(solution)/shard_map/ppermute | solution.py:464
  44.2 1.2 %collective-permute-start.19 = (bf16[96,768]{1,0:T(8,128)(2,1)S(1)}, bf16[96,768]{1,0:T(8,128)(2,1)S(1)}, u32[]{:S(2)}, u32[]{:S(2)}) collective-permute-start(bf16[96,768]{1,0:T(8,128)(2,1)S(1)} %total.7), channel_id=1, source_target_pairs={{0,24},{8,0},{16,8},{24,16},{1,25},{9,1},{17,9},{25,17},{2,26},{10... | collective-permute-start | bytes 442376 | tf_op jit(solution)/shard_map/ppermute | solution.py:516
  45.4 1.4 %collective-permute-start.16 = (bf16[96,768]{1,0:T(8,128)(2,1)S(1)}, bf16[96,768]{1,0:T(8,128)(2,1)S(1)}, u32[]{:S(2)}, u32[]{:S(2)}) collective-permute-start(bf16[96,768]{1,0:T(8,128)(2,1)S(1)} %total.6), channel_id=1, source_target_pairs={{0,16},{8,24},{16,0},{24,8},{1,17},{9,25},{17,1},{25,9},{2,18},{10... | collective-permute-start | bytes 442376 | tf_op jit(solution)/shard_map/ppermute | solution.py:516
  46.8 1.7 %collective-permute-start.13 = (bf16[96,768]{1,0:T(8,128)(2,1)S(1)}, bf16[96,768]{1,0:T(8,128)(2,1)S(1)}, u32[]{:S(2)}, u32[]{:S(2)}) collective-permute-start(bf16[96,768]{1,0:T(8,128)(2,1)S(1)} %total.4), channel_id=1, source_target_pairs={{0,8},{8,16},{16,24},{24,0},{1,9},{9,17},{17,25},{25,1},{2,10},{10... | collective-permute-start | bytes 442376 | tf_op jit(solution)/shard_map/ppermute | solution.py:516
  48.6 2.2 %collective-permute-done.19.refs_2_ = bf16[96,768]{1,0:T(8,128)(2,1)S(1)} collective-permute-done((bf16[96,768]{1,0:T(8,128)(2,1)S(1)}, bf16[96,768]{1,0:T(8,128)(2,1)S(1)}, u32[]{:S(2)}, u32[]{:S(2)}) %collective-permute-start.19) | collective-permute-done | bytes 147488 | tf_op jit(solution)/shard_map/ppermute | solution.py:516
  50.7 2.4 %collective-permute-done.16.refs_1_ = bf16[96,768]{1,0:T(8,128)(2,1)S(1)} collective-permute-done((bf16[96,768]{1,0:T(8,128)(2,1)S(1)}, bf16[96,768]{1,0:T(8,128)(2,1)S(1)}, u32[]{:S(2)}, u32[]{:S(2)}) %collective-permute-start.16) | collective-permute-done | bytes 147488 | tf_op jit(solution)/shard_map/ppermute | solution.py:516
  53.2 1.3 %place.2.refs_1_ = bf16[96,3072]{1,0:T(8,128)(2,1)} custom-call(s32[3]{0:T(128)S(1)} %pad_add_fusion.1.meta_ref, bf16[96,768]{1,0:T(8,128)(2,1)S(1)} %total.5.refs_0_, bf16[96,768]{1,0:T(8,128)(2,1)S(1)} %collective-permute-done.16.refs_1_, bf16[96,768]{1,0:T(8,128)(2,1)S(1)} %collective-permute-done.19.refs_2_), custom_call_target="tpu_custom_call" | custom-call | flops 1000 | bytes 1200000 | tf_op jit(solution)/shard_map/place/pallas_call | solution.py:523
  (48 shorter events, 7.1 us)
Async XLA Ops:
  0.0 2.2 %copy-start = (bf16[192,3072]{1,0:T(8,128)(2,1)S(1)}, bf16[192,3072]{1,0:T(8,128)(2,1)}, u32[]{:S(2)}) copy-start(bf16[192,3072]{1,0:T(8,128)(2,1)} %param.10) | copy-start | bytes 3538948
  1.3 0.7 %copy-start.1 = (s32[12,3]{0,1:T(4,128)S(1)}, s32[12,3]{0,1:T(4,128)}, u32[]{:S(2)}) copy-start(s32[12,3]{0,1:T(4,128)} %param.9) | copy-start | bytes 436
  1.4 1.9 %collective-permute-start = (bf16[3,3,32,768]{3,2,1,0:T(8,128)(2,1)S(1)}, bf16[3,3,32,768]{3,2,1,0:T(8,128)(2,1)S(1)}, u32[]{:S(2)}, u32[]{:S(2)}) collective-permute-start(bf16[3,3,32,768]{3,2,1,0:T(8,128)(2,1)S(1)} %get-tuple-element.37), channel_id=1, source_target_pairs={{0,4},{4,0},{1,5},{5,1},{2,6},{6,2},{3,7},{7,3},{8,12},{12,8},{9,1... | collective-permute-start | bytes 1327112 | tf_op jit(solution)/shard_map/ppermute | solution.py:377
  4.3 10.3 %collective-permute-start.1 = (bf16[2,3,32,768]{3,2,1,0:T(8,128)(2,1)S(1)}, bf16[2,3,32,768]{3,2,1,0:T(8,128)(2,1)S(1)}, u32[]{:S(2)}, u32[]{:S(2)}) collective-permute-start(bf16[2,3,32,768]{3,2,1,0:T(8,128)(2,1)S(1)} %get-tuple-element.20), channel_id=1, source_target_pairs={{0,1},{1,0},{2,3},{3,2},{4,5},{5,4},{6,7},{7,6},{8,9},{9,8},{10,11... | collective-permute-start | bytes 884744 | tf_op jit(solution)/shard_map/ppermute | solution.py:396
  7.3 7.3 %collective-permute-start.2 = (bf16[2,3,32,768]{3,2,1,0:T(8,128)(2,1)S(1)}, bf16[2,3,32,768]{3,2,1,0:T(8,128)(2,1)S(1)}, u32[]{:S(2)}, u32[]{:S(2)}) collective-permute-start(bf16[2,3,32,768]{3,2,1,0:T(8,128)(2,1)S(1)} %get-tuple-element.21), channel_id=1, source_target_pairs={{0,4},{1,2},{2,1},{3,7},{4,0},{5,6},{6,5},{7,3},{8,12},{9,10},{10,... | collective-permute-start | bytes 884744 | tf_op jit(solution)/shard_map/ppermute | solution.py:396
  7.3 5.3 %collective-permute-start.3 = (bf16[64,768]{1,0:T(8,128)(2,1)S(1)}, bf16[64,768]{1,0:T(8,128)(2,1)S(1)}, u32[]{:S(2)}, u32[]{:S(2)}) collective-permute-start(bf16[64,768]{1,0:T(8,128)(2,1)S(1)} %pad_maximum_fusion.1), channel_id=1, source_target_pairs={{0,8},{8,0},{16,24},{24,16},{4,12},{12,4},{20,28},{28,20},{1,9},{9... | collective-permute-start | bytes 294920 | tf_op jit(solution)/shard_map/ppermute | solution.py:401
  8.8 3.7 %collective-permute-start.4 = (bf16[64,768]{1,0:T(8,128)(2,1)S(1)}, bf16[64,768]{1,0:T(8,128)(2,1)S(1)}, u32[]{:S(2)}, u32[]{:S(2)}) collective-permute-start(bf16[64,768]{1,0:T(8,128)(2,1)S(1)} %pad_maximum_fusion.2), channel_id=1, source_target_pairs={{0,4},{8,16},{16,8},{24,28},{4,0},{12,20},{20,12},{28,24},{1,5},{9... | collective-permute-start | bytes 294920 | tf_op jit(solution)/shard_map/ppermute | solution.py:401
  16.0 12.7 %collective-permute-start.8 = (bf16[192,768]{1,0:T(8,128)(2,1)S(1)}, bf16[192,768]{1,0:T(8,128)(2,1)S(1)}, u32[]{:S(2)}, u32[]{:S(2)}) collective-permute-start(bf16[192,768]{1,0:T(8,128)(2,1)S(1)} %get-tuple-element.26.refs_0_), channel_id=1, source_target_pairs={{0,1},{1,2},{2,3},{3,0},{4,5},{5,6},{6,7},{7,4},{8,9},{9,10},{10,1... | collective-permute-start | bytes 884744 | tf_op jit(solution)/shard_map/ppermute | solution.py:432
  18.9 5.8 %collective-permute-start.5 = (bf16[64,896]{1,0:T(8,128)(2,1)S(1)}, bf16[64,896]{1,0:T(8,128)(2,1)S(1)}, u32[]{:S(2)}, u32[]{:S(2)}) collective-permute-start(bf16[64,896]{1,0:T(8,128)(2,1)S(1)} %get-tuple-element.24), channel_id=1, source_target_pairs={{0,8},{8,0},{16,24},{24,16},{4,12},{12,4},{20,28},{28,20},{1,9},{9... | collective-permute-start | bytes 344072 | tf_op jit(solution)/shard_map/ppermute | solution.py:434
  20.7 3.9 %collective-permute-start.6 = (bf16[64,896]{1,0:T(8,128)(2,1)S(1)}, bf16[64,896]{1,0:T(8,128)(2,1)S(1)}, u32[]{:S(2)}, u32[]{:S(2)}) collective-permute-start(bf16[64,896]{1,0:T(8,128)(2,1)S(1)} %get-tuple-element.25), channel_id=1, source_target_pairs={{0,4},{8,16},{16,8},{24,28},{4,0},{12,20},{20,12},{28,24},{1,5},{9... | collective-permute-start | bytes 344072 | tf_op jit(solution)/shard_map/ppermute | solution.py:434
  20.7 12.9 %collective-permute-start.10 = (bf16[192,768]{1,0:T(8,128)(2,1)S(1)}, bf16[192,768]{1,0:T(8,128)(2,1)S(1)}, u32[]{:S(2)}, u32[]{:S(2)}) collective-permute-start(bf16[192,768]{1,0:T(8,128)(2,1)S(1)} %get-tuple-element.26.refs_0_), channel_id=1, source_target_pairs={{0,3},{1,0},{2,1},{3,2},{4,7},{5,4},{6,5},{7,6},{8,11},{9,8},{10,9... | collective-permute-start | bytes 884744 | tf_op jit(solution)/shard_map/ppermute | solution.py:461
  25.6 15.0 %collective-permute-start.11 = (bf16[192,768]{1,0:T(8,128)(2,1)S(1)}, bf16[192,768]{1,0:T(8,128)(2,1)S(1)}, u32[]{:S(2)}, u32[]{:S(2)}) collective-permute-start(bf16[192,768]{1,0:T(8,128)(2,1)S(1)} %bitcast.30), channel_id=1, source_target_pairs={{0,16},{8,24},{16,0},{24,8},{1,17},{9,25},{17,1},{25,9},{2,18},{10... | collective-permute-start | bytes 884744 | tf_op jit(solution)/shard_map/ppermute | solution.py:464
  28.6 12.0 %collective-permute-start.9 = (bf16[192,768]{1,0:T(8,128)(2,1)S(1)}, bf16[192,768]{1,0:T(8,128)(2,1)S(1)}, u32[]{:S(2)}, u32[]{:S(2)}) collective-permute-start(bf16[192,768]{1,0:T(8,128)(2,1)S(1)} %collective-permute-done.8.refs_1_), channel_id=1, source_target_pairs={{0,1},{1,2},{2,3},{3,0},{4,5},{5,6},{6,7},{7,4},{8,9},{9,10},{10,1... | collective-permute-start | bytes 884744 | tf_op jit(solution)/shard_map/ppermute | solution.py:463
  30.5 11.2 %collective-permute-start.17 = (bf16[192,768]{1,0:T(8,128)(2,1)S(1)}, bf16[192,768]{1,0:T(8,128)(2,1)S(1)}, u32[]{:S(2)}, u32[]{:S(2)}) collective-permute-start(bf16[192,768]{1,0:T(8,128)(2,1)S(1)} %bitcast.31), channel_id=1, source_target_pairs={{0,8},{8,16},{16,24},{24,0},{1,9},{9,17},{17,25},{25,1},{2,10},{10... | collective-permute-start | bytes 884744 | tf_op jit(solution)/shard_map/ppermute | solution.py:464
  30.8 12.6 %collective-permute-start.7 = (bf16[192,768]{1,0:T(8,128)(2,1)S(1)}, bf16[192,768]{1,0:T(8,128)(2,1)S(1)}, u32[]{:S(2)}, u32[]{:S(2)}) collective-permute-start(bf16[192,768]{1,0:T(8,128)(2,1)S(1)} %bitcast.32), channel_id=1, source_target_pairs={{0,24},{8,0},{16,8},{24,16},{1,25},{9,1},{17,9},{25,17},{2,26},{10... | collective-permute-start | bytes 884744 | tf_op jit(solution)/shard_map/ppermute | solution.py:464
  42.1 2.0 %collective-permute-start.18 = (bf16[96,768]{1,0:T(8,128)(2,1)S(1)}, bf16[96,768]{1,0:T(8,128)(2,1)S(1)}, u32[]{:S(2)}, u32[]{:S(2)}) collective-permute-start(bf16[96,768]{1,0:T(8,128)(2,1)S(1)} %get-tuple-element.34), channel_id=1, source_target_pairs={{0,4},{4,0},{1,5},{5,1},{2,6},{6,2},{3,7},{7,3},{8,12},{12,8},{9,1... | collective-permute-start | bytes 442376 | tf_op jit(solution)/shard_map/ppermute | solution.py:514
  42.6 2.8 %collective-permute-start.15 = (bf16[96,768]{1,0:T(8,128)(2,1)S(1)}, bf16[96,768]{1,0:T(8,128)(2,1)S(1)}, u32[]{:S(2)}, u32[]{:S(2)}) collective-permute-start(bf16[96,768]{1,0:T(8,128)(2,1)S(1)} %get-tuple-element.32), channel_id=1, source_target_pairs={{0,4},{4,0},{1,5},{5,1},{2,6},{6,2},{3,7},{7,3},{8,12},{12,8},{9,1... | collective-permute-start | bytes 442376 | tf_op jit(solution)/shard_map/ppermute | solution.py:514
  43.2 5.4 %collective-permute-start.14 = (bf16[96,768]{1,0:T(8,128)(2,1)S(1)}, bf16[96,768]{1,0:T(8,128)(2,1)S(1)}, u32[]{:S(2)}, u32[]{:S(2)}) collective-permute-start(bf16[96,768]{1,0:T(8,128)(2,1)S(1)} %get-tuple-element.30), channel_id=1, source_target_pairs={{0,4},{4,0},{1,5},{5,1},{2,6},{6,2},{3,7},{7,3},{8,12},{12,8},{9,1... | collective-permute-start | bytes 442376 | tf_op jit(solution)/shard_map/ppermute | solution.py:514
  43.8 2.9 %collective-permute-start.12 = (bf16[96,768]{1,0:T(8,128)(2,1)S(1)}, bf16[96,768]{1,0:T(8,128)(2,1)S(1)}, u32[]{:S(2)}, u32[]{:S(2)}) collective-permute-start(bf16[96,768]{1,0:T(8,128)(2,1)S(1)} %get-tuple-element.28), channel_id=1, source_target_pairs={{0,4},{4,0},{1,5},{5,1},{2,6},{6,2},{3,7},{7,3},{8,12},{12,8},{9,1... | collective-permute-start | bytes 442376 | tf_op jit(solution)/shard_map/ppermute | solution.py:514
  44.2 6.6 %collective-permute-start.19 = (bf16[96,768]{1,0:T(8,128)(2,1)S(1)}, bf16[96,768]{1,0:T(8,128)(2,1)S(1)}, u32[]{:S(2)}, u32[]{:S(2)}) collective-permute-start(bf16[96,768]{1,0:T(8,128)(2,1)S(1)} %total.7), channel_id=1, source_target_pairs={{0,24},{8,0},{16,8},{24,16},{1,25},{9,1},{17,9},{25,17},{2,26},{10... | collective-permute-start | bytes 442376 | tf_op jit(solution)/shard_map/ppermute | solution.py:516
  45.4 7.7 %collective-permute-start.16 = (bf16[96,768]{1,0:T(8,128)(2,1)S(1)}, bf16[96,768]{1,0:T(8,128)(2,1)S(1)}, u32[]{:S(2)}, u32[]{:S(2)}) collective-permute-start(bf16[96,768]{1,0:T(8,128)(2,1)S(1)} %total.6), channel_id=1, source_target_pairs={{0,16},{8,24},{16,0},{24,8},{1,17},{9,25},{17,1},{25,9},{2,18},{10... | collective-permute-start | bytes 442376 | tf_op jit(solution)/shard_map/ppermute | solution.py:516
  46.8 7.9 %collective-permute-start.13 = (bf16[96,768]{1,0:T(8,128)(2,1)S(1)}, bf16[96,768]{1,0:T(8,128)(2,1)S(1)}, u32[]{:S(2)}, u32[]{:S(2)}) collective-permute-start(bf16[96,768]{1,0:T(8,128)(2,1)S(1)} %total.4), channel_id=1, source_target_pairs={{0,8},{8,16},{16,24},{24,0},{1,9},{9,17},{17,25},{25,1},{2,10},{10... | collective-permute-start | bytes 442376 | tf_op jit(solution)/shard_map/ppermute | solution.py:516

commit v10 on v8

--- a/solution.py
+++ b/solution.py
@@ -32,6 +32,10 @@
             ends = ((row, i), (row, p) if 0 <= p < count else (row ^ 1, i))
             pairs.append(tuple(r * count + j if rows_first else j * n_rows + r for r, j in ends))
     return pairs
+
+
+def exchange(count, step):
+    return cycle(count, step) if count & (count - 1) else [(i, i ^ step) for i in range(count)]
 
 
 def line(count, step):
@@ -461,7 +465,7 @@
         held[n_cols - 1] = lax.ppermute(sent, "wa", cycle(n_cols, -1))
     for s in range(2, n_cols - 1):
         held[s] = lax.ppermute(held[s - 1], "wa", cycle(n_cols, 1))
-    received = [lax.ppermute(attended, "ta", cycle(n_time, s)) for s in range(1, n_time)]
+    received = [lax.ppermute(attended, "ta", exchange(n_time, s)) for s in range(1, n_time)]
 
     def joined(shards, at):
         count = len(shards)
@@ -471,12 +475,12 @@
         return pl.pallas_call(
             functools.partial(join_kernel, count),
             out_shape=jax.ShapeDtypeStruct((count * shards[0].shape[0], wide), mine.dtype),
-            in_specs=[SMEM] + [VMEM] * count + [HBM],
+            in_specs=[SMEM] + [VMEM] * count + [HBM] * 1,
             out_specs=VMEM,
             compiler_params=PARAMS,
             cost_estimate=cost(1000, 2_400_000),
             name="join",
-        )(spots, *shards, (received + [attended] * 2)[1])
+        )(spots, *shards, (received + [attended] * 3)[2])
 
     near = joined([held[s] for s in range(n_cols)], at_col)
     if n_rows > PAIR:
@@ -512,14 +516,17 @@
     for block in [attended, *received]:
         part, given = project(block)
         products.append(total(part, lax.ppermute(given, "ha", pairs)))
+    paired = n_time & (n_time - 1) == 0
     back = [products[0]] + [
-        lax.ppermute(products[n_time - s], "ta", cycle(n_time, s)) for s in range(1, n_time)
+        lax.ppermute(products[s if paired else n_time - s], "ta", exchange(n_time, s))
+        for s in range(1, n_time)
     ]
     late = 1 % n_time
     out = None
     for group in ([s for s in range(n_time) if s != late], [late] if n_time > 1 else []):
         if group:
-            origins = jnp.stack([(at_time - s) % n_time for s in group]).astype(jnp.int32)
+            origins = [at_time ^ s if paired else (at_time - s) % n_time for s in group]
+            origins = jnp.stack(origins).astype(jnp.int32)
             out = pl.pallas_call(
                 functools.partial(place_kernel, len(group)),
                 out_shape=jax.ShapeDtypeStruct((tokens, wide * n_time), jnp.bfloat16),

time: 55.6 us -> 55.6 us (level)
  starting transfers between devices: 24.7 us -> 22.6 us
  waiting for transfers between devices: 18.7 us -> 20.7 us
    ppermute x1, waiting for transfers between devices: 0.01 us -> 2.41 us  [shards(): held[s] = lax.ppermute(held[s - 1], 'wa', cycle(n_cols, 1))]
    ppermute x6, waiting for transfers between devices: 12 us -> 9.74 us  [the longest x3 6.3 us: shards(): lax.ppermute(products[s if paired else n_time - s], 'ta', exchange(n_time...]
    ppermute x1, waiting for transfers between devices: 0.22 us -> 1.99 us  [shards(): held[n_cols - 1] = lax.ppermute(sent, 'wa', cycle(n_cols, -1))]
    ppermute x6, starting transfers between devices: 10.2 us -> 8.72 us  [the longest x3 4.83 us: shards(): lax.ppermute(attended, 'ta', exchange(n_time, s))]
  transfers between devices with their start and end apart: 20 -> 20, of which waited for: 10 -> 11; matrix products, arithmetic and copies ran while one was open for 2% -> 2% of each run, Pallas kernels for 11% -> 11%
where the time goes in v10:
time: 55.6 us; the launch traced here: 55.3 us
  starting transfers between devices  22.6 us (41%)
  waiting for transfers between devices  20.7 us (37%)
  Pallas kernels  9.19 us (17%)
  other arithmetic  1.5 us (3%)
  local copies, waits for them, and re-layouts  1.16 us (2%)
    ppermute x3, waiting for transfers between devices, shards(): lax.ppermute(products[s if paired else n_time - s], 'ta', exchange(n_time...  6.3 us
    ppermute x3, starting transfers between devices, shards(): lax.ppermute(attended, 'ta', exchange(n_time, s))  4.83 us
    ppermute x3, starting transfers between devices, shards(): lax.ppermute(products[s if paired else n_time - s], 'ta', exchange(n_time...  3.89 us
    ppermute x3, waiting for transfers between devices, shards(): lax.ppermute(attended, 'ta', exchange(n_time, s))  3.44 us
    ppermute x2, starting transfers between devices, shards(): lax.ppermute(x, ('ha', 'wa'), swaps(n_cols, phase, n_rows, True))  3 us
    ppermute x1, starting transfers between devices, shards(): held[1] = lax.ppermute(sent, 'wa', cycle(n_cols, 1))  2.91 us
    ppermute x2, waiting for transfers between devices, shards(): lax.ppermute(end, ('ta', 'ha'), swaps(n_time, phase, n_rows, False))  2.66 us
    ppermute x1, waiting for transfers between devices, shards(): held[s] = lax.ppermute(held[s - 1], 'wa', cycle(n_cols, 1))  2.41 us
  transfers between devices with their start and end apart: 20, of which 11 were waited for; matrix products, arithmetic and copies ran while one was open for 2% of the time, Pallas kernels for 11%

profile of v10, /device:TPU:0, one launch (start us, length us, event | category | flops | bytes accessed | tf_op | source)
XLA Modules:
  0.0 55.3 jit_solution(1885567915165522485)
XLA Ops:
  0.0 1.3 %pad_maximum_fusion = bf16[3,3,32,1536]{3,2,1,0:T(8,128)(2,1)S(1)} fusion(bf16[1,3,32,1536]{3,2,1,0:T(8,128)(2,1)} %bitcast.34, bf16[1,3,32,1536]{3,2,1,0:T(8,128)(2,1)} %bitcast.35, bf16[1,3,32,1536]{3,2,1,0:T(8,128)(2,1)} %bitcast.36), kind=kLoop, calls=%fused_computation | loop fusion | flops 884736 | bytes 1769472 | tf_op jit(solution)/shard_map/stack | solution.py:377
  2.3 1.1 %collective-permute-done.refs_1_ = bf16[3,3,32,768]{3,2,1,0:T(8,128)(2,1)S(1)} collective-permute-done((bf16[3,3,32,768]{3,2,1,0:T(8,128)(2,1)S(1)}, bf16[3,3,32,768]{3,2,1,0:T(8,128)(2,1)S(1)}, u32[]{:S(2)}, u32[]{:S(2)}) %collective-permute-start) | collective-permute-done | bytes 442400 | tf_op jit(solution)/shard_map/ppermute | solution.py:381
  4.3 3.0 %collective-permute-start.1 = (bf16[2,3,32,768]{3,2,1,0:T(8,128)(2,1)S(1)}, bf16[2,3,32,768]{3,2,1,0:T(8,128)(2,1)S(1)}, u32[]{:S(2)}, u32[]{:S(2)}) collective-permute-start(bf16[2,3,32,768]{3,2,1,0:T(8,128)(2,1)S(1)} %get-tuple-element.20), channel_id=1, source_target_pairs={{0,1},{1,0},{2,3},{3,2},{4,5},{5,4},{6,7},{7,6},{8,9},{9,8},{10,11... | collective-permute-start | bytes 884744 | tf_op jit(solution)/shard_map/ppermute | solution.py:400
  7.3 1.6 %collective-permute-start.3 = (bf16[64,768]{1,0:T(8,128)(2,1)S(1)}, bf16[64,768]{1,0:T(8,128)(2,1)S(1)}, u32[]{:S(2)}, u32[]{:S(2)}) collective-permute-start(bf16[64,768]{1,0:T(8,128)(2,1)S(1)} %pad_maximum_fusion.1), channel_id=1, source_target_pairs={{0,8},{8,0},{16,24},{24,16},{4,12},{12,4},{20,28},{28,20},{1,9},{9... | collective-permute-start | bytes 294920 | tf_op jit(solution)/shard_map/ppermute | solution.py:405
  9.9 2.7 %collective-permute-done.3.refs_4_ = bf16[64,768]{1,0:T(8,128)(2,1)S(1)} collective-permute-done((bf16[64,768]{1,0:T(8,128)(2,1)S(1)}, bf16[64,768]{1,0:T(8,128)(2,1)S(1)}, u32[]{:S(2)}, u32[]{:S(2)}) %collective-permute-start.3) | collective-permute-done | bytes 98336 | tf_op jit(solution)/shard_map/ppermute | solution.py:405
  12.5 2.0 %collective-permute-done.1.refs_2_ = bf16[2,3,32,768]{3,2,1,0:T(8,128)(2,1)S(1)} collective-permute-done((bf16[2,3,32,768]{3,2,1,0:T(8,128)(2,1)S(1)}, bf16[2,3,32,768]{3,2,1,0:T(8,128)(2,1)S(1)}, u32[]{:S(2)}, u32[]{:S(2)}) %collective-permute-start.1) | collective-permute-done | bytes 294944 | tf_op jit(solution)/shard_map/ppermute | solution.py:400
  14.6 1.4 %guest.1 = (bf16[64,896]{1,0:T(8,128)(2,1)S(1)}, bf16[64,896]{1,0:T(8,128)(2,1)S(1)}, bf16[192,768]{1,0:T(8,128)(2,1)S(1)}) custom-call(s32[7]{0:T(128)S(1)} %stack.73.meta_ref, s32[12,3]{1,0:T(8,128)S(1)} %copy.11.radius_ref, s32[64,128]{1,0:T(8,128)S(1)} %dynamic-slice_bitcast_fusion.4.code_ref, ...), custom_call_target="tpu_custom_call", output_to_operand_aliasing={{2}: (9, {})} | custom-call | flops 50331648 | bytes 4000000 | tf_op jit(solution)/shard_map/guest/pallas_call | solution.py:424
  16.0 2.9 %collective-permute-start.8 = (bf16[192,768]{1,0:T(8,128)(2,1)S(1)}, bf16[192,768]{1,0:T(8,128)(2,1)S(1)}, u32[]{:S(2)}, u32[]{:S(2)}) collective-permute-start(bf16[192,768]{1,0:T(8,128)(2,1)S(1)} %get-tuple-element.26.refs_0_), channel_id=1, source_target_pairs={{0,1},{1,2},{2,3},{3,0},{4,5},{5,6},{6,7},{7,4},{8,9},{9,10},{10,1... | collective-permute-start | bytes 884744 | tf_op jit(solution)/shard_map/ppermute | solution.py:436
  18.9 1.9 %collective-permute-start.5 = (bf16[64,896]{1,0:T(8,128)(2,1)S(1)}, bf16[64,896]{1,0:T(8,128)(2,1)S(1)}, u32[]{:S(2)}, u32[]{:S(2)}) collective-permute-start(bf16[64,896]{1,0:T(8,128)(2,1)S(1)} %get-tuple-element.24), channel_id=1, source_target_pairs={{0,8},{8,0},{16,24},{24,16},{4,12},{12,4},{20,28},{28,20},{1,9},{9... | collective-permute-start | bytes 344072 | tf_op jit(solution)/shard_map/ppermute | solution.py:438
  20.7 1.6 %collective-permute-start.10 = (bf16[192,768]{1,0:T(8,128)(2,1)S(1)}, bf16[192,768]{1,0:T(8,128)(2,1)S(1)}, u32[]{:S(2)}, u32[]{:S(2)}) collective-permute-start(bf16[192,768]{1,0:T(8,128)(2,1)S(1)} %get-tuple-element.26.refs_0_), channel_id=1, source_target_pairs={{0,3},{1,0},{2,1},{3,2},{4,7},{5,4},{6,5},{7,6},{8,11},{9,8},{10,9... | collective-permute-start | bytes 884744 | tf_op jit(solution)/shard_map/ppermute | solution.py:465
  22.4 1.6 %host.1 = (f32[3,64,768]{2,1,0:T(8,128)S(1)}, f32[3,64,128]{2,1,0:T(8,128)S(1)}) custom-call(s32[7]{0:T(128)S(1)} %stack.73.meta_ref, s32[12,3]{1,0:T(8,128)S(1)} %copy.11.radius_ref, s32[64,128]{1,0:T(8,128)S(1)} %dynamic-slice_bitcast_fusion.4.code_ref, bf16[3,3,32,768]{3,2,1,0:T(8,128)(2,1)S(1)} %get-tuple-element.38.refs_0_, ...), custom_call_target="tpu_custom_call" | custom-call | flops 176160768 | bytes 6000000 | tf_op jit(solution)/shard_map/host/pallas_call | solution.py:441
  24.7 1.0 %merge.1 = bf16[2,3,32,768]{3,2,1,0:T(8,128)(2,1)S(1)} custom-call(s32[7]{0:T(128)S(1)} %stack.73.meta_ref, s32[12,3]{1,0:T(8,128)S(1)} %copy.11.radius_ref, f32[3,64,768]{2,1,0:T(8,128)S(1)} %get-tuple-element.22.mixed_ref, f32[3,64,128]{2,1,0:T(8,128)S(1)} %get-tuple-element.23.stats_ref, bf16[64,896]{1,0:T(8,128)(2,1)S(1)} %collective-permute-done.5.ref_0, ...), custom_call_target="tpu_custom_call" | custom-call | flops 1000 | bytes 3000000 | tf_op jit(solution)/shard_map/merge/pallas_call | solution.py:453
  25.6 2.0 %collective-permute-start.11 = (bf16[192,768]{1,0:T(8,128)(2,1)S(1)}, bf16[192,768]{1,0:T(8,128)(2,1)S(1)}, u32[]{:S(2)}, u32[]{:S(2)}) collective-permute-start(bf16[192,768]{1,0:T(8,128)(2,1)S(1)} %bitcast.30), channel_id=1, source_target_pairs={{0,24},{8,16},{16,8},{24,0},{1,25},{9,17},{17,9},{25,1},{2,26},{10... | collective-permute-start | bytes 884744 | tf_op jit(solution)/shard_map/ppermute | solution.py:468
  27.7 1.4 %collective-permute-start.9 = (bf16[192,768]{1,0:T(8,128)(2,1)S(1)}, bf16[192,768]{1,0:T(8,128)(2,1)S(1)}, u32[]{:S(2)}, u32[]{:S(2)}) collective-permute-start(bf16[192,768]{1,0:T(8,128)(2,1)S(1)} %collective-permute-done.8.refs_1_), channel_id=1, source_target_pairs={{0,1},{1,2},{2,3},{3,0},{4,5},{5,6},{6,7},{7,4},{8,9},{9,10},{10,1... | collective-permute-start | bytes 884744 | tf_op jit(solution)/shard_map/ppermute | solution.py:467
  29.2 2.7 %collective-permute-start.15 = (bf16[192,768]{1,0:T(8,128)(2,1)S(1)}, bf16[192,768]{1,0:T(8,128)(2,1)S(1)}, u32[]{:S(2)}, u32[]{:S(2)}) collective-permute-start(bf16[192,768]{1,0:T(8,128)(2,1)S(1)} %bitcast.31), channel_id=1, source_target_pairs={{0,16},{8,24},{16,0},{24,8},{1,17},{9,25},{17,1},{25,9},{2,18},{10... | collective-permute-start | bytes 884744 | tf_op jit(solution)/shard_map/ppermute | solution.py:468
  32.1 2.0 %collective-permute-done.10.refs_3_ = bf16[192,768]{1,0:T(8,128)(2,1)S(1)} collective-permute-done((bf16[192,768]{1,0:T(8,128)(2,1)S(1)}, bf16[192,768]{1,0:T(8,128)(2,1)S(1)}, u32[]{:S(2)}, u32[]{:S(2)}) %collective-permute-start.10) | collective-permute-done | bytes 294944 | tf_op jit(solution)/shard_map/ppermute | solution.py:465
  34.0 2.5 %collective-permute-done.11.refs_4_.rows = bf16[192,768]{1,0:T(8,128)(2,1)S(1)} collective-permute-done((bf16[192,768]{1,0:T(8,128)(2,1)S(1)}, bf16[192,768]{1,0:T(8,128)(2,1)S(1)}, u32[]{:S(2)}, u32[]{:S(2)}) %collective-permute-start.11) | collective-permute-done | bytes 294944 | tf_op jit(solution)/shard_map/ppermute | solution.py:468
  36.6 2.4 %collective-permute-done.9.refs_2_ = bf16[192,768]{1,0:T(8,128)(2,1)S(1)} collective-permute-done((bf16[192,768]{1,0:T(8,128)(2,1)S(1)}, bf16[192,768]{1,0:T(8,128)(2,1)S(1)}, u32[]{:S(2)}, u32[]{:S(2)}) %collective-permute-start.9) | collective-permute-done | bytes 294944 | tf_op jit(solution)/shard_map/ppermute | solution.py:467
  40.5 0.9 %collective-permute-done.15.rows = bf16[192,768]{1,0:T(8,128)(2,1)S(1)} collective-permute-done((bf16[192,768]{1,0:T(8,128)(2,1)S(1)}, bf16[192,768]{1,0:T(8,128)(2,1)S(1)}, u32[]{:S(2)}, u32[]{:S(2)}) %collective-permute-start.15) | collective-permute-done | bytes 294944 | tf_op jit(solution)/shard_map/ppermute | solution.py:468
  43.0 1.9 %collective-permute-start.19 = (bf16[96,768]{1,0:T(8,128)(2,1)S(1)}, bf16[96,768]{1,0:T(8,128)(2,1)S(1)}, u32[]{:S(2)}, u32[]{:S(2)}) collective-permute-start(bf16[96,768]{1,0:T(8,128)(2,1)S(1)} %total.7), channel_id=1, source_target_pairs={{0,24},{8,16},{16,8},{24,0},{1,25},{9,17},{17,9},{25,1},{2,26},{10... | collective-permute-start | bytes 442376 | tf_op jit(solution)/shard_map/ppermute | solution.py:521
  45.0 1.8 %collective-permute-start.17 = (bf16[96,768]{1,0:T(8,128)(2,1)S(1)}, bf16[96,768]{1,0:T(8,128)(2,1)S(1)}, u32[]{:S(2)}, u32[]{:S(2)}) collective-permute-start(bf16[96,768]{1,0:T(8,128)(2,1)S(1)} %total.6), channel_id=1, source_target_pairs={{0,16},{8,24},{16,0},{24,8},{1,17},{9,25},{17,1},{25,9},{2,18},{10... | collective-permute-start | bytes 442376 | tf_op jit(solution)/shard_map/ppermute | solution.py:521
  47.0 3.6 %collective-permute-done.19.refs_2_ = bf16[96,768]{1,0:T(8,128)(2,1)S(1)} collective-permute-done((bf16[96,768]{1,0:T(8,128)(2,1)S(1)}, bf16[96,768]{1,0:T(8,128)(2,1)S(1)}, u32[]{:S(2)}, u32[]{:S(2)}) %collective-permute-start.19) | collective-permute-done | bytes 147488 | tf_op jit(solution)/shard_map/ppermute | solution.py:521
  50.7 2.7 %collective-permute-done.17.refs_1_ = bf16[96,768]{1,0:T(8,128)(2,1)S(1)} collective-permute-done((bf16[96,768]{1,0:T(8,128)(2,1)S(1)}, bf16[96,768]{1,0:T(8,128)(2,1)S(1)}, u32[]{:S(2)}, u32[]{:S(2)}) %collective-permute-start.17) | collective-permute-done | bytes 147488 | tf_op jit(solution)/shard_map/ppermute | solution.py:521
  53.3 1.3 %place.2.refs_1_ = bf16[96,3072]{1,0:T(8,128)(2,1)} custom-call(s32[3]{0:T(128)S(1)} %pad_add_fusion.1.meta_ref, bf16[96,768]{1,0:T(8,128)(2,1)S(1)} %total.5.refs_0_, bf16[96,768]{1,0:T(8,128)(2,1)S(1)} %collective-permute-done.17.refs_1_, bf16[96,768]{1,0:T(8,128)(2,1)S(1)} %collective-permute-done.19.refs_2_), custom_call_target="tpu_custom_call" | custom-call | flops 1000 | bytes 1200000 | tf_op jit(solution)/shard_map/place/pallas_call | solution.py:530
  (48 shorter events, 7.8 us)
Async XLA Ops:
  0.0 2.2 %copy-start = (bf16[192,3072]{1,0:T(8,128)(2,1)S(1)}, bf16[192,3072]{1,0:T(8,128)(2,1)}, u32[]{:S(2)}) copy-start(bf16[192,3072]{1,0:T(8,128)(2,1)} %param.10) | copy-start | bytes 3538948
  1.3 0.7 %copy-start.1 = (s32[12,3]{0,1:T(4,128)S(1)}, s32[12,3]{0,1:T(4,128)}, u32[]{:S(2)}) copy-start(s32[12,3]{0,1:T(4,128)} %param.9) | copy-start | bytes 436
  1.4 1.9 %collective-permute-start = (bf16[3,3,32,768]{3,2,1,0:T(8,128)(2,1)S(1)}, bf16[3,3,32,768]{3,2,1,0:T(8,128)(2,1)S(1)}, u32[]{:S(2)}, u32[]{:S(2)}) collective-permute-start(bf16[3,3,32,768]{3,2,1,0:T(8,128)(2,1)S(1)} %get-tuple-element.37), channel_id=1, source_target_pairs={{0,4},{4,0},{1,5},{5,1},{2,6},{6,2},{3,7},{7,3},{8,12},{12,8},{9,1... | collective-permute-start | bytes 1327112 | tf_op jit(solution)/shard_map/ppermute | solution.py:381
  4.3 10.3 %collective-permute-start.1 = (bf16[2,3,32,768]{3,2,1,0:T(8,128)(2,1)S(1)}, bf16[2,3,32,768]{3,2,1,0:T(8,128)(2,1)S(1)}, u32[]{:S(2)}, u32[]{:S(2)}) collective-permute-start(bf16[2,3,32,768]{3,2,1,0:T(8,128)(2,1)S(1)} %get-tuple-element.20), channel_id=1, source_target_pairs={{0,1},{1,0},{2,3},{3,2},{4,5},{5,4},{6,7},{7,6},{8,9},{9,8},{10,11... | collective-permute-start | bytes 884744 | tf_op jit(solution)/shard_map/ppermute | solution.py:400
  7.3 7.3 %collective-permute-start.2 = (bf16[2,3,32,768]{3,2,1,0:T(8,128)(2,1)S(1)}, bf16[2,3,32,768]{3,2,1,0:T(8,128)(2,1)S(1)}, u32[]{:S(2)}, u32[]{:S(2)}) collective-permute-start(bf16[2,3,32,768]{3,2,1,0:T(8,128)(2,1)S(1)} %get-tuple-element.21), channel_id=1, source_target_pairs={{0,4},{1,2},{2,1},{3,7},{4,0},{5,6},{6,5},{7,3},{8,12},{9,10},{10,... | collective-permute-start | bytes 884744 | tf_op jit(solution)/shard_map/ppermute | solution.py:400
  7.3 5.3 %collective-permute-start.3 = (bf16[64,768]{1,0:T(8,128)(2,1)S(1)}, bf16[64,768]{1,0:T(8,128)(2,1)S(1)}, u32[]{:S(2)}, u32[]{:S(2)}) collective-permute-start(bf16[64,768]{1,0:T(8,128)(2,1)S(1)} %pad_maximum_fusion.1), channel_id=1, source_target_pairs={{0,8},{8,0},{16,24},{24,16},{4,12},{12,4},{20,28},{28,20},{1,9},{9... | collective-permute-start | bytes 294920 | tf_op jit(solution)/shard_map/ppermute | solution.py:405
  8.8 3.7 %collective-permute-start.4 = (bf16[64,768]{1,0:T(8,128)(2,1)S(1)}, bf16[64,768]{1,0:T(8,128)(2,1)S(1)}, u32[]{:S(2)}, u32[]{:S(2)}) collective-permute-start(bf16[64,768]{1,0:T(8,128)(2,1)S(1)} %pad_maximum_fusion.2), channel_id=1, source_target_pairs={{0,4},{8,16},{16,8},{24,28},{4,0},{12,20},{20,12},{28,24},{1,5},{9... | collective-permute-start | bytes 294920 | tf_op jit(solution)/shard_map/ppermute | solution.py:405
  16.0 11.8 %collective-permute-start.8 = (bf16[192,768]{1,0:T(8,128)(2,1)S(1)}, bf16[192,768]{1,0:T(8,128)(2,1)S(1)}, u32[]{:S(2)}, u32[]{:S(2)}) collective-permute-start(bf16[192,768]{1,0:T(8,128)(2,1)S(1)} %get-tuple-element.26.refs_0_), channel_id=1, source_target_pairs={{0,1},{1,2},{2,3},{3,0},{4,5},{5,6},{6,7},{7,4},{8,9},{9,10},{10,1... | collective-permute-start | bytes 884744 | tf_op jit(solution)/shard_map/ppermute | solution.py:436
  18.9 5.8 %collective-permute-start.5 = (bf16[64,896]{1,0:T(8,128)(2,1)S(1)}, bf16[64,896]{1,0:T(8,128)(2,1)S(1)}, u32[]{:S(2)}, u32[]{:S(2)}) collective-permute-start(bf16[64,896]{1,0:T(8,128)(2,1)S(1)} %get-tuple-element.24), channel_id=1, source_target_pairs={{0,8},{8,0},{16,24},{24,16},{4,12},{12,4},{20,28},{28,20},{1,9},{9... | collective-permute-start | bytes 344072 | tf_op jit(solution)/shard_map/ppermute | solution.py:438
  20.7 3.9 %collective-permute-start.6 = (bf16[64,896]{1,0:T(8,128)(2,1)S(1)}, bf16[64,896]{1,0:T(8,128)(2,1)S(1)}, u32[]{:S(2)}, u32[]{:S(2)}) collective-permute-start(bf16[64,896]{1,0:T(8,128)(2,1)S(1)} %get-tuple-element.25), channel_id=1, source_target_pairs={{0,4},{8,16},{16,8},{24,28},{4,0},{12,20},{20,12},{28,24},{1,5},{9... | collective-permute-start | bytes 344072 | tf_op jit(solution)/shard_map/ppermute | solution.py:438
  20.7 13.3 %collective-permute-start.10 = (bf16[192,768]{1,0:T(8,128)(2,1)S(1)}, bf16[192,768]{1,0:T(8,128)(2,1)S(1)}, u32[]{:S(2)}, u32[]{:S(2)}) collective-permute-start(bf16[192,768]{1,0:T(8,128)(2,1)S(1)} %get-tuple-element.26.refs_0_), channel_id=1, source_target_pairs={{0,3},{1,0},{2,1},{3,2},{4,7},{5,4},{6,5},{7,6},{8,11},{9,8},{10,9... | collective-permute-start | bytes 884744 | tf_op jit(solution)/shard_map/ppermute | solution.py:465
  25.6 10.9 %collective-permute-start.11 = (bf16[192,768]{1,0:T(8,128)(2,1)S(1)}, bf16[192,768]{1,0:T(8,128)(2,1)S(1)}, u32[]{:S(2)}, u32[]{:S(2)}) collective-permute-start(bf16[192,768]{1,0:T(8,128)(2,1)S(1)} %bitcast.30), channel_id=1, source_target_pairs={{0,24},{8,16},{16,8},{24,0},{1,25},{9,17},{17,9},{25,1},{2,26},{10... | collective-permute-start | bytes 884744 | tf_op jit(solution)/shard_map/ppermute | solution.py:468
  27.7 11.3 %collective-permute-start.9 = (bf16[192,768]{1,0:T(8,128)(2,1)S(1)}, bf16[192,768]{1,0:T(8,128)(2,1)S(1)}, u32[]{:S(2)}, u32[]{:S(2)}) collective-permute-start(bf16[192,768]{1,0:T(8,128)(2,1)S(1)} %collective-permute-done.8.refs_1_), channel_id=1, source_target_pairs={{0,1},{1,2},{2,3},{3,0},{4,5},{5,6},{6,7},{7,4},{8,9},{9,10},{10,1... | collective-permute-start | bytes 884744 | tf_op jit(solution)/shard_map/ppermute | solution.py:467
  29.2 12.2 %collective-permute-start.15 = (bf16[192,768]{1,0:T(8,128)(2,1)S(1)}, bf16[192,768]{1,0:T(8,128)(2,1)S(1)}, u32[]{:S(2)}, u32[]{:S(2)}) collective-permute-start(bf16[192,768]{1,0:T(8,128)(2,1)S(1)} %bitcast.31), channel_id=1, source_target_pairs={{0,16},{8,24},{16,0},{24,8},{1,17},{9,25},{17,1},{25,9},{2,18},{10... | collective-permute-start | bytes 884744 | tf_op jit(solution)/shard_map/ppermute | solution.py:468
  31.9 10.5 %collective-permute-start.7 = (bf16[192,768]{1,0:T(8,128)(2,1)S(1)}, bf16[192,768]{1,0:T(8,128)(2,1)S(1)}, u32[]{:S(2)}, u32[]{:S(2)}) collective-permute-start(bf16[192,768]{1,0:T(8,128)(2,1)S(1)} %bitcast.32), channel_id=1, source_target_pairs={{0,8},{8,0},{16,24},{24,16},{1,9},{9,1},{17,25},{25,17},{2,10},{10... | collective-permute-start | bytes 884744 | tf_op jit(solution)/shard_map/ppermute | solution.py:468
  40.4 2.5 %collective-permute-start.18 = (f32[96,768]{1,0:T(8,128)S(1)}, f32[96,768]{1,0:T(8,128)S(1)}, u32[]{:S(2)}, u32[]{:S(2)}) collective-permute-start(f32[96,768]{1,0:T(8,128)S(1)} %get-tuple-element.34), channel_id=1, source_target_pairs={{0,4},{4,0},{1,5},{5,1},{2,6},{6,2},{3,7},{7,3},{8,12},{12,8},{9,1... | collective-permute-start | bytes 884744 | tf_op jit(solution)/shard_map/ppermute | solution.py:518
  41.8 3.1 %collective-permute-start.16 = (f32[96,768]{1,0:T(8,128)S(1)}, f32[96,768]{1,0:T(8,128)S(1)}, u32[]{:S(2)}, u32[]{:S(2)}) collective-permute-start(f32[96,768]{1,0:T(8,128)S(1)} %get-tuple-element.32), channel_id=1, source_target_pairs={{0,4},{4,0},{1,5},{5,1},{2,6},{6,2},{3,7},{7,3},{8,12},{12,8},{9,1... | collective-permute-start | bytes 884744 | tf_op jit(solution)/shard_map/ppermute | solution.py:518
  41.9 5.1 %collective-permute-start.14 = (f32[96,768]{1,0:T(8,128)S(1)}, f32[96,768]{1,0:T(8,128)S(1)}, u32[]{:S(2)}, u32[]{:S(2)}) collective-permute-start(f32[96,768]{1,0:T(8,128)S(1)} %get-tuple-element.30), channel_id=1, source_target_pairs={{0,4},{4,0},{1,5},{5,1},{2,6},{6,2},{3,7},{7,3},{8,12},{12,8},{9,1... | collective-permute-start | bytes 884744 | tf_op jit(solution)/shard_map/ppermute | solution.py:518
  42.8 4.0 %collective-permute-start.12 = (f32[96,768]{1,0:T(8,128)S(1)}, f32[96,768]{1,0:T(8,128)S(1)}, u32[]{:S(2)}, u32[]{:S(2)}) collective-permute-start(f32[96,768]{1,0:T(8,128)S(1)} %get-tuple-element.28), channel_id=1, source_target_pairs={{0,4},{4,0},{1,5},{5,1},{2,6},{6,2},{3,7},{7,3},{8,12},{12,8},{9,1... | collective-permute-start | bytes 884744 | tf_op jit(solution)/shard_map/ppermute | solution.py:518
  43.0 7.7 %collective-permute-start.19 = (bf16[96,768]{1,0:T(8,128)(2,1)S(1)}, bf16[96,768]{1,0:T(8,128)(2,1)S(1)}, u32[]{:S(2)}, u32[]{:S(2)}) collective-permute-start(bf16[96,768]{1,0:T(8,128)(2,1)S(1)} %total.7), channel_id=1, source_target_pairs={{0,24},{8,16},{16,8},{24,0},{1,25},{9,17},{17,9},{25,1},{2,26},{10... | collective-permute-start | bytes 442376 | tf_op jit(solution)/shard_map/ppermute | solution.py:521
  45.0 8.4 %collective-permute-start.17 = (bf16[96,768]{1,0:T(8,128)(2,1)S(1)}, bf16[96,768]{1,0:T(8,128)(2,1)S(1)}, u32[]{:S(2)}, u32[]{:S(2)}) collective-permute-start(bf16[96,768]{1,0:T(8,128)(2,1)S(1)} %total.6), channel_id=1, source_target_pairs={{0,16},{8,24},{16,0},{24,8},{1,17},{9,25},{17,1},{25,9},{2,18},{10... | collective-permute-start | bytes 442376 | tf_op jit(solution)/shard_map/ppermute | solution.py:521
  46.8 7.8 %collective-permute-start.13 = (bf16[96,768]{1,0:T(8,128)(2,1)S(1)}, bf16[96,768]{1,0:T(8,128)(2,1)S(1)}, u32[]{:S(2)}, u32[]{:S(2)}) collective-permute-start(bf16[96,768]{1,0:T(8,128)(2,1)S(1)} %total.4), channel_id=1, source_target_pairs={{0,8},{8,0},{16,24},{24,16},{1,9},{9,1},{17,25},{25,17},{2,10},{10... | collective-permute-start | bytes 442376 | tf_op jit(solution)/shard_map/ppermute | solution.py:521
